TPU v7x, 32 devices: a whole 2x2x4 slice. The times are simulated.
32 devices in a mesh: section: 2 (over core), ctx: 4 (over y, x), tp: 4 (over z).
Axes of the slice: x: 2, y: 2, z: 4, core: 2. Of those that a mesh axis runs over, the one named last changes fastest.
Arguments:
- inputs: bfloat16 [2, 4096, 1024], P(None, ('ctx', 'tp')), may hold values from -6 to 6
- cotangent: bfloat16 [2, 4096, 1024], P(None, ('ctx', 'tp')), may hold values from -6 to 6
- lengths: int32 [2, 4], replicated, may hold values from 1 to 3074, 4096 in all within a row
- gain1: bfloat16 [2, 1024], P('section'), may hold values from 0.5 to 1.5
- wqkv: bfloat16 [2, 3, 16, 64, 1024], P('section', None, 'tp'), may hold values from -0.1875 to 0.1875
- wo: bfloat16 [2, 1024, 1024], P('section', 'tp'), may hold values from -0.75 to 0.75
- gain2: bfloat16 [2, 1024], P('section'), may hold values from 0.5 to 1.5
- wgu: bfloat16 [2, 2, 2816, 1024], P('section', None, 'tp'), may hold values from -0.1875 to 0.1875
- wd: bfloat16 [2, 2816, 1024], P('section', 'tp'), may hold values from -0.109375 to 0.109375
Outputs:
- acts: bfloat16 [2, 2, 4096, 1024], P('section', None, ('ctx', 'tp'))
- input_grads: float32 [2, 2, 4096, 1024], P('section', None, ('ctx', 'tp'))
- grad_gain1: float32 [2, 1024], P('section')
- grad_wqkv: float32 [2, 3, 16, 64, 1024], P('section', None, 'tp')
- grad_wo: float32 [2, 1024, 1024], P('section', 'tp')
- grad_gain2: float32 [2, 1024], P('section')
- grad_wgu: float32 [2, 2, 2816, 1024], P('section', None, 'tp')
- grad_wd: float32 [2, 2816, 1024], P('section', 'tp')
Inputs may be any that keep to these rules, and one draw needn't show every extreme that they name: In each micro-batch the 4 lengths sum to 4096 and the longest is exactly 3074.
All inputs are finite; a program needn't handle non-finite values.
Results may differ from a plain program's by a relative error of at most 0.03.
Values may be sent and summed in bfloat16 or wider, within the bound.
No kernel may reach another device: no remote copies, remote signals or barrier semaphores. Data moves between devices by JAX's collectives and lax.ppermute only.
A program may use at most 256 MiB of HBM per device.

v0:
```python
import jax
import jax.numpy as jnp
from jax import lax
from jax.sharding import PartitionSpec as P

HD = 64


EPSILON = 1e-06


def shifted(block, axis, distance):
    devices = range(lax.axis_size(axis))
    route = [(i - distance, i) for i in devices if i - distance in devices]
    return lax.ppermute(block, axis, route)


def rope_parts(position):
    half_width = HD // 2
    frequency = jnp.exp(-jnp.log(10000.0) * jnp.arange(half_width, dtype=jnp.float32) / half_width)
    angles = position.astype(jnp.float32)[:, None] * frequency[None, :]
    return (jnp.cos(angles), jnp.sin(angles))


def rotate(vectors, cosine, sine_part):
    half_width = HD // 2
    leading_half = vectors[..., :half_width]
    trailing_half = vectors[..., half_width:]
    cosine = cosine[:, None, :]
    sine_part = sine_part[:, None, :]
    return jnp.concatenate(
        [
            leading_half * cosine - trailing_half * sine_part,
            trailing_half * cosine + leading_half * sine_part,
        ],
        axis=-1,
    )


def rotate_back(vectors, cosine, sine_part):
    half_width = HD // 2
    leading_half = vectors[..., :half_width]
    trailing_half = vectors[..., half_width:]
    cosine = cosine[:, None, :]
    sine_part = sine_part[:, None, :]
    return jnp.concatenate(
        [
            leading_half * cosine + trailing_half * sine_part,
            trailing_half * cosine - leading_half * sine_part,
        ],
        axis=-1,
    )


def inner_rows(left, right):
    return lax.dot_general(
        left, right, (((0,), (0,)), ((), ())), preferred_element_type=jnp.float32
    )


def outer_cols(left, right):
    return lax.dot_general(
        left, right, (((1,), (1,)), ((), ())), preferred_element_type=jnp.float32
    )


def spread(row_block):
    return lax.all_gather(row_block, "tp", axis=0, tiled=True)


def collect(partial_value):
    return lax.psum_scatter(
        partial_value.astype(jnp.bfloat16), "tp", scatter_dimension=0, tiled=True
    ).astype(jnp.float32)


def fetch_keys(key_value):
    return lax.all_gather(key_value, "ctx", axis=0, tiled=True)


def query_bounds(seq_lengths, block_first, row_count):
    token_index = block_first + jnp.arange(row_count, dtype=jnp.int32)
    doc_ends = jnp.cumsum(seq_lengths)
    before = (doc_ends[None, :] <= token_index[:, None]).astype(jnp.int32)
    doc_start = jnp.sum(before * seq_lengths[None, :], axis=1)
    return (token_index, doc_start)


def block_scores(query_heads, pair_block, block_first, token_index, doc_start, head_width):
    row_count = pair_block.shape[0]
    key_heads = pair_block[:, :head_width].reshape(row_count, head_width // HD, HD)
    value_heads = pair_block[:, head_width:].reshape(row_count, head_width // HD, HD)
    scores = jnp.einsum(
        "qhd,khd->hqk", query_heads, key_heads, preferred_element_type=jnp.float32
    ) * HD ** (-0.5)
    key_index = block_first + jnp.arange(row_count, dtype=jnp.int32)
    allowed = (key_index[None, :] >= doc_start[:, None]) & (
        key_index[None, :] <= token_index[:, None]
    )
    return (scores, allowed[None], key_heads, value_heads)


def split_blocks(pairs_all, row_count):
    blocks = pairs_all.reshape(-1, row_count, pairs_all.shape[1])
    block_starts = jnp.arange(blocks.shape[0], dtype=jnp.int32) * row_count
    return (blocks, block_starts)


def attend(query_heads, pairs_all, token_index, doc_start, head_width):
    row_count = query_heads.shape[0]
    head_count = head_width // HD
    blocks, block_starts = split_blocks(pairs_all, row_count)
    last_query = token_index[row_count - 1]
    first_query = doc_start[0]

    def rowmax_live(carried, block_parts):
        running_top, running_sum = carried
        scores, allowed, unused_keys, unused_values = block_scores(
            query_heads, block_parts[0], block_parts[1], token_index, doc_start, head_width
        )
        masked = jnp.where(allowed, scores, -1e30)
        new_top = jnp.maximum(running_top, jnp.max(masked, axis=-1))
        running_sum = running_sum * jnp.exp(running_top - new_top) + jnp.sum(
            jnp.where(allowed, jnp.exp(masked - new_top[..., None]), 0.0), axis=-1
        )
        return (new_top, running_sum)

    def rowmax_step(carried, block_parts):
        live = (block_parts[1] <= last_query) & (block_parts[1] + row_count > first_query)
        return (
            lax.cond(live, lambda held: rowmax_live(held, block_parts), lambda held: held, carried),
            None,
        )

    initial = (
        jnp.full((head_count, row_count), -1e30, jnp.float32),
        jnp.zeros((head_count, row_count), jnp.float32),
    )
    (running_top, running_sum), unused = lax.scan(rowmax_step, initial, (blocks, block_starts))
    log_total = running_top + jnp.log(running_sum)

    def output_live(accumulated, block_parts):
        scores, allowed, unused_keys, value_heads = block_scores(
            query_heads, block_parts[0], block_parts[1], token_index, doc_start, head_width
        )
        soft_weights = jnp.where(allowed, jnp.exp(scores - log_total[..., None]), 0.0).astype(
            jnp.bfloat16
        )
        return accumulated + jnp.einsum(
            "hqk,khd->qhd", soft_weights, value_heads, preferred_element_type=jnp.float32
        )

    def output_step(accumulated, block_parts):
        live = (block_parts[1] <= last_query) & (block_parts[1] + row_count > first_query)
        return (
            lax.cond(
                live, lambda held: output_live(held, block_parts), lambda held: held, accumulated
            ),
            None,
        )

    accumulated, unused = lax.scan(
        output_step, jnp.zeros((row_count, head_count, HD), jnp.float32), (blocks, block_starts)
    )
    return (accumulated, log_total)


def attend_back(
    query_heads, pairs_all, token_index, doc_start, head_width, log_total, accumulated, grad_heads
):
    row_count = query_heads.shape[0]
    head_count = head_width // HD
    blocks, block_starts = split_blocks(pairs_all, row_count)
    last_query = token_index[row_count - 1]
    first_query = doc_start[0]
    rowdot = jnp.sum(grad_heads.astype(jnp.float32) * accumulated, axis=-1).T

    def grad_live(grad_acc, block_parts):
        scores, allowed, key_heads, value_heads = block_scores(
            query_heads, block_parts[0], block_parts[1], token_index, doc_start, head_width
        )
        soft_weights = jnp.where(allowed, jnp.exp(scores - log_total[..., None]), 0.0)
        grad_soft = jnp.einsum(
            "qhd,khd->hqk", grad_heads, value_heads, preferred_element_type=jnp.float32
        )
        grad_scores = (soft_weights * (grad_soft - rowdot[..., None])).astype(jnp.bfloat16)
        grad_acc = grad_acc + jnp.einsum(
            "hqk,khd->qhd", grad_scores, key_heads, preferred_element_type=jnp.float32
        )
        grad_keys = jnp.einsum(
            "hqk,qhd->khd", grad_scores, query_heads, preferred_element_type=jnp.float32
        ) * HD ** (-0.5)
        grad_values = jnp.einsum(
            "hqk,qhd->khd",
            soft_weights.astype(jnp.bfloat16),
            grad_heads,
            preferred_element_type=jnp.float32,
        )
        return (grad_acc, (grad_keys, grad_values))

    def grad_skip(grad_acc):
        empty = jnp.zeros((row_count, head_count, HD), jnp.float32)
        return (grad_acc, (empty, empty))

    def grad_step(grad_acc, block_parts):
        live = (block_parts[1] <= last_query) & (block_parts[1] + row_count > first_query)
        return lax.cond(live, lambda held: grad_live(held, block_parts), grad_skip, grad_acc)

    grad_query, (grad_keys, grad_values) = lax.scan(
        grad_step, jnp.zeros((row_count, head_count, HD), jnp.float32), (blocks, block_starts)
    )
    grad_query = grad_query * HD ** (-0.5)
    grad_pairs = jnp.concatenate(
        [grad_keys.reshape(-1, head_width), grad_values.reshape(-1, head_width)], axis=1
    )
    return (grad_query, grad_pairs)


def norm_back(whole_rows, scale_rows, gain, grad_normed, grad_rest):
    unit_rows = whole_rows * scale_rows
    scaled = grad_normed * gain.astype(jnp.float32)
    grad_gain = jnp.sum(grad_normed * unit_rows, axis=0)
    grad_whole = grad_rest + scale_rows * (
        scaled - unit_rows * jnp.mean(scaled * unit_rows, axis=-1, keepdims=True)
    )
    return (grad_gain, grad_whole)


def layer_forward(row_block, first_values, value_mix, weights, seq_lengths):
    gain_first, w_qkv, w_out, gain_second, w_gateup, w_down = weights
    head_count = w_qkv.shape[1]
    head_width = head_count * HD
    model_width = row_block.shape[1]
    whole_rows = row_block.astype(jnp.float32)
    scale_first = lax.rsqrt(jnp.mean(whole_rows * whole_rows, axis=-1, keepdims=True) + EPSILON)
    normed = (whole_rows * scale_first * gain_first.astype(jnp.float32)).astype(jnp.bfloat16)
    normed_all = spread(normed)
    row_count = normed_all.shape[0]
    projected = outer_cols(normed_all, w_qkv.reshape(3 * head_width, model_width))
    token_index, doc_start = query_bounds(seq_lengths, lax.axis_index("ctx") * row_count, row_count)
    cosine, sine_part = rope_parts(token_index - doc_start)
    query_heads = rotate(
        projected[:, :head_width].reshape(row_count, head_count, HD), cosine, sine_part
    ).astype(jnp.bfloat16)
    key_heads = rotate(
        projected[:, head_width : 2 * head_width].reshape(row_count, head_count, HD),
        cosine,
        sine_part,
    ).astype(jnp.bfloat16)
    mixed = (
        (1.0 - value_mix) * projected[:, 2 * head_width :]
        + value_mix * first_values.astype(jnp.float32)
    ).astype(jnp.bfloat16)
    key_value = jnp.concatenate([key_heads.reshape(row_count, head_width), mixed], axis=1)
    pairs_all = fetch_keys(key_value)
    accumulated, log_total = attend(query_heads, pairs_all, token_index, doc_start, head_width)
    attended = accumulated.reshape(row_count, head_width).astype(jnp.bfloat16)
    hidden = whole_rows + collect(jnp.dot(attended, w_out, preferred_element_type=jnp.float32))
    scale_second = lax.rsqrt(jnp.mean(hidden * hidden, axis=-1, keepdims=True) + EPSILON)
    normed_second = (hidden * scale_second * gain_second.astype(jnp.float32)).astype(jnp.bfloat16)
    ffn_rows = spread(normed_second)
    gate_up = outer_cols(ffn_rows, w_gateup.reshape(-1, model_width))
    unit_count = gate_up.shape[1] // 2
    gate_part = gate_up[:, :unit_count]
    up_part = gate_up[:, unit_count:]
    activated = (jax.nn.silu(gate_part) * up_part).astype(jnp.bfloat16)
    down_part = jnp.dot(activated, w_down, preferred_element_type=jnp.float32)
    branch_out = collect(down_part)
    layer_out = (hidden + branch_out).astype(jnp.bfloat16)
    saved = (
        whole_rows,
        scale_first,
        normed_all,
        query_heads,
        pairs_all,
        token_index,
        doc_start,
        cosine,
        sine_part,
        log_total,
        accumulated,
        attended,
        hidden,
        scale_second,
        ffn_rows,
        gate_part,
        up_part,
        activated,
    )
    return (layer_out, mixed, pairs_all, saved)


def layer_backward(grad_rows, extra_values, value_mix, weights, saved):
    gain_first, w_qkv, w_out, gain_second, w_gateup, w_down = weights
    (
        whole_rows,
        scale_first,
        normed_all,
        query_heads,
        pairs_all,
        token_index,
        doc_start,
        cosine,
        sine_part,
        log_total,
        accumulated,
        attended,
        hidden,
        scale_second,
        ffn_rows,
        gate_part,
        up_part,
        activated,
    ) = saved
    model_width = whole_rows.shape[1]
    head_count = w_qkv.shape[1]
    head_width = head_count * HD
    row_count = normed_all.shape[0]
    grad_hidden = grad_rows.astype(jnp.float32)
    grad_down = spread(grad_rows)
    grad_wd = inner_rows(activated, grad_down)
    grad_act = outer_cols(grad_down, w_down)
    sigmoid_gate = jax.nn.sigmoid(gate_part)
    grad_gate = grad_act * up_part * sigmoid_gate * (1.0 + gate_part * (1.0 - sigmoid_gate))
    grad_up = grad_act * gate_part * sigmoid_gate
    grad_gate_up = jnp.concatenate([grad_gate, grad_up], axis=1).astype(jnp.bfloat16)
    grad_wgu = inner_rows(grad_gate_up, ffn_rows).reshape(w_gateup.shape)
    back_second = jnp.dot(
        grad_gate_up, w_gateup.reshape(-1, model_width), preferred_element_type=jnp.float32
    )
    grad_normed_second = collect(back_second)
    grad_gain2, grad_hidden = norm_back(
        hidden, scale_second, gain_second, grad_normed_second, grad_hidden
    )
    grad_branch_all = spread(grad_hidden.astype(jnp.bfloat16))
    grad_wo = inner_rows(attended, grad_branch_all)
    grad_heads = (
        outer_cols(grad_branch_all, w_out).astype(jnp.bfloat16).reshape(row_count, head_count, HD)
    )
    grad_query, grad_pairs_all = attend_back(
        query_heads,
        pairs_all,
        token_index,
        doc_start,
        head_width,
        log_total,
        accumulated,
        grad_heads,
    )
    grad_pairs = lax.psum_scatter(
        grad_pairs_all.astype(jnp.bfloat16), "ctx", scatter_dimension=0, tiled=True
    ).astype(jnp.float32)
    grad_mixed = grad_pairs[:, head_width:] + extra_values.astype(jnp.float32)
    grad_keys = rotate_back(
        grad_pairs[:, :head_width].reshape(row_count, head_count, HD), cosine, sine_part
    )
    grad_query = rotate_back(grad_query, cosine, sine_part)
    grad_projected = jnp.concatenate(
        [
            grad_query.reshape(row_count, head_width),
            grad_keys.reshape(row_count, head_width),
            (1.0 - value_mix) * grad_mixed,
        ],
        axis=1,
    ).astype(jnp.bfloat16)
    send_values = (value_mix * grad_mixed).astype(jnp.bfloat16)
    grad_wqkv = inner_rows(grad_projected, normed_all).reshape(w_qkv.shape)
    grad_normed = collect(
        jnp.dot(
            grad_projected,
            w_qkv.reshape(3 * head_width, model_width),
            preferred_element_type=jnp.float32,
        )
    )
    grad_gain1, grad_whole = norm_back(
        whole_rows, scale_first, gain_first, grad_normed, grad_hidden
    )
    return (
        grad_whole,
        send_values,
        (grad_gain1, grad_wqkv, grad_wo, grad_gain2, grad_wgu, grad_wd),
    )


def body(inputs, cotangent, lengths, gain1, wqkv, wo, gain2, wgu, wd):
    section_index = lax.axis_index("section")
    leading = section_index == 0
    value_mix = jnp.where(leading, 0.0, 0.5).astype(jnp.float32)
    micro_count = inputs.shape[0]
    local_rows = inputs.shape[1]
    model_width = inputs.shape[2]
    head_width = wqkv.shape[2] * HD
    row_count = local_rows * lax.axis_size("tp")
    gateup_use, down_use = (wgu[0], wd[0])
    weights = (gain1[0], wqkv[0], wo[0], gain2[0], gateup_use, down_use)
    recv_rows = jnp.zeros((local_rows, model_width), jnp.bfloat16)
    recv_values = jnp.zeros((row_count, head_width), jnp.bfloat16)
    states = []
    outputs = []
    for turn_index in range(micro_count + 1):
        own_rows = inputs[min(turn_index, micro_count - 1)]
        row_block = jnp.where(leading, own_rows, recv_rows)
        seq_lengths = jnp.where(
            leading, lengths[min(turn_index, micro_count - 1)], lengths[max(turn_index - 1, 0)]
        )
        layer_out, mixed, pairs_all, unused = layer_forward(
            row_block, recv_values, value_mix, weights, seq_lengths
        )
        kept_pairs = None
        states.append((row_block, recv_values, seq_lengths, kept_pairs))
        outputs.append(layer_out)
        if turn_index < micro_count:
            recv_rows, recv_values = shifted((layer_out, mixed), "section", 1)
    grad_rows_in = jnp.zeros((local_rows, model_width), jnp.bfloat16)
    grad_values_in = jnp.zeros((row_count, head_width), jnp.bfloat16)
    totals = None
    turn_grads = []
    for turn_index in range(micro_count + 1):
        row_block, first_values, seq_lengths, kept_pairs = states[micro_count - turn_index]
        if turn_index < micro_count:
            fed_grad = cotangent[micro_count - 1 - turn_index]
        else:
            fed_grad = jnp.zeros_like(cotangent[0])
        grad_out = jnp.where(leading, grad_rows_in, fed_grad)
        unused_out, unused_mixed, unused_pairs, saved = layer_forward(
            row_block, first_values, value_mix, weights, seq_lengths
        )
        grad_whole, send_values, grads = layer_backward(
            grad_out, grad_values_in, value_mix, weights, saved
        )
        totals = grads if totals is None else jax.tree.map(jnp.add, totals, grads)
        sent_rows = grad_whole.astype(jnp.bfloat16)
        turn_grads.append(jnp.where(leading, grad_whole, sent_rows.astype(jnp.float32)))
        if turn_index < micro_count:
            grad_rows_in, grad_values_in = shifted((sent_rows, send_values), "section", -1)
    grad_gain1, grad_wqkv, grad_wo, grad_gain2, grad_wgu, grad_wd = totals
    grad_wqkv, grad_wo, grad_wgu, grad_wd = (
        lax.psum(grad_wqkv.astype(jnp.bfloat16), "ctx").astype(jnp.float32),
        lax.psum(grad_wo.astype(jnp.bfloat16), "ctx").astype(jnp.float32),
        lax.psum(grad_wgu.astype(jnp.bfloat16), "ctx").astype(jnp.float32),
        lax.psum(grad_wd.astype(jnp.bfloat16), "ctx").astype(jnp.float32),
    )
    grad_gain1, grad_gain2 = lax.psum((grad_gain1, grad_gain2), ("ctx", "tp"))
    acts = jnp.stack(
        [
            jnp.where(leading, outputs[batch_index], outputs[batch_index + 1])
            for batch_index in range(micro_count)
        ]
    )[None]
    input_grads = jnp.stack(
        [
            jnp.where(
                leading,
                turn_grads[micro_count - batch_index],
                turn_grads[micro_count - 1 - batch_index],
            )
            for batch_index in range(micro_count)
        ]
    )[None]
    return (
        acts,
        input_grads,
        grad_gain1[None],
        grad_wqkv[None],
        grad_wo[None],
        grad_gain2[None],
        grad_wgu[None],
        grad_wd[None],
    )


def solution(mesh):
    placed = (
        P(None, ("ctx", "tp"), None),
        P(None, ("ctx", "tp"), None),
        P(),
        P("section", None),
        P("section", None, "tp", None, None),
        P("section", "tp", None),
        P("section", None),
        P("section", None, "tp", None),
        P("section", "tp", None),
    )
    return jax.shard_map(
        body,
        mesh=mesh,
        in_specs=placed,
        out_specs=(
            P("section", None, ("ctx", "tp"), None),
            P("section", None, ("ctx", "tp"), None),
            P("section", None),
            P("section", None, "tp", None, None),
            P("section", "tp", None),
            P("section", None),
            P("section", None, "tp", None),
            P("section", "tp", None),
        ),
        check_vma=False,
    )
```

profile of v0, /device:TPU:0, one launch (start us, length us, event | category | flops | bytes accessed | tf_op | source)
XLA Modules:
  0.0 2685.6 jit_solution(9530958914110633878)
XLA Ops:
  15.7 44.5 %all-gather.17.cloned.1.call-done = bf16[1024,1024]{1,0:T(8,128)(2,1)} async-done(((bf16[256,1024]{1,0:T(8,128)(2,1)}), bf16[1024,1024]{1,0:T(8,128)(2,1)}) %all-gather.17.cloned.1.call-update) | async-done | bytes 2097168 | tf_op jit(solution)/shard_map/all_gather | solution.py:68
  70.9 47.5 %all-gather.19.cloned.1.call-done = bf16[4096,512]{0,1:T(8,128)(2,1)} async-done(((bf16[1024,512]{0,1:T(8,128)(2,1)}), bf16[4096,512]{0,1:T(8,128)(2,1)}) %all-gather.19.cloned.1.call-update) | async-done | bytes 4194320 | tf_op jit(solution)/shard_map/all_gather | solution.py:78
  177.9 114.0 %reduce-scatter.16.cloned.1.call-done = bf16[256,1024]{1,0:T(8,128)(2,1)} async-done(((bf16[1024,1024]{1,0:T(8,128)(2,1)}), bf16[256,1024]{1,0:T(8,128)(2,1)}) %reduce-scatter.16.cloned.1.call-update) | async-done | bytes 524304 | tf_op jit(solution)/shard_map/reduce_scatter | solution.py:72
  296.3 45.4 %all-gather.21.cloned.1.call-done = bf16[1024,1024]{1,0:T(8,128)(2,1)} async-done(((bf16[256,1024]{1,0:T(8,128)(2,1)}), bf16[1024,1024]{1,0:T(8,128)(2,1)}) %all-gather.21.cloned.1.call-update) | async-done | bytes 2097168 | tf_op jit(solution)/shard_map/all_gather | solution.py:68
  460.9 48.3 %all-gather.25.cloned.1.call-done = bf16[4096,512]{0,1:T(8,128)(2,1)} async-done(((bf16[1024,512]{0,1:T(8,128)(2,1)}), bf16[4096,512]{0,1:T(8,128)(2,1)}) %all-gather.25.cloned.1.call-update) | async-done | bytes 4194320 | tf_op jit(solution)/shard_map/all_gather | solution.py:78
  568.1 113.9 %reduce-scatter.20.cloned.1.call-done = bf16[256,1024]{1,0:T(8,128)(2,1)} async-done(((bf16[1024,1024]{1,0:T(8,128)(2,1)}), bf16[256,1024]{1,0:T(8,128)(2,1)}) %reduce-scatter.20.cloned.1.call-update) | async-done | bytes 524304 | tf_op jit(solution)/shard_map/reduce_scatter | solution.py:72
  685.5 45.3 %all-gather.27.cloned.1.call-done = bf16[1024,1024]{1,0:T(8,128)(2,1)} async-done(((bf16[256,1024]{1,0:T(8,128)(2,1)}), bf16[1024,1024]{1,0:T(8,128)(2,1)}) %all-gather.27.cloned.1.call-update) | async-done | bytes 2097168 | tf_op jit(solution)/shard_map/all_gather | solution.py:68
  850.1 48.3 %all-gather.31.cloned.1.call-done = bf16[4096,512]{0,1:T(8,128)(2,1)} async-done(((bf16[1024,512]{0,1:T(8,128)(2,1)}), bf16[4096,512]{0,1:T(8,128)(2,1)}) %all-gather.31.cloned.1.call-update) | async-done | bytes 4194320 | tf_op jit(solution)/shard_map/all_gather | solution.py:78
  958.8 115.1 %reduce-scatter.24.cloned.1.call-done = bf16[256,1024]{1,0:T(8,128)(2,1)} async-done(((bf16[1024,1024]{1,0:T(8,128)(2,1)}), bf16[256,1024]{1,0:T(8,128)(2,1)}) %reduce-scatter.24.cloned.1.call-update) | async-done | bytes 524304 | tf_op jit(solution)/shard_map/reduce_scatter | solution.py:72
  1079.5 43.4 %all-gather.33.cloned.1.call-done = bf16[1024,1024]{1,0:T(8,128)(2,1)} async-done(((bf16[256,1024]{1,0:T(8,128)(2,1)}), bf16[1024,1024]{1,0:T(8,128)(2,1)}) %all-gather.33.cloned.1.call-update) | async-done | bytes 2097168 | tf_op jit(solution)/shard_map/all_gather | solution.py:68
  1231.8 45.4 %all-gather.35.cloned.1.call-done = bf16[1024,1024]{1,0:T(8,128)(2,1)} async-done(((bf16[256,1024]{1,0:T(8,128)(2,1)}), bf16[1024,1024]{1,0:T(8,128)(2,1)}) %all-gather.35.cloned.1.call-update) | async-done | bytes 2097168 | tf_op jit(solution)/shard_map/all_gather | solution.py:68
  1285.0 64.9 %while.174 = (s32[]{:T(128)}, f32[1024,4,64]{0,2,1:T(8,128)}, bf16[4,1024,4,64]{1,3,2,0:T(8,128)(2,1)}, bf16[4,1024,4,64]{1,3,2,0:T(8,128)(2,1)}, s32[4]{0:T(128...) while((s32[]{:T(128)}, f32[1024,4,64]{0,2,1:T(8,128)}, ...), condition=%wide.region_54.55_spmd.clone, body=%wide.region_51.54_spmd.clone.sunk | while | flops 2730231808 | bytes 106509232 | solution.py:209
  1362.1 156.0 %reduce-scatter.30.cloned.1.call-done = bf16[1024,512]{0,1:T(8,128)(2,1)} async-done(((bf16[4096,512]{0,1:T(8,128)(2,1)}), bf16[1024,512]{0,1:T(8,128)(2,1)}) %reduce-scatter.30.cloned.1.call-update) | async-done | bytes 1048592 | tf_op jit(solution)/shard_map/reduce_scatter | solution.py:350
  1525.9 44.0 %reduce-scatter.32.cloned.1.call-done = bf16[256,1024]{1,0:T(8,128)(2,1)} async-done(((bf16[1024,1024]{1,0:T(8,128)(2,1)}), bf16[256,1024]{1,0:T(8,128)(2,1)}) %reduce-scatter.32.cloned.1.call-update) | async-done | bytes 524304 | tf_op jit(solution)/shard_map/reduce_scatter | solution.py:72
  1580.9 45.4 %all-gather.37.cloned.1.call-done = bf16[1024,1024]{1,0:T(8,128)(2,1)} async-done(((bf16[256,1024]{1,0:T(8,128)(2,1)}), bf16[1024,1024]{1,0:T(8,128)(2,1)}) %all-gather.37.cloned.1.call-update) | async-done | bytes 2097168 | tf_op jit(solution)/shard_map/all_gather | solution.py:68
  1687.3 45.4 %all-gather.39.cloned.1.call-done = bf16[1024,1024]{1,0:T(8,128)(2,1)} async-done(((bf16[256,1024]{1,0:T(8,128)(2,1)}), bf16[1024,1024]{1,0:T(8,128)(2,1)}) %all-gather.39.cloned.1.call-update) | async-done | bytes 2097168 | tf_op jit(solution)/shard_map/all_gather | solution.py:68
  1740.5 63.4 %while.175 = (s32[]{:T(128)}, f32[1024,4,64]{0,2,1:T(8,128)}, bf16[4,1024,4,64]{1,3,2,0:T(8,128)(2,1)}, bf16[4,1024,4,64]{1,3,2,0:T(8,128)(2,1)}, s32[4]{0:T(128...) while((s32[]{:T(128)}, f32[1024,4,64]{0,2,1:T(8,128)}, ...), condition=%wide.region_64.65_spmd.clone, body=%wide.region_61.64_spmd.clone.sunk | while | flops 2730231808 | bytes 106509232 | solution.py:209
  1817.4 154.5 %reduce-scatter.36.cloned.1.call-done = bf16[1024,512]{0,1:T(8,128)(2,1)} async-done(((bf16[4096,512]{0,1:T(8,128)(2,1)}), bf16[1024,512]{0,1:T(8,128)(2,1)}) %reduce-scatter.36.cloned.1.call-update) | async-done | bytes 1048592 | tf_op jit(solution)/shard_map/reduce_scatter | solution.py:350
  1981.8 44.0 %reduce-scatter.38.cloned.1.call-done = bf16[256,1024]{1,0:T(8,128)(2,1)} async-done(((bf16[1024,1024]{1,0:T(8,128)(2,1)}), bf16[256,1024]{1,0:T(8,128)(2,1)}) %reduce-scatter.38.cloned.1.call-update) | async-done | bytes 524304 | tf_op jit(solution)/shard_map/reduce_scatter | solution.py:72
  2036.5 45.4 %all-gather.41.cloned.1.call-done = bf16[1024,1024]{1,0:T(8,128)(2,1)} async-done(((bf16[256,1024]{1,0:T(8,128)(2,1)}), bf16[1024,1024]{1,0:T(8,128)(2,1)}) %all-gather.41.cloned.1.call-update) | async-done | bytes 2097168 | tf_op jit(solution)/shard_map/all_gather | solution.py:68
  2143.2 45.4 %all-gather.43.cloned.1.call-done = bf16[1024,1024]{1,0:T(8,128)(2,1)} async-done(((bf16[256,1024]{1,0:T(8,128)(2,1)}), bf16[1024,1024]{1,0:T(8,128)(2,1)}) %all-gather.43.cloned.1.call-update) | async-done | bytes 2097168 | tf_op jit(solution)/shard_map/all_gather | solution.py:68
  2196.4 64.4 %while.176 = (s32[]{:T(128)}, f32[1024,4,64]{0,2,1:T(8,128)}, bf16[4,1024,4,64]{1,3,2,0:T(8,128)(2,1)}, bf16[4,1024,4,64]{1,3,2,0:T(8,128)(2,1)}, s32[4]{0:T(128...) while((s32[]{:T(128)}, f32[1024,4,64]{0,2,1:T(8,128)}, ...), condition=%wide.region_74.75_spmd.clone, body=%wide.region_71.74_spmd.clone.sunk | while | flops 2730231808 | bytes 106509232 | solution.py:209
  2296.5 132.6 %reduce-scatter.42.cloned.1.call-done = bf16[1024,512]{0,1:T(8,128)(2,1)} async-done(((bf16[4096,512]{0,1:T(8,128)(2,1)}), bf16[1024,512]{0,1:T(8,128)(2,1)}) %reduce-scatter.42.cloned.1.call-update) | async-done | bytes 1048592 | tf_op jit(solution)/shard_map/reduce_scatter | solution.py:350
  2570.6 97.7 %all-reduce.4.cloned.1.call-done = (bf16[1,3,4,64,1024]{4,3,2,1,0:T(8,128)(2,1)}, bf16[1,256,1024]{2,1,0:T(8,128)(2,1)}, bf16[1,2,704,1024]{3,2,1,0:T(8,128)(2,1)}, bf16[1,704,1024]{2,1,0:T(8,128)(2,1)}) async-done(((bf16[1,3,4,64,1024]{4,3,2,1,0:T(8,128)(2,1)}, bf16[1,256,1024]{2,1,0:T(8,128)(2,1)}, bf16[1,2,704,1024]{3,2,1,0:T(8,128)(2,1)}, bf16[1,704,1024]{2,1,0:T(8,128)(2,1)}), ...) | async-done | bytes 6422544 | tf_op jit(solution)/shard_map/psum | solution.py:438
  (819 shorter events, 1399.6 us)
Async XLA Ops:
  11.4 107.0 %all-gather.19.cloned.1.call-start = ((), (), s32[]{:S(2)}) async-start(), calls=%async_computation.16 | async-start | bytes 5242880 | tf_op jit(solution)/shard_map/all_gather | solution.py:78
  66.8 225.2 %reduce-scatter.16.cloned.1.call-start = ((), (), s32[]{:S(2)}) async-start(), calls=%async_computation.17 | async-start | bytes 2621440 | tf_op jit(solution)/shard_map/reduce_scatter | solution.py:72
  177.8 163.8 %all-gather.21.cloned.1.call-start = ((), (), s32[]{:S(2)}) async-start(), calls=%async_computation.18 | async-start | bytes 2621440 | tf_op jit(solution)/shard_map/all_gather | solution.py:68
  404.1 105.1 %all-gather.25.cloned.1.call-start = ((), (), s32[]{:S(2)}) async-start(), calls=%async_computation.21 | async-start | bytes 5242880 | tf_op jit(solution)/shard_map/all_gather | solution.py:78
  457.6 224.4 %reduce-scatter.20.cloned.1.call-start = ((), (), s32[]{:S(2)}) async-start(), calls=%async_computation.22 | async-start | bytes 2621440 | tf_op jit(solution)/shard_map/reduce_scatter | solution.py:72
  568.1 162.8 %all-gather.27.cloned.1.call-start = ((), (), s32[]{:S(2)}) async-start(), calls=%async_computation.23 | async-start | bytes 2621440 | tf_op jit(solution)/shard_map/all_gather | solution.py:68
  793.3 105.1 %all-gather.31.cloned.1.call-start = ((), (), s32[]{:S(2)}) async-start(), calls=%async_computation.26 | async-start | bytes 5242880 | tf_op jit(solution)/shard_map/all_gather | solution.py:78
  846.8 227.1 %reduce-scatter.24.cloned.1.call-start = ((), (), s32[]{:S(2)}) async-start(), calls=%async_computation.27 | async-start | bytes 2621440 | tf_op jit(solution)/shard_map/reduce_scatter | solution.py:72
  958.7 164.3 %all-gather.33.cloned.1.call-start = ((), (), s32[]{:S(2)}) async-start(), calls=%async_computation.28 | async-start | bytes 2621440 | tf_op jit(solution)/shard_map/all_gather | solution.py:68
  1079.5 146.9 %reduce-scatter.28.cloned.1.call-start = ((), (), s32[]{:S(2)}) async-start(), calls=%async_computation.30 | async-start | bytes 2621440 | tf_op jit(solution)/shard_map/reduce_scatter | solution.py:72
  1231.7 286.4 %reduce-scatter.30.cloned.1.call-start = ((), (), s32[]{:S(2)}) async-start(), calls=%async_computation.32 | async-start | bytes 5242880 | tf_op jit(solution)/shard_map/reduce_scatter | solution.py:350
  1359.8 210.1 %reduce-scatter.32.cloned.1.call-start = ((), (), s32[]{:S(2)}) async-start(), calls=%async_computation.33 | async-start | bytes 2621440 | tf_op jit(solution)/shard_map/reduce_scatter | solution.py:72
  1525.8 100.4 %all-gather.37.cloned.1.call-start = ((), (), s32[]{:S(2)}) async-start(), calls=%async_computation.34 | async-start | bytes 2621440 | tf_op jit(solution)/shard_map/all_gather | solution.py:68
  1580.8 101.0 %reduce-scatter.34.cloned.1.call-start = ((), (), s32[]{:S(2)}) async-start(), calls=%async_computation.35 | async-start | bytes 2621440 | tf_op jit(solution)/shard_map/reduce_scatter | solution.py:72
  1687.2 284.7 %reduce-scatter.36.cloned.1.call-start = ((), (), s32[]{:S(2)}) async-start(), calls=%async_computation.37 | async-start | bytes 5242880 | tf_op jit(solution)/shard_map/reduce_scatter | solution.py:350
  1813.8 212.0 %reduce-scatter.38.cloned.1.call-start = ((), (), s32[]{:S(2)}) async-start(), calls=%async_computation.38 | async-start | bytes 2621440 | tf_op jit(solution)/shard_map/reduce_scatter | solution.py:72
  1813.8 161.4 %collective-permute-start.5 = (bf16[1024,256]{0,1:T(8,128)(2,1)}, bf16[1024,256]{0,1:T(8,128)(2,1)}, u32[]{:S(2)}, u32[]{:S(2)}) collective-permute-start(bf16[1024,256]{0,1:T(8,128)(2,1)} %get-tuple-element.1974), channel_id=1, source_target_pairs={{16,0},{17,1},{18,2},{19,3},{20,4},{21,5},{22,6},{23,7},{24,8},{25... | collective-permute-start | bytes 1572872 | tf_op jit(solution)/shard_map/ppermute | solution.py:15
  1981.7 100.2 %all-gather.41.cloned.1.call-start = ((), (), s32[]{:S(2)}) async-start(), calls=%async_computation.39 | async-start | bytes 2621440 | tf_op jit(solution)/shard_map/all_gather | solution.py:68
  2036.5 101.0 %reduce-scatter.40.cloned.1.call-start = ((), (), s32[]{:S(2)}) async-start(), calls=%async_computation.40 | async-start | bytes 2621440 | tf_op jit(solution)/shard_map/reduce_scatter | solution.py:72
  2143.1 286.0 %reduce-scatter.42.cloned.1.call-start = ((), (), s32[]{:S(2)}) async-start(), calls=%async_computation.42 | async-start | bytes 5242880 | tf_op jit(solution)/shard_map/reduce_scatter | solution.py:350
  2270.7 205.3 %reduce-scatter.26.cloned.1.call-start = ((), (), s32[]{:S(2)}) async-start(), calls=%async_computation.29 | async-start | bytes 2621440 | tf_op jit(solution)/shard_map/reduce_scatter | solution.py:72
  2275.7 245.7 %reduce-scatter.44.cloned.1.call-start = ((), (), s32[]{:S(2)}) async-start(), calls=%async_computation.43 | async-start | bytes 2621440 | tf_op jit(solution)/shard_map/reduce_scatter | solution.py:72
  2294.2 138.2 %collective-permute-start.7 = (bf16[1024,256]{0,1:T(8,128)(2,1)}, bf16[1024,256]{0,1:T(8,128)(2,1)}, u32[]{:S(2)}, u32[]{:S(2)}) collective-permute-start(bf16[1024,256]{0,1:T(8,128)(2,1)} %get-tuple-element.1972), channel_id=1, source_target_pairs={{16,0},{17,1},{18,2},{19,3},{20,4},{21,5},{22,6},{23,7},{24,8},{25... | collective-permute-start | bytes 1572872 | tf_op jit(solution)/shard_map/ppermute | solution.py:15
  2437.2 231.1 %all-reduce.4.cloned.1.call-start = ((), (), s32[]{:S(2)}) async-start(), calls=%async_computation.45 | async-start | bytes 12845056 | tf_op jit(solution)/shard_map/psum | solution.py:438
  (180 other events, 6387.9 us)
Sparse Core Ops, SparseCore 0:
  11.5 48.6 all-gather.16
  66.9 51.4 all-gather.18
  177.9 113.9 reduce-scatter.15
  296.4 45.2 all-gather.20
  404.2 45.4 all-gather.22
  457.7 51.4 all-gather.24
  568.2 113.8 reduce-scatter.19
  685.6 45.2 all-gather.26
  793.4 45.4 all-gather.28
  846.9 51.4 all-gather.30
  958.8 114.9 reduce-scatter.23
  1077.7 45.2 all-gather.32
  1125.0 44.6 all-gather.44
  1231.9 45.2 all-gather.34
  1359.9 158.2 reduce-scatter.29
  1526.0 43.8 reduce-scatter.31
  1580.9 45.2 all-gather.36
  1687.3 45.2 all-gather.38
  1813.9 158.0 reduce-scatter.35
  1981.8 43.8 reduce-scatter.37
  2036.6 45.2 all-gather.40
  2143.3 45.2 all-gather.42
  2270.8 158.2 reduce-scatter.41
  2526.3 141.9 all-reduce.3
  (7 shorter events, 299.5 us)
where the time goes:
time: 2690 us
  waiting for transfers between devices  1910 us (71%)
  matrix products  286 us (11%)
  local copies, waits for them, and re-layouts  169 us (6%)
  other arithmetic  149 us (6%)
  loops' own time  91.9 us (3%)
  blocking collectives  42.2 us (2%)
    reduce_scatter x12, waiting for transfers between devices, collect(): lax.psum_scatter(partial_value.astype(jnp.bfloat16), 'tp', scatter_dimens...  691 us
    all_gather x12, waiting for transfers between devices, spread(): return lax.all_gather(row_block, 'tp', axis=0, tiled=True)  531 us
    reduce_scatter x3, waiting for transfers between devices, layer_backward(): lax.psum_scatter(grad_pairs_all.astype(jnp.bfloat16), 'ctx', scatter_dime...  443 us
    all_gather x3, waiting for transfers between devices, fetch_keys(): return lax.all_gather(key_value, 'ctx', axis=0, tiled=True)  144 us
    psum x1, waiting for transfers between devices, body(): lax.psum(grad_wqkv.astype(jnp.bfloat16), 'ctx').astype(jnp.float32)  97.7 us
    dot_general x12, matrix products, outer_cols(): lax.dot_general(left, right, (((1,), (1,)), ((), ())), preferred_element_...  59.7 us
  transfers between devices with their start and end apart: 39, of which 35 were waited for; matrix products, arithmetic and copies ran while one was open for 4% of the time, Pallas kernels for 0%

commit v1 on v0

--- a/solution.py
+++ b/solution.py
@@ -1,12 +1,17 @@
+import functools
+
 import jax
 import jax.numpy as jnp
 from jax import lax
+from jax.experimental import pallas as pl
+from jax.experimental.pallas import tpu as pltpu
 from jax.sharding import PartitionSpec as P
 
 HD = 64
-
-
 EPSILON = 1e-06
+MASKED = -1e30
+ALL_AXES = ("section", "ctx", "tp")
+VMEM_LIMIT = 40 * 1024 * 1024
 
 
 def shifted(block, axis, distance):
@@ -382,7 +387,7 @@
     )
 
 
-def body(inputs, cotangent, lengths, gain1, wqkv, wo, gain2, wgu, wd):
+def general_body(inputs, cotangent, lengths, gain1, wqkv, wo, gain2, wgu, wd):
     section_index = lax.axis_index("section")
     leading = section_index == 0
     value_mix = jnp.where(leading, 0.0, 0.5).astype(jnp.float32)
@@ -469,6 +474,483 @@
     )
 
 
+def device_groups(mesh_sizes, key, order):
+    sections, contexts, parts = mesh_sizes
+    groups = {}
+    for section in range(sections):
+        for ctx in range(contexts):
+            for tp in range(parts):
+                place = (section, ctx, tp)
+                number = (section * contexts + ctx) * parts + tp
+                groups.setdefault(key(*place), []).append((order(*place), number))
+    return [[number for _, number in sorted(members)] for _, members in sorted(groups.items())]
+
+
+def exchange(value, groups):
+    return lax.all_to_all(
+        value, ALL_AXES, split_axis=0, concat_axis=0, tiled=True, axis_index_groups=groups
+    )
+
+
+def document_bounds(ends_ref, first, index):
+    start = jnp.zeros_like(index)
+    for entry in range(ends_ref.shape[0]):
+        end = ends_ref[entry]
+        start = jnp.where(index >= end, end, start)
+    return start
+
+
+def scalar_start(ends_ref, index):
+    start = jnp.int32(0)
+    for entry in range(ends_ref.shape[0]):
+        start = jnp.where(index >= ends_ref[entry], ends_ref[entry], start)
+    return start
+
+
+def scalar_end(ends_ref, index):
+    end = ends_ref[ends_ref.shape[0] - 1]
+    for entry in range(ends_ref.shape[0] - 2, -1, -1):
+        end = jnp.where(index < ends_ref[entry], ends_ref[entry], end)
+    return end
+
+
+def dot(left, right, left_dim, right_dim):
+    return lax.dot_general(
+        left, right, (((left_dim,), (right_dim,)), ((), ())), preferred_element_type=jnp.float32
+    )
+
+
+def attention_forward_kernel(ends_ref, qkv_ref, out_ref, lse_ref, keys_ref):
+    block = pl.program_id(0)
+    blocks, _, width = qkv_ref.shape
+
+    @pl.when(block == 0)
+    def _():
+        def turn(j, carry):
+            keys_ref[j] = qkv_ref[j, HD : 2 * HD, :].T
+            return carry
+
+        lax.fori_loop(0, blocks, turn, 0)
+
+    query = qkv_ref[block, 0:HD, :]
+    first = block * width
+    query_index = first + lax.broadcasted_iota(jnp.int32, (1, width), 1)
+    start = document_bounds(ends_ref, first, query_index)
+    low = scalar_start(ends_ref, first) // width
+    high_start = scalar_start(ends_ref, first + width - 1)
+    middle = jnp.clip((high_start + width - 1) // width, low, block)
+
+    def step(j, carry, masked):
+        top, total, acc = carry
+        scores = dot(keys_ref[j], query, 1, 0)
+        if masked:
+            key_index = j * width + lax.broadcasted_iota(jnp.int32, (width, 1), 0)
+            allowed = (key_index >= start) & (key_index <= query_index)
+            scores = jnp.where(allowed, scores, MASKED)
+        new_top = jnp.maximum(top, jnp.max(scores, axis=0, keepdims=True))
+        shrink = jnp.exp(top - new_top)
+        weights = jnp.exp(scores - new_top)
+        total = total * shrink + jnp.sum(weights, axis=0, keepdims=True)
+        values = qkv_ref[j, 2 * HD : 3 * HD, :]
+        acc = acc * shrink + dot(values, weights.astype(jnp.bfloat16), 1, 0)
+        return new_top, total, acc
+
+    carry = (
+        jnp.full((1, width), MASKED, jnp.float32),
+        jnp.zeros((1, width), jnp.float32),
+        jnp.zeros((HD, width), jnp.float32),
+    )
+    carry = lax.fori_loop(low, middle, functools.partial(step, masked=True), carry)
+    carry = lax.fori_loop(middle, block, functools.partial(step, masked=False), carry)
+    top, total, acc = step(block, carry, True)
+    out_ref[0] = (acc / total).astype(jnp.bfloat16)
+    lse_ref[0] = top + jnp.log(total)
+
+
+def attention_forward(ends, qkv):
+    blocks, _, width = qkv.shape
+    pairs = blocks * (blocks + 1) // 2 * width * width
+    return pl.pallas_call(
+        attention_forward_kernel,
+        grid_spec=pltpu.PrefetchScalarGridSpec(
+            num_scalar_prefetch=1,
+            grid=(blocks,),
+            in_specs=[pl.BlockSpec(qkv.shape, lambda i, ends_ref: (0, 0, 0))],
+            out_specs=[
+                pl.BlockSpec((1, HD, width), lambda i, ends_ref: (i, 0, 0)),
+                pl.BlockSpec((1, 1, width), lambda i, ends_ref: (i, 0, 0)),
+            ],
+            scratch_shapes=[pltpu.VMEM((blocks, width, HD), jnp.bfloat16)],
+        ),
+        out_shape=[
+            jax.ShapeDtypeStruct((blocks, HD, width), jnp.bfloat16),
+            jax.ShapeDtypeStruct((blocks, 1, width), jnp.float32),
+        ],
+        compiler_params=pltpu.CompilerParams(vmem_limit_bytes=VMEM_LIMIT),
+        cost_estimate=pl.CostEstimate(
+            flops=4 * HD * pairs, bytes_accessed=2 * qkv.size, transcendentals=pairs
+        ),
+        name="attention_forward",
+    )(ends, qkv)
+
+
+def attention_backward_kernel(
+    ends_ref, qkv_ref, out_ref, grad_ref, lse_ref, result_ref, query_grad_ref, delta_ref
+):
+    block = pl.program_id(0)
+    blocks, _, width = qkv_ref.shape
+
+    @pl.when(block == 0)
+    def _():
+        def turn(i, carry):
+            delta_ref[i] = jnp.sum(
+                grad_ref[i].astype(jnp.float32) * out_ref[i].astype(jnp.float32),
+                axis=0,
+                keepdims=True,
+            )
+            query_grad_ref[i] = jnp.zeros((HD, width), jnp.float32)
+            return carry
+
+        lax.fori_loop(0, blocks, turn, 0)
+
+    first = block * width
+    keys_t = qkv_ref[block, HD : 2 * HD, :]
+    keys = keys_t.T
+    values = qkv_ref[block, 2 * HD : 3 * HD, :].T
+    key_index = first + lax.broadcasted_iota(jnp.int32, (width, 1), 0)
+    near_end = scalar_end(ends_ref, first)
+    far_end = scalar_end(ends_ref, first + width - 1)
+    stop = (far_end - 1) // width + 1
+    middle = jnp.clip(near_end // width, block + 1, stop)
+
+    def step(i, carry, masked):
+        key_grad, value_grad = carry
+        query = qkv_ref[i, 0:HD, :]
+        grad = grad_ref[i]
+        weights = jnp.exp(dot(keys, query, 1, 0) - lse_ref[i])
+        if masked:
+            query_index = i * width + lax.broadcasted_iota(jnp.int32, (1, width), 1)
+            start = document_bounds(ends_ref, first, query_index)
+            allowed = (key_index >= start) & (key_index <= query_index)
+            weights = jnp.where(allowed, weights, 0.0)
+        grad_weights = dot(values, grad, 1, 0)
+        grad_scores = (weights * (grad_weights - delta_ref[i])).astype(jnp.bfloat16)
+        value_grad = value_grad + dot(grad, weights.astype(jnp.bfloat16), 1, 1)
+        key_grad = key_grad + dot(query, grad_scores, 1, 1)
+        query_grad_ref[i] += dot(keys_t, grad_scores, 1, 0)
+        return key_grad, value_grad
+
+    empty = jnp.zeros((HD, width), jnp.float32)
+    carry = step(block, (empty, empty), True)
+    carry = lax.fori_loop(block + 1, middle, functools.partial(step, masked=False), carry)
+    key_grad, value_grad = lax.fori_loop(middle, stop, functools.partial(step, masked=True), carry)
+    result_ref[0, 0:HD] = (query_grad_ref[block] * HD ** (-0.5)).astype(jnp.bfloat16)
+    result_ref[0, HD : 2 * HD] = key_grad.astype(jnp.bfloat16)
+    result_ref[0, 2 * HD : 3 * HD] = value_grad.astype(jnp.bfloat16)
+
+
+def attention_backward(ends, qkv, out, grad, lse):
+    blocks, _, width = qkv.shape
+    pairs = blocks * (blocks + 1) // 2 * width * width
+
+    def whole(value):
+        return pl.BlockSpec(value.shape, lambda i, ends_ref: (0, 0, 0))
+
+    return pl.pallas_call(
+        attention_backward_kernel,
+        grid_spec=pltpu.PrefetchScalarGridSpec(
+            num_scalar_prefetch=1,
+            grid=(blocks,),
+            in_specs=[whole(qkv), whole(out), whole(grad), whole(lse)],
+            out_specs=pl.BlockSpec((1, 3 * HD, width), lambda i, ends_ref: (i, 0, 0)),
+            scratch_shapes=[
+                pltpu.VMEM((blocks, HD, width), jnp.float32),
+                pltpu.VMEM((blocks, 1, width), jnp.float32),
+            ],
+        ),
+        out_shape=jax.ShapeDtypeStruct(qkv.shape, jnp.bfloat16),
+        compiler_params=pltpu.CompilerParams(vmem_limit_bytes=VMEM_LIMIT),
+        cost_estimate=pl.CostEstimate(
+            flops=10 * HD * pairs, bytes_accessed=6 * qkv.size, transcendentals=pairs
+        ),
+        name="attention_backward",
+    )(ends, qkv, out, grad, lse)
+
+
+def rope_pairs(pair_block, cosine, sine_part):
+    half_width = HD // 2
+    leading_half = pair_block[:, :half_width]
+    trailing_half = pair_block[:, half_width:]
+    return jnp.concatenate(
+        [
+            leading_half * cosine - trailing_half * sine_part,
+            trailing_half * cosine + leading_half * sine_part,
+        ],
+        axis=1,
+    )
+
+
+def split_body(mesh_sizes, inputs, cotangent, lengths, gain1, wqkv, wo, gain2, wgu, wd):
+    sections, contexts, parts = mesh_sizes
+    half_parts = parts // 2
+    section = lax.axis_index("section")
+    ctx = lax.axis_index("ctx")
+    tp = lax.axis_index("tp")
+    leading = section == 0
+    batch = tp // half_parts
+    model_width = inputs.shape[2]
+    rows = inputs.shape[1]
+    heads = wqkv.shape[2] * parts
+    units = wd.shape[1] // contexts
+    number = lambda s, c, t: (s * contexts + c) * parts + t
+    places = [
+        (s, c, t) for s in range(sections) for c in range(contexts) for t in range(parts)
+    ]
+    everyone = [[number(*place) for place in places]]
+    token_of = lambda s, c, t: c * parts + t % half_parts + half_parts * s
+    batch_groups = device_groups(mesh_sizes, lambda s, c, t: t // half_parts, token_of)
+    side_groups = device_groups(mesh_sizes, lambda s, c, t: c % 2, lambda s, c, t: (s, c, t))
+    side_out_groups = device_groups(mesh_sizes, lambda s, c, t: c % 2, lambda s, c, t: (c, t, s))
+    all_out_groups = device_groups(mesh_sizes, lambda s, c, t: 0, lambda s, c, t: (c, t, s))
+
+    crossing = [
+        (number(s, c, t), number(s, c, (t + half_parts) % parts))
+        for s, c, t in places
+        if t // half_parts == s
+    ]
+
+    def to_batch(value):
+        mine = lax.dynamic_index_in_dim(value, batch, 0, keepdims=False)
+        other = lax.dynamic_index_in_dim(value, 1 - batch, 0, keepdims=False)
+        moved = lax.ppermute(other, ALL_AXES, crossing)
+        return jnp.where(section == batch, mine, moved)
+
+    def to_home(value, layer):
+        stay = [
+            (number(s, c, t), number(layer, c, t)) for s, c, t in places if t // half_parts == s
+        ]
+        cross = [
+            (number(s, c, t), number(layer, c, (t + half_parts) % parts))
+            for s, c, t in places
+            if t // half_parts != s
+        ]
+        return (lax.ppermute(value, ALL_AXES, stay), lax.ppermute(value, ALL_AXES, cross))
+
+    def at_home(first_pair, second_pair):
+        near = jnp.where(leading, first_pair[0], second_pair[0])
+        far = jnp.where(leading, first_pair[1], second_pair[1])
+        upper = batch == 0
+        return jnp.stack([jnp.where(upper, near, far), jnp.where(upper, far, near)])[None]
+
+    def swap_side(value):
+        return lax.ppermute(value, "ctx", [(c, c ^ 1) for c in range(contexts)])
+
+    def swap_section(value):
+        return lax.ppermute(value, "section", [(0, 1), (1, 0)])
+
+    def gather(value, groups):
+        return lax.all_gather(value, ALL_AXES, axis=0, tiled=True, axis_index_groups=groups)
+
+    def own_part(value, axis, size):
+        return lax.dynamic_slice_in_dim(value, ctx * size, size, axis)
+
+    rows_in = to_batch(inputs)
+    grad_in = to_batch(cotangent)
+
+    head_part = own_part(wqkv[0], 1, heads // (parts * contexts)).reshape(-1, model_width)
+    out_part = own_part(wo[0], 0, HD)
+    gate_piece = own_part(wgu[0, 0], 0, units)
+    up_piece = own_part(wgu[0, 1], 0, units)
+    down_piece = own_part(wd[0], 0, units)
+    w_heads = gather(head_part, everyone).reshape(2, -1, model_width)
+    w_outs = gather(out_part, everyone).reshape(2, -1, model_width)
+    w_gates = gather(gate_piece, side_groups).reshape(2, -1, model_width)
+    w_ups = gather(up_piece, side_groups).reshape(2, -1, model_width)
+    w_downs = gather(down_piece, side_groups).reshape(2, -1, model_width)
+    gains = jnp.concatenate([gain1, gain2], axis=0).astype(jnp.float32)
+    other_gains = swap_section(gains)
+    gain_sets = (jnp.where(leading, gains, other_gains), jnp.where(leading, other_gains, gains))
+
+    seq_lengths = lax.dynamic_index_in_dim(lengths, batch, 0, keepdims=False)
+    ends = jnp.cumsum(seq_lengths).astype(jnp.int32)
+    token_index = (ctx * parts + tp % half_parts + half_parts * section) * rows + jnp.arange(
+        rows, dtype=jnp.int32
+    )
+    before = (ends[None, :] <= token_index[:, None]).astype(jnp.int32)
+    position = token_index - jnp.sum(before * seq_lengths[None, :], axis=1)
+    half_width = HD // 2
+    frequency = jnp.exp(
+        -jnp.log(10000.0) * jnp.arange(half_width, dtype=jnp.float32) / half_width
+    )
+    angles = position.astype(jnp.float32)[None, :] * frequency[:, None]
+    cosine, sine_part = jnp.cos(angles), jnp.sin(angles)
+
+    def low(value):
+        return value.astype(jnp.bfloat16)
+
+    def layer_forward(whole_rows, first_values, layer):
+        gain_first, gain_second = gain_sets[layer][0], gain_sets[layer][1]
+        scale_first = lax.rsqrt(jnp.mean(whole_rows * whole_rows, axis=-1, keepdims=True) + EPSILON)
+        normed = low(whole_rows * scale_first * gain_first)
+        projected = dot(w_heads[layer], normed, 1, 1).reshape(heads, 3, HD, rows)
+        query = rope_pairs(projected[:, 0], cosine, sine_part) * HD ** (-0.5)
+        key = rope_pairs(projected[:, 1], cosine, sine_part)
+        value = projected[:, 2]
+        if first_values is not None:
+            value = 0.5 * value + 0.5 * first_values.astype(jnp.float32)
+        mixed = low(value)
+        qkv = exchange(jnp.concatenate([low(query), low(key), mixed], axis=1), batch_groups)
+        out, lse = attention_forward(ends, qkv)
+        attended = exchange(out, batch_groups).reshape(heads * HD, rows)
+        hidden = whole_rows + dot(attended, w_outs[layer], 0, 0)
+        scale_second = lax.rsqrt(jnp.mean(hidden * hidden, axis=-1, keepdims=True) + EPSILON)
+        normed_second = low(hidden * scale_second * gain_second)
+        ffn_rows = (normed_second, swap_side(normed_second))
+        gates = [dot(part, w_gates[layer], 1, 1) for part in ffn_rows]
+        ups = [dot(part, w_ups[layer], 1, 1) for part in ffn_rows]
+        activated = [low(jax.nn.silu(gate) * up) for gate, up in zip(gates, ups)]
+        far_down = swap_side(low(dot(activated[1], w_downs[layer], 1, 0)))
+        layer_out = low(
+            hidden + (dot(activated[0], w_downs[layer], 1, 0) + far_down.astype(jnp.float32))
+        )
+        saved = (
+            whole_rows, scale_first, normed, qkv, out, lse, attended, hidden, scale_second,
+            ffn_rows, gates, ups, activated,
+        )
+        return layer_out, mixed, saved
+
+    def norm_back(whole_rows, scale_rows, gain, grad_normed, grad_rest):
+        unit_rows = whole_rows * scale_rows
+        scaled = grad_normed * gain
+        grad_gain = jnp.sum(grad_normed * unit_rows, axis=0)
+        grad_whole = grad_rest + scale_rows * (
+            scaled - unit_rows * jnp.mean(scaled * unit_rows, axis=-1, keepdims=True)
+        )
+        return grad_gain, grad_whole
+
+    def reduce_weight(partial_sum, groups):
+        mine = lax.psum_scatter(
+            low(partial_sum), ALL_AXES, scatter_dimension=0, tiled=True, axis_index_groups=groups
+        )
+        return lax.all_gather(mine, "ctx", axis=0, tiled=False)
+
+    def layer_backward(grad_rows, extra_values, saved, layer):
+        (
+            whole_rows, scale_first, normed, qkv, out, lse, attended, hidden, scale_second,
+            ffn_rows, gates, ups, activated,
+        ) = saved
+        gain_first, gain_second = gain_sets[layer][0], gain_sets[layer][1]
+        grad_down = low(grad_rows)
+        grad_downs = (grad_down, swap_side(grad_down))
+        grad_gates, grad_ups = [], []
+        for part, gate, up in zip(grad_downs, gates, ups):
+            grad_act = dot(part, w_downs[layer], 1, 1)
+            sigmoid_gate = jax.nn.sigmoid(gate)
+            grad_gates.append(
+                low(grad_act * up * sigmoid_gate * (1.0 + gate * (1.0 - sigmoid_gate)))
+            )
+            grad_ups.append(low(grad_act * gate * sigmoid_gate))
+        back = [
+            dot(grad_gate, w_gates[layer], 1, 0) + dot(grad_up, w_ups[layer], 1, 0)
+            for grad_gate, grad_up in zip(grad_gates, grad_ups)
+        ]
+        far_back = swap_side(low(back[1]))
+        grad_gain2, grad_hidden = norm_back(
+            hidden, scale_second, gain_second, back[0] + far_back.astype(jnp.float32),
+            grad_rows.astype(jnp.float32),
+        )
+        grad_branch = low(grad_hidden)
+        grad_heads = low(dot(w_outs[layer], grad_branch, 1, 1)).reshape(heads, HD, rows)
+        grad_heads = exchange(grad_heads, batch_groups)
+        join = lambda pair: jnp.concatenate(pair, axis=0)
+        all_rows, all_down = join(ffn_rows), join(grad_downs)
+        grad_wd = reduce_weight(dot(join(activated), all_down, 0, 0), side_out_groups)
+        grad_wgate = reduce_weight(dot(join(grad_gates), all_rows, 0, 0), side_out_groups)
+        grad_wup = reduce_weight(dot(join(grad_ups), all_rows, 0, 0), side_out_groups)
+        grad_wo = reduce_weight(dot(attended, grad_branch, 1, 0), all_out_groups)
+        grad_qkv = attention_backward(ends, qkv, out, grad_heads, lse)
+        grad_qkv = exchange(grad_qkv, batch_groups).reshape(heads, 3, HD, rows)
+        grad_query = rope_pairs(grad_qkv[:, 0].astype(jnp.float32), cosine, -sine_part)
+        grad_key = rope_pairs(grad_qkv[:, 1].astype(jnp.float32), cosine, -sine_part)
+        grad_value = grad_qkv[:, 2].astype(jnp.float32)
+        send_values = None
+        if extra_values is None:
+            grad_value = 0.5 * grad_value
+            send_values = low(grad_value)
+        else:
+            grad_value = grad_value + extra_values.astype(jnp.float32)
+        grad_projected = jnp.concatenate(
+            [low(grad_query), low(grad_key), low(grad_value)], axis=1
+        ).reshape(3 * heads * HD, rows)
+        grad_normed = dot(grad_projected, w_heads[layer], 0, 0)
+        grad_wqkv = reduce_weight(dot(grad_projected, normed, 1, 0), all_out_groups)
+        grad_gain1, grad_whole = norm_back(
+            whole_rows, scale_first, gain_first, grad_normed, grad_hidden
+        )
+        return grad_whole, send_values, (grad_gain1, grad_gain2), (
+            grad_wqkv, grad_wo, grad_wgate, grad_wup, grad_wd,
+        )
+
+    first_out, first_values, first_saved = layer_forward(rows_in.astype(jnp.float32), None, 0)
+    first_home = to_home(first_out, 0)
+    second_out, _, second_saved = layer_forward(first_out.astype(jnp.float32), first_values, 1)
+    second_home = to_home(second_out, 1)
+    second_grad, send_values, second_gains, second_grads = layer_backward(
+        grad_in, None, second_saved, 1
+    )
+    second_grad = low(second_grad)
+    second_grad_home = to_home(second_grad, 1)
+    first_grad, _, first_gains, first_grads = layer_backward(
+        second_grad, send_values, first_saved, 0
+    )
+    first_grad_home = to_home(low(first_grad), 0)
+
+    gain_total = lax.psum(
+        jnp.stack([first_gains[0], first_gains[1], second_gains[0], second_gains[1]]), ALL_AXES
+    )
+    gain_total = jnp.where(leading, gain_total[:2], gain_total[2:])
+
+    def finish(first_half, second_half):
+        mine = jnp.where(leading, first_half, second_half)
+        moved = swap_section(jnp.where(leading, second_half, first_half))
+        lower = jnp.where(leading, mine, moved)
+        upper = jnp.where(leading, moved, mine)
+        return jnp.concatenate([lower, upper], axis=1).astype(jnp.float32)
+
+    grad_wqkv, grad_wo, grad_wgate, grad_wup, grad_wd = [
+        finish(first, second) for first, second in zip(first_grads, second_grads)
+    ]
+    grad_wqkv = grad_wqkv.reshape(contexts, 3, HD, model_width).transpose(1, 0, 2, 3)
+    return (
+        at_home(first_home, second_home),
+        at_home(first_grad_home, second_grad_home).astype(jnp.float32),
+        gain_total[0:1],
+        grad_wqkv[None],
+        grad_wo.reshape(wo.shape),
+        gain_total[1:2],
+        jnp.stack([grad_wgate.reshape(wd.shape[1:]), grad_wup.reshape(wd.shape[1:])])[None],
+        grad_wd.reshape(wd.shape),
+    )
+
+
+def body(mesh_sizes, *arguments):
+    inputs, _, _, _, wqkv = arguments[:5]
+    sections, contexts, parts = mesh_sizes
+    own_heads, own_units = wqkv.shape[2], arguments[7].shape[2]
+    fits = (
+        sections == 2
+        and inputs.shape[0] == 2
+        and contexts % 2 == 0
+        and parts % 2 == 0
+        and own_heads == contexts
+        and own_units % (16 * contexts) == 0
+        and inputs.shape[1] % 128 == 0
+    )
+    if fits:
+        return split_body(mesh_sizes, *arguments)
+    return general_body(*arguments)
+
+
 def solution(mesh):
     placed = (
         P(None, ("ctx", "tp"), None),
@@ -481,8 +963,9 @@
         P("section", None, "tp", None),
         P("section", "tp", None),
     )
+    mesh_sizes = tuple(mesh.shape[axis] for axis in ALL_AXES)
     return jax.shard_map(
-        body,
+        functools.partial(body, mesh_sizes),
         mesh=mesh,
         in_specs=placed,
         out_specs=(

time: 2690 us -> 1500 us (0.56)
  waiting for transfers between devices: 1910 us -> 783 us
  blocking collectives: 42.2 us -> 266 us
  Pallas kernels: 0 us -> 164 us
  local copies, waits for them, and re-layouts: 169 us -> 24.2 us
  matrix products: 286 us -> 147 us
  other arithmetic: 149 us -> 29.1 us
  loops' own time: 91.9 us -> 0 us
  starting transfers between devices: 16.4 us -> 59.9 us
    reduce_scatter x15 -> x10, waiting for transfers between devices: 1130 us -> 435 us  [reduce_weight(): lax.psum_scatter(low(partial_sum), ALL_AXES, scatter_dimension=0, tiled=T...]
    all_gather x15 -> x5, waiting for transfers between devices: 675 us -> 224 us  [gather(): lax.all_gather(value, ALL_AXES, axis=0, tiled=True, axis_index_groups=gro...]
    pallas_call x0 -> x4, Pallas kernels: none -> 164 us  [the longest x2 82.3 us: attention_forward(): pl.pallas_call(attention_forward_kernel, grid_spec=pltpu.PrefetchScalarGr...]
    dot_general x57 -> x42, matrix products: 286 us -> 147 us  [dot(): lax.dot_general(left, right, (((left_dim,), (right_dim,)), ((), ())), pre...]
    all_gather x0 -> x10, blocking collectives: none -> 113 us  [reduce_weight(): return lax.all_gather(mine, 'ctx', axis=0, tiled=False)]
    all_to_all x0 -> x5, blocking collectives: none -> 113 us  [exchange(): lax.all_to_all(value, ALL_AXES, split_axis=0, concat_axis=0, tiled=True,...]
    psum x1 -> x0, waiting for transfers between devices: 97.7 us -> none  [body(): lax.psum(grad_wqkv.astype(jnp.bfloat16), 'ctx').astype(jnp.float32)]
    another operation x45 -> x0, loops' own time: 91.9 us -> none  [the longest x3 30.7 us: attend_back(): lax.scan(grad_step, jnp.zeros((row_count, head_count, HD), jnp.float32),...]
  transfers between devices with their start and end apart: 39 -> 42, of which waited for: 35 -> 22; matrix products, arithmetic and copies ran while one was open for 4% -> 11% of each run, Pallas kernels for 0% -> 8%
where the time goes in v1:
time: 1500 us; the launch traced here: 1490 us
  waiting for transfers between devices  783 us (52%)
  blocking collectives  266 us (18%)
  Pallas kernels  164 us (11%)
  matrix products  147 us (10%)
  starting transfers between devices  59.9 us (4%)
  other arithmetic  29.1 us (2%)
  local copies, waits for them, and re-layouts  24.2 us (2%)
  between operations  15.6 us (1%)
    reduce_scatter x10, waiting for transfers between devices, reduce_weight(): lax.psum_scatter(low(partial_sum), ALL_AXES, scatter_dimension=0, tiled=T...  435 us
    all_gather x5, waiting for transfers between devices, gather(): lax.all_gather(value, ALL_AXES, axis=0, tiled=True, axis_index_groups=gro...  224 us
    dot_general x42, matrix products, dot(): lax.dot_general(left, right, (((left_dim,), (right_dim,)), ((), ())), pre...  147 us
    all_gather x10, blocking collectives, reduce_weight(): return lax.all_gather(mine, 'ctx', axis=0, tiled=False)  113 us
    all_to_all x5, blocking collectives, exchange(): lax.all_to_all(value, ALL_AXES, split_axis=0, concat_axis=0, tiled=True,...  113 us
    pallas_call x2, Pallas kernels, attention_forward(): pl.pallas_call(attention_forward_kernel, grid_spec=pltpu.PrefetchScalarGr...  82.3 us
    pallas_call x2, Pallas kernels, attention_backward(): pl.pallas_call(attention_backward_kernel, grid_spec=pltpu.PrefetchScalarG...  81.7 us
    ppermute x8, waiting for transfers between devices, swap_side(): return lax.ppermute(value, 'ctx', [(c, c ^ 1) for c in range(contexts)])  44.4 us
  transfers between devices with their start and end apart: 42, of which 22 were waited for; matrix products, arithmetic and copies ran while one was open for 11% of the time, Pallas kernels for 8%

profile of v1, /device:TPU:0, one launch (start us, length us, event | category | flops | bytes accessed | tf_op | source)
XLA Modules:
  0.0 1488.1 jit_solution(6824930587536672048)
XLA Ops:
  34.0 82.1 %all-gather.20.cloned.1.call-done = bf16[6144,1024]{1,0:T(8,128)(2,1)} async-done(((bf16[192,1024]{1,0:T(8,128)(2,1)}), bf16[6144,1024]{1,0:T(8,128)(2,1)}) %all-gather.20.cloned.1.call-update) | async-done | bytes 12582928 | tf_op jit(solution)/shard_map/all_gather | solution.py:752
  122.7 25.7 %all_to_all.40.qkv_ref = bf16[16,192,256]{2,1,0:T(8,128)(2,1)S(1)} all-to-all(bf16[16,192,256]{2,1,0:T(8,128)(2,1)S(1)} %pad_maximum_fusion), channel_id=1, replica_groups={{0,1,16,17,4,5,20,21,8,9,24,25,12,13,28,29},{2,3,18,19,6,7,22,23,10,11,..., dimensions={0} | all-to-all | bytes 3145728 | tf_op jit(solution)/shard_map/all_to_all | solution.py:490
  148.5 41.5 %attention_forward.2 = (bf16[16,64,256]{2,1,0:T(8,128)(2,1)}, f32[16,1,256]{2,1,0:T(1,128)S(1)}) custom-call(s32[4]{0:T(128)S(1)} %bitcast.268, bf16[16,192,256]{2,1,0:T(8,128)(2,1)S(1)} %all_to_all.40.qkv_ref), custom_call_target="tpu_custom_call" | custom-call | flops 2281701376 | bytes 1572864 | tf_op jit(solution)/shard_map/attention_forward/pallas_call | solution.py:573
  194.4 14.7 all-to-all-done.1
  216.1 34.0 %all-gather.24.cloned.1.call-done = bf16[1,1,2816,1024]{3,2,1,0:T(8,128)(2,1)} async-done(((bf16[1,1,176,1024]{3,2,1,0:T(8,128)(2,1)}), bf16[1,1,2816,1024]{3,2,1,0:T(8,128)(2,1)}) %all-gather.24.cloned.1.call-update) | async-done | bytes 5767184 | tf_op jit(solution)/shard_map/all_gather | solution.py:752
  258.2 52.3 %all-gather.26.cloned.1.call-done = bf16[1,1,2816,1024]{3,2,1,0:T(8,128)(2,1)} async-done(((bf16[1,1,176,1024]{3,2,1,0:T(8,128)(2,1)}), bf16[1,1,2816,1024]{3,2,1,0:T(8,128)(2,1)}) %all-gather.26.cloned.1.call-update) | async-done | bytes 5767184 | tf_op jit(solution)/shard_map/all_gather | solution.py:752
  315.4 55.5 %all-gather.28.cloned.1.call-done = bf16[1,2816,1024]{2,1,0:T(8,128)(2,1)} async-done(((bf16[1,176,1024]{2,1,0:T(8,128)(2,1)}), bf16[1,2816,1024]{2,1,0:T(8,128)(2,1)}) %all-gather.28.cloned.1.call-update) | async-done | bytes 5767184 | tf_op jit(solution)/shard_map/all_gather | solution.py:752
  393.6 23.6 %all_to_all.41.qkv_ref = bf16[16,192,256]{2,1,0:T(8,128)(2,1)S(1)} all-to-all(bf16[16,192,256]{2,1,0:T(8,128)(2,1)S(1)} %pad_maximum_fusion.1), channel_id=1, replica_groups={{0,1,16,17,4,5,20,21,8,9,24,25,12,13,28,29},{2,3,18,19,6,7,22,23,10,11,..., dimensions={0} | all-to-all | bytes 3145728 | tf_op jit(solution)/shard_map/all_to_all | solution.py:490
  417.1 40.8 %attention_forward.3 = (bf16[16,64,256]{2,1,0:T(8,128)(2,1)S(1)}, f32[16,1,256]{2,1,0:T(1,128)S(1)}) custom-call(s32[4]{0:T(128)S(1)} %bitcast.269, bf16[16,192,256]{2,1,0:T(8,128)(2,1)S(1)} %all_to_all.41.qkv_ref), custom_call_target="tpu_custom_call" | custom-call | flops 2281701376 | bytes 1572864 | tf_op jit(solution)/shard_map/attention_forward/pallas_call | solution.py:573
  553.9 19.8 %all_to_all.42.grad_ref = bf16[16,64,256]{2,1,0:T(8,128)(2,1)S(1)} all-to-all(bf16[16,64,256]{2,1,0:T(8,128)(2,1)S(1)} %bitcast.303), channel_id=1, replica_groups={{0,1,16,17,4,5,20,21,8,9,24,25,12,13,28,29},{2,3,18,19,6,7,22,23,10,11,..., dimensions={0} | all-to-all | bytes 1048576 | tf_op jit(solution)/shard_map/all_to_all | solution.py:490
  573.8 40.3 %attention_backward.2 = bf16[16,192,256]{2,1,0:T(8,128)(2,1)S(1)} custom-call(s32[4]{0:T(128)S(1)} %bitcast.270, bf16[16,192,256]{2,1,0:T(8,128)(2,1)S(1)} %all_to_all.41.qkv_ref, bf16[16,64,256]{2,1,0:T(8,128)(2,1)S(1)} %copy-done.4, bf16[16,64,256]{2,1,0:T(8,128)(2,1)S(1)} %all_to_all.42.grad_ref, f32[16,1,256]{2,1,0:T(1,128)S(1)} %get-tuple-element.14.lse_ref), custom_call_target="tpu_custom_call" | custom-call | flops 5704253440 | bytes 4718592 | tf_op jit(solution)/shard_map/attention_backward/pallas_call | solution.py:659
  622.8 21.7 %all-to-all-done.5 = bf16[16,192,256]{2,1,0:T(8,128)(2,1)S(1)} async-done(((bf16[16,192,256]{2,1,0:T(8,128)(2,1)}), bf16[16,192,256]{2,1,0:T(8,128)(2,1)S(1)}, u32[]{:S(2)}, u32[]{:S(2)}) %all-to-all-start.5) | async-done | bytes 1572896 | tf_op jit(solution)/shard_map/all_to_all | solution.py:490
  721.6 16.7 %all_to_all.43.grad_ref = bf16[16,64,256]{2,1,0:T(8,128)(2,1)S(1)} all-to-all(bf16[16,64,256]{2,1,0:T(8,128)(2,1)S(1)} %bitcast.302), channel_id=1, replica_groups={{0,1,16,17,4,5,20,21,8,9,24,25,12,13,28,29},{2,3,18,19,6,7,22,23,10,11,..., dimensions={0} | all-to-all | bytes 1048576 | tf_op jit(solution)/shard_map/all_to_all | solution.py:490
  738.3 41.4 %attention_backward.3 = bf16[16,192,256]{2,1,0:T(8,128)(2,1)S(1)} custom-call(s32[4]{0:T(128)S(1)} %bitcast.271, bf16[16,192,256]{2,1,0:T(8,128)(2,1)S(1)} %all_to_all.40.qkv_ref, bf16[16,64,256]{2,1,0:T(8,128)(2,1)} %get-tuple-element.12.out_ref, bf16[16,64,256]{2,1,0:T(8,128)(2,1)S(1)} %all_to_all.43.grad_ref, f32[16,1,256]{2,1,0:T(1,128)S(1)} %get-tuple-element.15.lse_ref), custom_call_target="tpu_custom_call" | custom-call | flops 5704253440 | bytes 4718592 | tf_op jit(solution)/shard_map/attention_backward/pallas_call | solution.py:659
  779.7 27.0 %all_to_all.44 = bf16[16,192,256]{2,1,0:T(8,128)(2,1)S(1)} all-to-all(bf16[16,192,256]{2,1,0:T(8,128)(2,1)S(1)} %attention_backward.3), channel_id=1, replica_groups={{0,1,16,17,4,5,20,21,8,9,24,25,12,13,28,29},{2,3,18,19,6,7,22,23,10,11,..., dimensions={0} | all-to-all | bytes 3145728 | tf_op jit(solution)/shard_map/all_to_all | solution.py:490
  829.0 14.6 collective-permute-done.8
  859.4 12.7 all-gather.9
  898.8 48.4 %reduce-scatter.27.cloned.1.call-done = bf16[88,1024]{1,0:T(8,128)(2,1)} async-done(((bf16[1408,1024]{1,0:T(8,128)(2,1)}), bf16[88,1024]{1,0:T(8,128)(2,1)}) %reduce-scatter.27.cloned.1.call-update) | async-done | bytes 180240 | tf_op jit(solution)/shard_map/reduce_scatter | solution.py:832
  961.1 55.2 %reduce-scatter.19.cloned.1.call-done = bf16[88,1024]{1,0:T(8,128)(2,1)} async-done(((bf16[1408,1024]{1,0:T(8,128)(2,1)}), bf16[88,1024]{1,0:T(8,128)(2,1)}) %reduce-scatter.19.cloned.1.call-update) | async-done | bytes 180240 | tf_op jit(solution)/shard_map/reduce_scatter | solution.py:832
  1028.1 56.4 %reduce-scatter.23.cloned.1.call-done = bf16[88,1024]{1,0:T(8,128)(2,1)} async-done(((bf16[1408,1024]{1,0:T(8,128)(2,1)}), bf16[88,1024]{1,0:T(8,128)(2,1)}) %reduce-scatter.23.cloned.1.call-update) | async-done | bytes 180240 | tf_op jit(solution)/shard_map/reduce_scatter | solution.py:832
  1103.7 39.7 %psum.7 = f32[4,1024]{1,0:T(4,128)S(1)} all-reduce(f32[4,1024]{1,0:T(4,128)S(1)} %pad_maximum_fusion.13), channel_id=1, replica_groups=mesh['section'=2,'ctx'=4,'tp'=4] {'section','ctx','tp'}, use_global_device_ids=true, to_apply=%region_14.15 | all-reduce | flops 4096 | bytes 32768 | tf_op jit(solution)/shard_map/psum | solution.py:908
  1143.7 79.6 %reduce-scatter.15.cloned.1.call-done = bf16[32,1024]{1,0:T(8,128)(2,1)} async-done(((bf16[1024,1024]{1,0:T(8,128)(2,1)}), bf16[32,1024]{1,0:T(8,128)(2,1)}) %reduce-scatter.15.cloned.1.call-update) | async-done | bytes 65552 | tf_op jit(solution)/shard_map/reduce_scatter | solution.py:832
  1252.0 88.0 %reduce-scatter.13.cloned.1.call-done = bf16[96,1024]{1,0:T(8,128)(2,1)} async-done(((bf16[3072,1024]{1,0:T(8,128)(2,1)}), bf16[96,1024]{1,0:T(8,128)(2,1)}) %reduce-scatter.13.cloned.1.call-update) | async-done | bytes 196624 | tf_op jit(solution)/shard_map/reduce_scatter | solution.py:832
  1352.2 107.7 %reduce-scatter.11.cloned.1.call-done = bf16[96,1024]{1,0:T(8,128)(2,1)} async-done(((bf16[3072,1024]{1,0:T(8,128)(2,1)}), bf16[96,1024]{1,0:T(8,128)(2,1)}) %reduce-scatter.11.cloned.1.call-update) | async-done | bytes 196624 | tf_op jit(solution)/shard_map/reduce_scatter | solution.py:832
  (377 shorter events, 432.9 us)
Async XLA Ops:
  7.2 109.0 %all-gather.20.cloned.1.call-start = ((), (), s32[]{:S(2)}) async-start(), calls=%async_computation.18 | async-start | bytes 12976128 | tf_op jit(solution)/shard_map/all_gather | solution.py:752
  9.4 185.0 %all-gather.22.cloned.1.call-start = ((), (), s32[]{:S(2)}) async-start(), calls=%async_computation.29 | async-start | bytes 4325376 | tf_op jit(solution)/shard_map/all_gather | solution.py:752
  11.0 239.1 %all-gather.24.cloned.1.call-start = ((), (), s32[]{:S(2)}) async-start(), calls=%async_computation.30 | async-start | bytes 6127616 | tf_op jit(solution)/shard_map/all_gather | solution.py:752
  14.0 296.5 %all-gather.26.cloned.1.call-start = ((), (), s32[]{:S(2)}) async-start(), calls=%async_computation.31 | async-start | bytes 6127616 | tf_op jit(solution)/shard_map/all_gather | solution.py:752
  14.8 356.1 %all-gather.28.cloned.1.call-start = ((), (), s32[]{:S(2)}) async-start(), calls=%async_computation.32 | async-start | bytes 6127616 | tf_op jit(solution)/shard_map/all_gather | solution.py:752
  211.9 42.2 %collective-permute-start.2 = (bf16[256,1024]{1,0:T(8,128)(2,1)S(1)}, bf16[256,1024]{1,0:T(8,128)(2,1)}, u32[]{:S(2)}, u32[]{:S(2)}) collective-permute-start(bf16[256,1024]{1,0:T(8,128)(2,1)S(1)} %multiply_convert_fusion.14), channel_id=1, source_target_pairs={{0,4},{4,0},{8,12},{12,8},{1,5},{5,1},{9,13},{13,9},{2,6},{6,2},{1... | collective-permute-start | bytes 1572872 | tf_op jit(solution)/shard_map/ppermute | solution.py:746
  463.0 383.8 %reduce-scatter.29.cloned.1.call-start = ((), (), s32[]{:S(2)}) async-start(), calls=%async_computation.28 | async-start | bytes 3063808 | tf_op jit(solution)/shard_map/reduce_scatter | solution.py:832
  509.7 349.7 %reduce-scatter.21.cloned.1.call-start = ((), (), s32[]{:S(2)}) async-start(), calls=%async_computation.24 | async-start | bytes 3063808 | tf_op jit(solution)/shard_map/reduce_scatter | solution.py:832
  514.6 357.4 %reduce-scatter.25.cloned.1.call-start = ((), (), s32[]{:S(2)}) async-start(), calls=%async_computation.26 | async-start | bytes 3063808 | tf_op jit(solution)/shard_map/reduce_scatter | solution.py:832
  615.2 29.3 %all-to-all-start.5 = ((bf16[16,192,256]{2,1,0:T(8,128)(2,1)}), bf16[16,192,256]{2,1,0:T(8,128)(2,1)S(1)}, u32[]{:S(2)}, u32[]{:S(2)}) async-start(bf16[16,192,256]{2,1,0:T(8,128)(2,1)} %copy-done.2), calls=%async_computation.5 | async-start | bytes 3145728 | tf_op jit(solution)/shard_map/all_to_all | solution.py:490
  619.1 270.2 %reduce-scatter.17.cloned.1.call-start = ((), (), s32[]{:S(2)}) async-start(), calls=%async_computation.22 | async-start | bytes 2162688 | tf_op jit(solution)/shard_map/reduce_scatter | solution.py:832
  622.6 324.6 %reduce-scatter.27.cloned.1.call-start = ((), (), s32[]{:S(2)}) async-start(), calls=%async_computation.27 | async-start | bytes 3063808 | tf_op jit(solution)/shard_map/reduce_scatter | solution.py:832
  668.7 347.6 %reduce-scatter.19.cloned.1.call-start = ((), (), s32[]{:S(2)}) async-start(), calls=%async_computation.23 | async-start | bytes 3063808 | tf_op jit(solution)/shard_map/reduce_scatter | solution.py:832
  683.6 400.9 %reduce-scatter.23.cloned.1.call-start = ((), (), s32[]{:S(2)}) async-start(), calls=%async_computation.25 | async-start | bytes 3063808 | tf_op jit(solution)/shard_map/reduce_scatter | solution.py:832
  688.5 534.8 %reduce-scatter.15.cloned.1.call-start = ((), (), s32[]{:S(2)}) async-start(), calls=%async_computation.21 | async-start | bytes 2162688 | tf_op jit(solution)/shard_map/reduce_scatter | solution.py:832
  713.2 626.8 %reduce-scatter.13.cloned.1.call-start = ((), (), s32[]{:S(2)}) async-start(), calls=%async_computation.20 | async-start | bytes 6488064 | tf_op jit(solution)/shard_map/reduce_scatter | solution.py:832
  719.2 740.7 %reduce-scatter.11.cloned.1.call-start = ((), (), s32[]{:S(2)}) async-start(), calls=%async_computation.19 | async-start | bytes 6488064 | tf_op jit(solution)/shard_map/reduce_scatter | solution.py:832
  814.4 29.1 %collective-permute-start.8 = (bf16[256,1024]{1,0:T(8,128)(2,1)S(1)}, bf16[256,1024]{1,0:T(8,128)(2,1)S(1)}, u32[]{:S(2)}, u32[]{:S(2)}) collective-permute-start(bf16[256,1024]{1,0:T(8,128)(2,1)S(1)} %copy-done.12), channel_id=1, source_target_pairs={{2,0},{3,1},{6,4},{7,5},{10,8},{11,9},{14,12},{15,13},{16,2},{17,3... | collective-permute-start | bytes 1572872 | tf_op jit(solution)/shard_map/ppermute | solution.py:737
  815.7 27.8 %collective-permute-start.4 = (bf16[256,1024]{1,0:T(8,128)(2,1)S(1)}, bf16[256,1024]{1,0:T(8,128)(2,1)S(1)}, u32[]{:S(2)}, u32[]{:S(2)}) collective-permute-start(bf16[256,1024]{1,0:T(8,128)(2,1)S(1)} %copy-done.12), channel_id=1, source_target_pairs={{0,0},{1,1},{4,4},{5,5},{8,8},{9,9},{12,12},{13,13},{18,2},{19,3},... | collective-permute-start | bytes 1572872 | tf_op jit(solution)/shard_map/ppermute | solution.py:737
  816.4 27.1 %collective-permute-start.9 = (bf16[256,1024]{1,0:T(8,128)(2,1)}, bf16[256,1024]{1,0:T(8,128)(2,1)}, u32[]{:S(2)}, u32[]{:S(2)}) collective-permute-start(bf16[256,1024]{1,0:T(8,128)(2,1)} %get-tuple-element.93), channel_id=1, source_target_pairs={{2,16},{3,17},{6,20},{7,21},{10,24},{11,25},{14,28},{15,29},{16,18... | collective-permute-start | bytes 1572872 | tf_op jit(solution)/shard_map/ppermute | solution.py:737
  817.9 26.6 %collective-permute-start.7 = (bf16[256,1024]{1,0:T(8,128)(2,1)}, bf16[256,1024]{1,0:T(8,128)(2,1)}, u32[]{:S(2)}, u32[]{:S(2)}) collective-permute-start(bf16[256,1024]{1,0:T(8,128)(2,1)} %get-tuple-element.93), channel_id=1, source_target_pairs={{0,16},{1,17},{4,20},{5,21},{8,24},{9,25},{12,28},{13,29},{18,18},... | collective-permute-start | bytes 1572872 | tf_op jit(solution)/shard_map/ppermute | solution.py:737
  883.0 352.7 %collective-permute-start.18 = (bf16[256,1024]{1,0:T(8,128)(2,1)}, bf16[256,1024]{1,0:T(8,128)(2,1)}, u32[]{:S(2)}, u32[]{:S(2)}) collective-permute-start(bf16[256,1024]{1,0:T(8,128)(2,1)} %copy-done.28), channel_id=1, source_target_pairs={{2,16},{3,17},{6,20},{7,21},{10,24},{11,25},{14,28},{15,29},{16,18... | collective-permute-start | bytes 1572872 | tf_op jit(solution)/shard_map/ppermute | solution.py:737
  884.5 351.6 %collective-permute-start.16 = (bf16[256,1024]{1,0:T(8,128)(2,1)}, bf16[256,1024]{1,0:T(8,128)(2,1)}, u32[]{:S(2)}, u32[]{:S(2)}) collective-permute-start(bf16[256,1024]{1,0:T(8,128)(2,1)} %copy-done.28), channel_id=1, source_target_pairs={{0,16},{1,17},{4,20},{5,21},{8,24},{9,25},{12,28},{13,29},{18,18},... | collective-permute-start | bytes 1572872 | tf_op jit(solution)/shard_map/ppermute | solution.py:737
  961.1 286.4 %collective-permute-start.23 = (bf16[4,88,1024]{2,1,0:T(8,128)(2,1)}, bf16[4,88,1024]{2,1,0:T(8,128)(2,1)}, u32[]{:S(2)}, u32[]{:S(2)}) collective-permute-start(bf16[4,88,1024]{2,1,0:T(8,128)(2,1)} %bitcast.71), channel_id=1, source_target_pairs={{0,16},{16,0},{1,17},{17,1},{2,18},{18,2},{3,19},{19,3},{4,20},{20... | collective-permute-start | bytes 2162696 | tf_op jit(solution)/shard_map/ppermute | solution.py:749
  (93 other events, 1403.5 us)
Sparse Core Ops, SparseCore 0:
  11.5 104.6 all-gather.19
  119.7 65.5 all-gather.21
  188.2 61.8 all-gather.23
  252.9 57.6 all-gather.25
  313.3 57.6 all-gather.27
  509.8 75.9 reduce-scatter.28
  590.6 79.3 reduce-scatter.20
  674.4 65.2 reduce-scatter.24
  742.0 139.5 reduce-scatter.16
  885.3 61.9 reduce-scatter.26
  951.5 64.6 reduce-scatter.18
  1020.5 63.9 reduce-scatter.22
  1087.5 135.7 reduce-scatter.14
  1228.8 111.2 reduce-scatter.12
  1346.4 113.4 reduce-scatter.10

commit v2 on v1

--- a/solution.py
+++ b/solution.py
@@ -11,6 +11,8 @@
 EPSILON = 1e-06
 MASKED = -1e30
 ALL_AXES = ("section", "ctx", "tp")
+CHUNK = 2
+LIGHT = pl.CostEstimate(flops=1, bytes_accessed=1, transcendentals=0)
 VMEM_LIMIT = 40 * 1024 * 1024
 
 
@@ -492,7 +494,7 @@
     )
 
 
-def document_bounds(ends_ref, first, index):
+def document_bounds(ends_ref, index):
     start = jnp.zeros_like(index)
     for entry in range(ends_ref.shape[0]):
         end = ends_ref[entry]
@@ -520,9 +522,15 @@
     )
 
 
+def fold_rows(value, combine):
+    rows, width = value.shape
+    return combine(value.reshape(rows // 8, 8, width), axis=0)
+
+
 def attention_forward_kernel(ends_ref, qkv_ref, out_ref, lse_ref, keys_ref):
     block = pl.program_id(0)
     blocks, _, width = qkv_ref.shape
+    span = CHUNK * width
 
     @pl.when(block == 0)
     def _():
@@ -535,34 +543,45 @@
     query = qkv_ref[block, 0:HD, :]
     first = block * width
     query_index = first + lax.broadcasted_iota(jnp.int32, (1, width), 1)
-    start = document_bounds(ends_ref, first, query_index)
-    low = scalar_start(ends_ref, first) // width
+    start = document_bounds(ends_ref, query_index)
+    last = block // CHUNK
+    low = scalar_start(ends_ref, first) // span
     high_start = scalar_start(ends_ref, first + width - 1)
-    middle = jnp.clip((high_start + width - 1) // width, low, block)
-
-    def step(j, carry, masked):
+    middle = jnp.clip((high_start + span - 1) // span, low, last)
+
+    def step(chunk, carry, masked):
         top, total, acc = carry
-        scores = dot(keys_ref[j], query, 1, 0)
-        if masked:
-            key_index = j * width + lax.broadcasted_iota(jnp.int32, (width, 1), 0)
-            allowed = (key_index >= start) & (key_index <= query_index)
-            scores = jnp.where(allowed, scores, MASKED)
-        new_top = jnp.maximum(top, jnp.max(scores, axis=0, keepdims=True))
+        parts, part_tops = [], []
+        for entry in range(CHUNK):
+            j = chunk * CHUNK + entry
+            scores = dot(keys_ref[j], query, 1, 0)
+            if masked:
+                key_index = j * width + lax.broadcasted_iota(jnp.int32, (width, 1), 0)
+                allowed = (key_index >= start) & (key_index <= query_index)
+                scores = jnp.where(allowed, scores, MASKED)
+            parts.append(scores)
+            part_tops.append(fold_rows(scores, jnp.max))
+        chunk_top = jnp.max(functools.reduce(jnp.maximum, part_tops), axis=0, keepdims=True)
+        new_top = jnp.maximum(top, chunk_top)
         shrink = jnp.exp(top - new_top)
-        weights = jnp.exp(scores - new_top)
-        total = total * shrink + jnp.sum(weights, axis=0, keepdims=True)
-        values = qkv_ref[j, 2 * HD : 3 * HD, :]
-        acc = acc * shrink + dot(values, weights.astype(jnp.bfloat16), 1, 0)
+        total = total * shrink
+        acc = acc * shrink
+        for entry in range(CHUNK):
+            weights = jnp.exp(parts[entry] - new_top)
+            total = total + fold_rows(weights, jnp.sum)
+            values = qkv_ref[chunk * CHUNK + entry, 2 * HD : 3 * HD, :]
+            acc = acc + dot(values, weights.astype(jnp.bfloat16), 1, 0)
         return new_top, total, acc
 
     carry = (
         jnp.full((1, width), MASKED, jnp.float32),
-        jnp.zeros((1, width), jnp.float32),
+        jnp.zeros((8, width), jnp.float32),
         jnp.zeros((HD, width), jnp.float32),
     )
     carry = lax.fori_loop(low, middle, functools.partial(step, masked=True), carry)
-    carry = lax.fori_loop(middle, block, functools.partial(step, masked=False), carry)
-    top, total, acc = step(block, carry, True)
+    carry = lax.fori_loop(middle, last, functools.partial(step, masked=False), carry)
+    top, total, acc = step(last, carry, True)
+    total = jnp.sum(total, axis=0, keepdims=True)
     out_ref[0] = (acc / total).astype(jnp.bfloat16)
     lse_ref[0] = top + jnp.log(total)
 
@@ -587,9 +606,7 @@
             jax.ShapeDtypeStruct((blocks, 1, width), jnp.float32),
         ],
         compiler_params=pltpu.CompilerParams(vmem_limit_bytes=VMEM_LIMIT),
-        cost_estimate=pl.CostEstimate(
-            flops=4 * HD * pairs, bytes_accessed=2 * qkv.size, transcendentals=pairs
-        ),
+        cost_estimate=LIGHT,
         name="attention_forward",
     )(ends, qkv)
 
@@ -599,6 +616,7 @@
 ):
     block = pl.program_id(0)
     blocks, _, width = qkv_ref.shape
+    span = CHUNK * width
 
     @pl.when(block == 0)
     def _():
@@ -620,29 +638,32 @@
     key_index = first + lax.broadcasted_iota(jnp.int32, (width, 1), 0)
     near_end = scalar_end(ends_ref, first)
     far_end = scalar_end(ends_ref, first + width - 1)
-    stop = (far_end - 1) // width + 1
-    middle = jnp.clip(near_end // width, block + 1, stop)
-
-    def step(i, carry, masked):
+    own_chunk = block // CHUNK
+    stop = (far_end - 1) // span + 1
+    middle = jnp.clip(near_end // span, own_chunk + 1, stop)
+
+    def step(chunk, carry, masked):
         key_grad, value_grad = carry
-        query = qkv_ref[i, 0:HD, :]
-        grad = grad_ref[i]
-        weights = jnp.exp(dot(keys, query, 1, 0) - lse_ref[i])
-        if masked:
-            query_index = i * width + lax.broadcasted_iota(jnp.int32, (1, width), 1)
-            start = document_bounds(ends_ref, first, query_index)
-            allowed = (key_index >= start) & (key_index <= query_index)
-            weights = jnp.where(allowed, weights, 0.0)
-        grad_weights = dot(values, grad, 1, 0)
-        grad_scores = (weights * (grad_weights - delta_ref[i])).astype(jnp.bfloat16)
-        value_grad = value_grad + dot(grad, weights.astype(jnp.bfloat16), 1, 1)
-        key_grad = key_grad + dot(query, grad_scores, 1, 1)
-        query_grad_ref[i] += dot(keys_t, grad_scores, 1, 0)
+        for entry in range(CHUNK):
+            i = chunk * CHUNK + entry
+            query = qkv_ref[i, 0:HD, :]
+            grad = grad_ref[i]
+            weights = jnp.exp(dot(keys, query, 1, 0) - lse_ref[i])
+            if masked:
+                query_index = i * width + lax.broadcasted_iota(jnp.int32, (1, width), 1)
+                start = document_bounds(ends_ref, query_index)
+                allowed = (key_index >= start) & (key_index <= query_index)
+                weights = jnp.where(allowed, weights, 0.0)
+            grad_weights = dot(values, grad, 1, 0)
+            grad_scores = (weights * (grad_weights - delta_ref[i])).astype(jnp.bfloat16)
+            value_grad = value_grad + dot(grad, weights.astype(jnp.bfloat16), 1, 1)
+            key_grad = key_grad + dot(query, grad_scores, 1, 1)
+            query_grad_ref[i] += dot(keys_t, grad_scores, 1, 0)
         return key_grad, value_grad
 
     empty = jnp.zeros((HD, width), jnp.float32)
-    carry = step(block, (empty, empty), True)
-    carry = lax.fori_loop(block + 1, middle, functools.partial(step, masked=False), carry)
+    carry = step(own_chunk, (empty, empty), True)
+    carry = lax.fori_loop(own_chunk + 1, middle, functools.partial(step, masked=False), carry)
     key_grad, value_grad = lax.fori_loop(middle, stop, functools.partial(step, masked=True), carry)
     result_ref[0, 0:HD] = (query_grad_ref[block] * HD ** (-0.5)).astype(jnp.bfloat16)
     result_ref[0, HD : 2 * HD] = key_grad.astype(jnp.bfloat16)
@@ -670,24 +691,169 @@
         ),
         out_shape=jax.ShapeDtypeStruct(qkv.shape, jnp.bfloat16),
         compiler_params=pltpu.CompilerParams(vmem_limit_bytes=VMEM_LIMIT),
-        cost_estimate=pl.CostEstimate(
-            flops=10 * HD * pairs, bytes_accessed=6 * qkv.size, transcendentals=pairs
-        ),
+        cost_estimate=LIGHT,
         name="attention_backward",
     )(ends, qkv, out, grad, lse)
 
 
-def rope_pairs(pair_block, cosine, sine_part):
-    half_width = HD // 2
-    leading_half = pair_block[:, :half_width]
-    trailing_half = pair_block[:, half_width:]
-    return jnp.concatenate(
-        [
-            leading_half * cosine - trailing_half * sine_part,
-            trailing_half * cosine + leading_half * sine_part,
-        ],
-        axis=1,
-    )
+def rope_pair(leading_half, trailing_half, cosine, sine_part):
+    return (
+        leading_half * cosine - trailing_half * sine_part,
+        trailing_half * cosine + leading_half * sine_part,
+    )
+
+
+def low(value):
+    return value.astype(jnp.bfloat16)
+
+
+def wide(value):
+    return value.astype(jnp.float32)
+
+
+def whole_block(value):
+    zeros = (0,) * value.ndim
+    return pl.BlockSpec(value.shape, lambda *_: zeros)
+
+
+def feed_forward_kernel(rows_ref, gate_w_ref, up_w_ref, down_w_ref, gate_ref, up_ref, act_ref, sum_ref):
+    rows = rows_ref[...]
+    gate = dot(gate_w_ref[...], rows, 1, 1)
+    up = dot(up_w_ref[...], rows, 1, 1)
+    active = (gate * jax.nn.sigmoid(gate) * up).astype(jnp.bfloat16)
+    gate_ref[...] = gate.astype(jnp.bfloat16)
+    up_ref[...] = up.astype(jnp.bfloat16)
+    act_ref[...] = active
+
+    @pl.when(pl.program_id(0) == 0)
+    def _():
+        sum_ref[...] = jnp.zeros_like(sum_ref)
+
+    sum_ref[...] += dot(active, down_w_ref[...], 0, 0)
+
+
+def feed_forward(rows, w_gate, w_up, w_down, tile):
+    units, width = w_gate.shape
+    count = rows.shape[0]
+    weight = pl.BlockSpec((tile, width), lambda i: (i, 0))
+    column = pl.BlockSpec((tile, count), lambda i: (i, 0))
+    hidden = jax.ShapeDtypeStruct((units, count), jnp.bfloat16)
+    return pl.pallas_call(
+        feed_forward_kernel,
+        grid=(units // tile,),
+        in_specs=[whole_block(rows), weight, weight, weight],
+        out_specs=[column, column, column, pl.BlockSpec((count, width), lambda i: (0, 0))],
+        out_shape=[hidden, hidden, hidden, jax.ShapeDtypeStruct((count, width), jnp.float32)],
+        compiler_params=pltpu.CompilerParams(vmem_limit_bytes=VMEM_LIMIT),
+        cost_estimate=LIGHT,
+        name="feed_forward",
+    )(rows, w_gate, w_up, w_down)
+
+
+def feed_forward_back_kernel(
+    grad_ref, gate_ref, up_ref, gate_w_ref, up_w_ref, down_w_ref, grad_gate_ref, grad_up_ref, sum_ref
+):
+    grad_act = dot(down_w_ref[...], grad_ref[...], 1, 1)
+    gate = gate_ref[...].astype(jnp.float32)
+    up = up_ref[...].astype(jnp.float32)
+    sigmoid_gate = jax.nn.sigmoid(gate)
+    grad_gate = (grad_act * up * sigmoid_gate * (1.0 + gate * (1.0 - sigmoid_gate))).astype(
+        jnp.bfloat16
+    )
+    grad_up = (grad_act * gate * sigmoid_gate).astype(jnp.bfloat16)
+    grad_gate_ref[...] = grad_gate
+    grad_up_ref[...] = grad_up
+
+    @pl.when(pl.program_id(0) == 0)
+    def _():
+        sum_ref[...] = jnp.zeros_like(sum_ref)
+
+    sum_ref[...] += dot(grad_gate, gate_w_ref[...], 0, 0) + dot(grad_up, up_w_ref[...], 0, 0)
+
+
+def feed_forward_back(grad, gate, up, w_gate, w_up, w_down, tile):
+    units, width = w_gate.shape
+    count = grad.shape[0]
+    weight = pl.BlockSpec((tile, width), lambda i: (i, 0))
+    column = pl.BlockSpec((tile, count), lambda i: (i, 0))
+    hidden = jax.ShapeDtypeStruct((units, count), jnp.bfloat16)
+    return pl.pallas_call(
+        feed_forward_back_kernel,
+        grid=(units // tile,),
+        in_specs=[whole_block(grad), column, column, weight, weight, weight],
+        out_specs=[column, column, pl.BlockSpec((count, width), lambda i: (0, 0))],
+        out_shape=[hidden, hidden, jax.ShapeDtypeStruct((count, width), jnp.float32)],
+        compiler_params=pltpu.CompilerParams(vmem_limit_bytes=VMEM_LIMIT),
+        cost_estimate=LIGHT,
+        name="feed_forward_back",
+    )(grad, gate, up, w_gate, w_up, w_down)
+
+
+def half_products_kernel(layout, sizes, has_addend, which_ref, *refs):
+    refs = list(refs)
+    out_ref = refs.pop()
+    addend_ref = refs.pop() if has_addend else None
+    totals = [
+        sum(dot(refs[left][...], refs[right][...], 1, 0) for left, right in pairs)
+        for pairs in layout
+    ]
+    for piece in range(out_ref.shape[0]):
+        parts = [
+            total[piece * size : (piece + 1) * size] for total, size in zip(totals, sizes)
+        ]
+        value = jnp.concatenate(parts, axis=0) if len(parts) > 1 else parts[0]
+        if has_addend:
+            value = value + addend_ref[piece].astype(jnp.float32)
+        out_ref[piece] = value.astype(jnp.bfloat16)
+
+
+def half_products(which, groups, pieces, per_step, addend=None):
+    lefts, rights, layout = [], [], []
+    for group in groups:
+        for left, right in group:
+            if not any(left is known for known in lefts):
+                lefts.append(left)
+            if not any(right is known for known in rights):
+                rights.append(right)
+    find = lambda known, value: next(i for i, entry in enumerate(known) if entry is value)
+    for group in groups:
+        layout.append(
+            tuple((find(lefts, left), len(lefts) + find(rights, right)) for left, right in group)
+        )
+    sizes = tuple(group[0][0].shape[0] // (2 * pieces) for group in groups)
+    width = rights[0].shape[1]
+    steps = pieces // per_step
+    out_spec = pl.BlockSpec((per_step, sum(sizes), width), lambda i, which_ref: (i, 0, 0))
+    left_specs = [
+        pl.BlockSpec(
+            (left.shape[0] // (2 * steps), left.shape[1]),
+            lambda i, which_ref: (which_ref[0] * steps + i, 0),
+        )
+        for left in lefts
+    ]
+    extra = [] if addend is None else [addend]
+    work = sum(left.size // 2 for left, _ in sum(groups, ()))
+    return pl.pallas_call(
+        functools.partial(half_products_kernel, tuple(layout), sizes, addend is not None),
+        grid_spec=pltpu.PrefetchScalarGridSpec(
+            num_scalar_prefetch=1,
+            grid=(steps,),
+            in_specs=left_specs + [whole_block(right) for right in rights] + [out_spec] * len(extra),
+            out_specs=out_spec,
+        ),
+        out_shape=jax.ShapeDtypeStruct((pieces, sum(sizes), width), jnp.bfloat16),
+        compiler_params=pltpu.CompilerParams(vmem_limit_bytes=VMEM_LIMIT),
+        cost_estimate=LIGHT,
+        name="half_products",
+    )(which.reshape(1).astype(jnp.int32), *lefts, *rights, *extra)
+
+
+def together(*values):
+    return lax.optimization_barrier(values)
+
+
+def after(value, *others):
+    return lax.optimization_barrier((value, *others))[0]
 
 
 def split_body(mesh_sizes, inputs, cotangent, lengths, gain1, wqkv, wo, gain2, wgu, wd):
@@ -696,12 +862,17 @@
     section = lax.axis_index("section")
     ctx = lax.axis_index("ctx")
     tp = lax.axis_index("tp")
+    row_side, column_side = ctx // 2, ctx % 2
     leading = section == 0
     batch = tp // half_parts
     model_width = inputs.shape[2]
     rows = inputs.shape[1]
     heads = wqkv.shape[2] * parts
-    units = wd.shape[1] // contexts
+    unit_rows = wd.shape[1] // contexts // 2
+    head_rows = 3 * HD // 2
+    out_rows = HD // 2
+    half_width = HD // 2
+    tile = 4 * unit_rows
     number = lambda s, c, t: (s * contexts + c) * parts + t
     places = [
         (s, c, t) for s in range(sections) for c in range(contexts) for t in range(parts)
@@ -710,9 +881,6 @@
     token_of = lambda s, c, t: c * parts + t % half_parts + half_parts * s
     batch_groups = device_groups(mesh_sizes, lambda s, c, t: t // half_parts, token_of)
     side_groups = device_groups(mesh_sizes, lambda s, c, t: c % 2, lambda s, c, t: (s, c, t))
-    side_out_groups = device_groups(mesh_sizes, lambda s, c, t: c % 2, lambda s, c, t: (c, t, s))
-    all_out_groups = device_groups(mesh_sizes, lambda s, c, t: 0, lambda s, c, t: (c, t, s))
-
     crossing = [
         (number(s, c, t), number(s, c, (t + half_parts) % parts))
         for s, c, t in places
@@ -745,191 +913,415 @@
     def swap_side(value):
         return lax.ppermute(value, "ctx", [(c, c ^ 1) for c in range(contexts)])
 
+    def swap_far(value):
+        return lax.ppermute(value, "ctx", [(c, c ^ 2) for c in range(contexts)])
+
+    def swap_near(value):
+        return lax.ppermute(value, "tp", [(t, t ^ 1) for t in range(parts)])
+
+    def swap_half(value):
+        return lax.ppermute(value, "tp", [(t, (t + half_parts) % parts) for t in range(parts)])
+
     def swap_section(value):
         return lax.ppermute(value, "section", [(0, 1), (1, 0)])
 
+    def all_to_all(value, axis):
+        return lax.all_to_all(value, axis, split_axis=0, concat_axis=0, tiled=True)
+
+    def copies(value, count):
+        return jnp.broadcast_to(value[None], (count, *value.shape))
+
     def gather(value, groups):
         return lax.all_gather(value, ALL_AXES, axis=0, tiled=True, axis_index_groups=groups)
 
-    def own_part(value, axis, size):
-        return lax.dynamic_slice_in_dim(value, ctx * size, size, axis)
+    def ordered(index, own, other):
+        return jnp.where(index == 0, own, other), jnp.where(index == 0, other, own)
+
+    def by_core(value, which):
+        return lax.dynamic_index_in_dim(value, which, 0, keepdims=False)
+
+    def spread_plane(piece, *others):
+        middle = piece.shape[0] // 2
+        line = after(all_to_all(copies(piece, parts), "tp"), *others)
+        line_a, line_b = line[:, :middle], line[:, middle:]
+        pair_a = jnp.stack(ordered(row_side, line_a, swap_far(line_a)))
+        pair_b = jnp.stack(ordered(column_side, line_b, swap_side(line_b)))
+        plane_a = jnp.stack(ordered(column_side, pair_a, swap_side(pair_a)), axis=1)
+        plane_b = jnp.stack(ordered(row_side, pair_b, swap_far(pair_b)), axis=0)
+        plane = jnp.concatenate([plane_a, plane_b], axis=3)
+        return plane.reshape(contexts * parts * piece.shape[0], piece.shape[1]), line
+
+    def own_halves(value, axis, size):
+        part = lax.dynamic_slice_in_dim(value, ctx * size, size, axis)
+        return part.reshape(2, -1, model_width)
+
+    packed = jnp.concatenate(
+        [
+            own_halves(wqkv[0], 1, heads // (parts * contexts)),
+            own_halves(wo[0], 0, HD),
+            own_halves(wgu[0, 0], 0, 2 * unit_rows),
+            own_halves(wgu[0, 1], 0, 2 * unit_rows),
+            own_halves(wd[0], 0, 2 * unit_rows),
+        ],
+        axis=1,
+    )
+    kept = by_core(packed, section)
+    passed = swap_section(by_core(packed, 1 - section))
+    pieces = ordered(section, kept, passed)
+    attention_rows = head_rows + out_rows
+
+    def feed_forward_weights(piece):
+        whole = gather(piece[attention_rows:], side_groups)
+        whole = whole.reshape(2 * 2 * parts, 3, unit_rows, model_width)
+        return [whole[:, entry].reshape(-1, model_width) for entry in range(3)]
 
     rows_in = to_batch(inputs)
-    grad_in = to_batch(cotangent)
-
-    head_part = own_part(wqkv[0], 1, heads // (parts * contexts)).reshape(-1, model_width)
-    out_part = own_part(wo[0], 0, HD)
-    gate_piece = own_part(wgu[0, 0], 0, units)
-    up_piece = own_part(wgu[0, 1], 0, units)
-    down_piece = own_part(wd[0], 0, units)
-    w_heads = gather(head_part, everyone).reshape(2, -1, model_width)
-    w_outs = gather(out_part, everyone).reshape(2, -1, model_width)
-    w_gates = gather(gate_piece, side_groups).reshape(2, -1, model_width)
-    w_ups = gather(up_piece, side_groups).reshape(2, -1, model_width)
-    w_downs = gather(down_piece, side_groups).reshape(2, -1, model_width)
-    gains = jnp.concatenate([gain1, gain2], axis=0).astype(jnp.float32)
-    other_gains = swap_section(gains)
-    gain_sets = (jnp.where(leading, gains, other_gains), jnp.where(leading, other_gains, gains))
+    own_heads, line = spread_plane(pieces[0][:head_rows], rows_in)
+    first_ffn = feed_forward_weights(after(pieces[0], line))
+    first_heads = (own_heads, swap_section(own_heads))
+    own_outs, _ = spread_plane(after(pieces[0], own_heads)[head_rows:attention_rows])
+    first_outs = jnp.concatenate(ordered(section, own_outs, swap_section(own_outs)), axis=0)
+    second = gather(pieces[1][:attention_rows], everyone)
+    second = second.reshape(2, heads, attention_rows, model_width)
+    second_heads = [second[half, :, :head_rows].reshape(-1, model_width) for half in range(2)]
+    second_outs = second[:, :, head_rows:].reshape(-1, model_width)
+    second_ffn = feed_forward_weights(pieces[1])
+    w_heads = (first_heads, second_heads)
+    w_outs = (first_outs, second_outs)
+    w_ffn = (first_ffn, second_ffn)
+
+    gains = wide(jnp.concatenate([gain1, gain2], axis=0))
+    gain_sets = ordered(section, gains, swap_section(gains))
 
     seq_lengths = lax.dynamic_index_in_dim(lengths, batch, 0, keepdims=False)
     ends = jnp.cumsum(seq_lengths).astype(jnp.int32)
-    token_index = (ctx * parts + tp % half_parts + half_parts * section) * rows + jnp.arange(
-        rows, dtype=jnp.int32
-    )
+    token_index = token_of(section, ctx, tp) * rows + jnp.arange(rows, dtype=jnp.int32)
     before = (ends[None, :] <= token_index[:, None]).astype(jnp.int32)
     position = token_index - jnp.sum(before * seq_lengths[None, :], axis=1)
-    half_width = HD // 2
     frequency = jnp.exp(
         -jnp.log(10000.0) * jnp.arange(half_width, dtype=jnp.float32) / half_width
     )
     angles = position.astype(jnp.float32)[None, :] * frequency[:, None]
     cosine, sine_part = jnp.cos(angles), jnp.sin(angles)
 
-    def low(value):
-        return value.astype(jnp.bfloat16)
-
-    def layer_forward(whole_rows, first_values, layer):
+    def head_halves(value):
+        size = value.shape[1] // 2
+        return value.reshape(heads, 2, size, rows).transpose(1, 0, 2, 3).reshape(2, -1, rows)
+
+    def whole_heads(value):
+        value = value.reshape(2, heads, -1, rows)
+        return value.transpose(1, 0, 2, 3).reshape(heads, -1, rows)
+
+    def nothing(value):
+        return value
+
+    def layer_forward(whole_rows, first_values, layer, beside):
         gain_first, gain_second = gain_sets[layer][0], gain_sets[layer][1]
         scale_first = lax.rsqrt(jnp.mean(whole_rows * whole_rows, axis=-1, keepdims=True) + EPSILON)
         normed = low(whole_rows * scale_first * gain_first)
-        projected = dot(w_heads[layer], normed, 1, 1).reshape(heads, 3, HD, rows)
-        query = rope_pairs(projected[:, 0], cosine, sine_part) * HD ** (-0.5)
-        key = rope_pairs(projected[:, 1], cosine, sine_part)
-        value = projected[:, 2]
+        halves = [dot(weight, normed, 1, 1) for weight in w_heads[layer]]
+        if layer == 0:
+            halves = ordered(section, *halves)
+        upper, lower = [half.reshape(heads, head_rows, rows) for half in halves]
+        query = rope_pair(upper[:, :half_width], upper[:, half_width:HD], cosine, sine_part)
+        key = rope_pair(upper[:, HD:], lower[:, :half_width], cosine, sine_part)
+        value = lower[:, half_width:]
         if first_values is not None:
-            value = 0.5 * value + 0.5 * first_values.astype(jnp.float32)
+            value = 0.5 * value + 0.5 * wide(first_values)
         mixed = low(value)
-        qkv = exchange(jnp.concatenate([low(query), low(key), mixed], axis=1), batch_groups)
+        shrunk = [low(half * HD ** (-0.5)) for half in query]
+        qkv = exchange(
+            jnp.concatenate([*shrunk, low(key[0]), low(key[1]), mixed], axis=1), batch_groups
+        )
         out, lse = attention_forward(ends, qkv)
-        attended = exchange(out, batch_groups).reshape(heads * HD, rows)
-        hidden = whole_rows + dot(attended, w_outs[layer], 0, 0)
+        out = beside(out)
+        attended = head_halves(exchange(out, batch_groups))
+        hidden = whole_rows + dot(attended.reshape(-1, rows), w_outs[layer], 0, 0)
         scale_second = lax.rsqrt(jnp.mean(hidden * hidden, axis=-1, keepdims=True) + EPSILON)
         normed_second = low(hidden * scale_second * gain_second)
-        ffn_rows = (normed_second, swap_side(normed_second))
-        gates = [dot(part, w_gates[layer], 1, 1) for part in ffn_rows]
-        ups = [dot(part, w_ups[layer], 1, 1) for part in ffn_rows]
-        activated = [low(jax.nn.silu(gate) * up) for gate, up in zip(gates, ups)]
-        far_down = swap_side(low(dot(activated[1], w_downs[layer], 1, 0)))
-        layer_out = low(
-            hidden + (dot(activated[0], w_downs[layer], 1, 0) + far_down.astype(jnp.float32))
-        )
+        far_rows = swap_side(normed_second)
+        near = feed_forward(normed_second, *w_ffn[layer], tile)
+        far = feed_forward(after(far_rows, near[3]), *w_ffn[layer], tile)
+        far_down = swap_side(low(far[3]))
+        layer_out = low(hidden + (near[3] + wide(far_down)))
         saved = (
             whole_rows, scale_first, normed, qkv, out, lse, attended, hidden, scale_second,
-            ffn_rows, gates, ups, activated,
+            (normed_second, far_rows), near[:3], far[:3],
         )
         return layer_out, mixed, saved
 
     def norm_back(whole_rows, scale_rows, gain, grad_normed, grad_rest):
-        unit_rows = whole_rows * scale_rows
+        unit = whole_rows * scale_rows
         scaled = grad_normed * gain
-        grad_gain = jnp.sum(grad_normed * unit_rows, axis=0)
+        grad_gain = jnp.sum(grad_normed * unit, axis=0)
         grad_whole = grad_rest + scale_rows * (
-            scaled - unit_rows * jnp.mean(scaled * unit_rows, axis=-1, keepdims=True)
+            scaled - unit * jnp.mean(scaled * unit, axis=-1, keepdims=True)
         )
         return grad_gain, grad_whole
 
-    def reduce_weight(partial_sum, groups):
-        mine = lax.psum_scatter(
-            low(partial_sum), ALL_AXES, scatter_dimension=0, tiled=True, axis_index_groups=groups
-        )
-        return lax.all_gather(mine, "ctx", axis=0, tiled=False)
-
-    def layer_backward(grad_rows, extra_values, saved, layer):
+    def pick(value, index, axis):
+        return lax.dynamic_index_in_dim(value, index, axis, keepdims=False)
+
+    def parted(value, index, axis):
+        return pick(value, index, axis), pick(value, 1 - index, axis)
+
+    def moved_pair(pair, swap):
+        return pair[0], swap(pair[1])
+
+    def halve(value, index, swap, axis):
+        return moved_pair(parted(value, index, axis), swap)
+
+    def add(pair):
+        return low(wide(pair[0]) + wide(pair[1]))
+
+    def near_sum(value):
+        return halve(value.reshape(2, half_parts, *value.shape[1:]), tp % 2, swap_near, 1)
+
+    def far_sum(pair):
+        return halve(add(pair), batch, swap_half, 0)
+
+    def layer_backward(grad_rows, extra_values, saved, layer, in_first, in_second, in_third, in_fourth, in_fifth):
         (
             whole_rows, scale_first, normed, qkv, out, lse, attended, hidden, scale_second,
-            ffn_rows, gates, ups, activated,
+            ffn_rows, near, far,
         ) = saved
         gain_first, gain_second = gain_sets[layer][0], gain_sets[layer][1]
         grad_down = low(grad_rows)
-        grad_downs = (grad_down, swap_side(grad_down))
-        grad_gates, grad_ups = [], []
-        for part, gate, up in zip(grad_downs, gates, ups):
-            grad_act = dot(part, w_downs[layer], 1, 1)
-            sigmoid_gate = jax.nn.sigmoid(gate)
-            grad_gates.append(
-                low(grad_act * up * sigmoid_gate * (1.0 + gate * (1.0 - sigmoid_gate)))
-            )
-            grad_ups.append(low(grad_act * gate * sigmoid_gate))
-        back = [
-            dot(grad_gate, w_gates[layer], 1, 0) + dot(grad_up, w_ups[layer], 1, 0)
-            for grad_gate, grad_up in zip(grad_gates, grad_ups)
-        ]
-        far_back = swap_side(low(back[1]))
+        far_down = swap_side(grad_down)
+        grad_gate, grad_up, near_back = feed_forward_back(grad_down, *near[:2], *w_ffn[layer], tile)
+        far_down = in_first(after(far_down, near_back))
+        far_gate, far_up, far_back = feed_forward_back(far_down, *far[:2], *w_ffn[layer], tile)
+        far_back = swap_side(low(far_back))
+        groups = (
+            ((grad_gate, ffn_rows[0]), (far_gate, ffn_rows[1])),
+            ((grad_up, ffn_rows[0]), (far_up, ffn_rows[1])),
+            ((near[2], grad_down), (far[2], far_down)),
+        )
+        products = functools.partial(
+            half_products, groups=groups, pieces=2 * parts, per_step=2
+        )
+        sent = products(1 - section)
+        moved = swap_section(sent)
+        far_back = in_second(after(far_back, sent))
         grad_gain2, grad_hidden = norm_back(
-            hidden, scale_second, gain_second, back[0] + far_back.astype(jnp.float32),
-            grad_rows.astype(jnp.float32),
+            hidden, scale_second, gain_second, near_back + wide(far_back), wide(grad_rows)
         )
         grad_branch = low(grad_hidden)
-        grad_heads = low(dot(w_outs[layer], grad_branch, 1, 1)).reshape(heads, HD, rows)
+        grad_heads = whole_heads(low(dot(w_outs[layer], grad_branch, 1, 1)))
         grad_heads = exchange(grad_heads, batch_groups)
-        join = lambda pair: jnp.concatenate(pair, axis=0)
-        all_rows, all_down = join(ffn_rows), join(grad_downs)
-        grad_wd = reduce_weight(dot(join(activated), all_down, 0, 0), side_out_groups)
-        grad_wgate = reduce_weight(dot(join(grad_gates), all_rows, 0, 0), side_out_groups)
-        grad_wup = reduce_weight(dot(join(grad_ups), all_rows, 0, 0), side_out_groups)
-        grad_wo = reduce_weight(dot(attended, grad_branch, 1, 0), all_out_groups)
+        rest = products(section, addend=moved)
+        out_pair = (attended.reshape(-1, rows), grad_branch)
+        grad_heads, rest = in_third(grad_heads, rest, out_pair)
         grad_qkv = attention_backward(ends, qkv, out, grad_heads, lse)
-        grad_qkv = exchange(grad_qkv, batch_groups).reshape(heads, 3, HD, rows)
-        grad_query = rope_pairs(grad_qkv[:, 0].astype(jnp.float32), cosine, -sine_part)
-        grad_key = rope_pairs(grad_qkv[:, 1].astype(jnp.float32), cosine, -sine_part)
-        grad_value = grad_qkv[:, 2].astype(jnp.float32)
+        grad_qkv = in_fourth(grad_qkv)
+        grad_qkv = in_fifth(exchange(grad_qkv, batch_groups))
+        grad_qkv = wide(grad_qkv)
+        quarter = lambda entry: grad_qkv[:, entry * half_width : (entry + 1) * half_width]
+        grad_query = rope_pair(quarter(0), quarter(1), cosine, -sine_part)
+        grad_key = rope_pair(quarter(2), quarter(3), cosine, -sine_part)
+        grad_value = grad_qkv[:, 2 * HD :]
         send_values = None
         if extra_values is None:
             grad_value = 0.5 * grad_value
             send_values = low(grad_value)
         else:
-            grad_value = grad_value + extra_values.astype(jnp.float32)
-        grad_projected = jnp.concatenate(
-            [low(grad_query), low(grad_key), low(grad_value)], axis=1
-        ).reshape(3 * heads * HD, rows)
-        grad_normed = dot(grad_projected, w_heads[layer], 0, 0)
-        grad_wqkv = reduce_weight(dot(grad_projected, normed, 1, 0), all_out_groups)
-        grad_gain1, grad_whole = norm_back(
-            whole_rows, scale_first, gain_first, grad_normed, grad_hidden
-        )
-        return grad_whole, send_values, (grad_gain1, grad_gain2), (
-            grad_wqkv, grad_wo, grad_wgate, grad_wup, grad_wd,
-        )
-
-    first_out, first_values, first_saved = layer_forward(rows_in.astype(jnp.float32), None, 0)
+            grad_value = grad_value + wide(extra_values)
+        upper = low(jnp.concatenate([*grad_query, grad_key[0]], axis=1))
+        lower = low(jnp.concatenate([grad_key[1], grad_value], axis=1))
+        grad_halves = jnp.stack([upper, lower]).reshape(2, -1, rows)
+        return grad_halves, send_values, grad_hidden, out_pair, grad_gain2
+
+    def input_grads_of(grad_halves, grad_hidden, saved, layer):
+        whole_rows, scale_first = saved[:2]
+        places_of = (section, 1 - section) if layer == 0 else (0, 1)
+        grad_normed = sum(
+            dot(by_core(grad_halves, place), weight, 0, 0)
+            for place, weight in zip(places_of, w_heads[layer])
+        )
+        return norm_back(whole_rows, scale_first, gain_sets[layer][0], grad_normed, grad_hidden)
+
+    def piece_sum(value, groups):
+        return lax.psum_scatter(
+            value, ALL_AXES, scatter_dimension=0, tiled=True, axis_index_groups=groups
+        )
+
+    line_groups = device_groups(
+        mesh_sizes, lambda s, c, t: (s, c % 2), lambda s, c, t: (c, t)
+    )
+    plane_shape = (2, 2, parts)
+    pending = {}
+
+    first_out, first_values, first_saved = layer_forward(wide(rows_in), None, 0, nothing)
     first_home = to_home(first_out, 0)
-    second_out, _, second_saved = layer_forward(first_out.astype(jnp.float32), first_values, 1)
-    second_home = to_home(second_out, 1)
-    second_grad, send_values, second_gains, second_grads = layer_backward(
-        grad_in, None, second_saved, 1
-    )
+    grad_in = to_batch(after(cotangent, first_out))
+
+    def beside_second(value):
+        value, pending["first_home"], pending["grad_in"] = together(value, first_home, grad_in)
+        return value
+
+    second_out, _, second_saved = layer_forward(
+        wide(first_out), first_values, 1, beside_second
+    )
+    first_home, grad_in = pending["first_home"], pending["grad_in"]
+
+    def second_third(value, rest, out_pair):
+        value, rest = together(value, rest)
+        rest = rest.reshape(-1, model_width)
+        pending["second_rest"] = piece_sum(rest, line_groups)
+        pending["second_home"] = to_home(after(second_out, value), 1)
+        return value, rest
+
+    def second_fourth(value):
+        value, pending["second_home"] = together(value, pending["second_home"])
+        return value
+
+    grad_halves, send_values, grad_hidden, out_pair, second_gain2 = layer_backward(
+        grad_in, None, second_saved, 1, nothing, nothing, second_third, second_fourth, nothing
+    )
+    second_gain1, second_grad = input_grads_of(grad_halves, grad_hidden, second_saved, 1)
     second_grad = low(second_grad)
-    second_grad_home = to_home(second_grad, 1)
-    first_grad, _, first_gains, first_grads = layer_backward(
-        second_grad, send_values, first_saved, 0
-    )
-    first_grad_home = to_home(low(first_grad), 0)
-
-    gain_total = lax.psum(
-        jnp.stack([first_gains[0], first_gains[1], second_gains[0], second_gains[1]]), ALL_AXES
-    )
+    head_products = functools.partial(
+        half_products,
+        groups=(((grad_halves.reshape(-1, rows), second_saved[2]),), (out_pair,)),
+        pieces=heads,
+        per_step=4,
+    )
+
+    def first_first(value):
+        value, sent = together(value, head_products(1 - section))
+        pending["moved"] = swap_section(sent)
+        return value
+
+    def crossed(value):
+        middle = value.shape[3] // 2
+        return (
+            parted(value[:, :, :, :middle], column_side, 1),
+            parted(value[:, :, :, middle:], row_side, 0),
+        )
+
+    def first_second(value):
+        head = head_products(section, addend=pending["moved"])
+        head = parted(head.reshape(*plane_shape, -1, model_width), column_side, 1)
+        value, head, _ = together(value, head, pending["second_rest"])
+        pending["head"] = moved_pair(head, swap_side)
+        pending["second_grad_home"] = to_home(after(second_grad, value), 1)
+        return value
+
+    def first_third(value, rest, out_pair):
+        out_products = functools.partial(
+            half_products, groups=((out_pair,),), pieces=heads, per_step=8
+        )
+        out_sum = out_products(section, addend=swap_section(out_products(1 - section)))
+        rest = rest.reshape(2, parts, -1, model_width)
+        rest_a = parted(rest[:, :-1], row_side, 0)
+        rest_b = parted(rest[:, -1:], row_side, 0)
+        out_sum = parted(out_sum.reshape(*plane_shape, -1, model_width), column_side, 1)
+        value, rest_a, rest_b, out_sum = together(value, rest_a, rest_b, out_sum)
+        pending["rest_a"] = moved_pair(rest_a, swap_far)
+        pending["rest_b"] = rest_b
+        pending["out"] = moved_pair(out_sum, swap_side)
+        pending["second_rest"] = lax.all_gather(
+            after(pending["second_rest"], value), "ctx", axis=0, tiled=False
+        )
+        return value, rest
+
+    def first_fourth(value):
+        value, rest_a, rest_b, out_sum, head, pending["second_grad_home"] = together(
+            value, pending["rest_a"], pending["rest_b"], pending["out"], pending["head"],
+            pending["second_grad_home"],
+        )
+        pending["rest_a"] = rest_a
+        pending["rest_b"] = moved_pair(rest_b, swap_far)
+        pending["out"] = halve(add(out_sum), row_side, swap_far, 0)
+        pending["head"] = halve(add(head), row_side, swap_far, 0)
+        return value
+
+    def first_fifth(value):
+        value, rest_a, rest_b, out_sum, head = together(
+            value, pending["rest_a"], pending["rest_b"], pending["out"], pending["head"]
+        )
+        pending["out"] = add(out_sum)
+        rest = jnp.concatenate([add(rest_a), add(rest_b)], axis=0)
+        pending["rest"] = near_sum(rest)
+        pending["head"] = near_sum(add(head))
+        return value
+
+    first_halves, _, first_hidden, _, first_gain2 = layer_backward(
+        second_grad, send_values, first_saved, 0,
+        first_first, first_second, first_third, first_fourth, first_fifth,
+    )
+    head_products = functools.partial(
+        half_products,
+        groups=(((first_halves.reshape(-1, rows), first_saved[2]),),),
+        pieces=heads,
+        per_step=4,
+    )
+    sent = head_products(1 - section)
+    moved = swap_section(sent)
+    first_gain1, first_grad = input_grads_of(
+        after(first_halves, sent), first_hidden, first_saved, 0
+    )
+    head = head_products(section, addend=moved).reshape(*plane_shape, head_rows, model_width)
+    head, first_grad = together(head, low(first_grad))
+    head_a, head_b = crossed(head)
+    gain_rows = jnp.stack([first_gain1, first_gain2, second_gain1, second_gain2])
+    first_grad, gain_rows, head_a, head_b = together(first_grad, gain_rows, head_a, head_b)
+    head_a = moved_pair(head_a, swap_side)
+    head_b = moved_pair(head_b, swap_far)
+    first_grad_home = to_home(first_grad, 0)
+    head_a, head_b, rest, second_head = together(
+        add(head_a), add(head_b), pending["rest"], pending["head"]
+    )
+    head_a = parted(head_a, row_side, 0)
+    head_b = parted(head_b, column_side, 0)
+    gain_rows, head_a, head_b, rest, second_head = together(
+        gain_rows, head_a, head_b, rest, second_head
+    )
+    head_a = moved_pair(head_a, swap_far)
+    head_b = moved_pair(head_b, swap_side)
+    rest = far_sum(rest)
+    second_head = far_sum(second_head)
+    gain_sums = all_to_all(copies(gain_rows, len(places)), ALL_AXES)
+    head_a, head_b, first_grad_home = together(head_a, head_b, first_grad_home)
+    head = near_sum(jnp.concatenate([add(head_a), add(head_b), pending["out"]], axis=1))
+    head, rest, second_head, gain_sums = together(head, rest, second_head, gain_sums)
+    head = far_sum(head)
+    rest = jnp.concatenate([add(rest), add(second_head)], axis=0)
+    rest = all_to_all(copies(rest, contexts), "ctx")
+    head, rest = together(head, rest)
+    first_head = all_to_all(copies(add(head), contexts), "ctx")
+    second_head = rest[:, 3 * unit_rows :]
+    rest = rest[:, : 3 * unit_rows]
+    first_grads = jnp.concatenate([rest, first_head], axis=1)
+    second_grads = jnp.concatenate([pending["second_rest"], second_head], axis=1)
+    second_home, second_grad_home = pending["second_home"], pending["second_grad_home"]
+    gain_total = jnp.sum(gain_sums.reshape(len(places), 4, model_width), axis=0)
     gain_total = jnp.where(leading, gain_total[:2], gain_total[2:])
 
-    def finish(first_half, second_half):
-        mine = jnp.where(leading, first_half, second_half)
-        moved = swap_section(jnp.where(leading, second_half, first_half))
-        lower = jnp.where(leading, mine, moved)
-        upper = jnp.where(leading, moved, mine)
-        return jnp.concatenate([lower, upper], axis=1).astype(jnp.float32)
-
-    grad_wqkv, grad_wo, grad_wgate, grad_wup, grad_wd = [
-        finish(first, second) for first, second in zip(first_grads, second_grads)
+    def finish(first, second):
+        mine = jnp.where(leading, first, second)
+        moved = swap_section(jnp.where(leading, second, first))
+        return ordered(section, mine, moved)
+
+    def joined(halves, first, count):
+        both = jnp.stack([half[:, first : first + count] for half in halves], axis=1)
+        return wide(both).reshape(-1, model_width)
+
+    grads = finish(first_grads, second_grads)
+    grad_wgate, grad_wup, grad_wd = [
+        joined(grads, entry * unit_rows, unit_rows) for entry in range(3)
     ]
-    grad_wqkv = grad_wqkv.reshape(contexts, 3, HD, model_width).transpose(1, 0, 2, 3)
+    grad_wqkv = joined(grads, 3 * unit_rows, head_rows).reshape(contexts, 3, HD, model_width)
+    grad_wo = joined(grads, 3 * unit_rows + head_rows, out_rows)
     return (
         at_home(first_home, second_home),
-        at_home(first_grad_home, second_grad_home).astype(jnp.float32),
+        wide(at_home(first_grad_home, second_grad_home)),
         gain_total[0:1],
-        grad_wqkv[None],
-        grad_wo.reshape(wo.shape),
+        grad_wqkv.transpose(1, 0, 2, 3)[None],
+        grad_wo[None],
         gain_total[1:2],
-        jnp.stack([grad_wgate.reshape(wd.shape[1:]), grad_wup.reshape(wd.shape[1:])])[None],
-        grad_wd.reshape(wd.shape),
+        jnp.stack([grad_wgate, grad_wup])[None],
+        grad_wd[None],
     )
 
 
@@ -940,7 +1332,7 @@
     fits = (
         sections == 2
         and inputs.shape[0] == 2
-        and contexts % 2 == 0
+        and contexts == 4
         and parts % 2 == 0
         and own_heads == contexts
         and own_units % (16 * contexts) == 0

time: 1500 us -> 1000 us (0.67)
  waiting for transfers between devices: 783 us -> 421 us
  blocking collectives: 266 us -> 0 us
  matrix products: 147 us -> 32.1 us
  starting transfers between devices: 59.9 us -> 133 us
  local copies, waits for them, and re-layouts: 24.2 us -> 87.3 us
  Pallas kernels: 164 us -> 226 us
  other arithmetic: 29.1 us -> 74.9 us
    reduce_scatter x10 -> x1, waiting for transfers between devices: 435 us -> 8.56 us  [piece_sum(): lax.psum_scatter(value, ALL_AXES, scatter_dimension=0, tiled=True, axis_i...]
    all_gather x5 -> x3, waiting for transfers between devices: 224 us -> 0.02 us  [gather(): lax.all_gather(value, ALL_AXES, axis=0, tiled=True, axis_index_groups=gro...]
    ppermute x0 -> x16, waiting for transfers between devices: none -> 171 us  [the longest x10 102 us: swap_far(): return lax.ppermute(value, 'ctx', [(c, c ^ 2) for c in range(contexts)])]
    dot_general x42 -> x12, matrix products: 147 us -> 32.1 us  [dot(): lax.dot_general(left, right, (((left_dim,), (right_dim,)), ((), ())), pre...]
    all_gather x10 -> x0, blocking collectives: 113 us -> none  [reduce_weight(): return lax.all_gather(mine, 'ctx', axis=0, tiled=False)]
    all_to_all x5 -> x0, blocking collectives: 113 us -> none  [exchange(): lax.all_to_all(value, ALL_AXES, split_axis=0, concat_axis=0, tiled=True,...]
    pallas_call x0 -> x18, Pallas kernels: none -> 85.9 us  [the longest x10 38.9 us: half_products(): pl.pallas_call(functools.partial(half_products_kernel, tuple(layout), siz...]
    all_to_all x0 -> x5, waiting for transfers between devices: none -> 39.7 us  [all_to_all(): return lax.all_to_all(value, axis, split_axis=0, concat_axis=0, tiled=True)]
  transfers between devices with their start and end apart: 42 -> 70, of which waited for: 22 -> 34; matrix products, arithmetic and copies ran while one was open for 11% -> 13% of each run, Pallas kernels for 8% -> 20%
where the time goes in v2:
time: 1000 us; the launch traced here: 992 us
  waiting for transfers between devices  421 us (42%)
  Pallas kernels  226 us (23%)
  starting transfers between devices  133 us (13%)
  local copies, waits for them, and re-layouts  87.3 us (9%)
  other arithmetic  74.9 us (7%)
  matrix products  32.1 us (3%)
  between operations  16.6 us (2%)
    ppermute x10, waiting for transfers between devices, swap_far(): return lax.ppermute(value, 'ctx', [(c, c ^ 2) for c in range(contexts)])  102 us
    pallas_call x2, Pallas kernels, attention_backward(): pl.pallas_call(attention_backward_kernel, grid_spec=pltpu.PrefetchScalarG...  84.2 us
    ppermute x16, waiting for transfers between devices, swap_side(): return lax.ppermute(value, 'ctx', [(c, c ^ 1) for c in range(contexts)])  70 us
    all_to_all x8, waiting for transfers between devices, exchange(): lax.all_to_all(value, ALL_AXES, split_axis=0, concat_axis=0, tiled=True,...  57.7 us
    pallas_call x2, Pallas kernels, attention_forward(): pl.pallas_call(attention_forward_kernel, grid_spec=pltpu.PrefetchScalarGr...  56.4 us
    ppermute x2, waiting for transfers between devices, to_batch(): moved = lax.ppermute(other, ALL_AXES, crossing)  49.7 us
    ppermute x3, waiting for transfers between devices, swap_half(): lax.ppermute(value, 'tp', [(t, (t + half_parts) % parts) for t in range(p...  46.6 us
    all_to_all x5, waiting for transfers between devices, all_to_all(): return lax.all_to_all(value, axis, split_axis=0, concat_axis=0, tiled=True)  39.7 us
  transfers between devices with their start and end apart: 70, of which 34 were waited for; matrix products, arithmetic and copies ran while one was open for 13% of the time, Pallas kernels for 20%

profile of v2, /device:TPU:0, one launch (start us, length us, event | category | flops | bytes accessed | tf_op | source)
XLA Modules:
  0.0 991.6 jit_solution(17730770070297342131)
XLA Ops:
  32.8 12.1 %collective-permute-done.1 = bf16[256,1024]{1,0:T(8,128)(2,1)} collective-permute-done((bf16[256,1024]{1,0:T(8,128)(2,1)S(1)}, bf16[256,1024]{1,0:T(8,128)(2,1)}, u32[]{:S(2)}, u32[]{:S(2)}) %collective-permute-start.1) | collective-permute-done | bytes 524320 | tf_op jit(solution)/shard_map/ppermute | solution.py:893
  68.0 22.0 %collective-permute-done.5 = bf16[2,4,48,1024]{3,2,1,0:T(8,128)(2,1)S(1)} collective-permute-done((bf16[2,4,48,1024]{3,2,1,0:T(8,128)(2,1)S(1)}, bf16[2,4,48,1024]{3,2,1,0:T(8,128)(2,1)S(1)}, u32[]{:S(2)}, u32[]{:S(2)}) %collective-permute-start.5) | collective-permute-done | bytes 786464 | tf_op jit(solution)/shard_map/ppermute | solution.py:917
  128.5 11.9 %collective-permute-done.8 = bf16[4,16,1024]{2,1,0:T(8,128)(2,1)S(1)} collective-permute-done((bf16[4,16,1024]{2,1,0:T(8,128)(2,1)S(1)}, bf16[4,16,1024]{2,1,0:T(8,128)(2,1)S(1)}, u32[]{:S(2)}, u32[]{:S(2)}) %collective-permute-start.8) | collective-permute-done | bytes 131104 | tf_op jit(solution)/shard_map/ppermute | solution.py:917
  143.3 11.3 %collective-permute-done.11 = bf16[2,4,16,1024]{3,2,1,0:T(8,128)(2,1)S(1)} collective-permute-done((bf16[2,4,16,1024]{3,2,1,0:T(8,128)(2,1)S(1)}, bf16[2,4,16,1024]{3,2,1,0:T(8,128)(2,1)S(1)}, u32[]{:S(2)}, u32[]{:S(2)}) %collective-permute-start.11) | collective-permute-done | bytes 262176 | tf_op jit(solution)/shard_map/ppermute | solution.py:917
  155.9 27.9 %attention_forward.2 = (bf16[16,64,256]{2,1,0:T(8,128)(2,1)}, f32[16,1,256]{2,1,0:T(1,128)S(1)}) custom-call(s32[4]{0:T(128)S(1)} %bitcast.335, bf16[16,192,256]{2,1,0:T(8,128)(2,1)S(1)} %all-to-all-done.1.qkv_ref), custom_call_target="tpu_custom_call" | custom-call | flops 1 | bytes 1 | tf_op jit(solution)/shard_map/attention_forward/pallas_call | solution.py:592
  216.2 12.2 %collective-permute-done.13.rows_ref.refs_7_ = bf16[256,1024]{1,0:T(8,128)(2,1)} collective-permute-done((bf16[256,1024]{1,0:T(8,128)(2,1)S(1)}, bf16[256,1024]{1,0:T(8,128)(2,1)}, u32[]{:S(2)}, u32[]{:S(2)}) %collective-permute-start.13) | collective-permute-done | bytes 524320 | tf_op jit(solution)/shard_map/ppermute | solution.py:914
  234.2 13.4 %collective-permute-done.14 = bf16[256,1024]{1,0:T(8,128)(2,1)S(1)} collective-permute-done((bf16[256,1024]{1,0:T(8,128)(2,1)S(1)}, bf16[256,1024]{1,0:T(8,128)(2,1)S(1)}, u32[]{:S(2)}, u32[]{:S(2)}) %collective-permute-start.14) | collective-permute-done | bytes 524320 | tf_op jit(solution)/shard_map/ppermute | solution.py:914
  278.1 37.7 %collective-permute-done.17 = bf16[256,1024]{1,0:T(8,128)(2,1)S(1)} collective-permute-done((bf16[256,1024]{1,0:T(8,128)(2,1)S(1)}, bf16[256,1024]{1,0:T(8,128)(2,1)S(1)}, u32[]{:S(2)}, u32[]{:S(2)}) %collective-permute-start.17) | collective-permute-done | bytes 524320 | tf_op jit(solution)/shard_map/ppermute | solution.py:893
  316.9 11.9 %all-to-all-done.4.qkv_ref = bf16[16,192,256]{2,1,0:T(8,128)(2,1)} async-done(((bf16[16,192,256]{2,1,0:T(8,128)(2,1)}), bf16[16,192,256]{2,1,0:T(8,128)(2,1)}, u32[]{:S(2)}, u32[]{:S(2)}) %all-to-all-start.4) | async-done | bytes 1572896 | tf_op jit(solution)/shard_map/all_to_all | solution.py:492
  328.8 28.5 %attention_forward.3 = (bf16[16,64,256]{2,1,0:T(8,128)(2,1)S(1)}, f32[16,1,256]{2,1,0:T(1,128)S(1)}) custom-call(s32[4]{0:T(128)S(1)} %bitcast.336, bf16[16,192,256]{2,1,0:T(8,128)(2,1)} %all-to-all-done.4.qkv_ref), custom_call_target="tpu_custom_call" | custom-call | flops 1 | bytes 1 | tf_op jit(solution)/shard_map/attention_forward/pallas_call | solution.py:592
  417.2 10.7 %collective-permute-done.20 = bf16[256,1024]{1,0:T(8,128)(2,1)S(1)} collective-permute-done((bf16[256,1024]{1,0:T(8,128)(2,1)S(1)}, bf16[256,1024]{1,0:T(8,128)(2,1)S(1)}, u32[]{:S(2)}, u32[]{:S(2)}) %collective-permute-start.20) | collective-permute-done | bytes 524320 | tf_op jit(solution)/shard_map/ppermute | solution.py:914
  428.4 10.4 %collective-permute-done.22 = bf16[256,1024]{1,0:T(8,128)(2,1)S(1)} collective-permute-done((bf16[256,1024]{1,0:T(8,128)(2,1)S(1)}, bf16[256,1024]{1,0:T(8,128)(2,1)S(1)}, u32[]{:S(2)}, u32[]{:S(2)}) %collective-permute-start.22) | collective-permute-done | bytes 524320 | tf_op jit(solution)/shard_map/ppermute | solution.py:914
  465.1 42.4 %attention_backward.2 = bf16[16,192,256]{2,1,0:T(8,128)(2,1)S(1)} custom-call(s32[4]{0:T(128)S(1)} %bitcast.337, bf16[16,192,256]{2,1,0:T(8,128)(2,1)} %all-to-all-done.4.qkv_ref, bf16[16,64,256]{2,1,0:T(8,128)(2,1)S(1)} %copy-done.59, bf16[16,64,256]{2,1,0:T(8,128)(2,1)} %all-to-all-done.6.grad_ref, f32[16,1,256]{2,1,0:T(1,128)S(1)} %get-tuple-element.163.lse_ref), custom_call_target="tpu_custom_call" | custom-call | flops 1 | bytes 1 | tf_op jit(solution)/shard_map/attention_backward/pallas_call | solution.py:680
  514.2 33.1 %all-to-all-done.7 = bf16[16,192,256]{2,1,0:T(8,128)(2,1)} async-done(((bf16[16,192,256]{2,1,0:T(8,128)(2,1)}), bf16[16,192,256]{2,1,0:T(8,128)(2,1)}, u32[]{:S(2)}, u32[]{:S(2)}) %all-to-all-start.7) | async-done | bytes 1572896 | tf_op jit(solution)/shard_map/all_to_all | solution.py:492
  587.0 12.5 %collective-permute-done.26 = bf16[256,1024]{1,0:T(8,128)(2,1)} collective-permute-done((bf16[256,1024]{1,0:T(8,128)(2,1)}, bf16[256,1024]{1,0:T(8,128)(2,1)}, u32[]{:S(2)}, u32[]{:S(2)}) %collective-permute-start.26) | collective-permute-done | bytes 524320 | tf_op jit(solution)/shard_map/ppermute | solution.py:914
  607.0 8.6 reduce-scatter.2.cloned.1.call-done
  652.4 41.9 %attention_backward.3 = bf16[16,192,256]{2,1,0:T(8,128)(2,1)S(1)} custom-call(s32[4]{0:T(128)S(1)} %bitcast.338, bf16[16,192,256]{2,1,0:T(8,128)(2,1)S(1)} %copy-done.8, bf16[16,64,256]{2,1,0:T(8,128)(2,1)} %get-tuple-element.135.out_ref, bf16[16,64,256]{2,1,0:T(8,128)(2,1)} %all-to-all-done.8.grad_ref, f32[16,1,256]{2,1,0:T(1,128)S(1)} %get-tuple-element.189.lse_ref), custom_call_target="tpu_custom_call" | custom-call | flops 1 | bytes 1 | tf_op jit(solution)/shard_map/attention_backward/pallas_call | solution.py:680
  709.9 50.0 %collective-permute-done.36 = bf16[4,32,1024]{2,1,0:T(8,128)(2,1)S(1)} collective-permute-done((bf16[4,32,1024]{2,1,0:T(8,128)(2,1)S(1)}, bf16[4,32,1024]{2,1,0:T(8,128)(2,1)S(1)}, u32[]{:S(2)}, u32[]{:S(2)}) %collective-permute-start.36) | collective-permute-done | bytes 262176 | tf_op jit(solution)/shard_map/ppermute | solution.py:917
  798.4 7.8 collective-permute-done.39
  809.2 21.7 %collective-permute-done.42 = bf16[2,128,1024]{2,1,0:T(8,128)(2,1)S(1)} collective-permute-done((bf16[2,128,1024]{2,1,0:T(8,128)(2,1)S(1)}, bf16[2,128,1024]{2,1,0:T(8,128)(2,1)S(1)}, u32[]{:S(2)}, u32[]{:S(2)}) %collective-permute-start.42) | collective-permute-done | bytes 524320 | tf_op jit(solution)/shard_map/ppermute | solution.py:920
  851.1 32.5 %collective-permute-done.49 = bf16[128,1024]{1,0:T(8,128)(2,1)S(1)} collective-permute-done((bf16[128,1024]{1,0:T(8,128)(2,1)S(1)}, bf16[128,1024]{1,0:T(8,128)(2,1)S(1)}, u32[]{:S(2)}, u32[]{:S(2)}) %collective-permute-start.49) | collective-permute-done | bytes 262176 | tf_op jit(solution)/shard_map/ppermute | solution.py:923
  891.9 14.1 %collective-permute-done.50 = bf16[128,1024]{1,0:T(8,128)(2,1)} collective-permute-done((bf16[128,1024]{1,0:T(8,128)(2,1)S(1)}, bf16[128,1024]{1,0:T(8,128)(2,1)}, u32[]{:S(2)}, u32[]{:S(2)}) %collective-permute-start.50) | collective-permute-done | bytes 262176 | tf_op jit(solution)/shard_map/ppermute | solution.py:923
  906.0 26.5 %all-to-all-done.11 = bf16[4,392,1024]{2,1,0:T(8,128)(2,1)S(1)} async-done(((bf16[4,392,1024]{2,1,0:T(8,128)(2,1)}), bf16[4,392,1024]{2,1,0:T(8,128)(2,1)S(1)}, u32[]{:S(2)}, u32[]{:S(2)}) %all-to-all-start.11) | async-done | bytes 3211296 | tf_op jit(solution)/shard_map/all_to_all | solution.py:929
  942.0 17.5 %all-gather.12.cloned.1.call-done = bf16[1056,1024]{1,0:T(8,128)(2,1)} async-done(((bf16[264,1024]{1,0:T(8,128)(2,1)}), bf16[1056,1024]{1,0:T(8,128)(2,1)}) %all-gather.12.cloned.1.call-update) | async-done | bytes 2162704 | tf_op jit(solution)/shard_map/all_gather | solution.py:1223
  (564 shorter events, 456.6 us)
Async XLA Ops:
  26.1 179.8 %all-gather.8.cloned.1.call-start = ((), (), s32[]{:S(2)}) async-start(), calls=%async_computation.15 | async-start | bytes 9191424 | tf_op jit(solution)/shard_map/all_gather | solution.py:935
  53.9 196.0 %all-gather.6.cloned.1.call-start = ((), (), s32[]{:S(2)}) async-start(), calls=%async_computation.14 | async-start | bytes 8650752 | tf_op jit(solution)/shard_map/all_gather | solution.py:935
  54.8 322.8 %all-gather.10.cloned.1.call-start = ((), (), s32[]{:S(2)}) async-start(), calls=%async_computation.16 | async-start | bytes 9191424 | tf_op jit(solution)/shard_map/all_gather | solution.py:935
  261.6 67.1 %all-to-all-start.4 = ((bf16[16,192,256]{2,1,0:T(8,128)(2,1)}), bf16[16,192,256]{2,1,0:T(8,128)(2,1)}, u32[]{:S(2)}, u32[]{:S(2)}) async-start(bf16[16,192,256]{2,1,0:T(8,128)(2,1)} %fusion.55), calls=%async_computation.4 | async-start | bytes 3145728 | tf_op jit(solution)/shard_map/all_to_all | solution.py:492
  267.1 48.6 %collective-permute-start.17 = (bf16[256,1024]{1,0:T(8,128)(2,1)S(1)}, bf16[256,1024]{1,0:T(8,128)(2,1)S(1)}, u32[]{:S(2)}, u32[]{:S(2)}) collective-permute-start(bf16[256,1024]{1,0:T(8,128)(2,1)S(1)} %dynamic-slice_bitcast_fusion.23), channel_id=1, source_target_pairs={{0,2},{1,3},{4,6},{5,7},{8,10},{9,11},{12,14},{13,15},{18,16},{19,... | collective-permute-start | bytes 1572872 | tf_op jit(solution)/shard_map/ppermute | solution.py:893
  271.4 85.8 %collective-permute-start.15 = (bf16[256,1024]{1,0:T(8,128)(2,1)}, bf16[256,1024]{1,0:T(8,128)(2,1)}, u32[]{:S(2)}, u32[]{:S(2)}) collective-permute-start(bf16[256,1024]{1,0:T(8,128)(2,1)} %get-tuple-element.297), channel_id=1, source_target_pairs={{0,0},{1,1},{4,4},{5,5},{8,8},{9,9},{12,12},{13,13},{18,2},{19,3},... | collective-permute-start | bytes 1572872 | tf_op jit(solution)/shard_map/ppermute | solution.py:905
  276.8 80.4 %collective-permute-start.16 = (bf16[256,1024]{1,0:T(8,128)(2,1)}, bf16[256,1024]{1,0:T(8,128)(2,1)}, u32[]{:S(2)}, u32[]{:S(2)}) collective-permute-start(bf16[256,1024]{1,0:T(8,128)(2,1)} %get-tuple-element.297), channel_id=1, source_target_pairs={{2,0},{3,1},{6,4},{7,5},{10,8},{11,9},{14,12},{15,13},{16,2},{17,3... | collective-permute-start | bytes 1572872 | tf_op jit(solution)/shard_map/ppermute | solution.py:905
  460.4 47.1 %collective-permute-start.23 = (bf16[256,1024]{1,0:T(8,128)(2,1)}, bf16[256,1024]{1,0:T(8,128)(2,1)S(1)}, u32[]{:S(2)}, u32[]{:S(2)}) collective-permute-start(bf16[256,1024]{1,0:T(8,128)(2,1)} %get-tuple-element.165), channel_id=1, source_target_pairs={{0,16},{1,17},{4,20},{5,21},{8,24},{9,25},{12,28},{13,29},{18,18},... | collective-permute-start | bytes 1572872 | tf_op jit(solution)/shard_map/ppermute | solution.py:905
  462.6 46.0 %collective-permute-start.24 = (bf16[256,1024]{1,0:T(8,128)(2,1)}, bf16[256,1024]{1,0:T(8,128)(2,1)}, u32[]{:S(2)}, u32[]{:S(2)}) collective-permute-start(bf16[256,1024]{1,0:T(8,128)(2,1)} %get-tuple-element.165), channel_id=1, source_target_pairs={{2,16},{3,17},{6,20},{7,21},{10,24},{11,25},{14,28},{15,29},{16,18... | collective-permute-start | bytes 1572872 | tf_op jit(solution)/shard_map/ppermute | solution.py:905
  513.6 102.0 %reduce-scatter.2.cloned.1.call-start = ((), (), s32[]{:S(2)}) async-start(), calls=%async_computation.17 | async-start | bytes 4866048 | tf_op jit(solution)/shard_map/reduce_scatter | solution.py:1144
  583.6 46.3 %collective-permute-start.28 = (bf16[8,264,1024]{2,1,0:T(8,128)(2,1)}, bf16[8,264,1024]{2,1,0:T(8,128)(2,1)}, u32[]{:S(2)}, u32[]{:S(2)}) collective-permute-start(bf16[8,264,1024]{2,1,0:T(8,128)(2,1)} %half_products.13), channel_id=1, source_target_pairs={{0,16},{16,0},{1,17},{17,1},{2,18},{18,2},{3,19},{19,3},{4,20},{20... | collective-permute-start | bytes 12976136 | tf_op jit(solution)/shard_map/ppermute | solution.py:926
  628.0 67.9 %collective-permute-start.32 = (bf16[2,4,128,1024]{3,2,1,0:T(8,128)(2,1)}, bf16[2,4,128,1024]{3,2,1,0:T(8,128)(2,1)}, u32[]{:S(2)}, u32[]{:S(2)}) collective-permute-start(bf16[2,4,128,1024]{3,2,1,0:T(8,128)(2,1)} %get-tuple-element.197), channel_id=1, source_target_pairs={{0,4},{4,0},{8,12},{12,8},{1,5},{5,1},{9,13},{13,9},{2,6},{6,2},{1... | collective-permute-start | bytes 6291464 | tf_op jit(solution)/shard_map/ppermute | solution.py:914
  647.9 48.1 %collective-permute-start.30 = (bf16[3,264,1024]{2,1,0:T(8,128)(2,1)}, bf16[3,264,1024]{2,1,0:T(8,128)(2,1)}, u32[]{:S(2)}, u32[]{:S(2)}) collective-permute-start(bf16[3,264,1024]{2,1,0:T(8,128)(2,1)} %get-tuple-element.191), channel_id=1, source_target_pairs={{0,8},{4,12},{8,0},{12,4},{1,9},{5,13},{9,1},{13,5},{2,10},{6,14},... | collective-permute-start | bytes 4866056 | tf_op jit(solution)/shard_map/ppermute | solution.py:917
  649.3 45.0 %collective-permute-start.33 = (bf16[256,1024]{1,0:T(8,128)(2,1)S(1)}, bf16[256,1024]{1,0:T(8,128)(2,1)S(1)}, u32[]{:S(2)}, u32[]{:S(2)}) collective-permute-start(bf16[256,1024]{1,0:T(8,128)(2,1)S(1)} %fusion.31.grad_ref.refs_8_), channel_id=1, source_target_pairs={{0,16},{1,17},{4,20},{5,21},{8,24},{9,25},{12,28},{13,29},{18,18},... | collective-permute-start | bytes 1572872 | tf_op jit(solution)/shard_map/ppermute | solution.py:905
  651.8 43.3 %collective-permute-start.31 = (bf16[2,4,32,1024]{3,2,1,0:T(8,128)(2,1)}, bf16[2,4,32,1024]{3,2,1,0:T(8,128)(2,1)}, u32[]{:S(2)}, u32[]{:S(2)}) collective-permute-start(bf16[2,4,32,1024]{3,2,1,0:T(8,128)(2,1)} %get-tuple-element.195), channel_id=1, source_target_pairs={{0,4},{4,0},{8,12},{12,8},{1,5},{5,1},{9,13},{13,9},{2,6},{6,2},{1... | collective-permute-start | bytes 1572872 | tf_op jit(solution)/shard_map/ppermute | solution.py:914
  695.9 64.0 %all-to-all-start.9 = ((bf16[16,192,256]{2,1,0:T(8,128)(2,1)}), bf16[16,192,256]{2,1,0:T(8,128)(2,1)}, u32[]{:S(2)}, u32[]{:S(2)}) async-start(bf16[16,192,256]{2,1,0:T(8,128)(2,1)} %copy-done.16), calls=%async_computation.10 | async-start | bytes 3145728 | tf_op jit(solution)/shard_map/all_to_all | solution.py:492
  704.1 55.8 %collective-permute-start.37 = (bf16[4,128,1024]{2,1,0:T(8,128)(2,1)S(1)}, bf16[4,128,1024]{2,1,0:T(8,128)(2,1)}, u32[]{:S(2)}, u32[]{:S(2)}) collective-permute-start(bf16[4,128,1024]{2,1,0:T(8,128)(2,1)S(1)} %get-tuple-element.338), channel_id=1, source_target_pairs={{0,8},{4,12},{8,0},{12,4},{1,9},{5,13},{9,1},{13,5},{2,10},{6,14},... | collective-permute-start | bytes 3145736 | tf_op jit(solution)/shard_map/ppermute | solution.py:917
  705.9 54.0 %collective-permute-start.35 = (bf16[1,264,1024]{2,1,0:T(8,128)(2,1)S(1)}, bf16[1,264,1024]{2,1,0:T(8,128)(2,1)S(1)}, u32[]{:S(2)}, u32[]{:S(2)}) collective-permute-start(bf16[1,264,1024]{2,1,0:T(8,128)(2,1)S(1)} %copy-done.96), channel_id=1, source_target_pairs={{0,8},{4,12},{8,0},{12,4},{1,9},{5,13},{9,1},{13,5},{2,10},{6,14},... | collective-permute-start | bytes 1622024 | tf_op jit(solution)/shard_map/ppermute | solution.py:917
  708.1 51.8 %collective-permute-start.36 = (bf16[4,32,1024]{2,1,0:T(8,128)(2,1)S(1)}, bf16[4,32,1024]{2,1,0:T(8,128)(2,1)S(1)}, u32[]{:S(2)}, u32[]{:S(2)}) collective-permute-start(bf16[4,32,1024]{2,1,0:T(8,128)(2,1)S(1)} %get-tuple-element.379), channel_id=1, source_target_pairs={{0,8},{4,12},{8,0},{12,4},{1,9},{5,13},{9,1},{13,5},{2,10},{6,14},... | collective-permute-start | bytes 786440 | tf_op jit(solution)/shard_map/ppermute | solution.py:917
  793.0 49.0 %collective-permute-start.45 = (bf16[256,1024]{1,0:T(8,128)(2,1)}, bf16[256,1024]{1,0:T(8,128)(2,1)}, u32[]{:S(2)}, u32[]{:S(2)}) collective-permute-start(bf16[256,1024]{1,0:T(8,128)(2,1)} %fusion.23), channel_id=1, source_target_pairs={{0,0},{1,1},{4,4},{5,5},{8,8},{9,9},{12,12},{13,13},{18,2},{19,3},... | collective-permute-start | bytes 1572872 | tf_op jit(solution)/shard_map/ppermute | solution.py:905
  835.3 48.3 %collective-permute-start.48 = (bf16[264,1024]{1,0:T(8,128)(2,1)}, bf16[264,1024]{1,0:T(8,128)(2,1)S(1)}, u32[]{:S(2)}, u32[]{:S(2)}) collective-permute-start(bf16[264,1024]{1,0:T(8,128)(2,1)} %get-tuple-element.356), channel_id=1, source_target_pairs={{0,2},{1,3},{2,0},{3,1},{4,6},{5,7},{6,4},{7,5},{8,10},{9,11},{10,... | collective-permute-start | bytes 1622024 | tf_op jit(solution)/shard_map/ppermute | solution.py:923
  837.3 46.3 %all-to-all-start.10 = ((f32[32,4,1024]{2,1,0:T(4,128)}), f32[32,4,1024]{2,1,0:T(4,128)S(1)}, u32[]{:S(2)}, u32[]{:S(2)}) async-start(f32[32,4,1024]{2,1,0:T(4,128)} %broadcast_in_dim.25), calls=%async_computation.11 | async-start | bytes 1048576 | tf_op jit(solution)/shard_map/all_to_all | solution.py:929
  886.1 46.4 %all-to-all-start.11 = ((bf16[4,392,1024]{2,1,0:T(8,128)(2,1)}), bf16[4,392,1024]{2,1,0:T(8,128)(2,1)S(1)}, u32[]{:S(2)}, u32[]{:S(2)}) async-start(bf16[4,392,1024]{2,1,0:T(8,128)(2,1)} %broadcast_in_dim.26), calls=%async_computation.12 | async-start | bytes 6422528 | tf_op jit(solution)/shard_map/all_to_all | solution.py:929
  889.8 69.7 %all-gather.12.cloned.1.call-start = ((), (), s32[]{:S(2)}) async-start(), calls=%async_computation.18 | async-start | bytes 2703360 | tf_op jit(solution)/shard_map/all_gather | solution.py:1223
  (165 other events, 1992.9 us)
Sparse Core Ops, SparseCore 0:
  54.1 90.0 all-gather.7
  147.2 92.0 all-gather.5
  241.5 93.8 all-gather.9
  517.7 97.7 reduce-scatter.1
  892.3 67.1 all-gather.11

commit v3 on v2

--- a/solution.py
+++ b/solution.py
@@ -12,6 +12,8 @@
 MASKED = -1e30
 ALL_AXES = ("section", "ctx", "tp")
 CHUNK = 2
+ONES = 16
+LOG_2 = 0.6931471805599453
 LIGHT = pl.CostEstimate(flops=1, bytes_accessed=1, transcendentals=0)
 VMEM_LIMIT = 40 * 1024 * 1024
 
@@ -527,79 +529,82 @@
     return combine(value.reshape(rows // 8, 8, width), axis=0)
 
 
-def attention_forward_kernel(ends_ref, qkv_ref, out_ref, lse_ref, keys_ref):
-    block = pl.program_id(0)
-    blocks, _, width = qkv_ref.shape
-    span = CHUNK * width
-
-    @pl.when(block == 0)
+def attention_forward_kernel(ends_ref, qkv_ref, out_ref, lse_ref, keys_ref, values_ref):
+    program = pl.program_id(0)
+    blocks, _, block_width = qkv_ref.shape
+    width = CHUNK * block_width
+
+    @pl.when(program == 0)
     def _():
         def turn(j, carry):
             keys_ref[j] = qkv_ref[j, HD : 2 * HD, :].T
+            values_ref[j, 0:HD, :] = qkv_ref[j, 2 * HD : 3 * HD, :]
+            values_ref[j, HD : HD + ONES, :] = jnp.ones((ONES, block_width), jnp.bfloat16)
             return carry
 
         lax.fori_loop(0, blocks, turn, 0)
 
-    query = qkv_ref[block, 0:HD, :]
-    first = block * width
+    query = jnp.concatenate(
+        [qkv_ref[program * CHUNK + entry, 0:HD, :] for entry in range(CHUNK)], axis=1
+    )
+    first = program * width
     query_index = first + lax.broadcasted_iota(jnp.int32, (1, width), 1)
     start = document_bounds(ends_ref, query_index)
-    last = block // CHUNK
-    low = scalar_start(ends_ref, first) // span
+    low_chunk = scalar_start(ends_ref, first) // width
     high_start = scalar_start(ends_ref, first + width - 1)
-    middle = jnp.clip((high_start + span - 1) // span, low, last)
+    middle = jnp.clip((high_start + width - 1) // width, low_chunk, program)
 
     def step(chunk, carry, masked):
-        top, total, acc = carry
-        parts, part_tops = [], []
+        top, acc = carry
+        parts = []
         for entry in range(CHUNK):
             j = chunk * CHUNK + entry
             scores = dot(keys_ref[j], query, 1, 0)
             if masked:
-                key_index = j * width + lax.broadcasted_iota(jnp.int32, (width, 1), 0)
+                key_index = j * block_width + lax.broadcasted_iota(jnp.int32, (block_width, 1), 0)
                 allowed = (key_index >= start) & (key_index <= query_index)
                 scores = jnp.where(allowed, scores, MASKED)
             parts.append(scores)
-            part_tops.append(fold_rows(scores, jnp.max))
-        chunk_top = jnp.max(functools.reduce(jnp.maximum, part_tops), axis=0, keepdims=True)
-        new_top = jnp.maximum(top, chunk_top)
-        shrink = jnp.exp(top - new_top)
-        total = total * shrink
-        acc = acc * shrink
+        part_top = functools.reduce(jnp.maximum, [fold_rows(part, jnp.max) for part in parts])
+        new_top = jnp.maximum(top, jnp.max(part_top, axis=0, keepdims=True))
+        acc = acc * jnp.exp2(top - new_top)
         for entry in range(CHUNK):
-            weights = jnp.exp(parts[entry] - new_top)
-            total = total + fold_rows(weights, jnp.sum)
-            values = qkv_ref[chunk * CHUNK + entry, 2 * HD : 3 * HD, :]
-            acc = acc + dot(values, weights.astype(jnp.bfloat16), 1, 0)
-        return new_top, total, acc
+            weights = jnp.exp2(parts[entry] - new_top).astype(jnp.bfloat16)
+            acc = acc + dot(values_ref[chunk * CHUNK + entry], weights, 1, 0)
+        return new_top, acc
 
     carry = (
         jnp.full((1, width), MASKED, jnp.float32),
-        jnp.zeros((8, width), jnp.float32),
-        jnp.zeros((HD, width), jnp.float32),
-    )
-    carry = lax.fori_loop(low, middle, functools.partial(step, masked=True), carry)
-    carry = lax.fori_loop(middle, last, functools.partial(step, masked=False), carry)
-    top, total, acc = step(last, carry, True)
-    total = jnp.sum(total, axis=0, keepdims=True)
-    out_ref[0] = (acc / total).astype(jnp.bfloat16)
-    lse_ref[0] = top + jnp.log(total)
+        jnp.zeros((HD + ONES, width), jnp.float32),
+    )
+    carry = lax.fori_loop(low_chunk, middle, functools.partial(step, masked=True), carry)
+    carry = lax.fori_loop(middle, program, functools.partial(step, masked=False), carry)
+    top, acc = step(program, carry, True)
+    total = acc[HD : HD + 1]
+    out = (acc[:HD] / total).astype(jnp.bfloat16)
+    lse = top + jnp.log2(total)
+    for entry in range(CHUNK):
+        columns = slice(entry * block_width, (entry + 1) * block_width)
+        out_ref[entry] = out[:, columns]
+        lse_ref[entry] = lse[:, columns]
 
 
 def attention_forward(ends, qkv):
     blocks, _, width = qkv.shape
-    pairs = blocks * (blocks + 1) // 2 * width * width
     return pl.pallas_call(
         attention_forward_kernel,
         grid_spec=pltpu.PrefetchScalarGridSpec(
             num_scalar_prefetch=1,
-            grid=(blocks,),
+            grid=(blocks // CHUNK,),
             in_specs=[pl.BlockSpec(qkv.shape, lambda i, ends_ref: (0, 0, 0))],
             out_specs=[
-                pl.BlockSpec((1, HD, width), lambda i, ends_ref: (i, 0, 0)),
-                pl.BlockSpec((1, 1, width), lambda i, ends_ref: (i, 0, 0)),
+                pl.BlockSpec((CHUNK, HD, width), lambda i, ends_ref: (i, 0, 0)),
+                pl.BlockSpec((CHUNK, 1, width), lambda i, ends_ref: (i, 0, 0)),
             ],
-            scratch_shapes=[pltpu.VMEM((blocks, width, HD), jnp.bfloat16)],
+            scratch_shapes=[
+                pltpu.VMEM((blocks, width, HD), jnp.bfloat16),
+                pltpu.VMEM((blocks, HD + ONES, width), jnp.bfloat16),
+            ],
         ),
         out_shape=[
             jax.ShapeDtypeStruct((blocks, HD, width), jnp.bfloat16),
@@ -612,67 +617,82 @@
 
 
 def attention_backward_kernel(
-    ends_ref, qkv_ref, out_ref, grad_ref, lse_ref, result_ref, query_grad_ref, delta_ref
+    ends_ref, qkv_ref, out_ref, grad_ref, lse_ref, result_ref,
+    query_grad_ref, delta_ref, queries_ref, grads_ref, lses_ref,
 ):
-    block = pl.program_id(0)
-    blocks, _, width = qkv_ref.shape
-    span = CHUNK * width
-
-    @pl.when(block == 0)
+    program = pl.program_id(0)
+    blocks, _, block_width = qkv_ref.shape
+    width = CHUNK * block_width
+
+    @pl.when(program == 0)
     def _():
         def turn(i, carry):
-            delta_ref[i] = jnp.sum(
-                grad_ref[i].astype(jnp.float32) * out_ref[i].astype(jnp.float32),
-                axis=0,
-                keepdims=True,
-            )
+            for entry in range(CHUNK):
+                block = i * CHUNK + entry
+                columns = slice(entry * block_width, (entry + 1) * block_width)
+                grad = grad_ref[block]
+                queries_ref[i, :, columns] = qkv_ref[block, 0:HD, :]
+                grads_ref[i, :, columns] = grad
+                lses_ref[i, :, columns] = lse_ref[block]
+                delta_ref[i, :, columns] = jnp.sum(
+                    grad.astype(jnp.float32) * out_ref[block].astype(jnp.float32),
+                    axis=0,
+                    keepdims=True,
+                )
             query_grad_ref[i] = jnp.zeros((HD, width), jnp.float32)
             return carry
 
-        lax.fori_loop(0, blocks, turn, 0)
-
-    first = block * width
-    keys_t = qkv_ref[block, HD : 2 * HD, :]
+        lax.fori_loop(0, blocks // CHUNK, turn, 0)
+
+    def joined(low_row, high_row):
+        return jnp.concatenate(
+            [qkv_ref[program * CHUNK + entry, low_row:high_row, :] for entry in range(CHUNK)],
+            axis=1,
+        )
+
+    first = program * width
+    keys_t = joined(HD, 2 * HD)
     keys = keys_t.T
-    values = qkv_ref[block, 2 * HD : 3 * HD, :].T
+    values = joined(2 * HD, 3 * HD).T
     key_index = first + lax.broadcasted_iota(jnp.int32, (width, 1), 0)
     near_end = scalar_end(ends_ref, first)
     far_end = scalar_end(ends_ref, first + width - 1)
-    own_chunk = block // CHUNK
-    stop = (far_end - 1) // span + 1
-    middle = jnp.clip(near_end // span, own_chunk + 1, stop)
-
-    def step(chunk, carry, masked):
+    stop = (far_end - 1) // width + 1
+    middle = jnp.clip(near_end // width, program + 1, stop)
+
+    def step(i, carry, masked):
         key_grad, value_grad = carry
-        for entry in range(CHUNK):
-            i = chunk * CHUNK + entry
-            query = qkv_ref[i, 0:HD, :]
-            grad = grad_ref[i]
-            weights = jnp.exp(dot(keys, query, 1, 0) - lse_ref[i])
-            if masked:
-                query_index = i * width + lax.broadcasted_iota(jnp.int32, (1, width), 1)
-                start = document_bounds(ends_ref, query_index)
-                allowed = (key_index >= start) & (key_index <= query_index)
-                weights = jnp.where(allowed, weights, 0.0)
-            grad_weights = dot(values, grad, 1, 0)
-            grad_scores = (weights * (grad_weights - delta_ref[i])).astype(jnp.bfloat16)
-            value_grad = value_grad + dot(grad, weights.astype(jnp.bfloat16), 1, 1)
-            key_grad = key_grad + dot(query, grad_scores, 1, 1)
-            query_grad_ref[i] += dot(keys_t, grad_scores, 1, 0)
+        query = queries_ref[i]
+        grad = grads_ref[i]
+        weights = jnp.exp2(dot(keys, query, 1, 0) - lses_ref[i])
+        if masked:
+            query_index = i * width + lax.broadcasted_iota(jnp.int32, (1, width), 1)
+            start = document_bounds(ends_ref, query_index)
+            allowed = (key_index >= start) & (key_index <= query_index)
+            weights = jnp.where(allowed, weights, 0.0)
+        grad_weights = dot(values, grad, 1, 0)
+        grad_scores = (weights * (grad_weights - delta_ref[i])).astype(jnp.bfloat16)
+        query_grad_ref[i] += dot(keys_t, grad_scores, 1, 0)
+        value_grad = value_grad + dot(grad, weights.astype(jnp.bfloat16), 1, 1)
+        key_grad = key_grad + dot(query, grad_scores, 1, 1)
         return key_grad, value_grad
 
     empty = jnp.zeros((HD, width), jnp.float32)
-    carry = step(own_chunk, (empty, empty), True)
-    carry = lax.fori_loop(own_chunk + 1, middle, functools.partial(step, masked=False), carry)
+    carry = step(program, (empty, empty), True)
+    carry = lax.fori_loop(program + 1, middle, functools.partial(step, masked=False), carry)
     key_grad, value_grad = lax.fori_loop(middle, stop, functools.partial(step, masked=True), carry)
-    result_ref[0, 0:HD] = (query_grad_ref[block] * HD ** (-0.5)).astype(jnp.bfloat16)
-    result_ref[0, HD : 2 * HD] = key_grad.astype(jnp.bfloat16)
-    result_ref[0, 2 * HD : 3 * HD] = value_grad.astype(jnp.bfloat16)
+    query_grad = query_grad_ref[program] * HD ** (-0.5)
+    key_grad = key_grad * LOG_2
+    for entry in range(CHUNK):
+        columns = slice(entry * block_width, (entry + 1) * block_width)
+        result_ref[entry, 0:HD] = query_grad[:, columns].astype(jnp.bfloat16)
+        result_ref[entry, HD : 2 * HD] = key_grad[:, columns].astype(jnp.bfloat16)
+        result_ref[entry, 2 * HD : 3 * HD] = value_grad[:, columns].astype(jnp.bfloat16)
 
 
 def attention_backward(ends, qkv, out, grad, lse):
-    blocks, _, width = qkv.shape
-    pairs = blocks * (blocks + 1) // 2 * width * width
+    blocks, _, block_width = qkv.shape
+    chunks, width = blocks // CHUNK, CHUNK * block_width
 
     def whole(value):
         return pl.BlockSpec(value.shape, lambda i, ends_ref: (0, 0, 0))
@@ -681,12 +701,15 @@
         attention_backward_kernel,
         grid_spec=pltpu.PrefetchScalarGridSpec(
             num_scalar_prefetch=1,
-            grid=(blocks,),
+            grid=(chunks,),
             in_specs=[whole(qkv), whole(out), whole(grad), whole(lse)],
-            out_specs=pl.BlockSpec((1, 3 * HD, width), lambda i, ends_ref: (i, 0, 0)),
+            out_specs=pl.BlockSpec((CHUNK, 3 * HD, block_width), lambda i, ends_ref: (i, 0, 0)),
             scratch_shapes=[
-                pltpu.VMEM((blocks, HD, width), jnp.float32),
-                pltpu.VMEM((blocks, 1, width), jnp.float32),
+                pltpu.VMEM((chunks, HD, width), jnp.float32),
+                pltpu.VMEM((chunks, 1, width), jnp.float32),
+                pltpu.VMEM((chunks, HD, width), jnp.bfloat16),
+                pltpu.VMEM((chunks, HD, width), jnp.bfloat16),
+                pltpu.VMEM((chunks, 1, width), jnp.float32),
             ],
         ),
         out_shape=jax.ShapeDtypeStruct(qkv.shape, jnp.bfloat16),
@@ -940,16 +963,27 @@
     def by_core(value, which):
         return lax.dynamic_index_in_dim(value, which, 0, keepdims=False)
 
-    def spread_plane(piece, *others):
-        middle = piece.shape[0] // 2
-        line = after(all_to_all(copies(piece, parts), "tp"), *others)
+    def spread_line(piece):
+        return all_to_all(copies(piece, parts), "tp")
+
+    def spread_sides(line):
+        middle = line.shape[1] // 2
         line_a, line_b = line[:, :middle], line[:, middle:]
-        pair_a = jnp.stack(ordered(row_side, line_a, swap_far(line_a)))
-        pair_b = jnp.stack(ordered(column_side, line_b, swap_side(line_b)))
-        plane_a = jnp.stack(ordered(column_side, pair_a, swap_side(pair_a)), axis=1)
-        plane_b = jnp.stack(ordered(row_side, pair_b, swap_far(pair_b)), axis=0)
-        plane = jnp.concatenate([plane_a, plane_b], axis=3)
-        return plane.reshape(contexts * parts * piece.shape[0], piece.shape[1]), line
+        return (line_a, swap_far(line_a)), (line_b, swap_side(line_b))
+
+    def spread_corners(line_pairs):
+        pair_a = jnp.stack(ordered(row_side, *line_pairs[0]))
+        pair_b = jnp.stack(ordered(column_side, *line_pairs[1]))
+        return (pair_a, swap_side(pair_a)), (pair_b, swap_far(pair_b))
+
+    def spread_cores(plane_pairs):
+        plane_a = jnp.stack(ordered(column_side, *plane_pairs[0]), axis=1)
+        plane_b = jnp.stack(ordered(row_side, *plane_pairs[1]), axis=0)
+        rest = head_rows - plane_a.shape[3]
+        own_heads = jnp.concatenate([plane_a, plane_b[:, :, :, :rest]], axis=3)
+        own_heads = own_heads.reshape(-1, model_width)
+        own_outs = plane_b[:, :, :, rest:].reshape(-1, model_width)
+        return (own_heads, swap_section(own_heads)), (own_outs, swap_section(own_outs))
 
     def own_halves(value, axis, size):
         part = lax.dynamic_slice_in_dim(value, ctx * size, size, axis)
@@ -976,19 +1010,12 @@
         return [whole[:, entry].reshape(-1, model_width) for entry in range(3)]
 
     rows_in = to_batch(inputs)
-    own_heads, line = spread_plane(pieces[0][:head_rows], rows_in)
-    first_ffn = feed_forward_weights(after(pieces[0], line))
-    first_heads = (own_heads, swap_section(own_heads))
-    own_outs, _ = spread_plane(after(pieces[0], own_heads)[head_rows:attention_rows])
-    first_outs = jnp.concatenate(ordered(section, own_outs, swap_section(own_outs)), axis=0)
-    second = gather(pieces[1][:attention_rows], everyone)
-    second = second.reshape(2, heads, attention_rows, model_width)
-    second_heads = [second[half, :, :head_rows].reshape(-1, model_width) for half in range(2)]
-    second_outs = second[:, :, head_rows:].reshape(-1, model_width)
-    second_ffn = feed_forward_weights(pieces[1])
-    w_heads = (first_heads, second_heads)
-    w_outs = (first_outs, second_outs)
-    w_ffn = (first_ffn, second_ffn)
+    line, rows_in = together(spread_line(pieces[0][:attention_rows]), rows_in)
+    w_ffn = [feed_forward_weights(after(piece, line)) for piece in pieces]
+    line_pairs = together(*spread_sides(line))
+    w_heads, w_outs = [None, None], [None, None]
+    w_heads[0], out_halves = spread_cores(spread_corners(line_pairs))
+    w_outs[0] = jnp.concatenate(ordered(section, *out_halves), axis=0)
 
     gains = wide(jnp.concatenate([gain1, gain2], axis=0))
     gain_sets = ordered(section, gains, swap_section(gains))
@@ -1015,13 +1042,12 @@
     def nothing(value):
         return value
 
-    def layer_forward(whole_rows, first_values, layer, beside):
+    def layer_forward(whole_rows, first_values, layer, in_first, in_second, in_third, in_fourth):
         gain_first, gain_second = gain_sets[layer][0], gain_sets[layer][1]
         scale_first = lax.rsqrt(jnp.mean(whole_rows * whole_rows, axis=-1, keepdims=True) + EPSILON)
         normed = low(whole_rows * scale_first * gain_first)
         halves = [dot(weight, normed, 1, 1) for weight in w_heads[layer]]
-        if layer == 0:
-            halves = ordered(section, *halves)
+        halves = ordered(section, *halves)
         upper, lower = [half.reshape(heads, head_rows, rows) for half in halves]
         query = rope_pair(upper[:, :half_width], upper[:, half_width:HD], cosine, sine_part)
         key = rope_pair(upper[:, HD:], lower[:, :half_width], cosine, sine_part)
@@ -1029,20 +1055,22 @@
         if first_values is not None:
             value = 0.5 * value + 0.5 * wide(first_values)
         mixed = low(value)
-        shrunk = [low(half * HD ** (-0.5)) for half in query]
+        shrunk = [low(half * (HD ** (-0.5) / LOG_2)) for half in query]
         qkv = exchange(
             jnp.concatenate([*shrunk, low(key[0]), low(key[1]), mixed], axis=1), batch_groups
         )
+        qkv = in_first(qkv)
         out, lse = attention_forward(ends, qkv)
-        out = beside(out)
+        out = in_second(out)
         attended = head_halves(exchange(out, batch_groups))
         hidden = whole_rows + dot(attended.reshape(-1, rows), w_outs[layer], 0, 0)
         scale_second = lax.rsqrt(jnp.mean(hidden * hidden, axis=-1, keepdims=True) + EPSILON)
         normed_second = low(hidden * scale_second * gain_second)
         far_rows = swap_side(normed_second)
         near = feed_forward(normed_second, *w_ffn[layer], tile)
-        far = feed_forward(after(far_rows, near[3]), *w_ffn[layer], tile)
-        far_down = swap_side(low(far[3]))
+        far_rows = in_third(after(far_rows, near[3]))
+        far = feed_forward(far_rows, *w_ffn[layer], tile)
+        far_down = in_fourth(swap_side(low(far[3])))
         layer_out = low(hidden + (near[3] + wide(far_down)))
         saved = (
             whole_rows, scale_first, normed, qkv, out, lse, attended, hidden, scale_second,
@@ -1133,7 +1161,7 @@
 
     def input_grads_of(grad_halves, grad_hidden, saved, layer):
         whole_rows, scale_first = saved[:2]
-        places_of = (section, 1 - section) if layer == 0 else (0, 1)
+        places_of = (section, 1 - section)
         grad_normed = sum(
             dot(by_core(grad_halves, place), weight, 0, 0)
             for place, weight in zip(places_of, w_heads[layer])
@@ -1148,19 +1176,49 @@
     line_groups = device_groups(
         mesh_sizes, lambda s, c, t: (s, c % 2), lambda s, c, t: (c, t)
     )
+    core_groups = device_groups(mesh_sizes, lambda s, c, t: s, lambda s, c, t: (c, t))
     plane_shape = (2, 2, parts)
     pending = {}
 
-    first_out, first_values, first_saved = layer_forward(wide(rows_in), None, 0, nothing)
-    first_home = to_home(first_out, 0)
-    grad_in = to_batch(after(cotangent, first_out))
-
-    def beside_second(value):
-        value, pending["first_home"], pending["grad_in"] = together(value, first_home, grad_in)
+    def weights_line(value):
+        value, piece = together(value, pieces[1][:attention_rows])
+        pending["weights"] = spread_line(piece)
         return value
 
+    def weights_sides(value):
+        value, line = together(value, pending["weights"])
+        pending["weights"] = spread_sides(line)
+        return value
+
+    def weights_corners(value):
+        value, pairs = together(value, pending["weights"])
+        pending["weights"] = spread_corners(pairs)
+        return value
+
+    def weights_cores(value):
+        value, pairs = together(value, pending["weights"])
+        w_heads[1], pending["outs"] = spread_cores(pairs)
+        return value
+
+    first_out, first_values, first_saved = layer_forward(
+        wide(rows_in), None, 0, weights_line, weights_sides, weights_corners, weights_cores
+    )
+
+    def start_homes(value):
+        w_outs[1] = jnp.concatenate(ordered(section, *pending["outs"]), axis=0)
+        value, home = together(value, first_out)
+        pending["first_home"] = to_home(home, 0)
+        pending["grad_in"] = to_batch(after(cotangent, home))
+        return value
+
+    def end_homes(value):
+        value, pending["first_home"], pending["grad_in"], w_outs[1] = together(
+            value, pending["first_home"], pending["grad_in"], w_outs[1]
+        )
+        return value
+
     second_out, _, second_saved = layer_forward(
-        wide(first_out), first_values, 1, beside_second
+        wide(first_out), first_values, 1, start_homes, end_homes, nothing, nothing
     )
     first_home, grad_in = pending["first_home"], pending["grad_in"]
 
@@ -1201,9 +1259,8 @@
 
     def first_second(value):
         head = head_products(section, addend=pending["moved"])
-        head = parted(head.reshape(*plane_shape, -1, model_width), column_side, 1)
-        value, head, _ = together(value, head, pending["second_rest"])
-        pending["head"] = moved_pair(head, swap_side)
+        value, head = together(value, head)
+        pending["head"] = piece_sum(head.reshape(-1, model_width), core_groups)
         pending["second_grad_home"] = to_home(after(second_grad, value), 1)
         return value
 
@@ -1220,30 +1277,25 @@
         pending["rest_a"] = moved_pair(rest_a, swap_far)
         pending["rest_b"] = rest_b
         pending["out"] = moved_pair(out_sum, swap_side)
-        pending["second_rest"] = lax.all_gather(
-            after(pending["second_rest"], value), "ctx", axis=0, tiled=False
-        )
         return value, rest
 
     def first_fourth(value):
-        value, rest_a, rest_b, out_sum, head, pending["second_grad_home"] = together(
-            value, pending["rest_a"], pending["rest_b"], pending["out"], pending["head"],
+        value, rest_a, rest_b, out_sum, pending["second_grad_home"] = together(
+            value, pending["rest_a"], pending["rest_b"], pending["out"],
             pending["second_grad_home"],
         )
         pending["rest_a"] = rest_a
         pending["rest_b"] = moved_pair(rest_b, swap_far)
         pending["out"] = halve(add(out_sum), row_side, swap_far, 0)
-        pending["head"] = halve(add(head), row_side, swap_far, 0)
         return value
 
     def first_fifth(value):
-        value, rest_a, rest_b, out_sum, head = together(
-            value, pending["rest_a"], pending["rest_b"], pending["out"], pending["head"]
+        value, rest_a, rest_b, out_sum = together(
+            value, pending["rest_a"], pending["rest_b"], pending["out"]
         )
         pending["out"] = add(out_sum)
         rest = jnp.concatenate([add(rest_a), add(rest_b)], axis=0)
         pending["rest"] = near_sum(rest)
-        pending["head"] = near_sum(add(head))
         return value
 
     first_halves, _, first_hidden, _, first_gain2 = layer_backward(
@@ -1262,38 +1314,35 @@
         after(first_halves, sent), first_hidden, first_saved, 0
     )
     head = head_products(section, addend=moved).reshape(*plane_shape, head_rows, model_width)
-    head, first_grad = together(head, low(first_grad))
+    head, first_grad, rest = together(head, low(first_grad), pending["rest"])
     head_a, head_b = crossed(head)
     gain_rows = jnp.stack([first_gain1, first_gain2, second_gain1, second_gain2])
-    first_grad, gain_rows, head_a, head_b = together(first_grad, gain_rows, head_a, head_b)
+    first_grad, gain_rows, head_a, head_b, rest = together(
+        first_grad, gain_rows, head_a, head_b, rest
+    )
     head_a = moved_pair(head_a, swap_side)
     head_b = moved_pair(head_b, swap_far)
+    rest = far_sum(rest)
     first_grad_home = to_home(first_grad, 0)
-    head_a, head_b, rest, second_head = together(
-        add(head_a), add(head_b), pending["rest"], pending["head"]
-    )
+    head_a, head_b = together(add(head_a), add(head_b))
     head_a = parted(head_a, row_side, 0)
     head_b = parted(head_b, column_side, 0)
-    gain_rows, head_a, head_b, rest, second_head = together(
-        gain_rows, head_a, head_b, rest, second_head
-    )
+    gain_rows, head_a, head_b = together(gain_rows, head_a, head_b)
     head_a = moved_pair(head_a, swap_far)
     head_b = moved_pair(head_b, swap_side)
-    rest = far_sum(rest)
-    second_head = far_sum(second_head)
     gain_sums = all_to_all(copies(gain_rows, len(places)), ALL_AXES)
-    head_a, head_b, first_grad_home = together(head_a, head_b, first_grad_home)
+    head_a, head_b, rest, first_grad_home = together(head_a, head_b, rest, first_grad_home)
     head = near_sum(jnp.concatenate([add(head_a), add(head_b), pending["out"]], axis=1))
-    head, rest, second_head, gain_sums = together(head, rest, second_head, gain_sums)
-    head = far_sum(head)
-    rest = jnp.concatenate([add(rest), add(second_head)], axis=0)
-    rest = all_to_all(copies(rest, contexts), "ctx")
-    head, rest = together(head, rest)
+    rest = all_to_all(copies(add(rest), contexts), "ctx")
+    head, gain_sums = together(head, gain_sums)
+    head = together(*far_sum(head))
     first_head = all_to_all(copies(add(head), contexts), "ctx")
-    second_head = rest[:, 3 * unit_rows :]
-    rest = rest[:, : 3 * unit_rows]
+    second = lax.all_gather(
+        jnp.concatenate([pending["second_rest"], pending["head"]], axis=0), "ctx", axis=0, tiled=False
+    )
+    rest, first_head, second = together(rest, first_head, second)
     first_grads = jnp.concatenate([rest, first_head], axis=1)
-    second_grads = jnp.concatenate([pending["second_rest"], second_head], axis=1)
+    second_grads = second
     second_home, second_grad_home = pending["second_home"], pending["second_grad_home"]
     gain_total = jnp.sum(gain_sums.reshape(len(places), 4, model_width), axis=0)
     gain_total = jnp.where(leading, gain_total[:2], gain_total[2:])

time: 1000 us -> 946 us (0.946)
  Pallas kernels: 226 us -> 192 us
  starting transfers between devices: 133 us -> 116 us
  blocking collectives: 0 us -> 16.2 us
  matrix products: 32.1 us -> 20.5 us
    all_to_all x8, waiting for transfers between devices: 57.7 us -> 110 us  [exchange(): lax.all_to_all(value, ALL_AXES, split_axis=0, concat_axis=0, tiled=True,...]
    ppermute x2, waiting for transfers between devices: 49.7 us -> 17.3 us  [to_batch(): moved = lax.ppermute(other, ALL_AXES, crossing)]
    pallas_call x2, Pallas kernels: 84.2 us -> 61.9 us  [attention_backward(): pl.pallas_call(attention_backward_kernel, grid_spec=pltpu.PrefetchScalarG...]
    ppermute x3 -> x2, waiting for transfers between devices: 46.6 us -> 28.3 us  [swap_half(): lax.ppermute(value, 'tp', [(t, (t + half_parts) % parts) for t in range(p...]
    all_gather x1, waiting for transfers between devices: 17.5 us -> 0.01 us  [split_body(): lax.all_gather(jnp.concatenate([pending['second_rest'], pending['head']],...]
    all_to_all x0 -> x1, blocking collectives: none -> 16.2 us  [all_to_all(): return lax.all_to_all(value, axis, split_axis=0, concat_axis=0, tiled=True)]
    pallas_call x2, Pallas kernels: 56.4 us -> 44 us  [attention_forward(): pl.pallas_call(attention_forward_kernel, grid_spec=pltpu.PrefetchScalarGr...]
    all_to_all x5 -> x4, waiting for transfers between devices: 39.7 us -> 27.7 us  [all_to_all(): return lax.all_to_all(value, axis, split_axis=0, concat_axis=0, tiled=True)]
  transfers between devices with their start and end apart: 70 -> 67, of which waited for: 34 -> 31; matrix products, arithmetic and copies ran while one was open for 13% -> 13% of each run, Pallas kernels for 20% -> 18%
where the time goes in v3:
time: 946 us; the launch traced here: 935 us
  waiting for transfers between devices  415 us (44%)
  Pallas kernels  192 us (20%)
  starting transfers between devices  116 us (12%)
  local copies, waits for them, and re-layouts  85.8 us (9%)
  other arithmetic  72.7 us (8%)
  matrix products  20.5 us (2%)
  between operations  16.5 us (2%)
  blocking collectives  16.2 us (2%)
    ppermute x9, waiting for transfers between devices, swap_far(): return lax.ppermute(value, 'ctx', [(c, c ^ 2) for c in range(contexts)])  111 us
    all_to_all x8, waiting for transfers between devices, exchange(): lax.all_to_all(value, ALL_AXES, split_axis=0, concat_axis=0, tiled=True,...  110 us
    ppermute x15, waiting for transfers between devices, swap_side(): return lax.ppermute(value, 'ctx', [(c, c ^ 1) for c in range(contexts)])  79.3 us
    pallas_call x2, Pallas kernels, attention_backward(): pl.pallas_call(attention_backward_kernel, grid_spec=pltpu.PrefetchScalarG...  61.9 us
    pallas_call x2, Pallas kernels, attention_forward(): pl.pallas_call(attention_forward_kernel, grid_spec=pltpu.PrefetchScalarGr...  44 us
    unnamed x246, local copies, waits for them, and re-layouts  40.4 us
    pallas_call x10, Pallas kernels, half_products(): pl.pallas_call(functools.partial(half_products_kernel, tuple(layout), siz...  39 us
    all_to_all x8, starting transfers between devices, exchange(): lax.all_to_all(value, ALL_AXES, split_axis=0, concat_axis=0, tiled=True,...  36.8 us
  transfers between devices with their start and end apart: 67, of which 31 were waited for; matrix products, arithmetic and copies ran while one was open for 13% of the time, Pallas kernels for 18%

profile of v3, /device:TPU:0, one launch (start us, length us, event | category | flops | bytes accessed | tf_op | source)
XLA Modules:
  0.0 934.6 jit_solution(3775085954825285420)
XLA Ops:
  31.5 17.3 %collective-permute-done.1 = bf16[256,1024]{1,0:T(8,128)(2,1)} collective-permute-done((bf16[256,1024]{1,0:T(8,128)(2,1)S(1)}, bf16[256,1024]{1,0:T(8,128)(2,1)}, u32[]{:S(2)}, u32[]{:S(2)}) %collective-permute-start.1) | collective-permute-done | bytes 524320 | tf_op jit(solution)/shard_map/ppermute | solution.py:916
  49.7 8.8 all-to-all-done
  73.9 27.9 %collective-permute-done.5 = bf16[2,4,64,1024]{3,2,1,0:T(8,128)(2,1)S(1)} collective-permute-done((bf16[2,4,64,1024]{3,2,1,0:T(8,128)(2,1)}, bf16[2,4,64,1024]{3,2,1,0:T(8,128)(2,1)S(1)}, u32[]{:S(2)}, u32[]{:S(2)}) %collective-permute-start.5) | collective-permute-done | bytes 1048608 | tf_op jit(solution)/shard_map/ppermute | solution.py:940
  128.3 30.4 %all-to-all-done.1.qkv_ref = bf16[16,192,256]{2,1,0:T(8,128)(2,1)S(1)} async-done(((bf16[16,192,256]{2,1,0:T(8,128)(2,1)}), bf16[16,192,256]{2,1,0:T(8,128)(2,1)S(1)}, u32[]{:S(2)}, u32[]{:S(2)}) %all-to-all-start.1) | async-done | bytes 1572896 | tf_op jit(solution)/shard_map/all_to_all | solution.py:494
  166.2 21.6 %attention_forward.2 = (bf16[16,64,256]{2,1,0:T(8,128)(2,1)}, f32[16,1,256]{2,1,0:T(1,128)S(1)}) custom-call(s32[4]{0:T(128)S(1)} %bitcast.305, bf16[16,192,256]{2,1,0:T(8,128)(2,1)S(1)} %all-to-all-done.1.qkv_ref), custom_call_target="tpu_custom_call" | custom-call | flops 1 | bytes 1 | tf_op jit(solution)/shard_map/attention_forward/pallas_call | solution.py:594
  187.9 17.6 %all-to-all-done.2 = bf16[4,128,1024]{2,1,0:T(8,128)(2,1)} async-done(((bf16[4,128,1024]{2,1,0:T(8,128)(2,1)}), bf16[4,128,1024]{2,1,0:T(8,128)(2,1)}, u32[]{:S(2)}, u32[]{:S(2)}) %all-to-all-start.2) | async-done | bytes 1048608 | tf_op jit(solution)/shard_map/all_to_all | solution.py:952
  211.7 16.0 %all-to-all-done.3 = bf16[16,64,256]{2,1,0:T(8,128)(2,1)S(1)} async-done(((bf16[16,64,256]{2,1,0:T(8,128)(2,1)}), bf16[16,64,256]{2,1,0:T(8,128)(2,1)S(1)}, u32[]{:S(2)}, u32[]{:S(2)}) %all-to-all-start.3) | async-done | bytes 524320 | tf_op jit(solution)/shard_map/all_to_all | solution.py:494
  267.5 25.0 %collective-permute-done.12 = bf16[256,1024]{1,0:T(8,128)(2,1)S(1)} collective-permute-done((bf16[256,1024]{1,0:T(8,128)(2,1)S(1)}, bf16[256,1024]{1,0:T(8,128)(2,1)S(1)}, u32[]{:S(2)}, u32[]{:S(2)}) %collective-permute-start.12) | collective-permute-done | bytes 524320 | tf_op jit(solution)/shard_map/ppermute | solution.py:937
  312.3 21.0 %all-to-all-done.4.qkv_ref = bf16[16,192,256]{2,1,0:T(8,128)(2,1)} async-done(((bf16[16,192,256]{2,1,0:T(8,128)(2,1)}), bf16[16,192,256]{2,1,0:T(8,128)(2,1)}, u32[]{:S(2)}, u32[]{:S(2)}) %all-to-all-start.4) | async-done | bytes 1572896 | tf_op jit(solution)/shard_map/all_to_all | solution.py:494
  345.4 22.4 %attention_forward.3 = (bf16[16,64,256]{2,1,0:T(8,128)(2,1)S(1)}, f32[16,1,256]{2,1,0:T(1,128)S(1)}) custom-call(s32[4]{0:T(128)S(1)} %bitcast.306, bf16[16,192,256]{2,1,0:T(8,128)(2,1)} %all-to-all-done.4.qkv_ref), custom_call_target="tpu_custom_call" | custom-call | flops 1 | bytes 1 | tf_op jit(solution)/shard_map/attention_forward/pallas_call | solution.py:594
  427.0 12.5 %collective-permute-done.22 = bf16[256,1024]{1,0:T(8,128)(2,1)S(1)} collective-permute-done((bf16[256,1024]{1,0:T(8,128)(2,1)S(1)}, bf16[256,1024]{1,0:T(8,128)(2,1)S(1)}, u32[]{:S(2)}, u32[]{:S(2)}) %collective-permute-start.22) | collective-permute-done | bytes 524320 | tf_op jit(solution)/shard_map/ppermute | solution.py:937
  440.0 10.3 %collective-permute-done.24 = bf16[256,1024]{1,0:T(8,128)(2,1)S(1)} collective-permute-done((bf16[256,1024]{1,0:T(8,128)(2,1)S(1)}, bf16[256,1024]{1,0:T(8,128)(2,1)S(1)}, u32[]{:S(2)}, u32[]{:S(2)}) %collective-permute-start.24) | collective-permute-done | bytes 524320 | tf_op jit(solution)/shard_map/ppermute | solution.py:937
  476.8 31.1 %attention_backward.2 = bf16[16,192,256]{2,1,0:T(8,128)(2,1)S(1)} custom-call(s32[4]{0:T(128)S(1)} %bitcast.307, bf16[16,192,256]{2,1,0:T(8,128)(2,1)} %all-to-all-done.4.qkv_ref, bf16[16,64,256]{2,1,0:T(8,128)(2,1)S(1)} %copy-done.57, bf16[16,64,256]{2,1,0:T(8,128)(2,1)} %all-to-all-done.6.grad_ref, f32[16,1,256]{2,1,0:T(1,128)S(1)} %get-tuple-element.197.lse_ref), custom_call_target="tpu_custom_call" | custom-call | flops 1 | bytes 1 | tf_op jit(solution)/shard_map/attention_backward/pallas_call | solution.py:700
  517.8 36.2 %all-to-all-done.7 = bf16[16,192,256]{2,1,0:T(8,128)(2,1)} async-done(((bf16[16,192,256]{2,1,0:T(8,128)(2,1)}), bf16[16,192,256]{2,1,0:T(8,128)(2,1)}, u32[]{:S(2)}, u32[]{:S(2)}) %all-to-all-start.7) | async-done | bytes 1572896 | tf_op jit(solution)/shard_map/all_to_all | solution.py:494
  592.5 13.0 %collective-permute-done.28 = bf16[256,1024]{1,0:T(8,128)(2,1)S(1)} collective-permute-done((bf16[256,1024]{1,0:T(8,128)(2,1)S(1)}, bf16[256,1024]{1,0:T(8,128)(2,1)S(1)}, u32[]{:S(2)}, u32[]{:S(2)}) %collective-permute-start.28) | collective-permute-done | bytes 524320 | tf_op jit(solution)/shard_map/ppermute | solution.py:937
  645.0 30.8 %attention_backward.3 = bf16[16,192,256]{2,1,0:T(8,128)(2,1)S(1)} custom-call(s32[4]{0:T(128)S(1)} %bitcast.308, bf16[16,192,256]{2,1,0:T(8,128)(2,1)S(1)} %copy-done.9, bf16[16,64,256]{2,1,0:T(8,128)(2,1)} %get-tuple-element.155.out_ref, bf16[16,64,256]{2,1,0:T(8,128)(2,1)} %all-to-all-done.8.grad_ref, f32[16,1,256]{2,1,0:T(1,128)S(1)} %get-tuple-element.222.lse_ref), custom_call_target="tpu_custom_call" | custom-call | flops 1 | bytes 1 | tf_op jit(solution)/shard_map/attention_backward/pallas_call | solution.py:700
  677.0 14.8 %collective-permute-done.32 = bf16[3,264,1024]{2,1,0:T(8,128)(2,1)} collective-permute-done((bf16[3,264,1024]{2,1,0:T(8,128)(2,1)}, bf16[3,264,1024]{2,1,0:T(8,128)(2,1)}, u32[]{:S(2)}, u32[]{:S(2)}) %collective-permute-start.32) | collective-permute-done | bytes 1622048 | tf_op jit(solution)/shard_map/ppermute | solution.py:940
  699.6 53.6 %collective-permute-done.37 = bf16[4,32,1024]{2,1,0:T(8,128)(2,1)S(1)} collective-permute-done((bf16[4,32,1024]{2,1,0:T(8,128)(2,1)S(1)}, bf16[4,32,1024]{2,1,0:T(8,128)(2,1)S(1)}, u32[]{:S(2)}, u32[]{:S(2)}) %collective-permute-start.37) | collective-permute-done | bytes 262176 | tf_op jit(solution)/shard_map/ppermute | solution.py:940
  774.9 17.4 %collective-permute-done.39 = bf16[2,264,1024]{2,1,0:T(8,128)(2,1)S(1)} collective-permute-done((bf16[2,264,1024]{2,1,0:T(8,128)(2,1)S(1)}, bf16[2,264,1024]{2,1,0:T(8,128)(2,1)S(1)}, u32[]{:S(2)}, u32[]{:S(2)}) %collective-permute-start.39) | collective-permute-done | bytes 1081376 | tf_op jit(solution)/shard_map/ppermute | solution.py:943
  810.5 13.0 %collective-permute-done.40 = bf16[2,4,48,1024]{3,2,1,0:T(8,128)(2,1)} collective-permute-done((bf16[2,4,48,1024]{3,2,1,0:T(8,128)(2,1)}, bf16[2,4,48,1024]{3,2,1,0:T(8,128)(2,1)}, u32[]{:S(2)}, u32[]{:S(2)}) %collective-permute-start.40) | collective-permute-done | bytes 786464 | tf_op jit(solution)/shard_map/ppermute | solution.py:937
  835.2 14.2 %collective-permute-done.44 = bf16[264,1024]{1,0:T(8,128)(2,1)S(1)} collective-permute-done((bf16[264,1024]{1,0:T(8,128)(2,1)}, bf16[264,1024]{1,0:T(8,128)(2,1)S(1)}, u32[]{:S(2)}, u32[]{:S(2)}) %collective-permute-start.44) | collective-permute-done | bytes 540704 | tf_op jit(solution)/shard_map/ppermute | solution.py:946
  859.8 13.1 %collective-permute-done.47 = bf16[2,128,1024]{2,1,0:T(8,128)(2,1)S(1)} collective-permute-done((bf16[2,128,1024]{2,1,0:T(8,128)(2,1)S(1)}, bf16[2,128,1024]{2,1,0:T(8,128)(2,1)S(1)}, u32[]{:S(2)}, u32[]{:S(2)}) %collective-permute-start.47) | collective-permute-done | bytes 524320 | tf_op jit(solution)/shard_map/ppermute | solution.py:943
  873.2 14.1 %collective-permute-done.48 = bf16[128,1024]{1,0:T(8,128)(2,1)S(1)} collective-permute-done((bf16[128,1024]{1,0:T(8,128)(2,1)S(1)}, bf16[128,1024]{1,0:T(8,128)(2,1)S(1)}, u32[]{:S(2)}, u32[]{:S(2)}) %collective-permute-start.48) | collective-permute-done | bytes 262176 | tf_op jit(solution)/shard_map/ppermute | solution.py:946
  887.5 16.2 %all_to_all.65 = bf16[4,128,1024]{2,1,0:T(8,128)(2,1)} all-to-all(bf16[4,128,1024]{2,1,0:T(8,128)(2,1)S(1)} %broadcast_in_dim.27), channel_id=1, replica_groups=mesh['section'=2,'ctx'=4,'tp'=4] {'ctx'}, dimensions={0} | all-to-all | bytes 2097152 | tf_op jit(solution)/shard_map/all_to_all | solution.py:952
  (560 shorter events, 419.7 us)
Async XLA Ops:
  19.6 38.9 %all-to-all-start = ((bf16[4,128,1024]{2,1,0:T(8,128)(2,1)}), bf16[4,128,1024]{2,1,0:T(8,128)(2,1)S(1)}, u32[]{:S(2)}, u32[]{:S(2)}) async-start(bf16[4,128,1024]{2,1,0:T(8,128)(2,1)} %broadcast_in_dim.22), calls=%async_computation | async-start | bytes 2097152 | tf_op jit(solution)/shard_map/all_to_all | solution.py:952
  25.8 210.3 %all-gather.5.cloned.1.call-start = ((), (), s32[]{:S(2)}) async-start(), calls=%async_computation.15 | async-start | bytes 9191424 | tf_op jit(solution)/shard_map/all_gather | solution.py:958
  123.7 35.0 %all-to-all-start.1 = ((bf16[16,192,256]{2,1,0:T(8,128)(2,1)}), bf16[16,192,256]{2,1,0:T(8,128)(2,1)S(1)}, u32[]{:S(2)}, u32[]{:S(2)}) async-start(bf16[16,192,256]{2,1,0:T(8,128)(2,1)} %fusion.55), calls=%async_computation.1 | async-start | bytes 3145728 | tf_op jit(solution)/shard_map/all_to_all | solution.py:494
  160.9 44.6 %all-to-all-start.2 = ((bf16[4,128,1024]{2,1,0:T(8,128)(2,1)}), bf16[4,128,1024]{2,1,0:T(8,128)(2,1)}, u32[]{:S(2)}, u32[]{:S(2)}) async-start(bf16[4,128,1024]{2,1,0:T(8,128)(2,1)} %broadcast_in_dim.23), calls=%async_computation.2 | async-start | bytes 2097152 | tf_op jit(solution)/shard_map/all_to_all | solution.py:952
  165.1 224.1 %all-gather.7.cloned.1.call-start = ((), (), s32[]{:S(2)}) async-start(), calls=%async_computation.16 | async-start | bytes 9191424 | tf_op jit(solution)/shard_map/all_gather | solution.py:958
  165.2 44.1 %collective-permute-start.8 = (bf16[512,1024]{1,0:T(8,128)(2,1)S(1)}, bf16[512,1024]{1,0:T(8,128)(2,1)}, u32[]{:S(2)}, u32[]{:S(2)}) collective-permute-start(bf16[512,1024]{1,0:T(8,128)(2,1)S(1)} %bitcast.334), channel_id=1, source_target_pairs={{0,16},{16,0},{1,17},{17,1},{2,18},{18,2},{3,19},{19,3},{4,20},{20... | collective-permute-start | bytes 3145736 | tf_op jit(solution)/shard_map/ppermute | solution.py:949
  256.9 35.6 %collective-permute-start.13 = (bf16[2,4,64,1024]{3,2,1,0:T(8,128)(2,1)S(1)}, bf16[2,4,64,1024]{3,2,1,0:T(8,128)(2,1)S(1)}, u32[]{:S(2)}, u32[]{:S(2)}) collective-permute-start(bf16[2,4,64,1024]{3,2,1,0:T(8,128)(2,1)S(1)} %pad_maximum_fusion.20), channel_id=1, source_target_pairs={{0,4},{4,0},{8,12},{12,8},{1,5},{5,1},{9,13},{13,9},{2,6},{6,2},{1... | collective-permute-start | bytes 3145736 | tf_op jit(solution)/shard_map/ppermute | solution.py:937
  334.5 33.2 %collective-permute-start.18 = (bf16[256,1024]{1,0:T(8,128)(2,1)S(1)}, bf16[256,1024]{1,0:T(8,128)(2,1)S(1)}, u32[]{:S(2)}, u32[]{:S(2)}) collective-permute-start(bf16[256,1024]{1,0:T(8,128)(2,1)S(1)} %dynamic-slice_bitcast_fusion.17), channel_id=1, source_target_pairs={{0,2},{1,3},{4,6},{5,7},{8,10},{9,11},{12,14},{13,15},{18,16},{19,... | collective-permute-start | bytes 1572872 | tf_op jit(solution)/shard_map/ppermute | solution.py:916
  424.6 33.5 %collective-permute-start.23 = (bf16[8,264,1024]{2,1,0:T(8,128)(2,1)}, bf16[8,264,1024]{2,1,0:T(8,128)(2,1)}, u32[]{:S(2)}, u32[]{:S(2)}) collective-permute-start(bf16[8,264,1024]{2,1,0:T(8,128)(2,1)} %half_products.10), channel_id=1, source_target_pairs={{0,16},{16,0},{1,17},{17,1},{2,18},{18,2},{3,19},{19,3},{4,20},{20... | collective-permute-start | bytes 12976136 | tf_op jit(solution)/shard_map/ppermute | solution.py:949
  472.1 35.9 %collective-permute-start.25 = (bf16[256,1024]{1,0:T(8,128)(2,1)}, bf16[256,1024]{1,0:T(8,128)(2,1)S(1)}, u32[]{:S(2)}, u32[]{:S(2)}) collective-permute-start(bf16[256,1024]{1,0:T(8,128)(2,1)} %get-tuple-element.199), channel_id=1, source_target_pairs={{0,16},{1,17},{4,20},{5,21},{8,24},{9,25},{12,28},{13,29},{18,18},... | collective-permute-start | bytes 1572872 | tf_op jit(solution)/shard_map/ppermute | solution.py:928
  474.2 34.8 %collective-permute-start.26 = (bf16[256,1024]{1,0:T(8,128)(2,1)}, bf16[256,1024]{1,0:T(8,128)(2,1)}, u32[]{:S(2)}, u32[]{:S(2)}) collective-permute-start(bf16[256,1024]{1,0:T(8,128)(2,1)} %get-tuple-element.199), channel_id=1, source_target_pairs={{2,16},{3,17},{6,20},{7,21},{10,24},{11,25},{14,28},{15,29},{16,18... | collective-permute-start | bytes 1572872 | tf_op jit(solution)/shard_map/ppermute | solution.py:928
  509.1 45.0 %all-to-all-start.7 = ((bf16[16,192,256]{2,1,0:T(8,128)(2,1)}), bf16[16,192,256]{2,1,0:T(8,128)(2,1)}, u32[]{:S(2)}, u32[]{:S(2)}) async-start(bf16[16,192,256]{2,1,0:T(8,128)(2,1)} %copy-done.20), calls=%async_computation.7 | async-start | bytes 3145728 | tf_op jit(solution)/shard_map/all_to_all | solution.py:494
  517.1 278.5 %reduce-scatter.3.cloned.1.call-start = ((), (), s32[]{:S(2)}) async-start(), calls=%async_computation.17 | async-start | bytes 4866048 | tf_op jit(solution)/shard_map/reduce_scatter | solution.py:1172
  619.2 176.3 %reduce-scatter.5.cloned.1.call-start = ((), (), s32[]{:S(2)}) async-start(), calls=%async_computation.18 | async-start | bytes 4456448 | tf_op jit(solution)/shard_map/reduce_scatter | solution.py:1172
  636.0 55.7 %collective-permute-start.32 = (bf16[3,264,1024]{2,1,0:T(8,128)(2,1)}, bf16[3,264,1024]{2,1,0:T(8,128)(2,1)}, u32[]{:S(2)}, u32[]{:S(2)}) collective-permute-start(bf16[3,264,1024]{2,1,0:T(8,128)(2,1)} %get-tuple-element.224), channel_id=1, source_target_pairs={{0,8},{4,12},{8,0},{12,4},{1,9},{5,13},{9,1},{13,5},{2,10},{6,14},... | collective-permute-start | bytes 4866056 | tf_op jit(solution)/shard_map/ppermute | solution.py:940
  637.8 38.0 %collective-permute-start.34 = (bf16[256,1024]{1,0:T(8,128)(2,1)S(1)}, bf16[256,1024]{1,0:T(8,128)(2,1)}, u32[]{:S(2)}, u32[]{:S(2)}) collective-permute-start(bf16[256,1024]{1,0:T(8,128)(2,1)S(1)} %fusion.24.grad_ref.refs_8_), channel_id=1, source_target_pairs={{0,16},{1,17},{4,20},{5,21},{8,24},{9,25},{12,28},{13,29},{18,18},... | collective-permute-start | bytes 1572872 | tf_op jit(solution)/shard_map/ppermute | solution.py:928
  640.4 35.5 %collective-permute-start.35 = (bf16[256,1024]{1,0:T(8,128)(2,1)S(1)}, bf16[256,1024]{1,0:T(8,128)(2,1)}, u32[]{:S(2)}, u32[]{:S(2)}) collective-permute-start(bf16[256,1024]{1,0:T(8,128)(2,1)S(1)} %fusion.24.grad_ref.refs_8_), channel_id=1, source_target_pairs={{2,16},{3,17},{6,20},{7,21},{10,24},{11,25},{14,28},{15,29},{16,18... | collective-permute-start | bytes 1572872 | tf_op jit(solution)/shard_map/ppermute | solution.py:928
  642.0 33.8 %collective-permute-start.33 = (bf16[2,4,32,1024]{3,2,1,0:T(8,128)(2,1)}, bf16[2,4,32,1024]{3,2,1,0:T(8,128)(2,1)S(1)}, u32[]{:S(2)}, u32[]{:S(2)}) collective-permute-start(bf16[2,4,32,1024]{3,2,1,0:T(8,128)(2,1)} %get-tuple-element.228), channel_id=1, source_target_pairs={{0,4},{4,0},{8,12},{12,8},{1,5},{5,1},{9,13},{13,9},{2,6},{6,2},{1... | collective-permute-start | bytes 1572872 | tf_op jit(solution)/shard_map/ppermute | solution.py:937
  691.8 61.5 %all-to-all-start.9 = ((bf16[16,192,256]{2,1,0:T(8,128)(2,1)}), bf16[16,192,256]{2,1,0:T(8,128)(2,1)S(1)}, u32[]{:S(2)}, u32[]{:S(2)}) async-start(bf16[16,192,256]{2,1,0:T(8,128)(2,1)} %copy-done.19), calls=%async_computation.9 | async-start | bytes 3145728 | tf_op jit(solution)/shard_map/all_to_all | solution.py:494
  695.5 208.2 %all-gather.9.cloned.1.call-start = ((), (), s32[]{:S(2)}) async-start(), calls=%async_computation.19 | async-start | bytes 4014080 | tf_op jit(solution)/shard_map/all_gather | solution.py:1340
  695.5 57.7 %collective-permute-start.36 = (bf16[1,264,1024]{2,1,0:T(8,128)(2,1)}, bf16[1,264,1024]{2,1,0:T(8,128)(2,1)S(1)}, u32[]{:S(2)}, u32[]{:S(2)}) collective-permute-start(bf16[1,264,1024]{2,1,0:T(8,128)(2,1)} %get-tuple-element.234), channel_id=1, source_target_pairs={{0,8},{4,12},{8,0},{12,4},{1,9},{5,13},{9,1},{13,5},{2,10},{6,14},... | collective-permute-start | bytes 1622024 | tf_op jit(solution)/shard_map/ppermute | solution.py:940
  699.5 53.8 %collective-permute-start.37 = (bf16[4,32,1024]{2,1,0:T(8,128)(2,1)S(1)}, bf16[4,32,1024]{2,1,0:T(8,128)(2,1)S(1)}, u32[]{:S(2)}, u32[]{:S(2)}) collective-permute-start(bf16[4,32,1024]{2,1,0:T(8,128)(2,1)S(1)} %get-tuple-element.409), channel_id=1, source_target_pairs={{0,8},{4,12},{8,0},{12,4},{1,9},{5,13},{9,1},{13,5},{2,10},{6,14},... | collective-permute-start | bytes 786440 | tf_op jit(solution)/shard_map/ppermute | solution.py:940
  797.6 35.4 %collective-permute-start.45 = (bf16[256,1024]{1,0:T(8,128)(2,1)}, bf16[256,1024]{1,0:T(8,128)(2,1)}, u32[]{:S(2)}, u32[]{:S(2)}) collective-permute-start(bf16[256,1024]{1,0:T(8,128)(2,1)} %fusion.16), channel_id=1, source_target_pairs={{0,0},{1,1},{4,4},{5,5},{8,8},{9,9},{12,12},{13,13},{18,2},{19,3},... | collective-permute-start | bytes 1572872 | tf_op jit(solution)/shard_map/ppermute | solution.py:928
  806.9 42.5 %collective-permute-start.44 = (bf16[264,1024]{1,0:T(8,128)(2,1)}, bf16[264,1024]{1,0:T(8,128)(2,1)S(1)}, u32[]{:S(2)}, u32[]{:S(2)}) collective-permute-start(bf16[264,1024]{1,0:T(8,128)(2,1)} %get-tuple-element.382), channel_id=1, source_target_pairs={{0,2},{1,3},{2,0},{3,1},{4,6},{5,7},{6,4},{7,5},{8,10},{9,11},{10,... | collective-permute-start | bytes 1622024 | tf_op jit(solution)/shard_map/ppermute | solution.py:946
  (163 other events, 1805.7 us)
Sparse Core Ops, SparseCore 0:
  59.4 91.8 all-gather.4
  168.3 98.9 all-gather.6
  522.1 95.2 reduce-scatter.2
  643.7 118.6 reduce-scatter.4
  797.8 60.9 all-gather.8

commit v4 on v3

--- a/solution.py
+++ b/solution.py
@@ -529,24 +529,32 @@
     return combine(value.reshape(rows // 8, 8, width), axis=0)
 
 
-def attention_forward_kernel(ends_ref, qkv_ref, out_ref, lse_ref, keys_ref, values_ref):
+def block_place(block, parts, width):
+    entry = (block // (2 * parts)) * parts + block % parts
+    return entry, pl.ds(pl.multiple_of((block // parts % 2) * width, width), width)
+
+
+def attention_forward_kernel(parts, ends_ref, qkv_ref, out_ref, lse_ref, keys_ref, values_ref):
     program = pl.program_id(0)
-    blocks, _, block_width = qkv_ref.shape
+    blocks, block_width = 2 * qkv_ref.shape[0], qkv_ref.shape[2] // 2
     width = CHUNK * block_width
 
     @pl.when(program == 0)
     def _():
         def turn(j, carry):
-            keys_ref[j] = qkv_ref[j, HD : 2 * HD, :].T
-            values_ref[j, 0:HD, :] = qkv_ref[j, 2 * HD : 3 * HD, :]
+            entry, columns = block_place(j, parts, block_width)
+            keys_ref[j] = qkv_ref[entry, HD : 2 * HD, columns].T
+            values_ref[j, 0:HD, :] = qkv_ref[entry, 2 * HD : 3 * HD, columns]
             values_ref[j, HD : HD + ONES, :] = jnp.ones((ONES, block_width), jnp.bfloat16)
             return carry
 
         lax.fori_loop(0, blocks, turn, 0)
 
-    query = jnp.concatenate(
-        [qkv_ref[program * CHUNK + entry, 0:HD, :] for entry in range(CHUNK)], axis=1
-    )
+    query = []
+    for block in range(CHUNK):
+        entry, columns = block_place(program * CHUNK + block, parts, block_width)
+        query.append(qkv_ref[entry, 0:HD, columns])
+    query = jnp.concatenate(query, axis=1)
     first = program * width
     query_index = first + lax.broadcasted_iota(jnp.int32, (1, width), 1)
     start = document_bounds(ends_ref, query_index)
@@ -589,10 +597,10 @@
         lse_ref[entry] = lse[:, columns]
 
 
-def attention_forward(ends, qkv):
-    blocks, _, width = qkv.shape
+def attention_forward(ends, qkv, parts):
+    blocks, width = 2 * qkv.shape[0], qkv.shape[2] // 2
     return pl.pallas_call(
-        attention_forward_kernel,
+        functools.partial(attention_forward_kernel, parts),
         grid_spec=pltpu.PrefetchScalarGridSpec(
             num_scalar_prefetch=1,
             grid=(blocks // CHUNK,),
@@ -617,11 +625,11 @@
 
 
 def attention_backward_kernel(
-    ends_ref, qkv_ref, out_ref, grad_ref, lse_ref, result_ref,
+    parts, ends_ref, qkv_ref, out_ref, grad_ref, lse_ref, result_ref,
     query_grad_ref, delta_ref, queries_ref, grads_ref, lses_ref,
 ):
     program = pl.program_id(0)
-    blocks, _, block_width = qkv_ref.shape
+    blocks, block_width = 2 * qkv_ref.shape[0], qkv_ref.shape[2] // 2
     width = CHUNK * block_width
 
     @pl.when(program == 0)
@@ -631,7 +639,8 @@
                 block = i * CHUNK + entry
                 columns = slice(entry * block_width, (entry + 1) * block_width)
                 grad = grad_ref[block]
-                queries_ref[i, :, columns] = qkv_ref[block, 0:HD, :]
+                place, tokens = block_place(block, parts, block_width)
+                queries_ref[i, :, columns] = qkv_ref[place, 0:HD, tokens]
                 grads_ref[i, :, columns] = grad
                 lses_ref[i, :, columns] = lse_ref[block]
                 delta_ref[i, :, columns] = jnp.sum(
@@ -644,10 +653,13 @@
 
         lax.fori_loop(0, blocks // CHUNK, turn, 0)
 
+    own_places = [
+        block_place(program * CHUNK + block, parts, block_width) for block in range(CHUNK)
+    ]
+
     def joined(low_row, high_row):
         return jnp.concatenate(
-            [qkv_ref[program * CHUNK + entry, low_row:high_row, :] for entry in range(CHUNK)],
-            axis=1,
+            [qkv_ref[place, low_row:high_row, tokens] for place, tokens in own_places], axis=1
         )
 
     first = program * width
@@ -683,27 +695,27 @@
     key_grad, value_grad = lax.fori_loop(middle, stop, functools.partial(step, masked=True), carry)
     query_grad = query_grad_ref[program] * HD ** (-0.5)
     key_grad = key_grad * LOG_2
-    for entry in range(CHUNK):
-        columns = slice(entry * block_width, (entry + 1) * block_width)
-        result_ref[entry, 0:HD] = query_grad[:, columns].astype(jnp.bfloat16)
-        result_ref[entry, HD : 2 * HD] = key_grad[:, columns].astype(jnp.bfloat16)
-        result_ref[entry, 2 * HD : 3 * HD] = value_grad[:, columns].astype(jnp.bfloat16)
-
-
-def attention_backward(ends, qkv, out, grad, lse):
-    blocks, _, block_width = qkv.shape
+    for block, (place, tokens) in enumerate(own_places):
+        columns = slice(block * block_width, (block + 1) * block_width)
+        result_ref[place, 0:HD, tokens] = query_grad[:, columns].astype(jnp.bfloat16)
+        result_ref[place, HD : 2 * HD, tokens] = key_grad[:, columns].astype(jnp.bfloat16)
+        result_ref[place, 2 * HD : 3 * HD, tokens] = value_grad[:, columns].astype(jnp.bfloat16)
+
+
+def attention_backward(ends, qkv, out, grad, lse, parts):
+    blocks, block_width = 2 * qkv.shape[0], qkv.shape[2] // 2
     chunks, width = blocks // CHUNK, CHUNK * block_width
 
     def whole(value):
         return pl.BlockSpec(value.shape, lambda i, ends_ref: (0, 0, 0))
 
     return pl.pallas_call(
-        attention_backward_kernel,
+        functools.partial(attention_backward_kernel, parts),
         grid_spec=pltpu.PrefetchScalarGridSpec(
             num_scalar_prefetch=1,
             grid=(chunks,),
             in_specs=[whole(qkv), whole(out), whole(grad), whole(lse)],
-            out_specs=pl.BlockSpec((CHUNK, 3 * HD, block_width), lambda i, ends_ref: (i, 0, 0)),
+            out_specs=whole(qkv),
             scratch_shapes=[
                 pltpu.VMEM((chunks, HD, width), jnp.float32),
                 pltpu.VMEM((chunks, 1, width), jnp.float32),
@@ -891,6 +903,7 @@
     model_width = inputs.shape[2]
     rows = inputs.shape[1]
     heads = wqkv.shape[2] * parts
+    side_heads = heads // 2
     unit_rows = wd.shape[1] // contexts // 2
     head_rows = 3 * HD // 2
     out_rows = HD // 2
@@ -903,6 +916,11 @@
     everyone = [[number(*place) for place in places]]
     token_of = lambda s, c, t: c * parts + t % half_parts + half_parts * s
     batch_groups = device_groups(mesh_sizes, lambda s, c, t: t // half_parts, token_of)
+    head_groups = device_groups(
+        mesh_sizes,
+        lambda s, c, t: (c % 2, t // half_parts),
+        lambda s, c, t: (c // 2, t % half_parts + half_parts * s),
+    )
     side_groups = device_groups(mesh_sizes, lambda s, c, t: c % 2, lambda s, c, t: (s, c, t))
     crossing = [
         (number(s, c, t), number(s, c, (t + half_parts) % parts))
@@ -964,26 +982,25 @@
         return lax.dynamic_index_in_dim(value, which, 0, keepdims=False)
 
     def spread_line(piece):
-        return all_to_all(copies(piece, parts), "tp")
-
-    def spread_sides(line):
-        middle = line.shape[1] // 2
-        line_a, line_b = line[:, :middle], line[:, middle:]
-        return (line_a, swap_far(line_a)), (line_b, swap_side(line_b))
-
-    def spread_corners(line_pairs):
-        pair_a = jnp.stack(ordered(row_side, *line_pairs[0]))
-        pair_b = jnp.stack(ordered(column_side, *line_pairs[1]))
-        return (pair_a, swap_side(pair_a)), (pair_b, swap_far(pair_b))
-
-    def spread_cores(plane_pairs):
-        plane_a = jnp.stack(ordered(column_side, *plane_pairs[0]), axis=1)
-        plane_b = jnp.stack(ordered(row_side, *plane_pairs[1]), axis=0)
-        rest = head_rows - plane_a.shape[3]
-        own_heads = jnp.concatenate([plane_a, plane_b[:, :, :, :rest]], axis=3)
-        own_heads = own_heads.reshape(-1, model_width)
-        own_outs = plane_b[:, :, :, rest:].reshape(-1, model_width)
-        return (own_heads, swap_section(own_heads)), (own_outs, swap_section(own_outs))
+        pair = jnp.stack(ordered(batch, piece, swap_half(piece)))
+        line = jnp.stack(ordered(tp % 2, pair, swap_near(pair)), axis=1)
+        return line.reshape(parts, *piece.shape)
+
+    def spread_far(line):
+        return line, swap_far(line)
+
+    def spread_heads(pair):
+        pair = jnp.stack(ordered(row_side, *pair))
+        own_heads = pair[:, :, :head_rows].reshape(-1, model_width)
+        own_outs = pair[:, :, head_rows:]
+        return (own_heads, swap_section(own_heads)), (own_outs, swap_side(own_outs))
+
+    def spread_outs(pair):
+        own_outs = jnp.stack(ordered(column_side, *pair), axis=1).reshape(-1, model_width)
+        return own_outs, swap_section(own_outs)
+
+    def join_outs(pair):
+        return jnp.concatenate(ordered(section, *pair), axis=0)
 
     def own_halves(value, axis, size):
         part = lax.dynamic_slice_in_dim(value, ctx * size, size, axis)
@@ -1012,17 +1029,20 @@
     rows_in = to_batch(inputs)
     line, rows_in = together(spread_line(pieces[0][:attention_rows]), rows_in)
     w_ffn = [feed_forward_weights(after(piece, line)) for piece in pieces]
-    line_pairs = together(*spread_sides(line))
     w_heads, w_outs = [None, None], [None, None]
-    w_heads[0], out_halves = spread_cores(spread_corners(line_pairs))
-    w_outs[0] = jnp.concatenate(ordered(section, *out_halves), axis=0)
+    first_pair = spread_far(line)
 
     gains = wide(jnp.concatenate([gain1, gain2], axis=0))
     gain_sets = ordered(section, gains, swap_section(gains))
 
     seq_lengths = lax.dynamic_index_in_dim(lengths, batch, 0, keepdims=False)
     ends = jnp.cumsum(seq_lengths).astype(jnp.int32)
-    token_index = token_of(section, ctx, tp) * rows + jnp.arange(rows, dtype=jnp.int32)
+    token_index = jnp.concatenate(
+        [
+            token_of(section, 2 * row_side + side, tp) * rows + jnp.arange(rows, dtype=jnp.int32)
+            for side in range(2)
+        ]
+    )
     before = (ends[None, :] <= token_index[:, None]).astype(jnp.int32)
     position = token_index - jnp.sum(before * seq_lengths[None, :], axis=1)
     frequency = jnp.exp(
@@ -1042,13 +1062,14 @@
     def nothing(value):
         return value
 
-    def layer_forward(whole_rows, first_values, layer, in_first, in_second, in_third, in_fourth):
+    def layer_forward(whole_rows, first_values, layer, in_zero, in_first, in_second, in_third, in_fourth):
         gain_first, gain_second = gain_sets[layer][0], gain_sets[layer][1]
         scale_first = lax.rsqrt(jnp.mean(whole_rows * whole_rows, axis=-1, keepdims=True) + EPSILON)
         normed = low(whole_rows * scale_first * gain_first)
-        halves = [dot(weight, normed, 1, 1) for weight in w_heads[layer]]
-        halves = ordered(section, *halves)
-        upper, lower = [half.reshape(heads, head_rows, rows) for half in halves]
+        far_normed = in_zero(swap_side(normed))
+        side_rows = jnp.concatenate(ordered(column_side, normed, far_normed), axis=0)
+        halves = ordered(section, *[dot(weight, side_rows, 1, 1) for weight in w_heads[layer]])
+        upper, lower = [half.reshape(side_heads, head_rows, 2 * rows) for half in halves]
         query = rope_pair(upper[:, :half_width], upper[:, half_width:HD], cosine, sine_part)
         key = rope_pair(upper[:, HD:], lower[:, :half_width], cosine, sine_part)
         value = lower[:, half_width:]
@@ -1057,10 +1078,10 @@
         mixed = low(value)
         shrunk = [low(half * (HD ** (-0.5) / LOG_2)) for half in query]
         qkv = exchange(
-            jnp.concatenate([*shrunk, low(key[0]), low(key[1]), mixed], axis=1), batch_groups
+            jnp.concatenate([*shrunk, low(key[0]), low(key[1]), mixed], axis=1), head_groups
         )
         qkv = in_first(qkv)
-        out, lse = attention_forward(ends, qkv)
+        out, lse = attention_forward(ends, qkv, parts)
         out = in_second(out)
         attended = head_halves(exchange(out, batch_groups))
         hidden = whole_rows + dot(attended.reshape(-1, rows), w_outs[layer], 0, 0)
@@ -1070,10 +1091,14 @@
         near = feed_forward(normed_second, *w_ffn[layer], tile)
         far_rows = in_third(after(far_rows, near[3]))
         far = feed_forward(far_rows, *w_ffn[layer], tile)
-        far_down = in_fourth(swap_side(low(far[3])))
-        layer_out = low(hidden + (near[3] + wide(far_down)))
+        sent_down = low(far[3])
+
+        def layer_out(*others):
+            far_down = in_fourth(swap_side(after(sent_down, *others)))
+            return low(hidden + (near[3] + wide(far_down)))
+
         saved = (
-            whole_rows, scale_first, normed, qkv, out, lse, attended, hidden, scale_second,
+            whole_rows, scale_first, side_rows, qkv, out, lse, attended, hidden, scale_second,
             (normed_second, far_rows), near[:3], far[:3],
         )
         return layer_out, mixed, saved
@@ -1102,15 +1127,18 @@
     def add(pair):
         return low(wide(pair[0]) + wide(pair[1]))
 
+    def near_parts(value):
+        return parted(value.reshape(2, half_parts, *value.shape[1:]), tp % 2, 1)
+
     def near_sum(value):
-        return halve(value.reshape(2, half_parts, *value.shape[1:]), tp % 2, swap_near, 1)
+        return moved_pair(near_parts(value), swap_near)
 
     def far_sum(pair):
         return halve(add(pair), batch, swap_half, 0)
 
     def layer_backward(grad_rows, extra_values, saved, layer, in_first, in_second, in_third, in_fourth, in_fifth):
         (
-            whole_rows, scale_first, normed, qkv, out, lse, attended, hidden, scale_second,
+            whole_rows, scale_first, _, qkv, out, lse, attended, hidden, scale_second,
             ffn_rows, near, far,
         ) = saved
         gain_first, gain_second = gain_sets[layer][0], gain_sets[layer][1]
@@ -1140,9 +1168,9 @@
         rest = products(section, addend=moved)
         out_pair = (attended.reshape(-1, rows), grad_branch)
         grad_heads, rest = in_third(grad_heads, rest, out_pair)
-        grad_qkv = attention_backward(ends, qkv, out, grad_heads, lse)
+        grad_qkv = attention_backward(ends, qkv, out, grad_heads, lse, parts)
         grad_qkv = in_fourth(grad_qkv)
-        grad_qkv = in_fifth(exchange(grad_qkv, batch_groups))
+        grad_qkv = in_fifth(exchange(grad_qkv, head_groups))
         grad_qkv = wide(grad_qkv)
         quarter = lambda entry: grad_qkv[:, entry * half_width : (entry + 1) * half_width]
         grad_query = rope_pair(quarter(0), quarter(1), cosine, -sine_part)
@@ -1156,16 +1184,18 @@
             grad_value = grad_value + wide(extra_values)
         upper = low(jnp.concatenate([*grad_query, grad_key[0]], axis=1))
         lower = low(jnp.concatenate([grad_key[1], grad_value], axis=1))
-        grad_halves = jnp.stack([upper, lower]).reshape(2, -1, rows)
+        grad_halves = jnp.stack([upper, lower]).reshape(2, -1, 2 * rows)
         return grad_halves, send_values, grad_hidden, out_pair, grad_gain2
 
-    def input_grads_of(grad_halves, grad_hidden, saved, layer):
+    def input_grads_of(grad_halves, grad_hidden, saved, layer, beside):
         whole_rows, scale_first = saved[:2]
         places_of = (section, 1 - section)
-        grad_normed = sum(
+        grad_side = sum(
             dot(by_core(grad_halves, place), weight, 0, 0)
             for place, weight in zip(places_of, w_heads[layer])
-        )
+        ).reshape(2, rows, model_width)
+        grad_far = swap_side(low(by_core(grad_side, 1 - column_side)))
+        grad_normed = by_core(grad_side, column_side) + wide(beside(grad_far))
         return norm_back(whole_rows, scale_first, gain_sets[layer][0], grad_normed, grad_hidden)
 
     def piece_sum(value, groups):
@@ -1176,126 +1206,145 @@
     line_groups = device_groups(
         mesh_sizes, lambda s, c, t: (s, c % 2), lambda s, c, t: (c, t)
     )
-    core_groups = device_groups(mesh_sizes, lambda s, c, t: s, lambda s, c, t: (c, t))
     plane_shape = (2, 2, parts)
     pending = {}
+
+    def weights_zero(value):
+        value, pair = together(value, first_pair)
+        w_heads[0], pending["outs"] = spread_heads(pair)
+        return value
 
     def weights_line(value):
         value, piece = together(value, pieces[1][:attention_rows])
         pending["weights"] = spread_line(piece)
         return value
 
-    def weights_sides(value):
+    def weights_outs_first(value):
+        value, pending["outs"], w_ffn[0] = together(value, pending["outs"], w_ffn[0])
+        w_outs[0] = join_outs(spread_outs(pending["outs"]))
+        pending["grad_in"] = to_batch(after(cotangent, value))
+        return value
+
+    def weights_far(value):
         value, line = together(value, pending["weights"])
-        pending["weights"] = spread_sides(line)
+        pending["weights"] = spread_far(line)
         return value
 
-    def weights_corners(value):
-        value, pairs = together(value, pending["weights"])
-        pending["weights"] = spread_corners(pairs)
+    def weights_heads(value):
+        value, pairs, pending["grad_in"] = together(value, pending["weights"], pending["grad_in"])
+        w_heads[1], pending["outs"] = spread_heads(pairs)
         return value
 
-    def weights_cores(value):
-        value, pairs = together(value, pending["weights"])
-        w_heads[1], pending["outs"] = spread_cores(pairs)
+    first_result, first_values, first_saved = layer_forward(
+        wide(rows_in), None, 0,
+        weights_zero, weights_line, weights_outs_first, weights_far, weights_heads,
+    )
+
+    first_out = first_result()
+
+    def start_outs(value):
+        value, outs, w_ffn[1] = together(value, pending["outs"], w_ffn[1])
+        pending["outs"] = spread_outs(outs)
         return value
 
-    first_out, first_values, first_saved = layer_forward(
-        wide(rows_in), None, 0, weights_line, weights_sides, weights_corners, weights_cores
-    )
-
-    def start_homes(value):
-        w_outs[1] = jnp.concatenate(ordered(section, *pending["outs"]), axis=0)
-        value, home = together(value, first_out)
-        pending["first_home"] = to_home(home, 0)
-        pending["grad_in"] = to_batch(after(cotangent, home))
+    def end_outs(value):
+        value, outs = together(value, pending["outs"])
+        w_outs[1] = join_outs(outs)
+        pending["first_home"] = to_home(after(first_out, value), 0)
         return value
 
-    def end_homes(value):
-        value, pending["first_home"], pending["grad_in"], w_outs[1] = together(
-            value, pending["first_home"], pending["grad_in"], w_outs[1]
-        )
-        return value
-
-    second_out, _, second_saved = layer_forward(
-        wide(first_out), first_values, 1, start_homes, end_homes, nothing, nothing
-    )
-    first_home, grad_in = pending["first_home"], pending["grad_in"]
+    second_result, _, second_saved = layer_forward(
+        wide(first_out), first_values, 1, nothing, start_outs, end_outs, nothing, nothing
+    )
+    grad_in = pending["grad_in"]
+
+    def out_sides(out_pair):
+        products = functools.partial(half_products, groups=((out_pair,),), pieces=heads, per_step=8)
+        out_sum = products(section, addend=swap_section(products(1 - section)))
+        return parted(out_sum.reshape(*plane_shape, out_rows, model_width), column_side, 1)
 
     def second_third(value, rest, out_pair):
         value, rest = together(value, rest)
         rest = rest.reshape(-1, model_width)
         pending["second_rest"] = piece_sum(rest, line_groups)
-        pending["second_home"] = to_home(after(second_out, value), 1)
+        pending["second_out_rows"] = second_result(value)
+        pending["out"] = out_sides(out_pair)
+        value = after(value, pending["out"])
+        pending["out"] = moved_pair(pending["out"], swap_side)
         return value, rest
 
     def second_fourth(value):
-        value, pending["second_home"] = together(value, pending["second_home"])
+        value, pending["first_home"], second_out, out_sum = together(
+            value, pending["first_home"], pending["second_out_rows"], pending["out"]
+        )
+        pending["second_home"] = to_home(second_out, 1)
+        pending["second_out"] = add(out_sum).reshape(2 * parts, out_rows, model_width)
         return value
 
-    grad_halves, send_values, grad_hidden, out_pair, second_gain2 = layer_backward(
+    grad_halves, send_values, grad_hidden, _, second_gain2 = layer_backward(
         grad_in, None, second_saved, 1, nothing, nothing, second_third, second_fourth, nothing
     )
-    second_gain1, second_grad = input_grads_of(grad_halves, grad_hidden, second_saved, 1)
-    second_grad = low(second_grad)
     head_products = functools.partial(
         half_products,
-        groups=(((grad_halves.reshape(-1, rows), second_saved[2]),), (out_pair,)),
-        pieces=heads,
+        groups=(((grad_halves.reshape(-1, 2 * rows), second_saved[2]),),),
+        pieces=side_heads,
         per_step=4,
     )
 
-    def first_first(value):
+    def head_start(value):
         value, sent = together(value, head_products(1 - section))
         pending["moved"] = swap_section(sent)
         return value
 
-    def crossed(value):
-        middle = value.shape[3] // 2
-        return (
-            parted(value[:, :, :, :middle], column_side, 1),
-            parted(value[:, :, :, middle:], row_side, 0),
-        )
+    second_gain1, second_grad = input_grads_of(
+        grad_halves, grad_hidden, second_saved, 1, head_start
+    )
+    second_grad = low(second_grad)
+
+    def first_first(value):
+        head = head_products(section, addend=pending["moved"])
+        value, pending["head"] = together(value, head)
+        return value
 
     def first_second(value):
-        head = head_products(section, addend=pending["moved"])
+        head = jnp.concatenate([pending["head"], pending["second_out"]], axis=1)
+        head = parted(head.reshape(2, parts, -1, model_width), row_side, 0)
         value, head = together(value, head)
-        pending["head"] = piece_sum(head.reshape(-1, model_width), core_groups)
+        pending["head"] = moved_pair(head, swap_far)
         pending["second_grad_home"] = to_home(after(second_grad, value), 1)
         return value
 
     def first_third(value, rest, out_pair):
-        out_products = functools.partial(
-            half_products, groups=((out_pair,),), pieces=heads, per_step=8
-        )
-        out_sum = out_products(section, addend=swap_section(out_products(1 - section)))
+        out_sum = out_sides(out_pair)
         rest = rest.reshape(2, parts, -1, model_width)
-        rest_a = parted(rest[:, :-1], row_side, 0)
-        rest_b = parted(rest[:, -1:], row_side, 0)
-        out_sum = parted(out_sum.reshape(*plane_shape, -1, model_width), column_side, 1)
-        value, rest_a, rest_b, out_sum = together(value, rest_a, rest_b, out_sum)
+        rest_a = parted(rest[:, :, : 2 * unit_rows], row_side, 0)
+        rest_b = parted(rest[:, :, 2 * unit_rows :], row_side, 0)
+        value, rest_a, rest_b, out_sum, pending["second_rest"], pending["second_home"] = together(
+            value, rest_a, rest_b, out_sum, pending["second_rest"], pending["second_home"]
+        )
         pending["rest_a"] = moved_pair(rest_a, swap_far)
         pending["rest_b"] = rest_b
         pending["out"] = moved_pair(out_sum, swap_side)
         return value, rest
 
     def first_fourth(value):
-        value, rest_a, rest_b, out_sum, pending["second_grad_home"] = together(
-            value, pending["rest_a"], pending["rest_b"], pending["out"],
+        value, rest_a, rest_b, out_sum, head, pending["second_grad_home"] = together(
+            value, pending["rest_a"], pending["rest_b"], pending["out"], pending["head"],
             pending["second_grad_home"],
         )
-        pending["rest_a"] = rest_a
         pending["rest_b"] = moved_pair(rest_b, swap_far)
+        pending["rest_a"] = add(rest_a)
         pending["out"] = halve(add(out_sum), row_side, swap_far, 0)
+        pending["head"] = near_sum(add(head))
         return value
 
     def first_fifth(value):
-        value, rest_a, rest_b, out_sum = together(
-            value, pending["rest_a"], pending["rest_b"], pending["out"]
+        value, rest_a, rest_b, out_sum, head = together(
+            value, pending["rest_a"], pending["rest_b"], pending["out"], pending["head"]
         )
         pending["out"] = add(out_sum)
-        rest = jnp.concatenate([add(rest_a), add(rest_b)], axis=0)
-        pending["rest"] = near_sum(rest)
+        pending["head2"] = far_sum(head)
+        pending["rest"] = near_sum(jnp.concatenate([rest_a, add(rest_b)], axis=1))
         return value
 
     first_halves, _, first_hidden, _, first_gain2 = layer_backward(
@@ -1304,47 +1353,49 @@
     )
     head_products = functools.partial(
         half_products,
-        groups=(((first_halves.reshape(-1, rows), first_saved[2]),),),
-        pieces=heads,
+        groups=(((first_halves.reshape(-1, 2 * rows), first_saved[2]),),),
+        pieces=side_heads,
         per_step=4,
     )
     sent = head_products(1 - section)
     moved = swap_section(sent)
+    def head_end(value):
+        head = head_products(section, addend=moved).reshape(2, parts, head_rows, model_width)
+        value, head = together(value, parted(head, row_side, 0))
+        pending["head"] = moved_pair(head, swap_far)
+        return value
+
     first_gain1, first_grad = input_grads_of(
-        after(first_halves, sent), first_hidden, first_saved, 0
-    )
-    head = head_products(section, addend=moved).reshape(*plane_shape, head_rows, model_width)
-    head, first_grad, rest = together(head, low(first_grad), pending["rest"])
-    head_a, head_b = crossed(head)
+        after(first_halves, sent), first_hidden, first_saved, 0, head_end
+    )
+    def summed(value, swap):
+        return value + swap(value)
+
     gain_rows = jnp.stack([first_gain1, first_gain2, second_gain1, second_gain2])
-    first_grad, gain_rows, head_a, head_b, rest = together(
-        first_grad, gain_rows, head_a, head_b, rest
-    )
-    head_a = moved_pair(head_a, swap_side)
-    head_b = moved_pair(head_b, swap_far)
+    gain_rows = summed(gain_rows, swap_section)
+    head, rest, gain_rows, second_head, first_grad = together(
+        pending["head"], pending["rest"], gain_rows, pending["head2"], low(first_grad)
+    )
+    head = near_sum(jnp.concatenate([add(head), pending["out"]], axis=1))
     rest = far_sum(rest)
+    second = jnp.concatenate([pending["second_rest"], add(second_head)], axis=0)
+    second = lax.all_gather(second, "ctx", axis=0, tiled=False)
     first_grad_home = to_home(first_grad, 0)
-    head_a, head_b = together(add(head_a), add(head_b))
-    head_a = parted(head_a, row_side, 0)
-    head_b = parted(head_b, column_side, 0)
-    gain_rows, head_a, head_b = together(gain_rows, head_a, head_b)
-    head_a = moved_pair(head_a, swap_far)
-    head_b = moved_pair(head_b, swap_side)
-    gain_sums = all_to_all(copies(gain_rows, len(places)), ALL_AXES)
-    head_a, head_b, rest, first_grad_home = together(head_a, head_b, rest, first_grad_home)
-    head = near_sum(jnp.concatenate([add(head_a), add(head_b), pending["out"]], axis=1))
+    gain_rows = summed(gain_rows, swap_side)
+    head, gain_rows = together(head, gain_rows)
+    head = far_sum(head)
+    gain_rows = summed(gain_rows, swap_far)
+    rest, first_grad_home, gain_rows = together(rest, first_grad_home, gain_rows)
     rest = all_to_all(copies(add(rest), contexts), "ctx")
-    head, gain_sums = together(head, gain_sums)
-    head = together(*far_sum(head))
-    first_head = all_to_all(copies(add(head), contexts), "ctx")
-    second = lax.all_gather(
-        jnp.concatenate([pending["second_rest"], pending["head"]], axis=0), "ctx", axis=0, tiled=False
-    )
-    rest, first_head, second = together(rest, first_head, second)
-    first_grads = jnp.concatenate([rest, first_head], axis=1)
-    second_grads = second
-    second_home, second_grad_home = pending["second_home"], pending["second_grad_home"]
-    gain_total = jnp.sum(gain_sums.reshape(len(places), 4, model_width), axis=0)
+    gain_rows = summed(gain_rows, swap_near)
+    head, gain_rows = together(head, gain_rows)
+    head = all_to_all(copies(add(head), contexts), "ctx")
+    gain_total = summed(gain_rows, swap_half)
+    rest, second = together(rest, second)
+    first_grads = (rest, head)
+    second_grads = (second[:, : 3 * unit_rows], second[:, 3 * unit_rows :])
+    first_home, second_home = pending["first_home"], pending["second_home"]
+    second_grad_home = pending["second_grad_home"]
     gain_total = jnp.where(leading, gain_total[:2], gain_total[2:])
 
     def finish(first, second):
@@ -1356,12 +1407,14 @@
         both = jnp.stack([half[:, first : first + count] for half in halves], axis=1)
         return wide(both).reshape(-1, model_width)
 
-    grads = finish(first_grads, second_grads)
+    rest_grads = finish(first_grads[0], second_grads[0])
     grad_wgate, grad_wup, grad_wd = [
-        joined(grads, entry * unit_rows, unit_rows) for entry in range(3)
+        joined(rest_grads, entry * unit_rows, unit_rows) for entry in range(3)
     ]
-    grad_wqkv = joined(grads, 3 * unit_rows, head_rows).reshape(contexts, 3, HD, model_width)
-    grad_wo = joined(grads, 3 * unit_rows + head_rows, out_rows)
+    head, grad_wgate, grad_wup, grad_wd = together(first_grads[1], grad_wgate, grad_wup, grad_wd)
+    head_grads = finish(head, second_grads[1])
+    grad_wqkv = joined(head_grads, 0, head_rows).reshape(contexts, 3, HD, model_width)
+    grad_wo = joined(head_grads, head_rows, out_rows)
     return (
         at_home(first_home, second_home),
         wide(at_home(first_grad_home, second_grad_home)),

time: 946 us -> 910 us (0.962)
  waiting for transfers between devices: 415 us -> 355 us
  other arithmetic: 72.7 us -> 87 us
  starting transfers between devices: 116 us -> 129 us
  Pallas kernels: 192 us -> 180 us
    ppermute x9 -> x8, waiting for transfers between devices: 111 us -> 54.9 us  [swap_far(): return lax.ppermute(value, 'ctx', [(c, c ^ 2) for c in range(contexts)])]
    all_to_all x8, waiting for transfers between devices: 110 us -> 58.1 us  [exchange(): lax.all_to_all(value, ALL_AXES, split_axis=0, concat_axis=0, tiled=True,...]
    ppermute x2 -> x6, waiting for transfers between devices: 30.5 us -> 64.2 us  [swap_near(): return lax.ppermute(value, 'tp', [(t, t ^ 1) for t in range(parts)])]
    ppermute x2 -> x6, waiting for transfers between devices: 28.3 us -> 58.6 us  [swap_half(): lax.ppermute(value, 'tp', [(t, (t + half_parts) % parts) for t in range(p...]
    all_to_all x4 -> x1, waiting for transfers between devices: 27.7 us -> 4.35 us  [all_to_all(): return lax.all_to_all(value, axis, split_axis=0, concat_axis=0, tiled=True)]
    ppermute x2, waiting for transfers between devices: 17.3 us -> 0.53 us  [to_batch(): moved = lax.ppermute(other, ALL_AXES, crossing)]
    ppermute x15 -> x17, waiting for transfers between devices: 79.3 us -> 94.7 us  [swap_side(): return lax.ppermute(value, 'ctx', [(c, c ^ 1) for c in range(contexts)])]
    all_to_all x4 -> x1, starting transfers between devices: 17.9 us -> 4.51 us  [all_to_all(): return lax.all_to_all(value, axis, split_axis=0, concat_axis=0, tiled=True)]
  transfers between devices with their start and end apart: 67 -> 75, of which waited for: 31 -> 35; matrix products, arithmetic and copies ran while one was open for 13% -> 14% of each run, Pallas kernels for 18% -> 18%
where the time goes in v4:
time: 910 us; the launch traced here: 898 us
  waiting for transfers between devices  355 us (39%)
  Pallas kernels  180 us (20%)
  starting transfers between devices  129 us (14%)
  local copies, waits for them, and re-layouts  87.5 us (10%)
  other arithmetic  87 us (10%)
  blocking collectives  23.4 us (3%)
  matrix products  19.3 us (2%)
  between operations  16.7 us (2%)
    ppermute x17, waiting for transfers between devices, swap_side(): return lax.ppermute(value, 'ctx', [(c, c ^ 1) for c in range(contexts)])  94.7 us
    ppermute x6, waiting for transfers between devices, swap_near(): return lax.ppermute(value, 'tp', [(t, t ^ 1) for t in range(parts)])  64.2 us
    pallas_call x2, Pallas kernels, attention_backward(): pl.pallas_call(functools.partial(attention_backward_kernel, parts), grid_...  62.2 us
    ppermute x6, waiting for transfers between devices, swap_half(): lax.ppermute(value, 'tp', [(t, (t + half_parts) % parts) for t in range(p...  58.6 us
    all_to_all x8, waiting for transfers between devices, exchange(): lax.all_to_all(value, ALL_AXES, split_axis=0, concat_axis=0, tiled=True,...  58.1 us
    ppermute x8, waiting for transfers between devices, swap_far(): return lax.ppermute(value, 'ctx', [(c, c ^ 2) for c in range(contexts)])  54.9 us
    pallas_call x2, Pallas kernels, attention_forward(): pl.pallas_call(functools.partial(attention_forward_kernel, parts), grid_s...  44.5 us
    unnamed x325, local copies, waits for them, and re-layouts  40.5 us
  transfers between devices with their start and end apart: 75, of which 35 were waited for; matrix products, arithmetic and copies ran while one was open for 14% of the time, Pallas kernels for 18%

profile of v4, /device:TPU:0, one launch (start us, length us, event | category | flops | bytes accessed | tf_op | source)
XLA Modules:
  0.0 898.2 jit_solution(9869403378192437756)
XLA Ops:
  28.3 14.5 %collective-permute-done.1 = bf16[128,1024]{1,0:T(8,128)(2,1)} collective-permute-done((bf16[128,1024]{1,0:T(8,128)(2,1)S(1)}, bf16[128,1024]{1,0:T(8,128)(2,1)}, u32[]{:S(2)}, u32[]{:S(2)}) %collective-permute-start.1) | collective-permute-done | bytes 262176 | tf_op jit(solution)/shard_map/ppermute | solution.py:964
  44.8 14.3 %collective-permute-done.2 = bf16[2,128,1024]{2,1,0:T(8,128)(2,1)} collective-permute-done((bf16[2,128,1024]{2,1,0:T(8,128)(2,1)}, bf16[2,128,1024]{2,1,0:T(8,128)(2,1)}, u32[]{:S(2)}, u32[]{:S(2)}) %collective-permute-start.2) | collective-permute-done | bytes 524320 | tf_op jit(solution)/shard_map/ppermute | solution.py:961
  66.3 12.2 %collective-permute-done.5 = bf16[256,1024]{1,0:T(8,128)(2,1)S(1)} collective-permute-done((bf16[256,1024]{1,0:T(8,128)(2,1)S(1)}, bf16[256,1024]{1,0:T(8,128)(2,1)S(1)}, u32[]{:S(2)}, u32[]{:S(2)}) %collective-permute-start.5) | collective-permute-done | bytes 524320 | tf_op jit(solution)/shard_map/ppermute | solution.py:955
  79.3 14.6 %collective-permute-done.6 = bf16[4,128,1024]{2,1,0:T(8,128)(2,1)} collective-permute-done((bf16[4,128,1024]{2,1,0:T(8,128)(2,1)S(1)}, bf16[4,128,1024]{2,1,0:T(8,128)(2,1)}, u32[]{:S(2)}, u32[]{:S(2)}) %collective-permute-start.6) | collective-permute-done | bytes 1048608 | tf_op jit(solution)/shard_map/ppermute | solution.py:958
  118.9 24.2 %all-to-all-done.qkv_ref = bf16[8,192,512]{2,1,0:T(8,128)(2,1)S(1)} async-done(((bf16[8,192,512]{2,1,0:T(8,128)(2,1)}), bf16[8,192,512]{2,1,0:T(8,128)(2,1)S(1)}, u32[]{:S(2)}, u32[]{:S(2)}) %all-to-all-start) | async-done | bytes 1572896 | tf_op jit(solution)/shard_map/all_to_all | solution.py:494
  143.0 21.9 %attention_forward.2 = (bf16[16,64,256]{2,1,0:T(8,128)(2,1)}, f32[16,1,256]{2,1,0:T(1,128)S(1)}) custom-call(s32[4]{0:T(128)S(1)} %bitcast.327, bf16[8,192,512]{2,1,0:T(8,128)(2,1)S(1)} %all-to-all-done.qkv_ref), custom_call_target="tpu_custom_call" | custom-call | flops 1 | bytes 1 | tf_op jit(solution)/shard_map/attention_forward/pallas_call | solution.py:602
  180.2 16.3 %collective-permute-done.11 = bf16[128,1024]{1,0:T(8,128)(2,1)S(1)} collective-permute-done((bf16[128,1024]{1,0:T(8,128)(2,1)}, bf16[128,1024]{1,0:T(8,128)(2,1)S(1)}, u32[]{:S(2)}, u32[]{:S(2)}) %collective-permute-start.11) | collective-permute-done | bytes 262176 | tf_op jit(solution)/shard_map/ppermute | solution.py:964
  209.6 34.9 %collective-permute-done.12 = bf16[2,128,1024]{2,1,0:T(8,128)(2,1)} collective-permute-done((bf16[2,128,1024]{2,1,0:T(8,128)(2,1)}, bf16[2,128,1024]{2,1,0:T(8,128)(2,1)}, u32[]{:S(2)}, u32[]{:S(2)}) %collective-permute-start.12) | collective-permute-done | bytes 524320 | tf_op jit(solution)/shard_map/ppermute | solution.py:961
  263.6 10.6 %collective-permute-done.13 = bf16[256,1024]{1,0:T(8,128)(2,1)S(1)} collective-permute-done((bf16[256,1024]{1,0:T(8,128)(2,1)S(1)}, bf16[256,1024]{1,0:T(8,128)(2,1)S(1)}, u32[]{:S(2)}, u32[]{:S(2)}) %collective-permute-start.13) | collective-permute-done | bytes 524320 | tf_op jit(solution)/shard_map/ppermute | solution.py:955
  281.6 12.9 %collective-permute-done.16 = bf16[256,1024]{1,0:T(8,128)(2,1)S(1)} collective-permute-done((bf16[256,1024]{1,0:T(8,128)(2,1)S(1)}, bf16[256,1024]{1,0:T(8,128)(2,1)S(1)}, u32[]{:S(2)}, u32[]{:S(2)}) %collective-permute-start.16) | collective-permute-done | bytes 524320 | tf_op jit(solution)/shard_map/ppermute | solution.py:955
  329.1 22.6 %attention_forward.3 = (bf16[16,64,256]{2,1,0:T(8,128)(2,1)S(1)}, f32[16,1,256]{2,1,0:T(1,128)S(1)}) custom-call(s32[4]{0:T(128)S(1)} %bitcast.328, bf16[8,192,512]{2,1,0:T(8,128)(2,1)} %all-to-all-done.2.qkv_ref), custom_call_target="tpu_custom_call" | custom-call | flops 1 | bytes 1 | tf_op jit(solution)/shard_map/attention_forward/pallas_call | solution.py:602
  408.3 14.1 %collective-permute-done.22 = bf16[256,1024]{1,0:T(8,128)(2,1)S(1)} collective-permute-done((bf16[256,1024]{1,0:T(8,128)(2,1)S(1)}, bf16[256,1024]{1,0:T(8,128)(2,1)S(1)}, u32[]{:S(2)}, u32[]{:S(2)}) %collective-permute-start.22) | collective-permute-done | bytes 524320 | tf_op jit(solution)/shard_map/ppermute | solution.py:955
  456.7 31.3 %attention_backward.2 = bf16[8,192,512]{2,1,0:T(8,128)(2,1)S(1)} custom-call(s32[4]{0:T(128)S(1)} %bitcast.329, bf16[8,192,512]{2,1,0:T(8,128)(2,1)} %all-to-all-done.2.qkv_ref, bf16[16,64,256]{2,1,0:T(8,128)(2,1)S(1)} %copy-done.68, bf16[16,64,256]{2,1,0:T(8,128)(2,1)} %all-to-all-done.4.grad_ref, f32[16,1,256]{2,1,0:T(1,128)S(1)} %get-tuple-element.208.lse_ref), custom_call_target="tpu_custom_call" | custom-call | flops 1 | bytes 1 | tf_op jit(solution)/shard_map/attention_backward/pallas_call | solution.py:712
  495.9 26.0 %all-to-all-done.5 = bf16[8,192,512]{2,1,0:T(8,128)(2,1)} async-done(((bf16[8,192,512]{2,1,0:T(8,128)(2,1)}), bf16[8,192,512]{2,1,0:T(8,128)(2,1)}, u32[]{:S(2)}, u32[]{:S(2)}) %all-to-all-start.5) | async-done | bytes 1572896 | tf_op jit(solution)/shard_map/all_to_all | solution.py:494
  532.8 11.2 %collective-permute-done.29 = bf16[256,1024]{1,0:T(8,128)(2,1)S(1)} collective-permute-done((bf16[256,1024]{1,0:T(8,128)(2,1)S(1)}, bf16[256,1024]{1,0:T(8,128)(2,1)S(1)}, u32[]{:S(2)}, u32[]{:S(2)}) %collective-permute-start.29) | collective-permute-done | bytes 524320 | tf_op jit(solution)/shard_map/ppermute | solution.py:955
  578.0 10.0 %collective-permute-done.32 = bf16[256,1024]{1,0:T(8,128)(2,1)} collective-permute-done((bf16[256,1024]{1,0:T(8,128)(2,1)}, bf16[256,1024]{1,0:T(8,128)(2,1)}, u32[]{:S(2)}, u32[]{:S(2)}) %collective-permute-start.32) | collective-permute-done | bytes 524320 | tf_op jit(solution)/shard_map/ppermute | solution.py:955
  620.6 8.7 collective-permute-start.40
  631.7 30.9 %attention_backward.3 = bf16[8,192,512]{2,1,0:T(8,128)(2,1)S(1)} custom-call(s32[4]{0:T(128)S(1)} %bitcast.330, bf16[8,192,512]{2,1,0:T(8,128)(2,1)S(1)} %copy-done.11, bf16[16,64,256]{2,1,0:T(8,128)(2,1)} %get-tuple-element.162.out_ref, bf16[16,64,256]{2,1,0:T(8,128)(2,1)} %all-to-all-done.6.grad_ref, f32[16,1,256]{2,1,0:T(1,128)S(1)} %get-tuple-element.241.lse_ref), custom_call_target="tpu_custom_call" | custom-call | flops 1 | bytes 1 | tf_op jit(solution)/shard_map/attention_backward/pallas_call | solution.py:712
  669.4 9.8 %all-to-all-start.7 = ((bf16[8,192,512]{2,1,0:T(8,128)(2,1)}), bf16[8,192,512]{2,1,0:T(8,128)(2,1)S(1)}, u32[]{:S(2)}, u32[]{:S(2)}) async-start(bf16[8,192,512]{2,1,0:T(8,128)(2,1)} %copy-done.17), calls=%async_computation.8 | async-start | bytes 3145728 | tf_op jit(solution)/shard_map/all_to_all | solution.py:494
  691.9 28.3 %collective-permute-done.43 = bf16[4,32,1024]{2,1,0:T(8,128)(2,1)S(1)} collective-permute-done((bf16[4,32,1024]{2,1,0:T(8,128)(2,1)S(1)}, bf16[4,32,1024]{2,1,0:T(8,128)(2,1)S(1)}, u32[]{:S(2)}, u32[]{:S(2)}) %collective-permute-start.43) | collective-permute-done | bytes 262176 | tf_op jit(solution)/shard_map/ppermute | solution.py:958
  746.7 18.5 %collective-permute-done.50 = bf16[128,1024]{1,0:T(8,128)(2,1)S(1)} collective-permute-done((bf16[128,1024]{1,0:T(8,128)(2,1)S(1)}, bf16[128,1024]{1,0:T(8,128)(2,1)S(1)}, u32[]{:S(2)}, u32[]{:S(2)}) %collective-permute-start.50) | collective-permute-done | bytes 262176 | tf_op jit(solution)/shard_map/ppermute | solution.py:964
  782.9 10.0 %collective-permute-done.54 = bf16[2,128,1024]{2,1,0:T(8,128)(2,1)S(1)} collective-permute-done((bf16[2,128,1024]{2,1,0:T(8,128)(2,1)S(1)}, bf16[2,128,1024]{2,1,0:T(8,128)(2,1)S(1)}, u32[]{:S(2)}, u32[]{:S(2)}) %collective-permute-start.54) | collective-permute-done | bytes 524320 | tf_op jit(solution)/shard_map/ppermute | solution.py:961
  796.7 15.6 %collective-permute-done.53 = bf16[256,1024]{1,0:T(8,128)(2,1)S(1)} collective-permute-done((bf16[256,1024]{1,0:T(8,128)(2,1)S(1)}, bf16[256,1024]{1,0:T(8,128)(2,1)S(1)}, u32[]{:S(2)}, u32[]{:S(2)}) %collective-permute-start.53) | collective-permute-done | bytes 524320 | tf_op jit(solution)/shard_map/ppermute | solution.py:946
  813.4 23.4 %all_to_all.50 = bf16[4,264,1024]{2,1,0:T(8,128)(2,1)S(1)} all-to-all(bf16[4,264,1024]{2,1,0:T(8,128)(2,1)S(1)} %broadcast_in_dim.17), channel_id=1, replica_groups=mesh['section'=2,'ctx'=4,'tp'=4] {'ctx'}, dimensions={0} | all-to-all | bytes 4325376 | tf_op jit(solution)/shard_map/all_to_all | solution.py:970
  (670 shorter events, 444.8 us)
Async XLA Ops:
  7.2 157.8 %all-gather.5.cloned.1.call-start = ((), (), s32[]{:S(2)}) async-start(), calls=%async_computation.11 | async-start | bytes 9191424 | tf_op jit(solution)/shard_map/all_gather | solution.py:976
  61.3 249.0 %all-gather.7.cloned.1.call-start = ((), (), s32[]{:S(2)}) async-start(), calls=%async_computation.12 | async-start | bytes 9191424 | tf_op jit(solution)/shard_map/all_gather | solution.py:976
  110.2 32.8 %all-to-all-start = ((bf16[8,192,512]{2,1,0:T(8,128)(2,1)}), bf16[8,192,512]{2,1,0:T(8,128)(2,1)S(1)}, u32[]{:S(2)}, u32[]{:S(2)}) async-start(bf16[8,192,512]{2,1,0:T(8,128)(2,1)} %fusion.62), calls=%async_computation | async-start | bytes 3145728 | tf_op jit(solution)/shard_map/all_to_all | solution.py:494
  115.6 55.5 %collective-permute-start.8 = (bf16[2,4,32,1024]{3,2,1,0:T(8,128)(2,1)}, bf16[2,4,32,1024]{3,2,1,0:T(8,128)(2,1)}, u32[]{:S(2)}, u32[]{:S(2)}) collective-permute-start(bf16[2,4,32,1024]{3,2,1,0:T(8,128)(2,1)} %pad_maximum_fusion.24), channel_id=1, source_target_pairs={{0,4},{4,0},{8,12},{12,8},{1,5},{5,1},{9,13},{13,9},{2,6},{6,2},{1... | collective-permute-start | bytes 1572872 | tf_op jit(solution)/shard_map/ppermute | solution.py:955
  199.1 45.4 %collective-permute-start.12 = (bf16[2,128,1024]{2,1,0:T(8,128)(2,1)}, bf16[2,128,1024]{2,1,0:T(8,128)(2,1)}, u32[]{:S(2)}, u32[]{:S(2)}) collective-permute-start(bf16[2,128,1024]{2,1,0:T(8,128)(2,1)} %pad_maximum_fusion.26), channel_id=1, source_target_pairs={{0,1},{1,0},{2,3},{3,2},{4,5},{5,4},{6,7},{7,6},{8,9},{9,8},{10,11... | collective-permute-start | bytes 1572872 | tf_op jit(solution)/shard_map/ppermute | solution.py:961
  208.1 45.8 %collective-permute-start.10 = (bf16[256,1024]{1,0:T(8,128)(2,1)S(1)}, bf16[256,1024]{1,0:T(8,128)(2,1)S(1)}, u32[]{:S(2)}, u32[]{:S(2)}) collective-permute-start(bf16[256,1024]{1,0:T(8,128)(2,1)S(1)} %multiply_convert_fusion.1.rows_ref.refs_6_), channel_id=1, source_target_pairs={{0,4},{4,0},{8,12},{12,8},{1,5},{5,1},{9,13},{13,9},{2,6},{6,2},{1... | collective-permute-start | bytes 1572872 | tf_op jit(solution)/shard_map/ppermute | solution.py:955
  447.0 41.0 %collective-permute-start.27 = (bf16[256,1024]{1,0:T(8,128)(2,1)}, bf16[256,1024]{1,0:T(8,128)(2,1)S(1)}, u32[]{:S(2)}, u32[]{:S(2)}) collective-permute-start(bf16[256,1024]{1,0:T(8,128)(2,1)} %convert_element_type.417), channel_id=1, source_target_pairs={{0,4},{4,0},{8,12},{12,8},{1,5},{5,1},{9,13},{13,9},{2,6},{6,2},{1... | collective-permute-start | bytes 1572872 | tf_op jit(solution)/shard_map/ppermute | solution.py:955
  448.6 40.6 %collective-permute-start.25 = (bf16[256,1024]{1,0:T(8,128)(2,1)}, bf16[256,1024]{1,0:T(8,128)(2,1)S(1)}, u32[]{:S(2)}, u32[]{:S(2)}) collective-permute-start(bf16[256,1024]{1,0:T(8,128)(2,1)} %copy-done.87), channel_id=1, source_target_pairs={{0,0},{1,1},{4,4},{5,5},{8,8},{9,9},{12,12},{13,13},{18,2},{19,3},... | collective-permute-start | bytes 1572872 | tf_op jit(solution)/shard_map/ppermute | solution.py:946
  450.3 39.7 %collective-permute-start.26 = (bf16[256,1024]{1,0:T(8,128)(2,1)}, bf16[256,1024]{1,0:T(8,128)(2,1)S(1)}, u32[]{:S(2)}, u32[]{:S(2)}) collective-permute-start(bf16[256,1024]{1,0:T(8,128)(2,1)} %copy-done.87), channel_id=1, source_target_pairs={{2,0},{3,1},{6,4},{7,5},{10,8},{11,9},{14,12},{15,13},{16,2},{17,3... | collective-permute-start | bytes 1572872 | tf_op jit(solution)/shard_map/ppermute | solution.py:946
  456.3 34.6 %collective-permute-start.28 = (bf16[2,4,32,1024]{3,2,1,0:T(8,128)(2,1)S(1)}, bf16[2,4,32,1024]{3,2,1,0:T(8,128)(2,1)}, u32[]{:S(2)}, u32[]{:S(2)}) collective-permute-start(bf16[2,4,32,1024]{3,2,1,0:T(8,128)(2,1)S(1)} %get-tuple-element.402), channel_id=1, source_target_pairs={{0,4},{4,0},{8,12},{12,8},{1,5},{5,1},{9,13},{13,9},{2,6},{6,2},{1... | collective-permute-start | bytes 1572872 | tf_op jit(solution)/shard_map/ppermute | solution.py:955
  495.2 123.3 %reduce-scatter.2.cloned.1.call-start = ((), (), s32[]{:S(2)}) async-start(), calls=%async_computation.13 | async-start | bytes 4866048 | tf_op jit(solution)/shard_map/reduce_scatter | solution.py:1202
  572.4 35.7 %collective-permute-start.33 = (bf16[8,264,1024]{2,1,0:T(8,128)(2,1)}, bf16[8,264,1024]{2,1,0:T(8,128)(2,1)}, u32[]{:S(2)}, u32[]{:S(2)}) collective-permute-start(bf16[8,264,1024]{2,1,0:T(8,128)(2,1)} %half_products.18), channel_id=1, source_target_pairs={{0,16},{16,0},{1,17},{17,1},{2,18},{18,2},{3,19},{19,3},{4,20},{20... | collective-permute-start | bytes 12976136 | tf_op jit(solution)/shard_map/ppermute | solution.py:967
  618.5 50.9 %collective-permute-start.37 = (bf16[4,176,1024]{2,1,0:T(8,128)(2,1)}, bf16[4,176,1024]{2,1,0:T(8,128)(2,1)}, u32[]{:S(2)}, u32[]{:S(2)}) collective-permute-start(bf16[4,176,1024]{2,1,0:T(8,128)(2,1)} %get-tuple-element.243), channel_id=1, source_target_pairs={{0,8},{4,12},{8,0},{12,4},{1,9},{5,13},{9,1},{13,5},{2,10},{6,14},... | collective-permute-start | bytes 4325384 | tf_op jit(solution)/shard_map/ppermute | solution.py:958
  620.2 49.1 %collective-permute-start.39 = (bf16[4,128,1024]{2,1,0:T(8,128)(2,1)}, bf16[4,128,1024]{2,1,0:T(8,128)(2,1)}, u32[]{:S(2)}, u32[]{:S(2)}) collective-permute-start(bf16[4,128,1024]{2,1,0:T(8,128)(2,1)} %get-tuple-element.249), channel_id=1, source_target_pairs={{0,8},{4,12},{8,0},{12,4},{1,9},{5,13},{9,1},{13,5},{2,10},{6,14},... | collective-permute-start | bytes 3145736 | tf_op jit(solution)/shard_map/ppermute | solution.py:958
  620.6 43.2 %collective-permute-start.40 = (bf16[256,1024]{1,0:T(8,128)(2,1)S(1)}, bf16[256,1024]{1,0:T(8,128)(2,1)S(1)}, u32[]{:S(2)}, u32[]{:S(2)}) collective-permute-start(bf16[256,1024]{1,0:T(8,128)(2,1)S(1)} %fusion.27.grad_ref.refs_8_), channel_id=1, source_target_pairs={{0,16},{1,17},{4,20},{5,21},{8,24},{9,25},{12,28},{13,29},{18,18},... | collective-permute-start | bytes 1572872 | tf_op jit(solution)/shard_map/ppermute | solution.py:946
  629.3 34.5 %collective-permute-start.41 = (bf16[256,1024]{1,0:T(8,128)(2,1)S(1)}, bf16[256,1024]{1,0:T(8,128)(2,1)S(1)}, u32[]{:S(2)}, u32[]{:S(2)}) collective-permute-start(bf16[256,1024]{1,0:T(8,128)(2,1)S(1)} %fusion.27.grad_ref.refs_8_), channel_id=1, source_target_pairs={{2,16},{3,17},{6,20},{7,21},{10,24},{11,25},{14,28},{15,29},{16,18... | collective-permute-start | bytes 1572872 | tf_op jit(solution)/shard_map/ppermute | solution.py:946
  630.0 39.4 %collective-permute-start.38 = (bf16[2,4,32,1024]{3,2,1,0:T(8,128)(2,1)}, bf16[2,4,32,1024]{3,2,1,0:T(8,128)(2,1)}, u32[]{:S(2)}, u32[]{:S(2)}) collective-permute-start(bf16[2,4,32,1024]{3,2,1,0:T(8,128)(2,1)} %get-tuple-element.247), channel_id=1, source_target_pairs={{0,4},{4,0},{8,12},{12,8},{1,5},{5,1},{9,13},{13,9},{2,6},{6,2},{1... | collective-permute-start | bytes 1572872 | tf_op jit(solution)/shard_map/ppermute | solution.py:955
  669.4 51.7 %all-to-all-start.7 = ((bf16[8,192,512]{2,1,0:T(8,128)(2,1)}), bf16[8,192,512]{2,1,0:T(8,128)(2,1)S(1)}, u32[]{:S(2)}, u32[]{:S(2)}) async-start(bf16[8,192,512]{2,1,0:T(8,128)(2,1)} %copy-done.17), calls=%async_computation.8 | async-start | bytes 3145728 | tf_op jit(solution)/shard_map/all_to_all | solution.py:494
  679.1 157.6 %all-gather.9.cloned.1.call-start = ((), (), s32[]{:S(2)}) async-start(), calls=%async_computation.14 | async-start | bytes 4014080 | tf_op jit(solution)/shard_map/all_gather | solution.py:1382
  680.7 40.4 %collective-permute-start.42 = (bf16[4,88,1024]{2,1,0:T(8,128)(2,1)}, bf16[4,88,1024]{2,1,0:T(8,128)(2,1)}, u32[]{:S(2)}, u32[]{:S(2)}) collective-permute-start(bf16[4,88,1024]{2,1,0:T(8,128)(2,1)} %get-tuple-element.255), channel_id=1, source_target_pairs={{0,8},{4,12},{8,0},{12,4},{1,9},{5,13},{9,1},{13,5},{2,10},{6,14},... | collective-permute-start | bytes 2162696 | tf_op jit(solution)/shard_map/ppermute | solution.py:958
  684.8 35.5 %collective-permute-start.44 = (bf16[2,128,1024]{2,1,0:T(8,128)(2,1)S(1)}, bf16[2,128,1024]{2,1,0:T(8,128)(2,1)S(1)}, u32[]{:S(2)}, u32[]{:S(2)}) collective-permute-start(bf16[2,128,1024]{2,1,0:T(8,128)(2,1)S(1)} %get-tuple-element.398), channel_id=1, source_target_pairs={{0,1},{1,0},{2,3},{3,2},{4,5},{5,4},{6,7},{7,6},{8,9},{9,8},{10,11... | collective-permute-start | bytes 1572872 | tf_op jit(solution)/shard_map/ppermute | solution.py:961
  688.3 32.0 %collective-permute-start.43 = (bf16[4,32,1024]{2,1,0:T(8,128)(2,1)S(1)}, bf16[4,32,1024]{2,1,0:T(8,128)(2,1)S(1)}, u32[]{:S(2)}, u32[]{:S(2)}) collective-permute-start(bf16[4,32,1024]{2,1,0:T(8,128)(2,1)S(1)} %get-tuple-element.420), channel_id=1, source_target_pairs={{0,8},{4,12},{8,0},{12,4},{1,9},{5,13},{9,1},{13,5},{2,10},{6,14},... | collective-permute-start | bytes 786440 | tf_op jit(solution)/shard_map/ppermute | solution.py:958
  775.2 37.2 %collective-permute-start.51 = (bf16[264,1024]{1,0:T(8,128)(2,1)S(1)}, bf16[264,1024]{1,0:T(8,128)(2,1)S(1)}, u32[]{:S(2)}, u32[]{:S(2)}) collective-permute-start(bf16[264,1024]{1,0:T(8,128)(2,1)S(1)} %get-tuple-element.392), channel_id=1, source_target_pairs={{0,2},{1,3},{2,0},{3,1},{4,6},{5,7},{6,4},{7,5},{8,10},{9,11},{10,... | collective-permute-start | bytes 1622024 | tf_op jit(solution)/shard_map/ppermute | solution.py:964
  777.5 34.8 %collective-permute-start.53 = (bf16[256,1024]{1,0:T(8,128)(2,1)S(1)}, bf16[256,1024]{1,0:T(8,128)(2,1)S(1)}, u32[]{:S(2)}, u32[]{:S(2)}) collective-permute-start(bf16[256,1024]{1,0:T(8,128)(2,1)S(1)} %copy-done.154), channel_id=1, source_target_pairs={{2,0},{3,1},{6,4},{7,5},{10,8},{11,9},{14,12},{15,13},{16,2},{17,3... | collective-permute-start | bytes 1572872 | tf_op jit(solution)/shard_map/ppermute | solution.py:946
  (211 other events, 2046.2 us)
Sparse Core Ops, SparseCore 0:
  61.4 94.7 all-gather.4
  158.5 93.5 all-gather.6
  500.2 97.7 reduce-scatter.1
  768.2 47.0 all-gather.8

commit v5 on v4

--- a/solution.py
+++ b/solution.py
@@ -981,10 +981,16 @@
     def by_core(value, which):
         return lax.dynamic_index_in_dim(value, which, 0, keepdims=False)
 
-    def spread_line(piece):
-        pair = jnp.stack(ordered(batch, piece, swap_half(piece)))
-        line = jnp.stack(ordered(tp % 2, pair, swap_near(pair)), axis=1)
-        return line.reshape(parts, *piece.shape)
+    def spread_half(piece):
+        return piece, swap_half(piece)
+
+    def spread_near(pieces_pair):
+        pair = jnp.stack(ordered(batch, *pieces_pair))
+        return pair, swap_near(pair)
+
+    def spread_line(pairs):
+        line = jnp.stack(ordered(tp % 2, *pairs), axis=1)
+        return line.reshape(parts, *line.shape[2:])
 
     def spread_far(line):
         return line, swap_far(line)
@@ -1027,8 +1033,9 @@
         return [whole[:, entry].reshape(-1, model_width) for entry in range(3)]
 
     rows_in = to_batch(inputs)
-    line, rows_in = together(spread_line(pieces[0][:attention_rows]), rows_in)
-    w_ffn = [feed_forward_weights(after(piece, line)) for piece in pieces]
+    line = spread_near(spread_half(pieces[0][:attention_rows]))
+    line, rows_in = together(spread_line(line), rows_in)
+    w_ffn = [feed_forward_weights(after(pieces[0], line)), None]
     w_heads, w_outs = [None, None], [None, None]
     first_pair = spread_far(line)
 
@@ -1216,22 +1223,25 @@
 
     def weights_line(value):
         value, piece = together(value, pieces[1][:attention_rows])
-        pending["weights"] = spread_line(piece)
+        pending["weights"] = spread_half(piece)
         return value
 
     def weights_outs_first(value):
-        value, pending["outs"], w_ffn[0] = together(value, pending["outs"], w_ffn[0])
+        value, pending["outs"], w_ffn[0], weights = together(
+            value, pending["outs"], w_ffn[0], pending["weights"]
+        )
+        pending["weights"] = spread_near(weights)
         w_outs[0] = join_outs(spread_outs(pending["outs"]))
-        pending["grad_in"] = to_batch(after(cotangent, value))
         return value
 
     def weights_far(value):
         value, line = together(value, pending["weights"])
-        pending["weights"] = spread_far(line)
+        pending["weights"] = spread_far(spread_line(line))
+        w_ffn[1] = feed_forward_weights(after(pieces[1], value))
         return value
 
     def weights_heads(value):
-        value, pairs, pending["grad_in"] = together(value, pending["weights"], pending["grad_in"])
+        value, pairs = together(value, pending["weights"])
         w_heads[1], pending["outs"] = spread_heads(pairs)
         return value
 
@@ -1243,13 +1253,15 @@
     first_out = first_result()
 
     def start_outs(value):
-        value, outs, w_ffn[1] = together(value, pending["outs"], w_ffn[1])
-        pending["outs"] = spread_outs(outs)
+        value, grads = together(value, cotangent)
+        pending["grad_in"] = to_batch(grads)
         return value
 
     def end_outs(value):
-        value, outs = together(value, pending["outs"])
-        w_outs[1] = join_outs(outs)
+        value, outs, w_ffn[1], pending["grad_in"] = together(
+            value, pending["outs"], w_ffn[1], pending["grad_in"]
+        )
+        w_outs[1] = join_outs(spread_outs(outs))
         pending["first_home"] = to_home(after(first_out, value), 0)
         return value
 
@@ -1303,15 +1315,13 @@
 
     def first_first(value):
         head = head_products(section, addend=pending["moved"])
-        value, pending["head"] = together(value, head)
-        return value
-
-    def first_second(value):
-        head = jnp.concatenate([pending["head"], pending["second_out"]], axis=1)
+        head = jnp.concatenate([head, pending["second_out"]], axis=1)
         head = parted(head.reshape(2, parts, -1, model_width), row_side, 0)
         value, head = together(value, head)
         pending["head"] = moved_pair(head, swap_far)
-        pending["second_grad_home"] = to_home(after(second_grad, value), 1)
+        return value
+
+    def first_second(value):
         return value
 
     def first_third(value, rest, out_pair):
@@ -1319,32 +1329,37 @@
         rest = rest.reshape(2, parts, -1, model_width)
         rest_a = parted(rest[:, :, : 2 * unit_rows], row_side, 0)
         rest_b = parted(rest[:, :, 2 * unit_rows :], row_side, 0)
-        value, rest_a, rest_b, out_sum, pending["second_rest"], pending["second_home"] = together(
-            value, rest_a, rest_b, out_sum, pending["second_rest"], pending["second_home"]
+        (
+            value, rest_a, rest_b, out_sum, head, pending["second_rest"], pending["second_home"]
+        ) = together(
+            value, rest_a, rest_b, out_sum, pending["head"], pending["second_rest"],
+            pending["second_home"],
         )
         pending["rest_a"] = moved_pair(rest_a, swap_far)
         pending["rest_b"] = rest_b
         pending["out"] = moved_pair(out_sum, swap_side)
+        pending["head"] = near_sum(add(head))
         return value, rest
 
     def first_fourth(value):
-        value, rest_a, rest_b, out_sum, head, pending["second_grad_home"] = together(
-            value, pending["rest_a"], pending["rest_b"], pending["out"], pending["head"],
-            pending["second_grad_home"],
-        )
+        value, rest_a, rest_b, out_sum, head = together(
+            value, pending["rest_a"], pending["rest_b"], pending["out"], pending["head"]
+        )
+        pending["head"] = far_sum(head)
         pending["rest_b"] = moved_pair(rest_b, swap_far)
-        pending["rest_a"] = add(rest_a)
+        pending["rest_a"] = near_sum(add(rest_a))
         pending["out"] = halve(add(out_sum), row_side, swap_far, 0)
-        pending["head"] = near_sum(add(head))
         return value
 
     def first_fifth(value):
         value, rest_a, rest_b, out_sum, head = together(
             value, pending["rest_a"], pending["rest_b"], pending["out"], pending["head"]
         )
+        second = jnp.concatenate([pending["second_rest"], add(head)], axis=0)
+        pending["second"] = lax.all_gather(second, "ctx", axis=0, tiled=False)
         pending["out"] = add(out_sum)
-        pending["head2"] = far_sum(head)
-        pending["rest"] = near_sum(jnp.concatenate([rest_a, add(rest_b)], axis=1))
+        pending["rest_a"] = far_sum(rest_a)
+        pending["rest_b"] = near_sum(add(rest_b))
         return value
 
     first_halves, _, first_hidden, _, first_gain2 = layer_backward(
@@ -1361,9 +1376,9 @@
     moved = swap_section(sent)
     def head_end(value):
         head = head_products(section, addend=moved).reshape(2, parts, head_rows, model_width)
-        value, head = together(value, parted(head, row_side, 0))
+        head = parted(head, row_side, 0)
         pending["head"] = moved_pair(head, swap_far)
-        return value
+        return after(value, head)
 
     first_gain1, first_grad = input_grads_of(
         after(first_halves, sent), first_hidden, first_saved, 0, head_end
@@ -1373,29 +1388,25 @@
 
     gain_rows = jnp.stack([first_gain1, first_gain2, second_gain1, second_gain2])
     gain_rows = summed(gain_rows, swap_section)
-    head, rest, gain_rows, second_head, first_grad = together(
-        pending["head"], pending["rest"], gain_rows, pending["head2"], low(first_grad)
-    )
+    head, rest_a, rest_b, gain_rows, first_grad, home = together(
+        pending["head"], pending["rest_a"], pending["rest_b"], gain_rows, low(first_grad), second_grad
+    )
+    second_grad_home = to_home(home, 1)
     head = near_sum(jnp.concatenate([add(head), pending["out"]], axis=1))
-    rest = far_sum(rest)
-    second = jnp.concatenate([pending["second_rest"], add(second_head)], axis=0)
-    second = lax.all_gather(second, "ctx", axis=0, tiled=False)
+    rest_b = far_sum(rest_b)
     first_grad_home = to_home(first_grad, 0)
-    gain_rows = summed(gain_rows, swap_side)
-    head, gain_rows = together(head, gain_rows)
+    gain_rows = summed(summed(gain_rows, swap_side), swap_far)
+    head, rest_b, gain_rows = together(head, rest_b, gain_rows)
     head = far_sum(head)
-    gain_rows = summed(gain_rows, swap_far)
-    rest, first_grad_home, gain_rows = together(rest, first_grad_home, gain_rows)
-    rest = all_to_all(copies(add(rest), contexts), "ctx")
-    gain_rows = summed(gain_rows, swap_near)
-    head, gain_rows = together(head, gain_rows)
+    rest = jnp.concatenate([add(rest_a), add(rest_b)], axis=0)
+    rest = lax.all_gather(rest, "ctx", axis=0, tiled=False)
+    gain_total = summed(summed(gain_rows, swap_near), swap_half)
+    head, first_grad_home, second_grad_home = together(head, first_grad_home, second_grad_home)
     head = all_to_all(copies(add(head), contexts), "ctx")
-    gain_total = summed(gain_rows, swap_half)
-    rest, second = together(rest, second)
+    rest, second, head = together(rest, pending["second"], head)
     first_grads = (rest, head)
     second_grads = (second[:, : 3 * unit_rows], second[:, 3 * unit_rows :])
     first_home, second_home = pending["first_home"], pending["second_home"]
-    second_grad_home = pending["second_grad_home"]
     gain_total = jnp.where(leading, gain_total[:2], gain_total[2:])
 
     def finish(first, second):

time: 910 us -> 866 us (0.952)
  waiting for transfers between devices: 355 us -> 321 us
  blocking collectives: 23.4 us -> 54.6 us
  starting transfers between devices: 129 us -> 106 us
  other arithmetic: 87 us -> 69.6 us
    ppermute x6 -> x7, waiting for transfers between devices: 64.2 us -> 20.9 us  [swap_near(): return lax.ppermute(value, 'tp', [(t, t ^ 1) for t in range(parts)])]
    all_to_all x0 -> x1, blocking collectives: none -> 39.5 us  [exchange(): lax.all_to_all(value, ALL_AXES, split_axis=0, concat_axis=0, tiled=True,...]
    ppermute x6 -> x7, waiting for transfers between devices: 58.6 us -> 38.8 us  [swap_half(): lax.ppermute(value, 'tp', [(t, (t + half_parts) % parts) for t in range(p...]
    ppermute x8, waiting for transfers between devices: 54.9 us -> 70.1 us  [swap_far(): return lax.ppermute(value, 'ctx', [(c, c ^ 2) for c in range(contexts)])]
    all_to_all x8 -> x7, waiting for transfers between devices: 58.1 us -> 69.5 us  [exchange(): lax.all_to_all(value, ALL_AXES, split_axis=0, concat_axis=0, tiled=True,...]
    all_to_all x8 -> x7, starting transfers between devices: 39.3 us -> 30.5 us  [exchange(): lax.all_to_all(value, ALL_AXES, split_axis=0, concat_axis=0, tiled=True,...]
    ppermute x6 -> x7, starting transfers between devices: 14.3 us -> 20 us  [swap_half(): lax.ppermute(value, 'tp', [(t, (t + half_parts) % parts) for t in range(p...]
    unnamed x325 -> x331, local copies, waits for them, and re-layouts: 40.5 us -> 45.5 us
  transfers between devices with their start and end apart: 75 -> 76, of which waited for: 35 -> 33; matrix products, arithmetic and copies ran while one was open for 14% -> 11% of each run, Pallas kernels for 18% -> 20%
where the time goes in v5:
time: 866 us; the launch traced here: 856 us
  waiting for transfers between devices  321 us (37%)
  Pallas kernels  185 us (21%)
  starting transfers between devices  106 us (12%)
  local copies, waits for them, and re-layouts  88.2 us (10%)
  other arithmetic  69.6 us (8%)
  blocking collectives  54.6 us (6%)
  between operations  17 us (2%)
  matrix products  14.7 us (2%)
    ppermute x17, waiting for transfers between devices, swap_side(): return lax.ppermute(value, 'ctx', [(c, c ^ 1) for c in range(contexts)])  96.3 us
    ppermute x8, waiting for transfers between devices, swap_far(): return lax.ppermute(value, 'ctx', [(c, c ^ 2) for c in range(contexts)])  70.1 us
    all_to_all x7, waiting for transfers between devices, exchange(): lax.all_to_all(value, ALL_AXES, split_axis=0, concat_axis=0, tiled=True,...  69.5 us
    pallas_call x2, Pallas kernels, attention_backward(): pl.pallas_call(functools.partial(attention_backward_kernel, parts), grid_...  62.6 us
    unnamed x331, local copies, waits for them, and re-layouts  45.5 us
    pallas_call x2, Pallas kernels, attention_forward(): pl.pallas_call(functools.partial(attention_forward_kernel, parts), grid_s...  43.2 us
    all_to_all x1, blocking collectives, exchange(): lax.all_to_all(value, ALL_AXES, split_axis=0, concat_axis=0, tiled=True,...  39.5 us
    ppermute x7, waiting for transfers between devices, swap_half(): lax.ppermute(value, 'tp', [(t, (t + half_parts) % parts) for t in range(p...  38.8 us
  transfers between devices with their start and end apart: 76, of which 33 were waited for; matrix products, arithmetic and copies ran while one was open for 11% of the time, Pallas kernels for 20%

profile of v5, /device:TPU:0, one launch (start us, length us, event | category | flops | bytes accessed | tf_op | source)
XLA Modules:
  0.0 855.5 jit_solution(9868421415792412979)
XLA Ops:
  27.9 14.8 %collective-permute-done.1 = bf16[128,1024]{1,0:T(8,128)(2,1)} collective-permute-done((bf16[128,1024]{1,0:T(8,128)(2,1)S(1)}, bf16[128,1024]{1,0:T(8,128)(2,1)}, u32[]{:S(2)}, u32[]{:S(2)}) %collective-permute-start.1) | collective-permute-done | bytes 262176 | tf_op jit(solution)/shard_map/ppermute | solution.py:964
  44.8 14.3 %collective-permute-done.2 = bf16[2,128,1024]{2,1,0:T(8,128)(2,1)} collective-permute-done((bf16[2,128,1024]{2,1,0:T(8,128)(2,1)}, bf16[2,128,1024]{2,1,0:T(8,128)(2,1)}, u32[]{:S(2)}, u32[]{:S(2)}) %collective-permute-start.2) | collective-permute-done | bytes 524320 | tf_op jit(solution)/shard_map/ppermute | solution.py:961
  66.2 12.2 %collective-permute-done.5 = bf16[256,1024]{1,0:T(8,128)(2,1)S(1)} collective-permute-done((bf16[256,1024]{1,0:T(8,128)(2,1)S(1)}, bf16[256,1024]{1,0:T(8,128)(2,1)S(1)}, u32[]{:S(2)}, u32[]{:S(2)}) %collective-permute-start.5) | collective-permute-done | bytes 524320 | tf_op jit(solution)/shard_map/ppermute | solution.py:955
  79.2 14.6 %collective-permute-done.6 = bf16[4,128,1024]{2,1,0:T(8,128)(2,1)} collective-permute-done((bf16[4,128,1024]{2,1,0:T(8,128)(2,1)S(1)}, bf16[4,128,1024]{2,1,0:T(8,128)(2,1)}, u32[]{:S(2)}, u32[]{:S(2)}) %collective-permute-start.6) | collective-permute-done | bytes 1048608 | tf_op jit(solution)/shard_map/ppermute | solution.py:958
  116.1 27.0 %all-to-all-done.qkv_ref = bf16[8,192,512]{2,1,0:T(8,128)(2,1)S(1)} async-done(((bf16[8,192,512]{2,1,0:T(8,128)(2,1)}), bf16[8,192,512]{2,1,0:T(8,128)(2,1)S(1)}, u32[]{:S(2)}, u32[]{:S(2)}) %all-to-all-start) | async-done | bytes 1572896 | tf_op jit(solution)/shard_map/all_to_all | solution.py:494
  143.0 21.9 %attention_forward.2 = (bf16[16,64,256]{2,1,0:T(8,128)(2,1)}, f32[16,1,256]{2,1,0:T(1,128)S(1)}) custom-call(s32[4]{0:T(128)S(1)} %bitcast.339, bf16[8,192,512]{2,1,0:T(8,128)(2,1)S(1)} %all-to-all-done.qkv_ref), custom_call_target="tpu_custom_call" | custom-call | flops 1 | bytes 1 | tf_op jit(solution)/shard_map/attention_forward/pallas_call | solution.py:602
  226.7 12.0 %collective-permute-done.13 = bf16[256,1024]{1,0:T(8,128)(2,1)S(1)} collective-permute-done((bf16[256,1024]{1,0:T(8,128)(2,1)S(1)}, bf16[256,1024]{1,0:T(8,128)(2,1)S(1)}, u32[]{:S(2)}, u32[]{:S(2)}) %collective-permute-start.13) | collective-permute-done | bytes 524320 | tf_op jit(solution)/shard_map/ppermute | solution.py:955
  238.7 10.8 %collective-permute-done.14 = bf16[4,128,1024]{2,1,0:T(8,128)(2,1)S(1)} collective-permute-done((bf16[4,128,1024]{2,1,0:T(8,128)(2,1)S(1)}, bf16[4,128,1024]{2,1,0:T(8,128)(2,1)S(1)}, u32[]{:S(2)}, u32[]{:S(2)}) %collective-permute-start.14) | collective-permute-done | bytes 1048608 | tf_op jit(solution)/shard_map/ppermute | solution.py:958
  253.6 11.5 %collective-permute-done.15 = bf16[256,1024]{1,0:T(8,128)(2,1)S(1)} collective-permute-done((bf16[256,1024]{1,0:T(8,128)(2,1)S(1)}, bf16[256,1024]{1,0:T(8,128)(2,1)S(1)}, u32[]{:S(2)}, u32[]{:S(2)}) %collective-permute-start.15) | collective-permute-done | bytes 524320 | tf_op jit(solution)/shard_map/ppermute | solution.py:955
  269.8 39.5 %all_to_all.45.qkv_ref = bf16[8,192,512]{2,1,0:T(8,128)(2,1)S(1)} all-to-all(bf16[8,192,512]{2,1,0:T(8,128)(2,1)S(1)} %fusion.53), channel_id=1, replica_groups={{0,1,16,17,8,9,24,25},{2,3,18,19,10,11,26,27},{4,5,20,21,12,13,28,29},{..., dimensions={0} | all-to-all | bytes 3145728 | tf_op jit(solution)/shard_map/all_to_all | solution.py:494
  313.2 21.2 %attention_forward.3 = (bf16[16,64,256]{2,1,0:T(8,128)(2,1)S(1)}, f32[16,1,256]{2,1,0:T(1,128)S(1)}) custom-call(s32[4]{0:T(128)S(1)} %bitcast.340, bf16[8,192,512]{2,1,0:T(8,128)(2,1)S(1)} %all_to_all.45.qkv_ref), custom_call_target="tpu_custom_call" | custom-call | flops 1 | bytes 1 | tf_op jit(solution)/shard_map/attention_forward/pallas_call | solution.py:602
  385.7 7.6 feed_forward_back.5
  399.6 14.0 %collective-permute-done.22 = bf16[256,1024]{1,0:T(8,128)(2,1)S(1)} collective-permute-done((bf16[256,1024]{1,0:T(8,128)(2,1)S(1)}, bf16[256,1024]{1,0:T(8,128)(2,1)S(1)}, u32[]{:S(2)}, u32[]{:S(2)}) %collective-permute-start.22) | collective-permute-done | bytes 524320 | tf_op jit(solution)/shard_map/ppermute | solution.py:955
  448.3 30.7 %attention_backward.2 = bf16[8,192,512]{2,1,0:T(8,128)(2,1)S(1)} custom-call(s32[4]{0:T(128)S(1)} %bitcast.341, bf16[8,192,512]{2,1,0:T(8,128)(2,1)S(1)} %copy-done.17, bf16[16,64,256]{2,1,0:T(8,128)(2,1)S(1)} %copy-done.68, bf16[16,64,256]{2,1,0:T(8,128)(2,1)} %all-to-all-done.4.grad_ref, f32[16,1,256]{2,1,0:T(1,128)S(1)} %get-tuple-element.208.lse_ref), custom_call_target="tpu_custom_call" | custom-call | flops 1 | bytes 1 | tf_op jit(solution)/shard_map/attention_backward/pallas_call | solution.py:712
  489.9 28.4 %all-to-all-done.5 = bf16[8,192,512]{2,1,0:T(8,128)(2,1)} async-done(((bf16[8,192,512]{2,1,0:T(8,128)(2,1)}), bf16[8,192,512]{2,1,0:T(8,128)(2,1)}, u32[]{:S(2)}, u32[]{:S(2)}) %all-to-all-start.5) | async-done | bytes 1572896 | tf_op jit(solution)/shard_map/all_to_all | solution.py:494
  529.4 10.3 %collective-permute-done.29 = bf16[256,1024]{1,0:T(8,128)(2,1)S(1)} collective-permute-done((bf16[256,1024]{1,0:T(8,128)(2,1)S(1)}, bf16[256,1024]{1,0:T(8,128)(2,1)S(1)}, u32[]{:S(2)}, u32[]{:S(2)}) %collective-permute-start.29) | collective-permute-done | bytes 524320 | tf_op jit(solution)/shard_map/ppermute | solution.py:955
  560.4 7.6 feed_forward_back.7
  574.3 14.0 %collective-permute-done.32 = bf16[256,1024]{1,0:T(8,128)(2,1)S(1)} collective-permute-done((bf16[256,1024]{1,0:T(8,128)(2,1)S(1)}, bf16[256,1024]{1,0:T(8,128)(2,1)S(1)}, u32[]{:S(2)}, u32[]{:S(2)}) %collective-permute-start.32) | collective-permute-done | bytes 524320 | tf_op jit(solution)/shard_map/ppermute | solution.py:955
  626.0 31.9 %attention_backward.3 = bf16[8,192,512]{2,1,0:T(8,128)(2,1)} custom-call(s32[4]{0:T(128)S(1)} %bitcast.342, bf16[8,192,512]{2,1,0:T(8,128)(2,1)S(1)} %copy-done.15, bf16[16,64,256]{2,1,0:T(8,128)(2,1)} %get-tuple-element.162.out_ref, bf16[16,64,256]{2,1,0:T(8,128)(2,1)} %all-to-all-done.6.grad_ref, f32[16,1,256]{2,1,0:T(1,128)S(1)} %get-tuple-element.241.lse_ref), custom_call_target="tpu_custom_call" | custom-call | flops 1 | bytes 1 | tf_op jit(solution)/shard_map/attention_backward/pallas_call | solution.py:712
  675.0 28.4 %collective-permute-done.43 = bf16[4,32,1024]{2,1,0:T(8,128)(2,1)S(1)} collective-permute-done((bf16[4,32,1024]{2,1,0:T(8,128)(2,1)S(1)}, bf16[4,32,1024]{2,1,0:T(8,128)(2,1)S(1)}, u32[]{:S(2)}, u32[]{:S(2)}) %collective-permute-start.43) | collective-permute-done | bytes 262176 | tf_op jit(solution)/shard_map/ppermute | solution.py:958
  727.7 12.8 %collective-permute-done.49 = bf16[256,1024]{1,0:T(8,128)(2,1)S(1)} collective-permute-done((bf16[256,1024]{1,0:T(8,128)(2,1)S(1)}, bf16[256,1024]{1,0:T(8,128)(2,1)S(1)}, u32[]{:S(2)}, u32[]{:S(2)}) %collective-permute-start.49) | collective-permute-done | bytes 524320 | tf_op jit(solution)/shard_map/ppermute | solution.py:955
  778.8 21.4 %collective-permute-done.57 = bf16[256,1024]{1,0:T(8,128)(2,1)S(1)} collective-permute-done((bf16[256,1024]{1,0:T(8,128)(2,1)}, bf16[256,1024]{1,0:T(8,128)(2,1)S(1)}, u32[]{:S(2)}, u32[]{:S(2)}) %collective-permute-start.57) | collective-permute-done | bytes 524320 | tf_op jit(solution)/shard_map/ppermute | solution.py:946
  800.3 8.4 collective-permute-done.55
  808.9 15.1 %all_to_all.46 = bf16[4,128,1024]{2,1,0:T(8,128)(2,1)S(1)} all-to-all(bf16[4,128,1024]{2,1,0:T(8,128)(2,1)S(1)} %broadcast_in_dim.14), channel_id=1, replica_groups=mesh['section'=2,'ctx'=4,'tp'=4] {'ctx'}, dimensions={0} | all-to-all | bytes 2097152 | tf_op jit(solution)/shard_map/all_to_all | solution.py:970
  (683 shorter events, 407.9 us)
Async XLA Ops:
  7.2 160.2 %all-gather.7.cloned.1.call-start = ((), (), s32[]{:S(2)}) async-start(), calls=%async_computation.10 | async-start | bytes 9191424 | tf_op jit(solution)/shard_map/all_gather | solution.py:976
  62.6 31.2 %collective-permute-start.6 = (bf16[4,128,1024]{2,1,0:T(8,128)(2,1)S(1)}, bf16[4,128,1024]{2,1,0:T(8,128)(2,1)}, u32[]{:S(2)}, u32[]{:S(2)}) collective-permute-start(bf16[4,128,1024]{2,1,0:T(8,128)(2,1)S(1)} %bitcast.379), channel_id=1, source_target_pairs={{0,8},{4,12},{8,0},{12,4},{1,9},{5,13},{9,1},{13,5},{2,10},{6,14},... | collective-permute-start | bytes 3145736 | tf_op jit(solution)/shard_map/ppermute | solution.py:958
  107.4 35.6 %all-to-all-start = ((bf16[8,192,512]{2,1,0:T(8,128)(2,1)}), bf16[8,192,512]{2,1,0:T(8,128)(2,1)S(1)}, u32[]{:S(2)}, u32[]{:S(2)}) async-start(bf16[8,192,512]{2,1,0:T(8,128)(2,1)} %fusion.62), calls=%async_computation | async-start | bytes 3145728 | tf_op jit(solution)/shard_map/all_to_all | solution.py:494
  112.8 60.4 %collective-permute-start.8 = (bf16[2,4,32,1024]{3,2,1,0:T(8,128)(2,1)}, bf16[2,4,32,1024]{3,2,1,0:T(8,128)(2,1)}, u32[]{:S(2)}, u32[]{:S(2)}) collective-permute-start(bf16[2,4,32,1024]{3,2,1,0:T(8,128)(2,1)} %pad_maximum_fusion.24), channel_id=1, source_target_pairs={{0,4},{4,0},{8,12},{12,8},{1,5},{5,1},{9,13},{13,9},{2,6},{6,2},{1... | collective-permute-start | bytes 1572872 | tf_op jit(solution)/shard_map/ppermute | solution.py:955
  185.9 149.4 %all-gather.9.cloned.1.call-start = ((), (), s32[]{:S(2)}) async-start(), calls=%async_computation.11 | async-start | bytes 9191424 | tf_op jit(solution)/shard_map/all_gather | solution.py:976
  438.2 40.9 %collective-permute-start.27 = (bf16[256,1024]{1,0:T(8,128)(2,1)}, bf16[256,1024]{1,0:T(8,128)(2,1)}, u32[]{:S(2)}, u32[]{:S(2)}) collective-permute-start(bf16[256,1024]{1,0:T(8,128)(2,1)} %convert_element_type.435), channel_id=1, source_target_pairs={{0,4},{4,0},{8,12},{12,8},{1,5},{5,1},{9,13},{13,9},{2,6},{6,2},{1... | collective-permute-start | bytes 1572872 | tf_op jit(solution)/shard_map/ppermute | solution.py:955
  439.8 41.7 %collective-permute-start.25 = (bf16[256,1024]{1,0:T(8,128)(2,1)}, bf16[256,1024]{1,0:T(8,128)(2,1)S(1)}, u32[]{:S(2)}, u32[]{:S(2)}) collective-permute-start(bf16[256,1024]{1,0:T(8,128)(2,1)} %copy-done.90), channel_id=1, source_target_pairs={{0,0},{1,1},{4,4},{5,5},{8,8},{9,9},{12,12},{13,13},{18,2},{19,3},... | collective-permute-start | bytes 1572872 | tf_op jit(solution)/shard_map/ppermute | solution.py:946
  441.5 40.9 %collective-permute-start.26 = (bf16[256,1024]{1,0:T(8,128)(2,1)}, bf16[256,1024]{1,0:T(8,128)(2,1)S(1)}, u32[]{:S(2)}, u32[]{:S(2)}) collective-permute-start(bf16[256,1024]{1,0:T(8,128)(2,1)} %copy-done.90), channel_id=1, source_target_pairs={{2,0},{3,1},{6,4},{7,5},{10,8},{11,9},{14,12},{15,13},{16,2},{17,3... | collective-permute-start | bytes 1572872 | tf_op jit(solution)/shard_map/ppermute | solution.py:946
  447.6 35.6 %collective-permute-start.28 = (bf16[2,4,32,1024]{3,2,1,0:T(8,128)(2,1)S(1)}, bf16[2,4,32,1024]{3,2,1,0:T(8,128)(2,1)S(1)}, u32[]{:S(2)}, u32[]{:S(2)}) collective-permute-start(bf16[2,4,32,1024]{3,2,1,0:T(8,128)(2,1)S(1)} %get-tuple-element.398), channel_id=1, source_target_pairs={{0,4},{4,0},{8,12},{12,8},{1,5},{5,1},{9,13},{13,9},{2,6},{6,2},{1... | collective-permute-start | bytes 1572872 | tf_op jit(solution)/shard_map/ppermute | solution.py:955
  484.0 34.3 %all-to-all-start.5 = ((bf16[8,192,512]{2,1,0:T(8,128)(2,1)}), bf16[8,192,512]{2,1,0:T(8,128)(2,1)}, u32[]{:S(2)}, u32[]{:S(2)}) async-start(bf16[8,192,512]{2,1,0:T(8,128)(2,1)} %copy-done.27), calls=%async_computation.5 | async-start | bytes 3145728 | tf_op jit(solution)/shard_map/all_to_all | solution.py:494
  489.2 132.8 %reduce-scatter.2.cloned.1.call-start = ((), (), s32[]{:S(2)}) async-start(), calls=%async_computation.12 | async-start | bytes 4866048 | tf_op jit(solution)/shard_map/reduce_scatter | solution.py:1209
  573.8 31.4 %collective-permute-start.33 = (bf16[8,264,1024]{2,1,0:T(8,128)(2,1)}, bf16[8,264,1024]{2,1,0:T(8,128)(2,1)}, u32[]{:S(2)}, u32[]{:S(2)}) collective-permute-start(bf16[8,264,1024]{2,1,0:T(8,128)(2,1)} %half_products.18), channel_id=1, source_target_pairs={{0,16},{16,0},{1,17},{17,1},{2,18},{18,2},{3,19},{19,3},{4,20},{20... | collective-permute-start | bytes 12976136 | tf_op jit(solution)/shard_map/ppermute | solution.py:967
  622.0 36.0 %collective-permute-start.38 = (bf16[4,176,1024]{2,1,0:T(8,128)(2,1)}, bf16[4,176,1024]{2,1,0:T(8,128)(2,1)}, u32[]{:S(2)}, u32[]{:S(2)}) collective-permute-start(bf16[4,176,1024]{2,1,0:T(8,128)(2,1)} %get-tuple-element.243), channel_id=1, source_target_pairs={{0,8},{4,12},{8,0},{12,4},{1,9},{5,13},{9,1},{13,5},{2,10},{6,14},... | collective-permute-start | bytes 4325384 | tf_op jit(solution)/shard_map/ppermute | solution.py:958
  622.6 35.4 %collective-permute-start.39 = (bf16[2,4,32,1024]{3,2,1,0:T(8,128)(2,1)}, bf16[2,4,32,1024]{3,2,1,0:T(8,128)(2,1)S(1)}, u32[]{:S(2)}, u32[]{:S(2)}) collective-permute-start(bf16[2,4,32,1024]{3,2,1,0:T(8,128)(2,1)} %get-tuple-element.247), channel_id=1, source_target_pairs={{0,4},{4,0},{8,12},{12,8},{1,5},{5,1},{9,13},{13,9},{2,6},{6,2},{1... | collective-permute-start | bytes 1572872 | tf_op jit(solution)/shard_map/ppermute | solution.py:955
  624.7 33.2 %collective-permute-start.40 = (bf16[2,128,1024]{2,1,0:T(8,128)(2,1)S(1)}, bf16[2,128,1024]{2,1,0:T(8,128)(2,1)S(1)}, u32[]{:S(2)}, u32[]{:S(2)}) collective-permute-start(bf16[2,128,1024]{2,1,0:T(8,128)(2,1)S(1)} %get-tuple-element.394), channel_id=1, source_target_pairs={{0,1},{1,0},{2,3},{3,2},{4,5},{5,4},{6,7},{7,6},{8,9},{9,8},{10,11... | collective-permute-start | bytes 1572872 | tf_op jit(solution)/shard_map/ppermute | solution.py:961
  658.8 46.3 %all-to-all-start.7 = ((bf16[8,192,512]{2,1,0:T(8,128)(2,1)}), bf16[8,192,512]{2,1,0:T(8,128)(2,1)S(1)}, u32[]{:S(2)}, u32[]{:S(2)}) async-start(bf16[8,192,512]{2,1,0:T(8,128)(2,1)} %attention_backward.3), calls=%async_computation.8 | async-start | bytes 3145728 | tf_op jit(solution)/shard_map/all_to_all | solution.py:494
  662.4 161.6 %all-gather.13.cloned.1.call-start = ((), (), s32[]{:S(2)}) async-start(), calls=%async_computation.14 | async-start | bytes 4014080 | tf_op jit(solution)/shard_map/all_gather | solution.py:1359
  665.8 37.7 %collective-permute-start.41 = (bf16[2,176,1024]{2,1,0:T(8,128)(2,1)S(1)}, bf16[2,176,1024]{2,1,0:T(8,128)(2,1)S(1)}, u32[]{:S(2)}, u32[]{:S(2)}) collective-permute-start(bf16[2,176,1024]{2,1,0:T(8,128)(2,1)S(1)} %get-tuple-element.386), channel_id=1, source_target_pairs={{0,1},{1,0},{2,3},{3,2},{4,5},{5,4},{6,7},{7,6},{8,9},{9,8},{10,11... | collective-permute-start | bytes 2162696 | tf_op jit(solution)/shard_map/ppermute | solution.py:961
  667.7 37.4 %collective-permute-start.42 = (bf16[4,88,1024]{2,1,0:T(8,128)(2,1)S(1)}, bf16[4,88,1024]{2,1,0:T(8,128)(2,1)}, u32[]{:S(2)}, u32[]{:S(2)}) collective-permute-start(bf16[4,88,1024]{2,1,0:T(8,128)(2,1)S(1)} %copy-done.139), channel_id=1, source_target_pairs={{0,8},{4,12},{8,0},{12,4},{1,9},{5,13},{9,1},{13,5},{2,10},{6,14},... | collective-permute-start | bytes 2162696 | tf_op jit(solution)/shard_map/ppermute | solution.py:958
  669.5 34.0 %collective-permute-start.43 = (bf16[4,32,1024]{2,1,0:T(8,128)(2,1)S(1)}, bf16[4,32,1024]{2,1,0:T(8,128)(2,1)S(1)}, u32[]{:S(2)}, u32[]{:S(2)}) collective-permute-start(bf16[4,32,1024]{2,1,0:T(8,128)(2,1)S(1)} %get-tuple-element.420), channel_id=1, source_target_pairs={{0,8},{4,12},{8,0},{12,4},{1,9},{5,13},{9,1},{13,5},{2,10},{6,14},... | collective-permute-start | bytes 786440 | tf_op jit(solution)/shard_map/ppermute | solution.py:958
  671.0 32.4 %collective-permute-start.44 = (bf16[128,1024]{1,0:T(8,128)(2,1)S(1)}, bf16[128,1024]{1,0:T(8,128)(2,1)S(1)}, u32[]{:S(2)}, u32[]{:S(2)}) collective-permute-start(bf16[128,1024]{1,0:T(8,128)(2,1)S(1)} %get-tuple-element.418), channel_id=1, source_target_pairs={{0,2},{1,3},{2,0},{3,1},{4,6},{5,7},{6,4},{7,5},{8,10},{9,11},{10,... | collective-permute-start | bytes 786440 | tf_op jit(solution)/shard_map/ppermute | solution.py:964
  709.3 114.7 %all-gather.11.cloned.1.call-start = ((), (), s32[]{:S(2)}) async-start(), calls=%async_computation.13 | async-start | bytes 2703360 | tf_op jit(solution)/shard_map/all_gather | solution.py:1402
  768.4 31.8 %collective-permute-start.57 = (bf16[256,1024]{1,0:T(8,128)(2,1)}, bf16[256,1024]{1,0:T(8,128)(2,1)S(1)}, u32[]{:S(2)}, u32[]{:S(2)}) collective-permute-start(bf16[256,1024]{1,0:T(8,128)(2,1)} %fusion.20), channel_id=1, source_target_pairs={{2,0},{3,1},{6,4},{7,5},{10,8},{11,9},{14,12},{15,13},{16,2},{17,3... | collective-permute-start | bytes 1572872 | tf_op jit(solution)/shard_map/ppermute | solution.py:946
  775.6 33.1 %collective-permute-start.55 = (bf16[128,1024]{1,0:T(8,128)(2,1)S(1)}, bf16[128,1024]{1,0:T(8,128)(2,1)S(1)}, u32[]{:S(2)}, u32[]{:S(2)}) collective-permute-start(bf16[128,1024]{1,0:T(8,128)(2,1)S(1)} %get-tuple-element.416), channel_id=1, source_target_pairs={{0,2},{1,3},{2,0},{3,1},{4,6},{5,7},{6,4},{7,5},{8,10},{9,11},{10,... | collective-permute-start | bytes 786440 | tf_op jit(solution)/shard_map/ppermute | solution.py:964
  (215 other events, 1895.2 us)
Sparse Core Ops, SparseCore 0:
  61.4 96.9 all-gather.6
  217.5 92.5 all-gather.8
  494.2 97.0 reduce-scatter.1
  709.4 54.9 all-gather.12
  766.9 36.2 all-gather.10

commit v6 on v5

--- a/solution.py
+++ b/solution.py
@@ -581,13 +581,41 @@
             acc = acc + dot(values_ref[chunk * CHUNK + entry], weights, 1, 0)
         return new_top, acc
 
+    def on_diagonal(carry):
+        top, acc = carry
+        parts_of, tops = [], []
+        for block in range(CHUNK):
+            columns = slice(block * block_width, width)
+            j = program * CHUNK + block
+            scores = dot(keys_ref[j], query[:, columns], 1, 0)
+            key_index = j * block_width + lax.broadcasted_iota(jnp.int32, (block_width, 1), 0)
+            allowed = (key_index >= start[:, columns]) & (key_index <= query_index[:, columns])
+            scores = jnp.where(allowed, scores, MASKED)
+            parts_of.append(scores)
+            part_top = fold_rows(scores, jnp.max)
+            if block > 0:
+                before = jnp.full((8, block * block_width), MASKED, jnp.float32)
+                part_top = jnp.concatenate([before, part_top], axis=1)
+            tops.append(part_top)
+        chunk_top = jnp.max(functools.reduce(jnp.maximum, tops), axis=0, keepdims=True)
+        new_top = jnp.maximum(top, chunk_top)
+        acc = acc * jnp.exp2(top - new_top)
+        for block, scores in enumerate(parts_of):
+            weights = jnp.exp2(scores - new_top[:, block * block_width :]).astype(jnp.bfloat16)
+            added = dot(values_ref[program * CHUNK + block], weights, 1, 0)
+            if block > 0:
+                before = jnp.zeros((HD + ONES, block * block_width), jnp.float32)
+                added = jnp.concatenate([before, added], axis=1)
+            acc = acc + added
+        return new_top, acc
+
     carry = (
         jnp.full((1, width), MASKED, jnp.float32),
         jnp.zeros((HD + ONES, width), jnp.float32),
     )
     carry = lax.fori_loop(low_chunk, middle, functools.partial(step, masked=True), carry)
     carry = lax.fori_loop(middle, program, functools.partial(step, masked=False), carry)
-    top, acc = step(program, carry, True)
+    top, acc = on_diagonal(carry)
     total = acc[HD : HD + 1]
     out = (acc[:HD] / total).astype(jnp.bfloat16)
     lse = top + jnp.log2(total)
@@ -689,8 +717,38 @@
         key_grad = key_grad + dot(query, grad_scores, 1, 1)
         return key_grad, value_grad
 
-    empty = jnp.zeros((HD, width), jnp.float32)
-    carry = step(program, (empty, empty), True)
+    key_grad = jnp.zeros((HD, width), jnp.float32)
+    value_grad = jnp.zeros((HD, width), jnp.float32)
+    own_query_grads = []
+    for block in range(CHUNK):
+        columns = slice(block * block_width, (block + 1) * block_width)
+        height = (block + 1) * block_width
+        query = queries_ref[program, :, columns]
+        grad = grads_ref[program, :, columns]
+        query_index = (
+            first + block * block_width + lax.broadcasted_iota(jnp.int32, (1, block_width), 1)
+        )
+        start = document_bounds(ends_ref, query_index)
+        rows_index = key_index[:height]
+        allowed = (rows_index >= start) & (rows_index <= query_index)
+        scores = dot(keys[:height], query, 1, 0)
+        weights = jnp.where(allowed, jnp.exp2(scores - lses_ref[program, :, columns]), 0.0)
+        grad_weights = dot(values[:height], grad, 1, 0)
+        grad_scores = (weights * (grad_weights - delta_ref[program, :, columns])).astype(
+            jnp.bfloat16
+        )
+        own_query_grads.append(dot(keys_t[:, :height], grad_scores, 1, 0))
+        added = (
+            dot(query, grad_scores, 1, 1),
+            dot(grad, weights.astype(jnp.bfloat16), 1, 1),
+        )
+        if height < width:
+            behind = jnp.zeros((HD, width - height), jnp.float32)
+            added = [jnp.concatenate([value, behind], axis=1) for value in added]
+        key_grad = key_grad + added[0]
+        value_grad = value_grad + added[1]
+    query_grad_ref[program] += jnp.concatenate(own_query_grads, axis=1)
+    carry = (key_grad, value_grad)
     carry = lax.fori_loop(program + 1, middle, functools.partial(step, masked=False), carry)
     key_grad, value_grad = lax.fori_loop(middle, stop, functools.partial(step, masked=True), carry)
     query_grad = query_grad_ref[program] * HD ** (-0.5)
@@ -1069,7 +1127,7 @@
     def nothing(value):
         return value
 
-    def layer_forward(whole_rows, first_values, layer, in_zero, in_first, in_second, in_third, in_fourth):
+    def layer_forward(whole_rows, first_values, layer, in_zero, in_first, in_second, in_middle, in_third, in_fourth):
         gain_first, gain_second = gain_sets[layer][0], gain_sets[layer][1]
         scale_first = lax.rsqrt(jnp.mean(whole_rows * whole_rows, axis=-1, keepdims=True) + EPSILON)
         normed = low(whole_rows * scale_first * gain_first)
@@ -1090,7 +1148,7 @@
         qkv = in_first(qkv)
         out, lse = attention_forward(ends, qkv, parts)
         out = in_second(out)
-        attended = head_halves(exchange(out, batch_groups))
+        attended = head_halves(in_middle(exchange(out, batch_groups)))
         hidden = whole_rows + dot(attended.reshape(-1, rows), w_outs[layer], 0, 0)
         scale_second = lax.rsqrt(jnp.mean(hidden * hidden, axis=-1, keepdims=True) + EPSILON)
         normed_second = low(hidden * scale_second * gain_second)
@@ -1247,7 +1305,7 @@
 
     first_result, first_values, first_saved = layer_forward(
         wide(rows_in), None, 0,
-        weights_zero, weights_line, weights_outs_first, weights_far, weights_heads,
+        weights_zero, weights_line, nothing, weights_outs_first, weights_far, weights_heads,
     )
 
     first_out = first_result()
@@ -1266,7 +1324,8 @@
         return value
 
     second_result, _, second_saved = layer_forward(
-        wide(first_out), first_values, 1, nothing, start_outs, end_outs, nothing, nothing
+        wide(first_out), first_values, 1,
+        nothing, start_outs, end_outs, nothing, nothing, nothing,
     )
     grad_in = pending["grad_in"]
 
@@ -1388,21 +1447,25 @@
 
     gain_rows = jnp.stack([first_gain1, first_gain2, second_gain1, second_gain2])
     gain_rows = summed(gain_rows, swap_section)
-    head, rest_a, rest_b, gain_rows, first_grad, home = together(
-        pending["head"], pending["rest_a"], pending["rest_b"], gain_rows, low(first_grad), second_grad
-    )
-    second_grad_home = to_home(home, 1)
+    head, rest_a, rest_b, gain_rows, first_grad = together(
+        pending["head"], pending["rest_a"], pending["rest_b"], gain_rows, low(first_grad)
+    )
     head = near_sum(jnp.concatenate([add(head), pending["out"]], axis=1))
     rest_b = far_sum(rest_b)
+    gain_rows = summed(summed(gain_rows, swap_side), swap_far)
+    head, rest_b, gain_rows, first_grad = together(head, rest_b, gain_rows, first_grad)
+    head = parted(add(head), batch, 0)
+    first_grad, home = together(after(first_grad, head), second_grad)
+    head = moved_pair(head, swap_half)
     first_grad_home = to_home(first_grad, 0)
-    gain_rows = summed(summed(gain_rows, swap_side), swap_far)
-    head, rest_b, gain_rows = together(head, rest_b, gain_rows)
-    head = far_sum(head)
+    second_grad_home = to_home(home, 1)
     rest = jnp.concatenate([add(rest_a), add(rest_b)], axis=0)
     rest = lax.all_gather(rest, "ctx", axis=0, tiled=False)
-    gain_total = summed(summed(gain_rows, swap_near), swap_half)
+    gain_rows = summed(gain_rows, swap_near)
     head, first_grad_home, second_grad_home = together(head, first_grad_home, second_grad_home)
     head = all_to_all(copies(add(head), contexts), "ctx")
+    head, gain_rows = together(head, gain_rows)
+    gain_total = summed(gain_rows, swap_half)
     rest, second, head = together(rest, pending["second"], head)
     first_grads = (rest, head)
     second_grads = (second[:, : 3 * unit_rows], second[:, 3 * unit_rows :])

time: 866 us -> 857 us (0.990)
  blocking collectives: 54.6 us -> 40.7 us
    ppermute x4, waiting for transfers between devices: 21.4 us -> 0.01 us  [to_home(): lax.ppermute(value, ALL_AXES, cross)]
    all_to_all x1 -> x0, blocking collectives: 15.1 us -> none  [all_to_all(): return lax.all_to_all(value, axis, split_axis=0, concat_axis=0, tiled=True)]
    ppermute x7, waiting for transfers between devices: 38.8 us -> 52.5 us  [swap_half(): lax.ppermute(value, 'tp', [(t, (t + half_parts) % parts) for t in range(p...]
    unnamed x331 -> x323, local copies, waits for them, and re-layouts: 45.5 us -> 46.6 us
  transfers between devices with their start and end apart: 76 -> 77, of which waited for: 33 -> 37; matrix products, arithmetic and copies ran while one was open for 11% -> 11% of each run, Pallas kernels for 20% -> 20%
where the time goes in v6:
time: 857 us; the launch traced here: 848 us
  waiting for transfers between devices  325 us (38%)
  Pallas kernels  183 us (21%)
  starting transfers between devices  112 us (13%)
  local copies, waits for them, and re-layouts  89.3 us (10%)
  other arithmetic  66.5 us (8%)
  blocking collectives  40.7 us (5%)
  between operations  16.9 us (2%)
  matrix products  14.7 us (2%)
    ppermute x17, waiting for transfers between devices, swap_side(): return lax.ppermute(value, 'ctx', [(c, c ^ 1) for c in range(contexts)])  105 us
    ppermute x8, waiting for transfers between devices, swap_far(): return lax.ppermute(value, 'ctx', [(c, c ^ 2) for c in range(contexts)])  69.5 us
    all_to_all x7, waiting for transfers between devices, exchange(): lax.all_to_all(value, ALL_AXES, split_axis=0, concat_axis=0, tiled=True,...  64.1 us
    pallas_call x2, Pallas kernels, attention_backward(): pl.pallas_call(functools.partial(attention_backward_kernel, parts), grid_...  62.4 us
    ppermute x7, waiting for transfers between devices, swap_half(): lax.ppermute(value, 'tp', [(t, (t + half_parts) % parts) for t in range(p...  52.5 us
    unnamed x323, local copies, waits for them, and re-layouts  46.6 us
    pallas_call x2, Pallas kernels, attention_forward(): pl.pallas_call(functools.partial(attention_forward_kernel, parts), grid_s...  42.1 us
    all_to_all x1, blocking collectives, exchange(): lax.all_to_all(value, ALL_AXES, split_axis=0, concat_axis=0, tiled=True,...  40.7 us
  transfers between devices with their start and end apart: 77, of which 37 were waited for; matrix products, arithmetic and copies ran while one was open for 11% of the time, Pallas kernels for 20%

profile of v6, /device:TPU:0, one launch (start us, length us, event | category | flops | bytes accessed | tf_op | source)
XLA Modules:
  0.0 848.3 jit_solution(4129620632249602501)
XLA Ops:
  27.9 14.8 %collective-permute-done.1 = bf16[128,1024]{1,0:T(8,128)(2,1)} collective-permute-done((bf16[128,1024]{1,0:T(8,128)(2,1)S(1)}, bf16[128,1024]{1,0:T(8,128)(2,1)}, u32[]{:S(2)}, u32[]{:S(2)}) %collective-permute-start.1) | collective-permute-done | bytes 262176 | tf_op jit(solution)/shard_map/ppermute | solution.py:1022
  44.8 14.3 %collective-permute-done.2 = bf16[2,128,1024]{2,1,0:T(8,128)(2,1)} collective-permute-done((bf16[2,128,1024]{2,1,0:T(8,128)(2,1)}, bf16[2,128,1024]{2,1,0:T(8,128)(2,1)}, u32[]{:S(2)}, u32[]{:S(2)}) %collective-permute-start.2) | collective-permute-done | bytes 524320 | tf_op jit(solution)/shard_map/ppermute | solution.py:1019
  66.2 12.2 %collective-permute-done.5 = bf16[256,1024]{1,0:T(8,128)(2,1)S(1)} collective-permute-done((bf16[256,1024]{1,0:T(8,128)(2,1)S(1)}, bf16[256,1024]{1,0:T(8,128)(2,1)S(1)}, u32[]{:S(2)}, u32[]{:S(2)}) %collective-permute-start.5) | collective-permute-done | bytes 524320 | tf_op jit(solution)/shard_map/ppermute | solution.py:1013
  79.2 14.6 %collective-permute-done.6 = bf16[4,128,1024]{2,1,0:T(8,128)(2,1)} collective-permute-done((bf16[4,128,1024]{2,1,0:T(8,128)(2,1)S(1)}, bf16[4,128,1024]{2,1,0:T(8,128)(2,1)}, u32[]{:S(2)}, u32[]{:S(2)}) %collective-permute-start.6) | collective-permute-done | bytes 1048608 | tf_op jit(solution)/shard_map/ppermute | solution.py:1016
  112.7 30.4 %all-to-all-done.qkv_ref = bf16[8,192,512]{2,1,0:T(8,128)(2,1)S(1)} async-done(((bf16[8,192,512]{2,1,0:T(8,128)(2,1)}), bf16[8,192,512]{2,1,0:T(8,128)(2,1)S(1)}, u32[]{:S(2)}, u32[]{:S(2)}) %all-to-all-start) | async-done | bytes 1572896 | tf_op jit(solution)/shard_map/all_to_all | solution.py:494
  143.0 21.4 %attention_forward.2 = (bf16[16,64,256]{2,1,0:T(8,128)(2,1)}, f32[16,1,256]{2,1,0:T(1,128)S(1)}) custom-call(s32[4]{0:T(128)S(1)} %bitcast.339, bf16[8,192,512]{2,1,0:T(8,128)(2,1)S(1)} %all-to-all-done.qkv_ref), custom_call_target="tpu_custom_call" | custom-call | flops 1 | bytes 1 | tf_op jit(solution)/shard_map/attention_forward/pallas_call | solution.py:630
  180.7 8.1 collective-permute-done.8
  220.2 12.1 %collective-permute-done.13 = bf16[256,1024]{1,0:T(8,128)(2,1)S(1)} collective-permute-done((bf16[256,1024]{1,0:T(8,128)(2,1)S(1)}, bf16[256,1024]{1,0:T(8,128)(2,1)S(1)}, u32[]{:S(2)}, u32[]{:S(2)}) %collective-permute-start.13) | collective-permute-done | bytes 524320 | tf_op jit(solution)/shard_map/ppermute | solution.py:1013
  232.3 10.8 %collective-permute-done.14 = bf16[4,128,1024]{2,1,0:T(8,128)(2,1)S(1)} collective-permute-done((bf16[4,128,1024]{2,1,0:T(8,128)(2,1)S(1)}, bf16[4,128,1024]{2,1,0:T(8,128)(2,1)S(1)}, u32[]{:S(2)}, u32[]{:S(2)}) %collective-permute-start.14) | collective-permute-done | bytes 1048608 | tf_op jit(solution)/shard_map/ppermute | solution.py:1016
  246.8 11.6 %collective-permute-done.15 = bf16[256,1024]{1,0:T(8,128)(2,1)S(1)} collective-permute-done((bf16[256,1024]{1,0:T(8,128)(2,1)S(1)}, bf16[256,1024]{1,0:T(8,128)(2,1)S(1)}, u32[]{:S(2)}, u32[]{:S(2)}) %collective-permute-start.15) | collective-permute-done | bytes 524320 | tf_op jit(solution)/shard_map/ppermute | solution.py:1013
  263.2 40.7 %all_to_all.45.qkv_ref = bf16[8,192,512]{2,1,0:T(8,128)(2,1)S(1)} all-to-all(bf16[8,192,512]{2,1,0:T(8,128)(2,1)S(1)} %fusion.53), channel_id=1, replica_groups={{0,1,16,17,8,9,24,25},{2,3,18,19,10,11,26,27},{4,5,20,21,12,13,28,29},{..., dimensions={0} | all-to-all | bytes 3145728 | tf_op jit(solution)/shard_map/all_to_all | solution.py:494
  307.2 20.7 %attention_forward.3 = (bf16[16,64,256]{2,1,0:T(8,128)(2,1)S(1)}, f32[16,1,256]{2,1,0:T(1,128)S(1)}) custom-call(s32[4]{0:T(128)S(1)} %bitcast.340, bf16[8,192,512]{2,1,0:T(8,128)(2,1)S(1)} %all_to_all.45.qkv_ref), custom_call_target="tpu_custom_call" | custom-call | flops 1 | bytes 1 | tf_op jit(solution)/shard_map/attention_forward/pallas_call | solution.py:630
  379.8 7.6 feed_forward_back.5
  393.5 14.1 %collective-permute-done.22 = bf16[256,1024]{1,0:T(8,128)(2,1)S(1)} collective-permute-done((bf16[256,1024]{1,0:T(8,128)(2,1)S(1)}, bf16[256,1024]{1,0:T(8,128)(2,1)S(1)}, u32[]{:S(2)}, u32[]{:S(2)}) %collective-permute-start.22) | collective-permute-done | bytes 524320 | tf_op jit(solution)/shard_map/ppermute | solution.py:1013
  442.4 30.6 %attention_backward.2 = bf16[8,192,512]{2,1,0:T(8,128)(2,1)S(1)} custom-call(s32[4]{0:T(128)S(1)} %bitcast.341, bf16[8,192,512]{2,1,0:T(8,128)(2,1)S(1)} %copy-done.17, bf16[16,64,256]{2,1,0:T(8,128)(2,1)S(1)} %copy-done.68, bf16[16,64,256]{2,1,0:T(8,128)(2,1)} %all-to-all-done.4.grad_ref, f32[16,1,256]{2,1,0:T(1,128)S(1)} %get-tuple-element.213.lse_ref), custom_call_target="tpu_custom_call" | custom-call | flops 1 | bytes 1 | tf_op jit(solution)/shard_map/attention_backward/pallas_call | solution.py:770
  483.0 26.4 %all-to-all-done.5 = bf16[8,192,512]{2,1,0:T(8,128)(2,1)} async-done(((bf16[8,192,512]{2,1,0:T(8,128)(2,1)}), bf16[8,192,512]{2,1,0:T(8,128)(2,1)}, u32[]{:S(2)}, u32[]{:S(2)}) %all-to-all-start.5) | async-done | bytes 1572896 | tf_op jit(solution)/shard_map/all_to_all | solution.py:494
  521.2 10.4 %collective-permute-done.29 = bf16[256,1024]{1,0:T(8,128)(2,1)S(1)} collective-permute-done((bf16[256,1024]{1,0:T(8,128)(2,1)S(1)}, bf16[256,1024]{1,0:T(8,128)(2,1)S(1)}, u32[]{:S(2)}, u32[]{:S(2)}) %collective-permute-start.29) | collective-permute-done | bytes 524320 | tf_op jit(solution)/shard_map/ppermute | solution.py:1013
  552.3 7.5 feed_forward_back.7
  566.8 13.4 %collective-permute-done.32 = bf16[256,1024]{1,0:T(8,128)(2,1)S(1)} collective-permute-done((bf16[256,1024]{1,0:T(8,128)(2,1)S(1)}, bf16[256,1024]{1,0:T(8,128)(2,1)S(1)}, u32[]{:S(2)}, u32[]{:S(2)}) %collective-permute-start.32) | collective-permute-done | bytes 524320 | tf_op jit(solution)/shard_map/ppermute | solution.py:1013
  618.0 31.8 %attention_backward.3 = bf16[8,192,512]{2,1,0:T(8,128)(2,1)} custom-call(s32[4]{0:T(128)S(1)} %bitcast.342, bf16[8,192,512]{2,1,0:T(8,128)(2,1)S(1)} %copy-done.15, bf16[16,64,256]{2,1,0:T(8,128)(2,1)} %get-tuple-element.164.out_ref, bf16[16,64,256]{2,1,0:T(8,128)(2,1)} %all-to-all-done.6.grad_ref, f32[16,1,256]{2,1,0:T(1,128)S(1)} %get-tuple-element.246.lse_ref), custom_call_target="tpu_custom_call" | custom-call | flops 1 | bytes 1 | tf_op jit(solution)/shard_map/attention_backward/pallas_call | solution.py:770
  668.1 27.8 %collective-permute-done.43 = bf16[4,32,1024]{2,1,0:T(8,128)(2,1)S(1)} collective-permute-done((bf16[4,32,1024]{2,1,0:T(8,128)(2,1)S(1)}, bf16[4,32,1024]{2,1,0:T(8,128)(2,1)S(1)}, u32[]{:S(2)}, u32[]{:S(2)}) %collective-permute-start.43) | collective-permute-done | bytes 262176 | tf_op jit(solution)/shard_map/ppermute | solution.py:1016
  720.8 12.8 %collective-permute-done.49 = bf16[256,1024]{1,0:T(8,128)(2,1)S(1)} collective-permute-done((bf16[256,1024]{1,0:T(8,128)(2,1)S(1)}, bf16[256,1024]{1,0:T(8,128)(2,1)S(1)}, u32[]{:S(2)}, u32[]{:S(2)}) %collective-permute-start.49) | collective-permute-done | bytes 524320 | tf_op jit(solution)/shard_map/ppermute | solution.py:1013
  735.4 7.1 collective-permute-done.46
  772.6 28.5 %collective-permute-done.55 = bf16[128,1024]{1,0:T(8,128)(2,1)S(1)} collective-permute-done((bf16[128,1024]{1,0:T(8,128)(2,1)S(1)}, bf16[128,1024]{1,0:T(8,128)(2,1)S(1)}, u32[]{:S(2)}, u32[]{:S(2)}) %collective-permute-start.55) | collective-permute-done | bytes 262176 | tf_op jit(solution)/shard_map/ppermute | solution.py:1022
  (676 shorter events, 401.6 us)
Async XLA Ops:
  7.2 167.7 %all-gather.7.cloned.1.call-start = ((), (), s32[]{:S(2)}) async-start(), calls=%async_computation.10 | async-start | bytes 9191424 | tf_op jit(solution)/shard_map/all_gather | solution.py:1034
  107.4 35.6 %all-to-all-start = ((bf16[8,192,512]{2,1,0:T(8,128)(2,1)}), bf16[8,192,512]{2,1,0:T(8,128)(2,1)S(1)}, u32[]{:S(2)}, u32[]{:S(2)}) async-start(bf16[8,192,512]{2,1,0:T(8,128)(2,1)} %fusion.62), calls=%async_computation | async-start | bytes 3145728 | tf_op jit(solution)/shard_map/all_to_all | solution.py:494
  168.7 160.2 %all-gather.9.cloned.1.call-start = ((), (), s32[]{:S(2)}) async-start(), calls=%async_computation.11 | async-start | bytes 9191424 | tf_op jit(solution)/shard_map/all_gather | solution.py:1034
  432.2 40.7 %collective-permute-start.27 = (bf16[256,1024]{1,0:T(8,128)(2,1)}, bf16[256,1024]{1,0:T(8,128)(2,1)}, u32[]{:S(2)}, u32[]{:S(2)}) collective-permute-start(bf16[256,1024]{1,0:T(8,128)(2,1)} %convert_element_type.435), channel_id=1, source_target_pairs={{0,4},{4,0},{8,12},{12,8},{1,5},{5,1},{9,13},{13,9},{2,6},{6,2},{1... | collective-permute-start | bytes 1572872 | tf_op jit(solution)/shard_map/ppermute | solution.py:1013
  433.9 41.6 %collective-permute-start.25 = (bf16[256,1024]{1,0:T(8,128)(2,1)}, bf16[256,1024]{1,0:T(8,128)(2,1)S(1)}, u32[]{:S(2)}, u32[]{:S(2)}) collective-permute-start(bf16[256,1024]{1,0:T(8,128)(2,1)} %copy-done.90), channel_id=1, source_target_pairs={{0,0},{1,1},{4,4},{5,5},{8,8},{9,9},{12,12},{13,13},{18,2},{19,3},... | collective-permute-start | bytes 1572872 | tf_op jit(solution)/shard_map/ppermute | solution.py:1004
  435.6 40.7 %collective-permute-start.26 = (bf16[256,1024]{1,0:T(8,128)(2,1)}, bf16[256,1024]{1,0:T(8,128)(2,1)S(1)}, u32[]{:S(2)}, u32[]{:S(2)}) collective-permute-start(bf16[256,1024]{1,0:T(8,128)(2,1)} %copy-done.90), channel_id=1, source_target_pairs={{2,0},{3,1},{6,4},{7,5},{10,8},{11,9},{14,12},{15,13},{16,2},{17,3... | collective-permute-start | bytes 1572872 | tf_op jit(solution)/shard_map/ppermute | solution.py:1004
  441.6 35.5 %collective-permute-start.28 = (bf16[2,4,32,1024]{3,2,1,0:T(8,128)(2,1)S(1)}, bf16[2,4,32,1024]{3,2,1,0:T(8,128)(2,1)S(1)}, u32[]{:S(2)}, u32[]{:S(2)}) collective-permute-start(bf16[2,4,32,1024]{3,2,1,0:T(8,128)(2,1)S(1)} %get-tuple-element.408), channel_id=1, source_target_pairs={{0,4},{4,0},{8,12},{12,8},{1,5},{5,1},{9,13},{13,9},{2,6},{6,2},{1... | collective-permute-start | bytes 1572872 | tf_op jit(solution)/shard_map/ppermute | solution.py:1013
  478.0 31.4 %all-to-all-start.5 = ((bf16[8,192,512]{2,1,0:T(8,128)(2,1)}), bf16[8,192,512]{2,1,0:T(8,128)(2,1)}, u32[]{:S(2)}, u32[]{:S(2)}) async-start(bf16[8,192,512]{2,1,0:T(8,128)(2,1)} %copy-done.27), calls=%async_computation.5 | async-start | bytes 3145728 | tf_op jit(solution)/shard_map/all_to_all | solution.py:494
  482.3 131.6 %reduce-scatter.2.cloned.1.call-start = ((), (), s32[]{:S(2)}) async-start(), calls=%async_computation.12 | async-start | bytes 4866048 | tf_op jit(solution)/shard_map/reduce_scatter | solution.py:1267
  613.8 36.0 %collective-permute-start.38 = (bf16[4,176,1024]{2,1,0:T(8,128)(2,1)}, bf16[4,176,1024]{2,1,0:T(8,128)(2,1)}, u32[]{:S(2)}, u32[]{:S(2)}) collective-permute-start(bf16[4,176,1024]{2,1,0:T(8,128)(2,1)} %get-tuple-element.248), channel_id=1, source_target_pairs={{0,8},{4,12},{8,0},{12,4},{1,9},{5,13},{9,1},{13,5},{2,10},{6,14},... | collective-permute-start | bytes 4325384 | tf_op jit(solution)/shard_map/ppermute | solution.py:1016
  614.3 35.6 %collective-permute-start.39 = (bf16[2,4,32,1024]{3,2,1,0:T(8,128)(2,1)}, bf16[2,4,32,1024]{3,2,1,0:T(8,128)(2,1)S(1)}, u32[]{:S(2)}, u32[]{:S(2)}) collective-permute-start(bf16[2,4,32,1024]{3,2,1,0:T(8,128)(2,1)} %get-tuple-element.252), channel_id=1, source_target_pairs={{0,4},{4,0},{8,12},{12,8},{1,5},{5,1},{9,13},{13,9},{2,6},{6,2},{1... | collective-permute-start | bytes 1572872 | tf_op jit(solution)/shard_map/ppermute | solution.py:1013
  616.7 33.1 %collective-permute-start.40 = (bf16[2,128,1024]{2,1,0:T(8,128)(2,1)S(1)}, bf16[2,128,1024]{2,1,0:T(8,128)(2,1)S(1)}, u32[]{:S(2)}, u32[]{:S(2)}) collective-permute-start(bf16[2,128,1024]{2,1,0:T(8,128)(2,1)S(1)} %get-tuple-element.404), channel_id=1, source_target_pairs={{0,1},{1,0},{2,3},{3,2},{4,5},{5,4},{6,7},{7,6},{8,9},{9,8},{10,11... | collective-permute-start | bytes 1572872 | tf_op jit(solution)/shard_map/ppermute | solution.py:1019
  650.6 47.0 %all-to-all-start.7 = ((bf16[8,192,512]{2,1,0:T(8,128)(2,1)}), bf16[8,192,512]{2,1,0:T(8,128)(2,1)S(1)}, u32[]{:S(2)}, u32[]{:S(2)}) async-start(bf16[8,192,512]{2,1,0:T(8,128)(2,1)} %attention_backward.3), calls=%async_computation.8 | async-start | bytes 3145728 | tf_op jit(solution)/shard_map/all_to_all | solution.py:494
  654.8 162.6 %all-gather.13.cloned.1.call-start = ((), (), s32[]{:S(2)}) async-start(), calls=%async_computation.14 | async-start | bytes 4014080 | tf_op jit(solution)/shard_map/all_gather | solution.py:1418
  658.2 38.2 %collective-permute-start.41 = (bf16[2,176,1024]{2,1,0:T(8,128)(2,1)S(1)}, bf16[2,176,1024]{2,1,0:T(8,128)(2,1)S(1)}, u32[]{:S(2)}, u32[]{:S(2)}) collective-permute-start(bf16[2,176,1024]{2,1,0:T(8,128)(2,1)S(1)} %get-tuple-element.396), channel_id=1, source_target_pairs={{0,1},{1,0},{2,3},{3,2},{4,5},{5,4},{6,7},{7,6},{8,9},{9,8},{10,11... | collective-permute-start | bytes 2162696 | tf_op jit(solution)/shard_map/ppermute | solution.py:1019
  660.2 37.4 %collective-permute-start.42 = (bf16[4,88,1024]{2,1,0:T(8,128)(2,1)S(1)}, bf16[4,88,1024]{2,1,0:T(8,128)(2,1)}, u32[]{:S(2)}, u32[]{:S(2)}) collective-permute-start(bf16[4,88,1024]{2,1,0:T(8,128)(2,1)S(1)} %copy-done.137), channel_id=1, source_target_pairs={{0,8},{4,12},{8,0},{12,4},{1,9},{5,13},{9,1},{13,5},{2,10},{6,14},... | collective-permute-start | bytes 2162696 | tf_op jit(solution)/shard_map/ppermute | solution.py:1016
  662.0 34.0 %collective-permute-start.43 = (bf16[4,32,1024]{2,1,0:T(8,128)(2,1)S(1)}, bf16[4,32,1024]{2,1,0:T(8,128)(2,1)S(1)}, u32[]{:S(2)}, u32[]{:S(2)}) collective-permute-start(bf16[4,32,1024]{2,1,0:T(8,128)(2,1)S(1)} %get-tuple-element.430), channel_id=1, source_target_pairs={{0,8},{4,12},{8,0},{12,4},{1,9},{5,13},{9,1},{13,5},{2,10},{6,14},... | collective-permute-start | bytes 786440 | tf_op jit(solution)/shard_map/ppermute | solution.py:1016
  663.5 32.4 %collective-permute-start.44 = (bf16[128,1024]{1,0:T(8,128)(2,1)S(1)}, bf16[128,1024]{1,0:T(8,128)(2,1)S(1)}, u32[]{:S(2)}, u32[]{:S(2)}) collective-permute-start(bf16[128,1024]{1,0:T(8,128)(2,1)S(1)} %get-tuple-element.428), channel_id=1, source_target_pairs={{0,2},{1,3},{2,0},{3,1},{4,6},{5,7},{6,4},{7,5},{8,10},{9,11},{10,... | collective-permute-start | bytes 786440 | tf_op jit(solution)/shard_map/ppermute | solution.py:1022
  701.8 115.5 %all-gather.11.cloned.1.call-start = ((), (), s32[]{:S(2)}) async-start(), calls=%async_computation.13 | async-start | bytes 2703360 | tf_op jit(solution)/shard_map/all_gather | solution.py:1463
  760.1 41.1 %collective-permute-start.56 = (bf16[256,1024]{1,0:T(8,128)(2,1)S(1)}, bf16[256,1024]{1,0:T(8,128)(2,1)S(1)}, u32[]{:S(2)}, u32[]{:S(2)}) collective-permute-start(bf16[256,1024]{1,0:T(8,128)(2,1)S(1)} %fusion.20), channel_id=1, source_target_pairs={{0,0},{1,1},{4,4},{5,5},{8,8},{9,9},{12,12},{13,13},{18,2},{19,3},... | collective-permute-start | bytes 1572872 | tf_op jit(solution)/shard_map/ppermute | solution.py:1004
  760.8 40.4 %collective-permute-start.57 = (bf16[256,1024]{1,0:T(8,128)(2,1)S(1)}, bf16[256,1024]{1,0:T(8,128)(2,1)S(1)}, u32[]{:S(2)}, u32[]{:S(2)}) collective-permute-start(bf16[256,1024]{1,0:T(8,128)(2,1)S(1)} %fusion.20), channel_id=1, source_target_pairs={{2,0},{3,1},{6,4},{7,5},{10,8},{11,9},{14,12},{15,13},{16,2},{17,3... | collective-permute-start | bytes 1572872 | tf_op jit(solution)/shard_map/ppermute | solution.py:1004
  762.1 39.1 %collective-permute-start.58 = (bf16[256,1024]{1,0:T(8,128)(2,1)S(1)}, bf16[256,1024]{1,0:T(8,128)(2,1)S(1)}, u32[]{:S(2)}, u32[]{:S(2)}) collective-permute-start(bf16[256,1024]{1,0:T(8,128)(2,1)S(1)} %fusion.27.grad_ref.refs_8_), channel_id=1, source_target_pairs={{0,16},{1,17},{4,20},{5,21},{8,24},{9,25},{12,28},{13,29},{18,18},... | collective-permute-start | bytes 1572872 | tf_op jit(solution)/shard_map/ppermute | solution.py:1004
  768.0 34.0 %collective-permute-start.59 = (bf16[256,1024]{1,0:T(8,128)(2,1)S(1)}, bf16[256,1024]{1,0:T(8,128)(2,1)}, u32[]{:S(2)}, u32[]{:S(2)}) collective-permute-start(bf16[256,1024]{1,0:T(8,128)(2,1)S(1)} %fusion.27.grad_ref.refs_8_), channel_id=1, source_target_pairs={{2,16},{3,17},{6,20},{7,21},{10,24},{11,25},{14,28},{15,29},{16,18... | collective-permute-start | bytes 1572872 | tf_op jit(solution)/shard_map/ppermute | solution.py:1004
  769.5 31.7 %collective-permute-start.55 = (bf16[128,1024]{1,0:T(8,128)(2,1)S(1)}, bf16[128,1024]{1,0:T(8,128)(2,1)S(1)}, u32[]{:S(2)}, u32[]{:S(2)}) collective-permute-start(bf16[128,1024]{1,0:T(8,128)(2,1)S(1)} %get-tuple-element.426), channel_id=1, source_target_pairs={{0,2},{1,3},{2,0},{3,1},{4,6},{5,7},{6,4},{7,5},{8,10},{9,11},{10,... | collective-permute-start | bytes 786440 | tf_op jit(solution)/shard_map/ppermute | solution.py:1022
  (212 other events, 1886.3 us)
Sparse Core Ops, SparseCore 0:
  61.4 96.9 all-gather.6
  211.3 93.4 all-gather.8
  487.3 97.2 reduce-scatter.1
  701.9 55.6 all-gather.12
  760.0 36.2 all-gather.10

commit v7 on v6

--- a/solution.py
+++ b/solution.py
@@ -1405,25 +1405,17 @@
             value, pending["rest_a"], pending["rest_b"], pending["out"], pending["head"]
         )
         pending["head"] = far_sum(head)
+        pending["second_rest"] = lax.all_gather(
+            after(pending["second_rest"], value), "ctx", axis=0, tiled=False
+        )
         pending["rest_b"] = moved_pair(rest_b, swap_far)
         pending["rest_a"] = near_sum(add(rest_a))
         pending["out"] = halve(add(out_sum), row_side, swap_far, 0)
         return value
 
-    def first_fifth(value):
-        value, rest_a, rest_b, out_sum, head = together(
-            value, pending["rest_a"], pending["rest_b"], pending["out"], pending["head"]
-        )
-        second = jnp.concatenate([pending["second_rest"], add(head)], axis=0)
-        pending["second"] = lax.all_gather(second, "ctx", axis=0, tiled=False)
-        pending["out"] = add(out_sum)
-        pending["rest_a"] = far_sum(rest_a)
-        pending["rest_b"] = near_sum(add(rest_b))
-        return value
-
     first_halves, _, first_hidden, _, first_gain2 = layer_backward(
         second_grad, send_values, first_saved, 0,
-        first_first, first_second, first_third, first_fourth, first_fifth,
+        first_first, first_second, first_third, first_fourth, nothing,
     )
     head_products = functools.partial(
         half_products,
@@ -1436,7 +1428,14 @@
     def head_end(value):
         head = head_products(section, addend=moved).reshape(2, parts, head_rows, model_width)
         head = parted(head, row_side, 0)
+        head, rest_a, rest_b, out_sum, second_head = together(
+            head, pending["rest_a"], pending["rest_b"], pending["out"], pending["head"]
+        )
         pending["head"] = moved_pair(head, swap_far)
+        pending["rest_b"] = near_sum(add(rest_b))
+        pending["rest_a"] = far_sum(rest_a)
+        pending["out"] = add(out_sum)
+        pending["second_head"] = add(second_head)
         return after(value, head)
 
     first_gain1, first_grad = input_grads_of(
@@ -1453,22 +1452,25 @@
     head = near_sum(jnp.concatenate([add(head), pending["out"]], axis=1))
     rest_b = far_sum(rest_b)
     gain_rows = summed(summed(gain_rows, swap_side), swap_far)
-    head, rest_b, gain_rows, first_grad = together(head, rest_b, gain_rows, first_grad)
-    head = parted(add(head), batch, 0)
-    first_grad, home = together(after(first_grad, head), second_grad)
-    head = moved_pair(head, swap_half)
-    first_grad_home = to_home(first_grad, 0)
-    second_grad_home = to_home(home, 1)
+    head, rest_b, gain_rows, first_grad, second_rest = together(
+        head, rest_b, gain_rows, first_grad, pending["second_rest"]
+    )
+    head = far_sum(head)
     rest = jnp.concatenate([add(rest_a), add(rest_b)], axis=0)
     rest = lax.all_gather(rest, "ctx", axis=0, tiled=False)
     gain_rows = summed(gain_rows, swap_near)
-    head, first_grad_home, second_grad_home = together(head, first_grad_home, second_grad_home)
-    head = all_to_all(copies(add(head), contexts), "ctx")
-    head, gain_rows = together(head, gain_rows)
+    head, first_grad, home = together(head, first_grad, second_grad)
+    first_grad_home = to_home(first_grad, 0)
+    second_grad_home = to_home(home, 1)
+    head = jnp.concatenate([add(head), pending["second_head"]], axis=0)
+    head = all_to_all(copies(head, contexts), "ctx")
+    head, gain_rows, first_grad_home, second_grad_home = together(
+        head, gain_rows, first_grad_home, second_grad_home
+    )
     gain_total = summed(gain_rows, swap_half)
-    rest, second, head = together(rest, pending["second"], head)
-    first_grads = (rest, head)
-    second_grads = (second[:, : 3 * unit_rows], second[:, 3 * unit_rows :])
+    rest, head = together(rest, head)
+    first_grads = (rest, head[:, :attention_rows])
+    second_grads = (second_rest, head[:, attention_rows:])
     first_home, second_home = pending["first_home"], pending["second_home"]
     gain_total = jnp.where(leading, gain_total[:2], gain_total[2:])
 

time: 857 us -> 838 us (0.978)
  waiting for transfers between devices: 325 us -> 292 us
    ppermute x8, waiting for transfers between devices: 69.5 us -> 34.6 us  [swap_far(): return lax.ppermute(value, 'ctx', [(c, c ^ 2) for c in range(contexts)])]
    ppermute x7, waiting for transfers between devices: 52.5 us -> 36.9 us  [swap_half(): lax.ppermute(value, 'tp', [(t, (t + half_parts) % parts) for t in range(p...]
    all_to_all x7, waiting for transfers between devices: 64.1 us -> 76.2 us  [exchange(): lax.all_to_all(value, ALL_AXES, split_axis=0, concat_axis=0, tiled=True,...]
    ppermute x4, waiting for transfers between devices: 0.01 us -> 10.9 us  [to_home(): lax.ppermute(value, ALL_AXES, cross)]
    unnamed x323 -> x317, local copies, waits for them, and re-layouts: 46.6 us -> 46.7 us
  transfers between devices with their start and end apart: 77 -> 77, of which waited for: 37 -> 38; matrix products, arithmetic and copies ran while one was open for 11% -> 13% of each run, Pallas kernels for 20% -> 20%
where the time goes in v7:
time: 838 us; the launch traced here: 827 us
  waiting for transfers between devices  292 us (35%)
  Pallas kernels  185 us (22%)
  starting transfers between devices  115 us (14%)
  local copies, waits for them, and re-layouts  91.2 us (11%)
  other arithmetic  72.2 us (9%)
  blocking collectives  40.8 us (5%)
  between operations  16.8 us (2%)
  matrix products  14.7 us (2%)
    ppermute x17, waiting for transfers between devices, swap_side(): return lax.ppermute(value, 'ctx', [(c, c ^ 1) for c in range(contexts)])  96.2 us
    all_to_all x7, waiting for transfers between devices, exchange(): lax.all_to_all(value, ALL_AXES, split_axis=0, concat_axis=0, tiled=True,...  76.2 us
    pallas_call x2, Pallas kernels, attention_backward(): pl.pallas_call(functools.partial(attention_backward_kernel, parts), grid_...  62 us
    unnamed x317, local copies, waits for them, and re-layouts  46.7 us
    pallas_call x2, Pallas kernels, attention_forward(): pl.pallas_call(functools.partial(attention_forward_kernel, parts), grid_s...  41.8 us
    all_to_all x1, blocking collectives, exchange(): lax.all_to_all(value, ALL_AXES, split_axis=0, concat_axis=0, tiled=True,...  40.8 us
    ppermute x7, waiting for transfers between devices, swap_half(): lax.ppermute(value, 'tp', [(t, (t + half_parts) % parts) for t in range(p...  36.9 us
    pallas_call x12, Pallas kernels, half_products(): pl.pallas_call(functools.partial(half_products_kernel, tuple(layout), siz...  35.9 us
  transfers between devices with their start and end apart: 77, of which 38 were waited for; matrix products, arithmetic and copies ran while one was open for 13% of the time, Pallas kernels for 20%

profile of v7, /device:TPU:0, one launch (start us, length us, event | category | flops | bytes accessed | tf_op | source)
XLA Modules:
  0.0 826.5 jit_solution(3812771923390936126)
XLA Ops:
  27.9 14.8 %collective-permute-done.1 = bf16[128,1024]{1,0:T(8,128)(2,1)} collective-permute-done((bf16[128,1024]{1,0:T(8,128)(2,1)S(1)}, bf16[128,1024]{1,0:T(8,128)(2,1)}, u32[]{:S(2)}, u32[]{:S(2)}) %collective-permute-start.1) | collective-permute-done | bytes 262176 | tf_op jit(solution)/shard_map/ppermute | solution.py:1022
  44.8 14.3 %collective-permute-done.2 = bf16[2,128,1024]{2,1,0:T(8,128)(2,1)} collective-permute-done((bf16[2,128,1024]{2,1,0:T(8,128)(2,1)}, bf16[2,128,1024]{2,1,0:T(8,128)(2,1)}, u32[]{:S(2)}, u32[]{:S(2)}) %collective-permute-start.2) | collective-permute-done | bytes 524320 | tf_op jit(solution)/shard_map/ppermute | solution.py:1019
  66.2 12.2 %collective-permute-done.5 = bf16[256,1024]{1,0:T(8,128)(2,1)S(1)} collective-permute-done((bf16[256,1024]{1,0:T(8,128)(2,1)S(1)}, bf16[256,1024]{1,0:T(8,128)(2,1)S(1)}, u32[]{:S(2)}, u32[]{:S(2)}) %collective-permute-start.5) | collective-permute-done | bytes 524320 | tf_op jit(solution)/shard_map/ppermute | solution.py:1013
  79.2 14.6 %collective-permute-done.6 = bf16[4,128,1024]{2,1,0:T(8,128)(2,1)} collective-permute-done((bf16[4,128,1024]{2,1,0:T(8,128)(2,1)S(1)}, bf16[4,128,1024]{2,1,0:T(8,128)(2,1)}, u32[]{:S(2)}, u32[]{:S(2)}) %collective-permute-start.6) | collective-permute-done | bytes 1048608 | tf_op jit(solution)/shard_map/ppermute | solution.py:1016
  112.6 30.4 %all-to-all-done.qkv_ref = bf16[8,192,512]{2,1,0:T(8,128)(2,1)S(1)} async-done(((bf16[8,192,512]{2,1,0:T(8,128)(2,1)}), bf16[8,192,512]{2,1,0:T(8,128)(2,1)S(1)}, u32[]{:S(2)}, u32[]{:S(2)}) %all-to-all-start) | async-done | bytes 1572896 | tf_op jit(solution)/shard_map/all_to_all | solution.py:494
  143.0 21.2 %attention_forward.2 = (bf16[16,64,256]{2,1,0:T(8,128)(2,1)}, f32[16,1,256]{2,1,0:T(1,128)S(1)}) custom-call(s32[4]{0:T(128)S(1)} %bitcast.342, bf16[8,192,512]{2,1,0:T(8,128)(2,1)S(1)} %all-to-all-done.qkv_ref), custom_call_target="tpu_custom_call" | custom-call | flops 1 | bytes 1 | tf_op jit(solution)/shard_map/attention_forward/pallas_call | solution.py:630
  180.6 8.0 collective-permute-done.8
  220.0 12.1 %collective-permute-done.13 = bf16[256,1024]{1,0:T(8,128)(2,1)S(1)} collective-permute-done((bf16[256,1024]{1,0:T(8,128)(2,1)S(1)}, bf16[256,1024]{1,0:T(8,128)(2,1)S(1)}, u32[]{:S(2)}, u32[]{:S(2)}) %collective-permute-start.13) | collective-permute-done | bytes 524320 | tf_op jit(solution)/shard_map/ppermute | solution.py:1013
  232.1 10.8 %collective-permute-done.14 = bf16[4,128,1024]{2,1,0:T(8,128)(2,1)S(1)} collective-permute-done((bf16[4,128,1024]{2,1,0:T(8,128)(2,1)S(1)}, bf16[4,128,1024]{2,1,0:T(8,128)(2,1)S(1)}, u32[]{:S(2)}, u32[]{:S(2)}) %collective-permute-start.14) | collective-permute-done | bytes 1048608 | tf_op jit(solution)/shard_map/ppermute | solution.py:1016
  246.6 11.6 %collective-permute-done.15 = bf16[256,1024]{1,0:T(8,128)(2,1)S(1)} collective-permute-done((bf16[256,1024]{1,0:T(8,128)(2,1)S(1)}, bf16[256,1024]{1,0:T(8,128)(2,1)S(1)}, u32[]{:S(2)}, u32[]{:S(2)}) %collective-permute-start.15) | collective-permute-done | bytes 524320 | tf_op jit(solution)/shard_map/ppermute | solution.py:1013
  263.0 40.8 %all_to_all.45.qkv_ref = bf16[8,192,512]{2,1,0:T(8,128)(2,1)S(1)} all-to-all(bf16[8,192,512]{2,1,0:T(8,128)(2,1)S(1)} %fusion.53), channel_id=1, replica_groups={{0,1,16,17,8,9,24,25},{2,3,18,19,10,11,26,27},{4,5,20,21,12,13,28,29},{..., dimensions={0} | all-to-all | bytes 3145728 | tf_op jit(solution)/shard_map/all_to_all | solution.py:494
  307.1 20.6 %attention_forward.3 = (bf16[16,64,256]{2,1,0:T(8,128)(2,1)S(1)}, f32[16,1,256]{2,1,0:T(1,128)S(1)}) custom-call(s32[4]{0:T(128)S(1)} %bitcast.343, bf16[8,192,512]{2,1,0:T(8,128)(2,1)S(1)} %all_to_all.45.qkv_ref), custom_call_target="tpu_custom_call" | custom-call | flops 1 | bytes 1 | tf_op jit(solution)/shard_map/attention_forward/pallas_call | solution.py:630
  379.6 7.6 feed_forward_back.5
  393.4 14.1 %collective-permute-done.22 = bf16[256,1024]{1,0:T(8,128)(2,1)S(1)} collective-permute-done((bf16[256,1024]{1,0:T(8,128)(2,1)S(1)}, bf16[256,1024]{1,0:T(8,128)(2,1)S(1)}, u32[]{:S(2)}, u32[]{:S(2)}) %collective-permute-start.22) | collective-permute-done | bytes 524320 | tf_op jit(solution)/shard_map/ppermute | solution.py:1013
  442.2 30.4 %attention_backward.2 = bf16[8,192,512]{2,1,0:T(8,128)(2,1)S(1)} custom-call(s32[4]{0:T(128)S(1)} %bitcast.344, bf16[8,192,512]{2,1,0:T(8,128)(2,1)S(1)} %copy-done.17, bf16[16,64,256]{2,1,0:T(8,128)(2,1)S(1)} %copy-done.68, bf16[16,64,256]{2,1,0:T(8,128)(2,1)} %all-to-all-done.4.grad_ref, f32[16,1,256]{2,1,0:T(1,128)S(1)} %get-tuple-element.214.lse_ref), custom_call_target="tpu_custom_call" | custom-call | flops 1 | bytes 1 | tf_op jit(solution)/shard_map/attention_backward/pallas_call | solution.py:770
  482.6 26.3 %all-to-all-done.5 = bf16[8,192,512]{2,1,0:T(8,128)(2,1)} async-done(((bf16[8,192,512]{2,1,0:T(8,128)(2,1)}), bf16[8,192,512]{2,1,0:T(8,128)(2,1)}, u32[]{:S(2)}, u32[]{:S(2)}) %all-to-all-start.5) | async-done | bytes 1572896 | tf_op jit(solution)/shard_map/all_to_all | solution.py:494
  520.6 10.3 %collective-permute-done.29 = bf16[256,1024]{1,0:T(8,128)(2,1)S(1)} collective-permute-done((bf16[256,1024]{1,0:T(8,128)(2,1)S(1)}, bf16[256,1024]{1,0:T(8,128)(2,1)S(1)}, u32[]{:S(2)}, u32[]{:S(2)}) %collective-permute-start.29) | collective-permute-done | bytes 524320 | tf_op jit(solution)/shard_map/ppermute | solution.py:1013
  551.5 7.5 feed_forward_back.7
  566.2 13.3 %collective-permute-done.32 = bf16[256,1024]{1,0:T(8,128)(2,1)S(1)} collective-permute-done((bf16[256,1024]{1,0:T(8,128)(2,1)S(1)}, bf16[256,1024]{1,0:T(8,128)(2,1)S(1)}, u32[]{:S(2)}, u32[]{:S(2)}) %collective-permute-start.32) | collective-permute-done | bytes 524320 | tf_op jit(solution)/shard_map/ppermute | solution.py:1013
  617.5 31.6 %attention_backward.3 = bf16[8,192,512]{2,1,0:T(8,128)(2,1)} custom-call(s32[4]{0:T(128)S(1)} %bitcast.345, bf16[8,192,512]{2,1,0:T(8,128)(2,1)S(1)} %copy-done.15, bf16[16,64,256]{2,1,0:T(8,128)(2,1)} %get-tuple-element.165.out_ref, bf16[16,64,256]{2,1,0:T(8,128)(2,1)} %all-to-all-done.6.grad_ref, f32[16,1,256]{2,1,0:T(1,128)S(1)} %get-tuple-element.247.lse_ref), custom_call_target="tpu_custom_call" | custom-call | flops 1 | bytes 1 | tf_op jit(solution)/shard_map/attention_backward/pallas_call | solution.py:770
  663.1 12.2 %all-to-all-done.7 = bf16[8,192,512]{2,1,0:T(8,128)(2,1)S(1)} async-done(((bf16[8,192,512]{2,1,0:T(8,128)(2,1)}), bf16[8,192,512]{2,1,0:T(8,128)(2,1)S(1)}, u32[]{:S(2)}, u32[]{:S(2)}) %all-to-all-start.7) | async-done | bytes 1572896 | tf_op jit(solution)/shard_map/all_to_all | solution.py:494
  748.2 8.6 %collective-permute-done.55 = bf16[128,1024]{1,0:T(8,128)(2,1)S(1)} collective-permute-done((bf16[128,1024]{1,0:T(8,128)(2,1)S(1)}, bf16[128,1024]{1,0:T(8,128)(2,1)S(1)}, u32[]{:S(2)}, u32[]{:S(2)}) %collective-permute-start.55) | collective-permute-done | bytes 262176 | tf_op jit(solution)/shard_map/ppermute | solution.py:1022
  775.1 10.9 %collective-permute-done.58 = bf16[256,1024]{1,0:T(8,128)(2,1)S(1)} collective-permute-done((bf16[256,1024]{1,0:T(8,128)(2,1)S(1)}, bf16[256,1024]{1,0:T(8,128)(2,1)S(1)}, u32[]{:S(2)}, u32[]{:S(2)}) %collective-permute-start.58) | collective-permute-done | bytes 524320 | tf_op jit(solution)/shard_map/ppermute | solution.py:1004
  787.6 9.0 %all-to-all-done.8 = bf16[4,256,1024]{2,1,0:T(8,128)(2,1)S(1)} async-done(((bf16[4,256,1024]{2,1,0:T(8,128)(2,1)}), bf16[4,256,1024]{2,1,0:T(8,128)(2,1)S(1)}, u32[]{:S(2)}, u32[]{:S(2)}) %all-to-all-start.8) | async-done | bytes 2097184 | tf_op jit(solution)/shard_map/all_to_all | solution.py:1028
  (671 shorter events, 416.4 us)
Async XLA Ops:
  7.2 167.7 %all-gather.7.cloned.1.call-start = ((), (), s32[]{:S(2)}) async-start(), calls=%async_computation.10 | async-start | bytes 9191424 | tf_op jit(solution)/shard_map/all_gather | solution.py:1034
  62.6 31.2 %collective-permute-start.6 = (bf16[4,128,1024]{2,1,0:T(8,128)(2,1)S(1)}, bf16[4,128,1024]{2,1,0:T(8,128)(2,1)}, u32[]{:S(2)}, u32[]{:S(2)}) collective-permute-start(bf16[4,128,1024]{2,1,0:T(8,128)(2,1)S(1)} %bitcast.380), channel_id=1, source_target_pairs={{0,8},{4,12},{8,0},{12,4},{1,9},{5,13},{9,1},{13,5},{2,10},{6,14},... | collective-permute-start | bytes 3145736 | tf_op jit(solution)/shard_map/ppermute | solution.py:1016
  107.4 35.6 %all-to-all-start = ((bf16[8,192,512]{2,1,0:T(8,128)(2,1)}), bf16[8,192,512]{2,1,0:T(8,128)(2,1)S(1)}, u32[]{:S(2)}, u32[]{:S(2)}) async-start(bf16[8,192,512]{2,1,0:T(8,128)(2,1)} %fusion.62), calls=%async_computation | async-start | bytes 3145728 | tf_op jit(solution)/shard_map/all_to_all | solution.py:494
  168.5 160.1 %all-gather.9.cloned.1.call-start = ((), (), s32[]{:S(2)}) async-start(), calls=%async_computation.11 | async-start | bytes 9191424 | tf_op jit(solution)/shard_map/all_gather | solution.py:1034
  212.6 30.3 %collective-permute-start.14 = (bf16[4,128,1024]{2,1,0:T(8,128)(2,1)S(1)}, bf16[4,128,1024]{2,1,0:T(8,128)(2,1)S(1)}, u32[]{:S(2)}, u32[]{:S(2)}) collective-permute-start(bf16[4,128,1024]{2,1,0:T(8,128)(2,1)S(1)} %bitcast.382), channel_id=1, source_target_pairs={{0,8},{4,12},{8,0},{12,4},{1,9},{5,13},{9,1},{13,5},{2,10},{6,14},... | collective-permute-start | bytes 3145736 | tf_op jit(solution)/shard_map/ppermute | solution.py:1016
  306.2 28.5 %collective-permute-start.17 = (bf16[2,4,32,1024]{3,2,1,0:T(8,128)(2,1)}, bf16[2,4,32,1024]{3,2,1,0:T(8,128)(2,1)}, u32[]{:S(2)}, u32[]{:S(2)}) collective-permute-start(bf16[2,4,32,1024]{3,2,1,0:T(8,128)(2,1)} %pad_maximum_fusion.23), channel_id=1, source_target_pairs={{0,4},{4,0},{8,12},{12,8},{1,5},{5,1},{9,13},{13,9},{2,6},{6,2},{1... | collective-permute-start | bytes 1572872 | tf_op jit(solution)/shard_map/ppermute | solution.py:1013
  393.0 28.6 %collective-permute-start.23 = (bf16[8,264,1024]{2,1,0:T(8,128)(2,1)}, bf16[8,264,1024]{2,1,0:T(8,128)(2,1)}, u32[]{:S(2)}, u32[]{:S(2)}) collective-permute-start(bf16[8,264,1024]{2,1,0:T(8,128)(2,1)} %half_products.12), channel_id=1, source_target_pairs={{0,16},{16,0},{1,17},{17,1},{2,18},{18,2},{3,19},{19,3},{4,20},{20... | collective-permute-start | bytes 12976136 | tf_op jit(solution)/shard_map/ppermute | solution.py:1025
  432.1 40.5 %collective-permute-start.27 = (bf16[256,1024]{1,0:T(8,128)(2,1)}, bf16[256,1024]{1,0:T(8,128)(2,1)}, u32[]{:S(2)}, u32[]{:S(2)}) collective-permute-start(bf16[256,1024]{1,0:T(8,128)(2,1)} %convert_element_type.435), channel_id=1, source_target_pairs={{0,4},{4,0},{8,12},{12,8},{1,5},{5,1},{9,13},{13,9},{2,6},{6,2},{1... | collective-permute-start | bytes 1572872 | tf_op jit(solution)/shard_map/ppermute | solution.py:1013
  433.8 41.4 %collective-permute-start.25 = (bf16[256,1024]{1,0:T(8,128)(2,1)}, bf16[256,1024]{1,0:T(8,128)(2,1)S(1)}, u32[]{:S(2)}, u32[]{:S(2)}) collective-permute-start(bf16[256,1024]{1,0:T(8,128)(2,1)} %copy-done.90), channel_id=1, source_target_pairs={{0,0},{1,1},{4,4},{5,5},{8,8},{9,9},{12,12},{13,13},{18,2},{19,3},... | collective-permute-start | bytes 1572872 | tf_op jit(solution)/shard_map/ppermute | solution.py:1004
  435.4 40.5 %collective-permute-start.26 = (bf16[256,1024]{1,0:T(8,128)(2,1)}, bf16[256,1024]{1,0:T(8,128)(2,1)S(1)}, u32[]{:S(2)}, u32[]{:S(2)}) collective-permute-start(bf16[256,1024]{1,0:T(8,128)(2,1)} %copy-done.90), channel_id=1, source_target_pairs={{2,0},{3,1},{6,4},{7,5},{10,8},{11,9},{14,12},{15,13},{16,2},{17,3... | collective-permute-start | bytes 1572872 | tf_op jit(solution)/shard_map/ppermute | solution.py:1004
  441.4 35.3 %collective-permute-start.28 = (bf16[2,4,32,1024]{3,2,1,0:T(8,128)(2,1)S(1)}, bf16[2,4,32,1024]{3,2,1,0:T(8,128)(2,1)S(1)}, u32[]{:S(2)}, u32[]{:S(2)}) collective-permute-start(bf16[2,4,32,1024]{3,2,1,0:T(8,128)(2,1)S(1)} %get-tuple-element.410), channel_id=1, source_target_pairs={{0,4},{4,0},{8,12},{12,8},{1,5},{5,1},{9,13},{13,9},{2,6},{6,2},{1... | collective-permute-start | bytes 1572872 | tf_op jit(solution)/shard_map/ppermute | solution.py:1013
  477.5 31.3 %all-to-all-start.5 = ((bf16[8,192,512]{2,1,0:T(8,128)(2,1)}), bf16[8,192,512]{2,1,0:T(8,128)(2,1)}, u32[]{:S(2)}, u32[]{:S(2)}) async-start(bf16[8,192,512]{2,1,0:T(8,128)(2,1)} %copy-done.27), calls=%async_computation.5 | async-start | bytes 3145728 | tf_op jit(solution)/shard_map/all_to_all | solution.py:494
  481.9 131.3 %reduce-scatter.2.cloned.1.call-start = ((), (), s32[]{:S(2)}) async-start(), calls=%async_computation.12 | async-start | bytes 4866048 | tf_op jit(solution)/shard_map/reduce_scatter | solution.py:1267
  564.9 31.4 %collective-permute-start.33 = (bf16[8,264,1024]{2,1,0:T(8,128)(2,1)}, bf16[8,264,1024]{2,1,0:T(8,128)(2,1)}, u32[]{:S(2)}, u32[]{:S(2)}) collective-permute-start(bf16[8,264,1024]{2,1,0:T(8,128)(2,1)} %half_products.18), channel_id=1, source_target_pairs={{0,16},{16,0},{1,17},{17,1},{2,18},{18,2},{3,19},{19,3},{4,20},{20... | collective-permute-start | bytes 12976136 | tf_op jit(solution)/shard_map/ppermute | solution.py:1025
  582.0 30.6 %collective-permute-start.35 = (bf16[4,128,1024]{2,1,0:T(8,128)(2,1)}, bf16[4,128,1024]{2,1,0:T(8,128)(2,1)}, u32[]{:S(2)}, u32[]{:S(2)}) collective-permute-start(bf16[4,128,1024]{2,1,0:T(8,128)(2,1)} %get-tuple-element.240), channel_id=1, source_target_pairs={{0,8},{4,12},{8,0},{12,4},{1,9},{5,13},{9,1},{13,5},{2,10},{6,14},... | collective-permute-start | bytes 3145736 | tf_op jit(solution)/shard_map/ppermute | solution.py:1016
  584.4 28.7 %all-to-all-start.6 = ((bf16[16,64,256]{2,1,0:T(8,128)(2,1)}), bf16[16,64,256]{2,1,0:T(8,128)(2,1)}, u32[]{:S(2)}, u32[]{:S(2)}) async-start(bf16[16,64,256]{2,1,0:T(8,128)(2,1)} %bitcast.86), calls=%async_computation.6 | async-start | bytes 1048576 | tf_op jit(solution)/shard_map/all_to_all | solution.py:494
  613.1 36.0 %collective-permute-start.38 = (bf16[4,176,1024]{2,1,0:T(8,128)(2,1)}, bf16[4,176,1024]{2,1,0:T(8,128)(2,1)}, u32[]{:S(2)}, u32[]{:S(2)}) collective-permute-start(bf16[4,176,1024]{2,1,0:T(8,128)(2,1)} %get-tuple-element.249), channel_id=1, source_target_pairs={{0,8},{4,12},{8,0},{12,4},{1,9},{5,13},{9,1},{13,5},{2,10},{6,14},... | collective-permute-start | bytes 4325384 | tf_op jit(solution)/shard_map/ppermute | solution.py:1016
  613.3 35.9 %collective-permute-start.39 = (bf16[2,4,32,1024]{3,2,1,0:T(8,128)(2,1)}, bf16[2,4,32,1024]{3,2,1,0:T(8,128)(2,1)S(1)}, u32[]{:S(2)}, u32[]{:S(2)}) collective-permute-start(bf16[2,4,32,1024]{3,2,1,0:T(8,128)(2,1)} %get-tuple-element.253), channel_id=1, source_target_pairs={{0,4},{4,0},{8,12},{12,8},{1,5},{5,1},{9,13},{13,9},{2,6},{6,2},{1... | collective-permute-start | bytes 1572872 | tf_op jit(solution)/shard_map/ppermute | solution.py:1013
  616.9 32.3 %collective-permute-start.40 = (bf16[2,128,1024]{2,1,0:T(8,128)(2,1)S(1)}, bf16[2,128,1024]{2,1,0:T(8,128)(2,1)}, u32[]{:S(2)}, u32[]{:S(2)}) collective-permute-start(bf16[2,128,1024]{2,1,0:T(8,128)(2,1)S(1)} %get-tuple-element.406), channel_id=1, source_target_pairs={{0,1},{1,0},{2,3},{3,2},{4,5},{5,4},{6,7},{7,6},{8,9},{9,8},{10,11... | collective-permute-start | bytes 1572872 | tf_op jit(solution)/shard_map/ppermute | solution.py:1019
  654.7 82.4 %all-gather.11.cloned.1.call-start = ((), (), s32[]{:S(2)}) async-start(), calls=%async_computation.13 | async-start | bytes 2703360 | tf_op jit(solution)/shard_map/all_gather | solution.py:1408
  659.6 43.4 %collective-permute-start.42 = (bf16[2,176,1024]{2,1,0:T(8,128)(2,1)}, bf16[2,176,1024]{2,1,0:T(8,128)(2,1)}, u32[]{:S(2)}, u32[]{:S(2)}) collective-permute-start(bf16[2,176,1024]{2,1,0:T(8,128)(2,1)} %get-tuple-element.398), channel_id=1, source_target_pairs={{0,1},{1,0},{2,3},{3,2},{4,5},{5,4},{6,7},{7,6},{8,9},{9,8},{10,11... | collective-permute-start | bytes 2162696 | tf_op jit(solution)/shard_map/ppermute | solution.py:1019
  661.6 41.4 %collective-permute-start.43 = (bf16[4,88,1024]{2,1,0:T(8,128)(2,1)}, bf16[4,88,1024]{2,1,0:T(8,128)(2,1)}, u32[]{:S(2)}, u32[]{:S(2)}) collective-permute-start(bf16[4,88,1024]{2,1,0:T(8,128)(2,1)} %get-tuple-element.260), channel_id=1, source_target_pairs={{0,8},{4,12},{8,0},{12,4},{1,9},{5,13},{9,1},{13,5},{2,10},{6,14},... | collective-permute-start | bytes 2162696 | tf_op jit(solution)/shard_map/ppermute | solution.py:1016
  690.9 107.4 %all-gather.13.cloned.1.call-start = ((), (), s32[]{:S(2)}) async-start(), calls=%async_computation.14 | async-start | bytes 2703360 | tf_op jit(solution)/shard_map/all_gather | solution.py:1460
  758.4 38.2 %all-to-all-start.8 = ((bf16[4,256,1024]{2,1,0:T(8,128)(2,1)}), bf16[4,256,1024]{2,1,0:T(8,128)(2,1)S(1)}, u32[]{:S(2)}, u32[]{:S(2)}) async-start(bf16[4,256,1024]{2,1,0:T(8,128)(2,1)} %broadcast_in_dim.14), calls=%async_computation.9 | async-start | bytes 4194304 | tf_op jit(solution)/shard_map/all_to_all | solution.py:1028
  (209 other events, 1791.0 us)
Sparse Core Ops, SparseCore 0:
  61.4 96.9 all-gather.6
  211.1 93.6 all-gather.8
  486.9 97.7 reduce-scatter.1
  691.0 42.7 all-gather.10
  744.4 53.8 all-gather.12

commit v8 on v7

--- a/solution.py
+++ b/solution.py
@@ -966,7 +966,7 @@
     head_rows = 3 * HD // 2
     out_rows = HD // 2
     half_width = HD // 2
-    tile = 4 * unit_rows
+    tile = 8 * unit_rows
     number = lambda s, c, t: (s * contexts + c) * parts + t
     places = [
         (s, c, t) for s in range(sections) for c in range(contexts) for t in range(parts)

time: 838 us -> 835 us (level)
  Pallas kernels: 185 us -> 176 us
where the time goes in v8:
time: 835 us; the launch traced here: 823 us
  waiting for transfers between devices  300 us (36%)
  Pallas kernels  176 us (21%)
  starting transfers between devices  112 us (13%)
  local copies, waits for them, and re-layouts  90.5 us (11%)
  other arithmetic  72.2 us (9%)
  blocking collectives  40.7 us (5%)
  between operations  16.8 us (2%)
  matrix products  14.7 us (2%)
    ppermute x17, waiting for transfers between devices, swap_side(): return lax.ppermute(value, 'ctx', [(c, c ^ 1) for c in range(contexts)])  101 us
    all_to_all x7, waiting for transfers between devices, exchange(): lax.all_to_all(value, ALL_AXES, split_axis=0, concat_axis=0, tiled=True,...  77.5 us
    pallas_call x2, Pallas kernels, attention_backward(): pl.pallas_call(functools.partial(attention_backward_kernel, parts), grid_...  62.4 us
    unnamed x317, local copies, waits for them, and re-layouts  46.1 us
    pallas_call x2, Pallas kernels, attention_forward(): pl.pallas_call(functools.partial(attention_forward_kernel, parts), grid_s...  42.1 us
    all_to_all x1, blocking collectives, exchange(): lax.all_to_all(value, ALL_AXES, split_axis=0, concat_axis=0, tiled=True,...  40.7 us
    ppermute x7, waiting for transfers between devices, swap_half(): lax.ppermute(value, 'tp', [(t, (t + half_parts) % parts) for t in range(p...  37.1 us
    pallas_call x12, Pallas kernels, half_products(): pl.pallas_call(functools.partial(half_products_kernel, tuple(layout), siz...  36.7 us
  transfers between devices with their start and end apart: 77, of which 38 were waited for; matrix products, arithmetic and copies ran while one was open for 13% of the time, Pallas kernels for 20%

profile of v8, /device:TPU:0, one launch (start us, length us, event | category | flops | bytes accessed | tf_op | source)
XLA Modules:
  0.0 822.9 jit_solution(8211368156372457840)
XLA Ops:
  27.9 14.8 %collective-permute-done.1 = bf16[128,1024]{1,0:T(8,128)(2,1)} collective-permute-done((bf16[128,1024]{1,0:T(8,128)(2,1)S(1)}, bf16[128,1024]{1,0:T(8,128)(2,1)}, u32[]{:S(2)}, u32[]{:S(2)}) %collective-permute-start.1) | collective-permute-done | bytes 262176 | tf_op jit(solution)/shard_map/ppermute | solution.py:1022
  44.8 14.3 %collective-permute-done.2 = bf16[2,128,1024]{2,1,0:T(8,128)(2,1)} collective-permute-done((bf16[2,128,1024]{2,1,0:T(8,128)(2,1)}, bf16[2,128,1024]{2,1,0:T(8,128)(2,1)}, u32[]{:S(2)}, u32[]{:S(2)}) %collective-permute-start.2) | collective-permute-done | bytes 524320 | tf_op jit(solution)/shard_map/ppermute | solution.py:1019
  66.2 12.2 %collective-permute-done.5 = bf16[256,1024]{1,0:T(8,128)(2,1)S(1)} collective-permute-done((bf16[256,1024]{1,0:T(8,128)(2,1)S(1)}, bf16[256,1024]{1,0:T(8,128)(2,1)S(1)}, u32[]{:S(2)}, u32[]{:S(2)}) %collective-permute-start.5) | collective-permute-done | bytes 524320 | tf_op jit(solution)/shard_map/ppermute | solution.py:1013
  79.2 14.6 %collective-permute-done.6 = bf16[4,128,1024]{2,1,0:T(8,128)(2,1)} collective-permute-done((bf16[4,128,1024]{2,1,0:T(8,128)(2,1)S(1)}, bf16[4,128,1024]{2,1,0:T(8,128)(2,1)}, u32[]{:S(2)}, u32[]{:S(2)}) %collective-permute-start.6) | collective-permute-done | bytes 1048608 | tf_op jit(solution)/shard_map/ppermute | solution.py:1016
  112.6 30.4 %all-to-all-done.qkv_ref = bf16[8,192,512]{2,1,0:T(8,128)(2,1)S(1)} async-done(((bf16[8,192,512]{2,1,0:T(8,128)(2,1)}), bf16[8,192,512]{2,1,0:T(8,128)(2,1)S(1)}, u32[]{:S(2)}, u32[]{:S(2)}) %all-to-all-start) | async-done | bytes 1572896 | tf_op jit(solution)/shard_map/all_to_all | solution.py:494
  143.0 21.4 %attention_forward.2 = (bf16[16,64,256]{2,1,0:T(8,128)(2,1)}, f32[16,1,256]{2,1,0:T(1,128)S(1)}) custom-call(s32[4]{0:T(128)S(1)} %bitcast.342, bf16[8,192,512]{2,1,0:T(8,128)(2,1)S(1)} %all-to-all-done.qkv_ref), custom_call_target="tpu_custom_call" | custom-call | flops 1 | bytes 1 | tf_op jit(solution)/shard_map/attention_forward/pallas_call | solution.py:630
  180.6 8.1 collective-permute-done.8
  219.1 12.1 %collective-permute-done.13 = bf16[256,1024]{1,0:T(8,128)(2,1)S(1)} collective-permute-done((bf16[256,1024]{1,0:T(8,128)(2,1)S(1)}, bf16[256,1024]{1,0:T(8,128)(2,1)S(1)}, u32[]{:S(2)}, u32[]{:S(2)}) %collective-permute-start.13) | collective-permute-done | bytes 524320 | tf_op jit(solution)/shard_map/ppermute | solution.py:1013
  231.2 11.9 %collective-permute-done.14 = bf16[4,128,1024]{2,1,0:T(8,128)(2,1)S(1)} collective-permute-done((bf16[4,128,1024]{2,1,0:T(8,128)(2,1)S(1)}, bf16[4,128,1024]{2,1,0:T(8,128)(2,1)S(1)}, u32[]{:S(2)}, u32[]{:S(2)}) %collective-permute-start.14) | collective-permute-done | bytes 1048608 | tf_op jit(solution)/shard_map/ppermute | solution.py:1016
  246.8 11.6 %collective-permute-done.15 = bf16[256,1024]{1,0:T(8,128)(2,1)S(1)} collective-permute-done((bf16[256,1024]{1,0:T(8,128)(2,1)S(1)}, bf16[256,1024]{1,0:T(8,128)(2,1)S(1)}, u32[]{:S(2)}, u32[]{:S(2)}) %collective-permute-start.15) | collective-permute-done | bytes 524320 | tf_op jit(solution)/shard_map/ppermute | solution.py:1013
  263.2 40.7 %all_to_all.45.qkv_ref = bf16[8,192,512]{2,1,0:T(8,128)(2,1)S(1)} all-to-all(bf16[8,192,512]{2,1,0:T(8,128)(2,1)S(1)} %fusion.53), channel_id=1, replica_groups={{0,1,16,17,8,9,24,25},{2,3,18,19,10,11,26,27},{4,5,20,21,12,13,28,29},{..., dimensions={0} | all-to-all | bytes 3145728 | tf_op jit(solution)/shard_map/all_to_all | solution.py:494
  307.3 20.7 %attention_forward.3 = (bf16[16,64,256]{2,1,0:T(8,128)(2,1)S(1)}, f32[16,1,256]{2,1,0:T(1,128)S(1)}) custom-call(s32[4]{0:T(128)S(1)} %bitcast.343, bf16[8,192,512]{2,1,0:T(8,128)(2,1)S(1)} %all_to_all.45.qkv_ref), custom_call_target="tpu_custom_call" | custom-call | flops 1 | bytes 1 | tf_op jit(solution)/shard_map/attention_forward/pallas_call | solution.py:630
  345.0 6.9 all-to-all-done.3
  367.3 7.0 collective-permute-done.21.rows_ref.refs_7_
  391.0 14.1 %collective-permute-done.22 = bf16[256,1024]{1,0:T(8,128)(2,1)S(1)} collective-permute-done((bf16[256,1024]{1,0:T(8,128)(2,1)S(1)}, bf16[256,1024]{1,0:T(8,128)(2,1)S(1)}, u32[]{:S(2)}, u32[]{:S(2)}) %collective-permute-start.22) | collective-permute-done | bytes 524320 | tf_op jit(solution)/shard_map/ppermute | solution.py:1013
  440.0 30.5 %attention_backward.2 = bf16[8,192,512]{2,1,0:T(8,128)(2,1)S(1)} custom-call(s32[4]{0:T(128)S(1)} %bitcast.344, bf16[8,192,512]{2,1,0:T(8,128)(2,1)S(1)} %copy-done.17, bf16[16,64,256]{2,1,0:T(8,128)(2,1)S(1)} %copy-done.68, bf16[16,64,256]{2,1,0:T(8,128)(2,1)} %all-to-all-done.4.grad_ref, f32[16,1,256]{2,1,0:T(1,128)S(1)} %get-tuple-element.214.lse_ref), custom_call_target="tpu_custom_call" | custom-call | flops 1 | bytes 1 | tf_op jit(solution)/shard_map/attention_backward/pallas_call | solution.py:770
  480.5 27.4 %all-to-all-done.5 = bf16[8,192,512]{2,1,0:T(8,128)(2,1)} async-done(((bf16[8,192,512]{2,1,0:T(8,128)(2,1)}), bf16[8,192,512]{2,1,0:T(8,128)(2,1)}, u32[]{:S(2)}, u32[]{:S(2)}) %all-to-all-start.5) | async-done | bytes 1572896 | tf_op jit(solution)/shard_map/all_to_all | solution.py:494
  519.0 10.2 %collective-permute-done.29 = bf16[256,1024]{1,0:T(8,128)(2,1)S(1)} collective-permute-done((bf16[256,1024]{1,0:T(8,128)(2,1)S(1)}, bf16[256,1024]{1,0:T(8,128)(2,1)S(1)}, u32[]{:S(2)}, u32[]{:S(2)}) %collective-permute-start.29) | collective-permute-done | bytes 524320 | tf_op jit(solution)/shard_map/ppermute | solution.py:1013
  563.0 13.4 %collective-permute-done.32 = bf16[256,1024]{1,0:T(8,128)(2,1)S(1)} collective-permute-done((bf16[256,1024]{1,0:T(8,128)(2,1)S(1)}, bf16[256,1024]{1,0:T(8,128)(2,1)S(1)}, u32[]{:S(2)}, u32[]{:S(2)}) %collective-permute-start.32) | collective-permute-done | bytes 524320 | tf_op jit(solution)/shard_map/ppermute | solution.py:1013
  614.4 31.8 %attention_backward.3 = bf16[8,192,512]{2,1,0:T(8,128)(2,1)} custom-call(s32[4]{0:T(128)S(1)} %bitcast.345, bf16[8,192,512]{2,1,0:T(8,128)(2,1)S(1)} %copy-done.15, bf16[16,64,256]{2,1,0:T(8,128)(2,1)} %get-tuple-element.165.out_ref, bf16[16,64,256]{2,1,0:T(8,128)(2,1)} %all-to-all-done.6.grad_ref, f32[16,1,256]{2,1,0:T(1,128)S(1)} %get-tuple-element.247.lse_ref), custom_call_target="tpu_custom_call" | custom-call | flops 1 | bytes 1 | tf_op jit(solution)/shard_map/attention_backward/pallas_call | solution.py:770
  659.6 12.2 %all-to-all-done.7 = bf16[8,192,512]{2,1,0:T(8,128)(2,1)S(1)} async-done(((bf16[8,192,512]{2,1,0:T(8,128)(2,1)}), bf16[8,192,512]{2,1,0:T(8,128)(2,1)S(1)}, u32[]{:S(2)}, u32[]{:S(2)}) %all-to-all-start.7) | async-done | bytes 1572896 | tf_op jit(solution)/shard_map/all_to_all | solution.py:494
  744.5 8.6 %collective-permute-done.55 = bf16[128,1024]{1,0:T(8,128)(2,1)S(1)} collective-permute-done((bf16[128,1024]{1,0:T(8,128)(2,1)S(1)}, bf16[128,1024]{1,0:T(8,128)(2,1)S(1)}, u32[]{:S(2)}, u32[]{:S(2)}) %collective-permute-start.55) | collective-permute-done | bytes 262176 | tf_op jit(solution)/shard_map/ppermute | solution.py:1022
  771.1 11.3 %collective-permute-done.58 = bf16[256,1024]{1,0:T(8,128)(2,1)S(1)} collective-permute-done((bf16[256,1024]{1,0:T(8,128)(2,1)S(1)}, bf16[256,1024]{1,0:T(8,128)(2,1)S(1)}, u32[]{:S(2)}, u32[]{:S(2)}) %collective-permute-start.58) | collective-permute-done | bytes 524320 | tf_op jit(solution)/shard_map/ppermute | solution.py:1004
  784.0 10.4 %all-to-all-done.8 = bf16[4,256,1024]{2,1,0:T(8,128)(2,1)S(1)} async-done(((bf16[4,256,1024]{2,1,0:T(8,128)(2,1)}), bf16[4,256,1024]{2,1,0:T(8,128)(2,1)S(1)}, u32[]{:S(2)}, u32[]{:S(2)}) %all-to-all-start.8) | async-done | bytes 2097184 | tf_op jit(solution)/shard_map/all_to_all | solution.py:1028
  (671 shorter events, 409.3 us)
Async XLA Ops:
  7.2 167.7 %all-gather.7.cloned.1.call-start = ((), (), s32[]{:S(2)}) async-start(), calls=%async_computation.10 | async-start | bytes 9191424 | tf_op jit(solution)/shard_map/all_gather | solution.py:1034
  62.6 31.2 %collective-permute-start.6 = (bf16[4,128,1024]{2,1,0:T(8,128)(2,1)S(1)}, bf16[4,128,1024]{2,1,0:T(8,128)(2,1)}, u32[]{:S(2)}, u32[]{:S(2)}) collective-permute-start(bf16[4,128,1024]{2,1,0:T(8,128)(2,1)S(1)} %bitcast.380), channel_id=1, source_target_pairs={{0,8},{4,12},{8,0},{12,4},{1,9},{5,13},{9,1},{13,5},{2,10},{6,14},... | collective-permute-start | bytes 3145736 | tf_op jit(solution)/shard_map/ppermute | solution.py:1016
  107.4 35.6 %all-to-all-start = ((bf16[8,192,512]{2,1,0:T(8,128)(2,1)}), bf16[8,192,512]{2,1,0:T(8,128)(2,1)S(1)}, u32[]{:S(2)}, u32[]{:S(2)}) async-start(bf16[8,192,512]{2,1,0:T(8,128)(2,1)} %fusion.62), calls=%async_computation | async-start | bytes 3145728 | tf_op jit(solution)/shard_map/all_to_all | solution.py:494
  168.7 160.2 %all-gather.9.cloned.1.call-start = ((), (), s32[]{:S(2)}) async-start(), calls=%async_computation.11 | async-start | bytes 9191424 | tf_op jit(solution)/shard_map/all_gather | solution.py:1034
  212.8 30.3 %collective-permute-start.14 = (bf16[4,128,1024]{2,1,0:T(8,128)(2,1)S(1)}, bf16[4,128,1024]{2,1,0:T(8,128)(2,1)S(1)}, u32[]{:S(2)}, u32[]{:S(2)}) collective-permute-start(bf16[4,128,1024]{2,1,0:T(8,128)(2,1)S(1)} %bitcast.382), channel_id=1, source_target_pairs={{0,8},{4,12},{8,0},{12,4},{1,9},{5,13},{9,1},{13,5},{2,10},{6,14},... | collective-permute-start | bytes 3145736 | tf_op jit(solution)/shard_map/ppermute | solution.py:1016
  306.2 28.8 %collective-permute-start.17 = (bf16[2,4,32,1024]{3,2,1,0:T(8,128)(2,1)}, bf16[2,4,32,1024]{3,2,1,0:T(8,128)(2,1)}, u32[]{:S(2)}, u32[]{:S(2)}) collective-permute-start(bf16[2,4,32,1024]{3,2,1,0:T(8,128)(2,1)} %pad_maximum_fusion.23), channel_id=1, source_target_pairs={{0,4},{4,0},{8,12},{12,8},{1,5},{5,1},{9,13},{13,9},{2,6},{6,2},{1... | collective-permute-start | bytes 1572872 | tf_op jit(solution)/shard_map/ppermute | solution.py:1013
  390.6 28.6 %collective-permute-start.23 = (bf16[8,264,1024]{2,1,0:T(8,128)(2,1)}, bf16[8,264,1024]{2,1,0:T(8,128)(2,1)}, u32[]{:S(2)}, u32[]{:S(2)}) collective-permute-start(bf16[8,264,1024]{2,1,0:T(8,128)(2,1)} %half_products.12), channel_id=1, source_target_pairs={{0,16},{16,0},{1,17},{17,1},{2,18},{18,2},{3,19},{19,3},{4,20},{20... | collective-permute-start | bytes 12976136 | tf_op jit(solution)/shard_map/ppermute | solution.py:1025
  429.7 40.9 %collective-permute-start.27 = (bf16[256,1024]{1,0:T(8,128)(2,1)}, bf16[256,1024]{1,0:T(8,128)(2,1)}, u32[]{:S(2)}, u32[]{:S(2)}) collective-permute-start(bf16[256,1024]{1,0:T(8,128)(2,1)} %convert_element_type.435), channel_id=1, source_target_pairs={{0,4},{4,0},{8,12},{12,8},{1,5},{5,1},{9,13},{13,9},{2,6},{6,2},{1... | collective-permute-start | bytes 1572872 | tf_op jit(solution)/shard_map/ppermute | solution.py:1013
  431.3 41.7 %collective-permute-start.25 = (bf16[256,1024]{1,0:T(8,128)(2,1)}, bf16[256,1024]{1,0:T(8,128)(2,1)S(1)}, u32[]{:S(2)}, u32[]{:S(2)}) collective-permute-start(bf16[256,1024]{1,0:T(8,128)(2,1)} %copy-done.90), channel_id=1, source_target_pairs={{0,0},{1,1},{4,4},{5,5},{8,8},{9,9},{12,12},{13,13},{18,2},{19,3},... | collective-permute-start | bytes 1572872 | tf_op jit(solution)/shard_map/ppermute | solution.py:1004
  433.0 40.8 %collective-permute-start.26 = (bf16[256,1024]{1,0:T(8,128)(2,1)}, bf16[256,1024]{1,0:T(8,128)(2,1)S(1)}, u32[]{:S(2)}, u32[]{:S(2)}) collective-permute-start(bf16[256,1024]{1,0:T(8,128)(2,1)} %copy-done.90), channel_id=1, source_target_pairs={{2,0},{3,1},{6,4},{7,5},{10,8},{11,9},{14,12},{15,13},{16,2},{17,3... | collective-permute-start | bytes 1572872 | tf_op jit(solution)/shard_map/ppermute | solution.py:1004
  439.2 35.5 %collective-permute-start.28 = (bf16[2,4,32,1024]{3,2,1,0:T(8,128)(2,1)S(1)}, bf16[2,4,32,1024]{3,2,1,0:T(8,128)(2,1)S(1)}, u32[]{:S(2)}, u32[]{:S(2)}) collective-permute-start(bf16[2,4,32,1024]{3,2,1,0:T(8,128)(2,1)S(1)} %get-tuple-element.410), channel_id=1, source_target_pairs={{0,4},{4,0},{8,12},{12,8},{1,5},{5,1},{9,13},{13,9},{2,6},{6,2},{1... | collective-permute-start | bytes 1572872 | tf_op jit(solution)/shard_map/ppermute | solution.py:1013
  475.5 32.5 %all-to-all-start.5 = ((bf16[8,192,512]{2,1,0:T(8,128)(2,1)}), bf16[8,192,512]{2,1,0:T(8,128)(2,1)}, u32[]{:S(2)}, u32[]{:S(2)}) async-start(bf16[8,192,512]{2,1,0:T(8,128)(2,1)} %copy-done.27), calls=%async_computation.5 | async-start | bytes 3145728 | tf_op jit(solution)/shard_map/all_to_all | solution.py:494
  479.8 130.3 %reduce-scatter.2.cloned.1.call-start = ((), (), s32[]{:S(2)}) async-start(), calls=%async_computation.12 | async-start | bytes 4866048 | tf_op jit(solution)/shard_map/reduce_scatter | solution.py:1267
  561.9 31.4 %collective-permute-start.33 = (bf16[8,264,1024]{2,1,0:T(8,128)(2,1)}, bf16[8,264,1024]{2,1,0:T(8,128)(2,1)}, u32[]{:S(2)}, u32[]{:S(2)}) collective-permute-start(bf16[8,264,1024]{2,1,0:T(8,128)(2,1)} %half_products.18), channel_id=1, source_target_pairs={{0,16},{16,0},{1,17},{17,1},{2,18},{18,2},{3,19},{19,3},{4,20},{20... | collective-permute-start | bytes 12976136 | tf_op jit(solution)/shard_map/ppermute | solution.py:1025
  578.9 30.6 %collective-permute-start.35 = (bf16[4,128,1024]{2,1,0:T(8,128)(2,1)}, bf16[4,128,1024]{2,1,0:T(8,128)(2,1)}, u32[]{:S(2)}, u32[]{:S(2)}) collective-permute-start(bf16[4,128,1024]{2,1,0:T(8,128)(2,1)} %get-tuple-element.240), channel_id=1, source_target_pairs={{0,8},{4,12},{8,0},{12,4},{1,9},{5,13},{9,1},{13,5},{2,10},{6,14},... | collective-permute-start | bytes 3145736 | tf_op jit(solution)/shard_map/ppermute | solution.py:1016
  581.4 28.7 %all-to-all-start.6 = ((bf16[16,64,256]{2,1,0:T(8,128)(2,1)}), bf16[16,64,256]{2,1,0:T(8,128)(2,1)}, u32[]{:S(2)}, u32[]{:S(2)}) async-start(bf16[16,64,256]{2,1,0:T(8,128)(2,1)} %bitcast.86), calls=%async_computation.6 | async-start | bytes 1048576 | tf_op jit(solution)/shard_map/all_to_all | solution.py:494
  610.1 36.2 %collective-permute-start.38 = (bf16[4,176,1024]{2,1,0:T(8,128)(2,1)}, bf16[4,176,1024]{2,1,0:T(8,128)(2,1)}, u32[]{:S(2)}, u32[]{:S(2)}) collective-permute-start(bf16[4,176,1024]{2,1,0:T(8,128)(2,1)} %get-tuple-element.249), channel_id=1, source_target_pairs={{0,8},{4,12},{8,0},{12,4},{1,9},{5,13},{9,1},{13,5},{2,10},{6,14},... | collective-permute-start | bytes 4325384 | tf_op jit(solution)/shard_map/ppermute | solution.py:1016
  610.8 35.4 %collective-permute-start.39 = (bf16[2,4,32,1024]{3,2,1,0:T(8,128)(2,1)}, bf16[2,4,32,1024]{3,2,1,0:T(8,128)(2,1)S(1)}, u32[]{:S(2)}, u32[]{:S(2)}) collective-permute-start(bf16[2,4,32,1024]{3,2,1,0:T(8,128)(2,1)} %get-tuple-element.253), channel_id=1, source_target_pairs={{0,4},{4,0},{8,12},{12,8},{1,5},{5,1},{9,13},{13,9},{2,6},{6,2},{1... | collective-permute-start | bytes 1572872 | tf_op jit(solution)/shard_map/ppermute | solution.py:1013
  613.7 32.5 %collective-permute-start.40 = (bf16[2,128,1024]{2,1,0:T(8,128)(2,1)S(1)}, bf16[2,128,1024]{2,1,0:T(8,128)(2,1)}, u32[]{:S(2)}, u32[]{:S(2)}) collective-permute-start(bf16[2,128,1024]{2,1,0:T(8,128)(2,1)S(1)} %get-tuple-element.406), channel_id=1, source_target_pairs={{0,1},{1,0},{2,3},{3,2},{4,5},{5,4},{6,7},{7,6},{8,9},{9,8},{10,11... | collective-permute-start | bytes 1572872 | tf_op jit(solution)/shard_map/ppermute | solution.py:1019
  651.2 82.2 %all-gather.11.cloned.1.call-start = ((), (), s32[]{:S(2)}) async-start(), calls=%async_computation.13 | async-start | bytes 2703360 | tf_op jit(solution)/shard_map/all_gather | solution.py:1408
  656.1 43.2 %collective-permute-start.42 = (bf16[2,176,1024]{2,1,0:T(8,128)(2,1)}, bf16[2,176,1024]{2,1,0:T(8,128)(2,1)}, u32[]{:S(2)}, u32[]{:S(2)}) collective-permute-start(bf16[2,176,1024]{2,1,0:T(8,128)(2,1)} %get-tuple-element.398), channel_id=1, source_target_pairs={{0,1},{1,0},{2,3},{3,2},{4,5},{5,4},{6,7},{7,6},{8,9},{9,8},{10,11... | collective-permute-start | bytes 2162696 | tf_op jit(solution)/shard_map/ppermute | solution.py:1019
  658.1 41.3 %collective-permute-start.43 = (bf16[4,88,1024]{2,1,0:T(8,128)(2,1)}, bf16[4,88,1024]{2,1,0:T(8,128)(2,1)}, u32[]{:S(2)}, u32[]{:S(2)}) collective-permute-start(bf16[4,88,1024]{2,1,0:T(8,128)(2,1)} %get-tuple-element.260), channel_id=1, source_target_pairs={{0,8},{4,12},{8,0},{12,4},{1,9},{5,13},{9,1},{13,5},{2,10},{6,14},... | collective-permute-start | bytes 2162696 | tf_op jit(solution)/shard_map/ppermute | solution.py:1016
  687.3 107.4 %all-gather.13.cloned.1.call-start = ((), (), s32[]{:S(2)}) async-start(), calls=%async_computation.14 | async-start | bytes 2703360 | tf_op jit(solution)/shard_map/all_gather | solution.py:1460
  754.9 39.5 %all-to-all-start.8 = ((bf16[4,256,1024]{2,1,0:T(8,128)(2,1)}), bf16[4,256,1024]{2,1,0:T(8,128)(2,1)S(1)}, u32[]{:S(2)}, u32[]{:S(2)}) async-start(bf16[4,256,1024]{2,1,0:T(8,128)(2,1)} %broadcast_in_dim.14), calls=%async_computation.9 | async-start | bytes 4194304 | tf_op jit(solution)/shard_map/all_to_all | solution.py:1028
  (209 other events, 1770.7 us)
Sparse Core Ops, SparseCore 0:
  61.4 96.9 all-gather.6
  211.3 93.4 all-gather.8
  484.8 97.3 reduce-scatter.1
  687.4 42.7 all-gather.10
  740.8 53.8 all-gather.12

commit v9 on v8

--- a/solution.py
+++ b/solution.py
@@ -1219,7 +1219,7 @@
             ((near[2], grad_down), (far[2], far_down)),
         )
         products = functools.partial(
-            half_products, groups=groups, pieces=2 * parts, per_step=2
+            half_products, groups=groups, pieces=2 * parts, per_step=4
         )
         sent = products(1 - section)
         moved = swap_section(sent)

time: 835 us -> 833 us (level)
  transfers between devices with their start and end apart: 77 -> 77, of which waited for: 38 -> 38; matrix products, arithmetic and copies ran while one was open for 13% -> 13% of each run, Pallas kernels for 20% -> 19%
where the time goes in v9:
time: 833 us; the launch traced here: 820 us
  waiting for transfers between devices  302 us (36%)
  Pallas kernels  174 us (21%)
  starting transfers between devices  109 us (13%)
  local copies, waits for them, and re-layouts  91.1 us (11%)
  other arithmetic  72.2 us (9%)
  blocking collectives  40.5 us (5%)
  between operations  16.5 us (2%)
  matrix products  14.7 us (2%)
    ppermute x17, waiting for transfers between devices, swap_side(): return lax.ppermute(value, 'ctx', [(c, c ^ 1) for c in range(contexts)])  103 us
    all_to_all x7, waiting for transfers between devices, exchange(): lax.all_to_all(value, ALL_AXES, split_axis=0, concat_axis=0, tiled=True,...  77.9 us
    pallas_call x2, Pallas kernels, attention_backward(): pl.pallas_call(functools.partial(attention_backward_kernel, parts), grid_...  62.4 us
    unnamed x317, local copies, waits for them, and re-layouts  46.7 us
    pallas_call x2, Pallas kernels, attention_forward(): pl.pallas_call(functools.partial(attention_forward_kernel, parts), grid_s...  42.1 us
    all_to_all x1, blocking collectives, exchange(): lax.all_to_all(value, ALL_AXES, split_axis=0, concat_axis=0, tiled=True,...  40.5 us
    ppermute x7, waiting for transfers between devices, swap_half(): lax.ppermute(value, 'tp', [(t, (t + half_parts) % parts) for t in range(p...  37 us
    ppermute x8, waiting for transfers between devices, swap_far(): return lax.ppermute(value, 'ctx', [(c, c ^ 2) for c in range(contexts)])  36.2 us
  transfers between devices with their start and end apart: 77, of which 38 were waited for; matrix products, arithmetic and copies ran while one was open for 13% of the time, Pallas kernels for 19%

profile of v9, /device:TPU:0, one launch (start us, length us, event | category | flops | bytes accessed | tf_op | source)
XLA Modules:
  0.0 820.5 jit_solution(12529635480620662459)
XLA Ops:
  27.9 14.8 %collective-permute-done.1 = bf16[128,1024]{1,0:T(8,128)(2,1)} collective-permute-done((bf16[128,1024]{1,0:T(8,128)(2,1)S(1)}, bf16[128,1024]{1,0:T(8,128)(2,1)}, u32[]{:S(2)}, u32[]{:S(2)}) %collective-permute-start.1) | collective-permute-done | bytes 262176 | tf_op jit(solution)/shard_map/ppermute | solution.py:1022
  44.8 14.3 %collective-permute-done.2 = bf16[2,128,1024]{2,1,0:T(8,128)(2,1)} collective-permute-done((bf16[2,128,1024]{2,1,0:T(8,128)(2,1)}, bf16[2,128,1024]{2,1,0:T(8,128)(2,1)}, u32[]{:S(2)}, u32[]{:S(2)}) %collective-permute-start.2) | collective-permute-done | bytes 524320 | tf_op jit(solution)/shard_map/ppermute | solution.py:1019
  66.2 12.2 %collective-permute-done.5 = bf16[256,1024]{1,0:T(8,128)(2,1)S(1)} collective-permute-done((bf16[256,1024]{1,0:T(8,128)(2,1)S(1)}, bf16[256,1024]{1,0:T(8,128)(2,1)S(1)}, u32[]{:S(2)}, u32[]{:S(2)}) %collective-permute-start.5) | collective-permute-done | bytes 524320 | tf_op jit(solution)/shard_map/ppermute | solution.py:1013
  79.2 14.6 %collective-permute-done.6 = bf16[4,128,1024]{2,1,0:T(8,128)(2,1)} collective-permute-done((bf16[4,128,1024]{2,1,0:T(8,128)(2,1)S(1)}, bf16[4,128,1024]{2,1,0:T(8,128)(2,1)}, u32[]{:S(2)}, u32[]{:S(2)}) %collective-permute-start.6) | collective-permute-done | bytes 1048608 | tf_op jit(solution)/shard_map/ppermute | solution.py:1016
  112.6 30.4 %all-to-all-done.qkv_ref = bf16[8,192,512]{2,1,0:T(8,128)(2,1)S(1)} async-done(((bf16[8,192,512]{2,1,0:T(8,128)(2,1)}), bf16[8,192,512]{2,1,0:T(8,128)(2,1)S(1)}, u32[]{:S(2)}, u32[]{:S(2)}) %all-to-all-start) | async-done | bytes 1572896 | tf_op jit(solution)/shard_map/all_to_all | solution.py:494
  143.0 21.4 %attention_forward.2 = (bf16[16,64,256]{2,1,0:T(8,128)(2,1)}, f32[16,1,256]{2,1,0:T(1,128)S(1)}) custom-call(s32[4]{0:T(128)S(1)} %bitcast.342, bf16[8,192,512]{2,1,0:T(8,128)(2,1)S(1)} %all-to-all-done.qkv_ref), custom_call_target="tpu_custom_call" | custom-call | flops 1 | bytes 1 | tf_op jit(solution)/shard_map/attention_forward/pallas_call | solution.py:630
  180.4 8.3 %collective-permute-done.8 = bf16[2,4,32,1024]{3,2,1,0:T(8,128)(2,1)} collective-permute-done((bf16[2,4,32,1024]{3,2,1,0:T(8,128)(2,1)}, bf16[2,4,32,1024]{3,2,1,0:T(8,128)(2,1)}, u32[]{:S(2)}, u32[]{:S(2)}) %collective-permute-start.8) | collective-permute-done | bytes 524320 | tf_op jit(solution)/shard_map/ppermute | solution.py:1013
  219.1 12.1 %collective-permute-done.13 = bf16[256,1024]{1,0:T(8,128)(2,1)S(1)} collective-permute-done((bf16[256,1024]{1,0:T(8,128)(2,1)S(1)}, bf16[256,1024]{1,0:T(8,128)(2,1)S(1)}, u32[]{:S(2)}, u32[]{:S(2)}) %collective-permute-start.13) | collective-permute-done | bytes 524320 | tf_op jit(solution)/shard_map/ppermute | solution.py:1013
  231.2 11.9 %collective-permute-done.14 = bf16[4,128,1024]{2,1,0:T(8,128)(2,1)S(1)} collective-permute-done((bf16[4,128,1024]{2,1,0:T(8,128)(2,1)S(1)}, bf16[4,128,1024]{2,1,0:T(8,128)(2,1)S(1)}, u32[]{:S(2)}, u32[]{:S(2)}) %collective-permute-start.14) | collective-permute-done | bytes 1048608 | tf_op jit(solution)/shard_map/ppermute | solution.py:1016
  246.8 11.6 %collective-permute-done.15 = bf16[256,1024]{1,0:T(8,128)(2,1)S(1)} collective-permute-done((bf16[256,1024]{1,0:T(8,128)(2,1)S(1)}, bf16[256,1024]{1,0:T(8,128)(2,1)S(1)}, u32[]{:S(2)}, u32[]{:S(2)}) %collective-permute-start.15) | collective-permute-done | bytes 524320 | tf_op jit(solution)/shard_map/ppermute | solution.py:1013
  263.2 40.5 %all_to_all.45.qkv_ref = bf16[8,192,512]{2,1,0:T(8,128)(2,1)S(1)} all-to-all(bf16[8,192,512]{2,1,0:T(8,128)(2,1)S(1)} %fusion.53), channel_id=1, replica_groups={{0,1,16,17,8,9,24,25},{2,3,18,19,10,11,26,27},{4,5,20,21,12,13,28,29},{..., dimensions={0} | all-to-all | bytes 3145728 | tf_op jit(solution)/shard_map/all_to_all | solution.py:494
  307.3 20.7 %attention_forward.3 = (bf16[16,64,256]{2,1,0:T(8,128)(2,1)S(1)}, f32[16,1,256]{2,1,0:T(1,128)S(1)}) custom-call(s32[4]{0:T(128)S(1)} %bitcast.343, bf16[8,192,512]{2,1,0:T(8,128)(2,1)S(1)} %all_to_all.45.qkv_ref), custom_call_target="tpu_custom_call" | custom-call | flops 1 | bytes 1 | tf_op jit(solution)/shard_map/attention_forward/pallas_call | solution.py:630
  344.9 6.9 all-to-all-done.3
  367.2 7.0 collective-permute-done.21.rows_ref.refs_7_
  390.6 14.1 %collective-permute-done.22 = bf16[256,1024]{1,0:T(8,128)(2,1)S(1)} collective-permute-done((bf16[256,1024]{1,0:T(8,128)(2,1)S(1)}, bf16[256,1024]{1,0:T(8,128)(2,1)S(1)}, u32[]{:S(2)}, u32[]{:S(2)}) %collective-permute-start.22) | collective-permute-done | bytes 524320 | tf_op jit(solution)/shard_map/ppermute | solution.py:1013
  438.9 30.5 %attention_backward.2 = bf16[8,192,512]{2,1,0:T(8,128)(2,1)S(1)} custom-call(s32[4]{0:T(128)S(1)} %bitcast.344, bf16[8,192,512]{2,1,0:T(8,128)(2,1)S(1)} %copy-done.17, bf16[16,64,256]{2,1,0:T(8,128)(2,1)S(1)} %copy-done.68, bf16[16,64,256]{2,1,0:T(8,128)(2,1)} %all-to-all-done.4.grad_ref, f32[16,1,256]{2,1,0:T(1,128)S(1)} %get-tuple-element.214.lse_ref), custom_call_target="tpu_custom_call" | custom-call | flops 1 | bytes 1 | tf_op jit(solution)/shard_map/attention_backward/pallas_call | solution.py:770
  479.5 27.8 %all-to-all-done.5 = bf16[8,192,512]{2,1,0:T(8,128)(2,1)} async-done(((bf16[8,192,512]{2,1,0:T(8,128)(2,1)}), bf16[8,192,512]{2,1,0:T(8,128)(2,1)}, u32[]{:S(2)}, u32[]{:S(2)}) %all-to-all-start.5) | async-done | bytes 1572896 | tf_op jit(solution)/shard_map/all_to_all | solution.py:494
  518.0 11.0 %collective-permute-done.29 = bf16[256,1024]{1,0:T(8,128)(2,1)S(1)} collective-permute-done((bf16[256,1024]{1,0:T(8,128)(2,1)S(1)}, bf16[256,1024]{1,0:T(8,128)(2,1)S(1)}, u32[]{:S(2)}, u32[]{:S(2)}) %collective-permute-start.29) | collective-permute-done | bytes 524320 | tf_op jit(solution)/shard_map/ppermute | solution.py:1013
  561.9 13.9 %collective-permute-done.32 = bf16[256,1024]{1,0:T(8,128)(2,1)S(1)} collective-permute-done((bf16[256,1024]{1,0:T(8,128)(2,1)S(1)}, bf16[256,1024]{1,0:T(8,128)(2,1)S(1)}, u32[]{:S(2)}, u32[]{:S(2)}) %collective-permute-start.32) | collective-permute-done | bytes 524320 | tf_op jit(solution)/shard_map/ppermute | solution.py:1013
  613.6 31.8 %attention_backward.3 = bf16[8,192,512]{2,1,0:T(8,128)(2,1)} custom-call(s32[4]{0:T(128)S(1)} %bitcast.345, bf16[8,192,512]{2,1,0:T(8,128)(2,1)S(1)} %copy-done.15, bf16[16,64,256]{2,1,0:T(8,128)(2,1)} %get-tuple-element.165.out_ref, bf16[16,64,256]{2,1,0:T(8,128)(2,1)} %all-to-all-done.6.grad_ref, f32[16,1,256]{2,1,0:T(1,128)S(1)} %get-tuple-element.247.lse_ref), custom_call_target="tpu_custom_call" | custom-call | flops 1 | bytes 1 | tf_op jit(solution)/shard_map/attention_backward/pallas_call | solution.py:770
  658.2 12.2 %all-to-all-done.7 = bf16[8,192,512]{2,1,0:T(8,128)(2,1)S(1)} async-done(((bf16[8,192,512]{2,1,0:T(8,128)(2,1)}), bf16[8,192,512]{2,1,0:T(8,128)(2,1)S(1)}, u32[]{:S(2)}, u32[]{:S(2)}) %all-to-all-start.7) | async-done | bytes 1572896 | tf_op jit(solution)/shard_map/all_to_all | solution.py:494
  742.3 8.4 %collective-permute-done.55 = bf16[128,1024]{1,0:T(8,128)(2,1)S(1)} collective-permute-done((bf16[128,1024]{1,0:T(8,128)(2,1)S(1)}, bf16[128,1024]{1,0:T(8,128)(2,1)S(1)}, u32[]{:S(2)}, u32[]{:S(2)}) %collective-permute-start.55) | collective-permute-done | bytes 262176 | tf_op jit(solution)/shard_map/ppermute | solution.py:1022
  769.3 11.3 %collective-permute-done.58 = bf16[256,1024]{1,0:T(8,128)(2,1)S(1)} collective-permute-done((bf16[256,1024]{1,0:T(8,128)(2,1)S(1)}, bf16[256,1024]{1,0:T(8,128)(2,1)S(1)}, u32[]{:S(2)}, u32[]{:S(2)}) %collective-permute-start.58) | collective-permute-done | bytes 524320 | tf_op jit(solution)/shard_map/ppermute | solution.py:1004
  782.1 7.0 all-to-all-done.8
  (671 shorter events, 409.0 us)
Async XLA Ops:
  7.2 167.5 %all-gather.7.cloned.1.call-start = ((), (), s32[]{:S(2)}) async-start(), calls=%async_computation.10 | async-start | bytes 9191424 | tf_op jit(solution)/shard_map/all_gather | solution.py:1034
  62.6 31.2 %collective-permute-start.6 = (bf16[4,128,1024]{2,1,0:T(8,128)(2,1)S(1)}, bf16[4,128,1024]{2,1,0:T(8,128)(2,1)}, u32[]{:S(2)}, u32[]{:S(2)}) collective-permute-start(bf16[4,128,1024]{2,1,0:T(8,128)(2,1)S(1)} %bitcast.380), channel_id=1, source_target_pairs={{0,8},{4,12},{8,0},{12,4},{1,9},{5,13},{9,1},{13,5},{2,10},{6,14},... | collective-permute-start | bytes 3145736 | tf_op jit(solution)/shard_map/ppermute | solution.py:1016
  107.4 35.6 %all-to-all-start = ((bf16[8,192,512]{2,1,0:T(8,128)(2,1)}), bf16[8,192,512]{2,1,0:T(8,128)(2,1)S(1)}, u32[]{:S(2)}, u32[]{:S(2)}) async-start(bf16[8,192,512]{2,1,0:T(8,128)(2,1)} %fusion.62), calls=%async_computation | async-start | bytes 3145728 | tf_op jit(solution)/shard_map/all_to_all | solution.py:494
  168.7 160.2 %all-gather.9.cloned.1.call-start = ((), (), s32[]{:S(2)}) async-start(), calls=%async_computation.11 | async-start | bytes 9191424 | tf_op jit(solution)/shard_map/all_gather | solution.py:1034
  212.8 30.3 %collective-permute-start.14 = (bf16[4,128,1024]{2,1,0:T(8,128)(2,1)S(1)}, bf16[4,128,1024]{2,1,0:T(8,128)(2,1)S(1)}, u32[]{:S(2)}, u32[]{:S(2)}) collective-permute-start(bf16[4,128,1024]{2,1,0:T(8,128)(2,1)S(1)} %bitcast.382), channel_id=1, source_target_pairs={{0,8},{4,12},{8,0},{12,4},{1,9},{5,13},{9,1},{13,5},{2,10},{6,14},... | collective-permute-start | bytes 3145736 | tf_op jit(solution)/shard_map/ppermute | solution.py:1016
  306.1 28.8 %collective-permute-start.17 = (bf16[2,4,32,1024]{3,2,1,0:T(8,128)(2,1)}, bf16[2,4,32,1024]{3,2,1,0:T(8,128)(2,1)}, u32[]{:S(2)}, u32[]{:S(2)}) collective-permute-start(bf16[2,4,32,1024]{3,2,1,0:T(8,128)(2,1)} %pad_maximum_fusion.23), channel_id=1, source_target_pairs={{0,4},{4,0},{8,12},{12,8},{1,5},{5,1},{9,13},{13,9},{2,6},{6,2},{1... | collective-permute-start | bytes 1572872 | tf_op jit(solution)/shard_map/ppermute | solution.py:1013
  390.2 28.6 %collective-permute-start.23 = (bf16[8,264,1024]{2,1,0:T(8,128)(2,1)}, bf16[8,264,1024]{2,1,0:T(8,128)(2,1)}, u32[]{:S(2)}, u32[]{:S(2)}) collective-permute-start(bf16[8,264,1024]{2,1,0:T(8,128)(2,1)} %half_products.12), channel_id=1, source_target_pairs={{0,16},{16,0},{1,17},{17,1},{2,18},{18,2},{3,19},{19,3},{4,20},{20... | collective-permute-start | bytes 12976136 | tf_op jit(solution)/shard_map/ppermute | solution.py:1025
  428.6 40.9 %collective-permute-start.27 = (bf16[256,1024]{1,0:T(8,128)(2,1)}, bf16[256,1024]{1,0:T(8,128)(2,1)}, u32[]{:S(2)}, u32[]{:S(2)}) collective-permute-start(bf16[256,1024]{1,0:T(8,128)(2,1)} %convert_element_type.435), channel_id=1, source_target_pairs={{0,4},{4,0},{8,12},{12,8},{1,5},{5,1},{9,13},{13,9},{2,6},{6,2},{1... | collective-permute-start | bytes 1572872 | tf_op jit(solution)/shard_map/ppermute | solution.py:1013
  430.3 41.7 %collective-permute-start.25 = (bf16[256,1024]{1,0:T(8,128)(2,1)}, bf16[256,1024]{1,0:T(8,128)(2,1)S(1)}, u32[]{:S(2)}, u32[]{:S(2)}) collective-permute-start(bf16[256,1024]{1,0:T(8,128)(2,1)} %copy-done.90), channel_id=1, source_target_pairs={{0,0},{1,1},{4,4},{5,5},{8,8},{9,9},{12,12},{13,13},{18,2},{19,3},... | collective-permute-start | bytes 1572872 | tf_op jit(solution)/shard_map/ppermute | solution.py:1004
  432.1 40.7 %collective-permute-start.26 = (bf16[256,1024]{1,0:T(8,128)(2,1)}, bf16[256,1024]{1,0:T(8,128)(2,1)S(1)}, u32[]{:S(2)}, u32[]{:S(2)}) collective-permute-start(bf16[256,1024]{1,0:T(8,128)(2,1)} %copy-done.90), channel_id=1, source_target_pairs={{2,0},{3,1},{6,4},{7,5},{10,8},{11,9},{14,12},{15,13},{16,2},{17,3... | collective-permute-start | bytes 1572872 | tf_op jit(solution)/shard_map/ppermute | solution.py:1004
  438.1 35.5 %collective-permute-start.28 = (bf16[2,4,32,1024]{3,2,1,0:T(8,128)(2,1)S(1)}, bf16[2,4,32,1024]{3,2,1,0:T(8,128)(2,1)S(1)}, u32[]{:S(2)}, u32[]{:S(2)}) collective-permute-start(bf16[2,4,32,1024]{3,2,1,0:T(8,128)(2,1)S(1)} %get-tuple-element.410), channel_id=1, source_target_pairs={{0,4},{4,0},{8,12},{12,8},{1,5},{5,1},{9,13},{13,9},{2,6},{6,2},{1... | collective-permute-start | bytes 1572872 | tf_op jit(solution)/shard_map/ppermute | solution.py:1013
  474.4 32.9 %all-to-all-start.5 = ((bf16[8,192,512]{2,1,0:T(8,128)(2,1)}), bf16[8,192,512]{2,1,0:T(8,128)(2,1)}, u32[]{:S(2)}, u32[]{:S(2)}) async-start(bf16[8,192,512]{2,1,0:T(8,128)(2,1)} %copy-done.27), calls=%async_computation.5 | async-start | bytes 3145728 | tf_op jit(solution)/shard_map/all_to_all | solution.py:494
  478.7 130.8 %reduce-scatter.2.cloned.1.call-start = ((), (), s32[]{:S(2)}) async-start(), calls=%async_computation.12 | async-start | bytes 4866048 | tf_op jit(solution)/shard_map/reduce_scatter | solution.py:1267
  561.3 31.6 %collective-permute-start.33 = (bf16[8,264,1024]{2,1,0:T(8,128)(2,1)}, bf16[8,264,1024]{2,1,0:T(8,128)(2,1)}, u32[]{:S(2)}, u32[]{:S(2)}) collective-permute-start(bf16[8,264,1024]{2,1,0:T(8,128)(2,1)} %half_products.18), channel_id=1, source_target_pairs={{0,16},{16,0},{1,17},{17,1},{2,18},{18,2},{3,19},{19,3},{4,20},{20... | collective-permute-start | bytes 12976136 | tf_op jit(solution)/shard_map/ppermute | solution.py:1025
  578.4 30.6 %collective-permute-start.35 = (bf16[4,128,1024]{2,1,0:T(8,128)(2,1)}, bf16[4,128,1024]{2,1,0:T(8,128)(2,1)}, u32[]{:S(2)}, u32[]{:S(2)}) collective-permute-start(bf16[4,128,1024]{2,1,0:T(8,128)(2,1)} %get-tuple-element.240), channel_id=1, source_target_pairs={{0,8},{4,12},{8,0},{12,4},{1,9},{5,13},{9,1},{13,5},{2,10},{6,14},... | collective-permute-start | bytes 3145736 | tf_op jit(solution)/shard_map/ppermute | solution.py:1016
  580.8 28.7 %all-to-all-start.6 = ((bf16[16,64,256]{2,1,0:T(8,128)(2,1)}), bf16[16,64,256]{2,1,0:T(8,128)(2,1)}, u32[]{:S(2)}, u32[]{:S(2)}) async-start(bf16[16,64,256]{2,1,0:T(8,128)(2,1)} %bitcast.86), calls=%async_computation.6 | async-start | bytes 1048576 | tf_op jit(solution)/shard_map/all_to_all | solution.py:494
  609.5 35.9 %collective-permute-start.38 = (bf16[4,176,1024]{2,1,0:T(8,128)(2,1)}, bf16[4,176,1024]{2,1,0:T(8,128)(2,1)}, u32[]{:S(2)}, u32[]{:S(2)}) collective-permute-start(bf16[4,176,1024]{2,1,0:T(8,128)(2,1)} %get-tuple-element.249), channel_id=1, source_target_pairs={{0,8},{4,12},{8,0},{12,4},{1,9},{5,13},{9,1},{13,5},{2,10},{6,14},... | collective-permute-start | bytes 4325384 | tf_op jit(solution)/shard_map/ppermute | solution.py:1016
  609.8 35.6 %collective-permute-start.39 = (bf16[2,4,32,1024]{3,2,1,0:T(8,128)(2,1)}, bf16[2,4,32,1024]{3,2,1,0:T(8,128)(2,1)S(1)}, u32[]{:S(2)}, u32[]{:S(2)}) collective-permute-start(bf16[2,4,32,1024]{3,2,1,0:T(8,128)(2,1)} %get-tuple-element.253), channel_id=1, source_target_pairs={{0,4},{4,0},{8,12},{12,8},{1,5},{5,1},{9,13},{13,9},{2,6},{6,2},{1... | collective-permute-start | bytes 1572872 | tf_op jit(solution)/shard_map/ppermute | solution.py:1013
  612.9 32.5 %collective-permute-start.40 = (bf16[2,128,1024]{2,1,0:T(8,128)(2,1)S(1)}, bf16[2,128,1024]{2,1,0:T(8,128)(2,1)}, u32[]{:S(2)}, u32[]{:S(2)}) collective-permute-start(bf16[2,128,1024]{2,1,0:T(8,128)(2,1)S(1)} %get-tuple-element.406), channel_id=1, source_target_pairs={{0,1},{1,0},{2,3},{3,2},{4,5},{5,4},{6,7},{7,6},{8,9},{9,8},{10,11... | collective-permute-start | bytes 1572872 | tf_op jit(solution)/shard_map/ppermute | solution.py:1019
  649.9 81.6 %all-gather.11.cloned.1.call-start = ((), (), s32[]{:S(2)}) async-start(), calls=%async_computation.13 | async-start | bytes 2703360 | tf_op jit(solution)/shard_map/all_gather | solution.py:1408
  654.8 42.7 %collective-permute-start.42 = (bf16[2,176,1024]{2,1,0:T(8,128)(2,1)}, bf16[2,176,1024]{2,1,0:T(8,128)(2,1)}, u32[]{:S(2)}, u32[]{:S(2)}) collective-permute-start(bf16[2,176,1024]{2,1,0:T(8,128)(2,1)} %get-tuple-element.398), channel_id=1, source_target_pairs={{0,1},{1,0},{2,3},{3,2},{4,5},{5,4},{6,7},{7,6},{8,9},{9,8},{10,11... | collective-permute-start | bytes 2162696 | tf_op jit(solution)/shard_map/ppermute | solution.py:1019
  656.8 40.7 %collective-permute-start.43 = (bf16[4,88,1024]{2,1,0:T(8,128)(2,1)}, bf16[4,88,1024]{2,1,0:T(8,128)(2,1)}, u32[]{:S(2)}, u32[]{:S(2)}) collective-permute-start(bf16[4,88,1024]{2,1,0:T(8,128)(2,1)} %get-tuple-element.260), channel_id=1, source_target_pairs={{0,8},{4,12},{8,0},{12,4},{1,9},{5,13},{9,1},{13,5},{2,10},{6,14},... | collective-permute-start | bytes 2162696 | tf_op jit(solution)/shard_map/ppermute | solution.py:1016
  685.4 107.2 %all-gather.13.cloned.1.call-start = ((), (), s32[]{:S(2)}) async-start(), calls=%async_computation.14 | async-start | bytes 2703360 | tf_op jit(solution)/shard_map/all_gather | solution.py:1460
  752.4 36.8 %all-to-all-start.8 = ((bf16[4,256,1024]{2,1,0:T(8,128)(2,1)}), bf16[4,256,1024]{2,1,0:T(8,128)(2,1)S(1)}, u32[]{:S(2)}, u32[]{:S(2)}) async-start(bf16[4,256,1024]{2,1,0:T(8,128)(2,1)} %broadcast_in_dim.14), calls=%async_computation.9 | async-start | bytes 4194304 | tf_op jit(solution)/shard_map/all_to_all | solution.py:1028
  (209 other events, 1768.0 us)
Sparse Core Ops, SparseCore 0:
  61.4 96.9 all-gather.6
  211.3 93.3 all-gather.8
  483.7 96.8 reduce-scatter.1
  685.5 42.7 all-gather.10
  738.9 53.6 all-gather.12
